TPU v7x, 32 devices: a whole 2x2x4 slice. The times are simulated.
32 devices in a mesh: dp: 8 (over z, y), ctx: 4 (over x, core).
Axes of the slice: x: 2, y: 2, z: 4, core: 2. Of those that a mesh axis runs over, the one named last changes fastest.
Arguments:
- tokens: bfloat16 [8, 2048, 1024], P('dp', 'ctx'), may hold values from -6 to 6
- w_query: bfloat16 [1024, 2048], P(('dp', 'ctx')), may hold values from -0.1875 to 0.1875
- key_weight: bfloat16 [1024, 1024], P(('dp', 'ctx')), may hold values from -0.1875 to 0.1875
- value_weight: bfloat16 [1024, 1024], P(('dp', 'ctx')), may hold values from -0.1875 to 0.1875
- w_out: bfloat16 [2048, 1024], P(('dp', 'ctx')), may hold values from -1.5 to 1.5
- w_gate: bfloat16 [1024, 3072], P(('dp', 'ctx')), may hold values from -0.1875 to 0.1875
- w_up: bfloat16 [1024, 3072], P(('dp', 'ctx')), may hold values from -0.1875 to 0.1875
- w_down: bfloat16 [3072, 1024], P(('dp', 'ctx')), may hold values from -0.109375 to 0.109375
- gains: bfloat16 [2304], P(('dp', 'ctx')), may hold values from 0.25 to 1.75
- segment_ids: int32 [8, 2048], P('dp', 'ctx'), may hold values from 0 to 3, as said below
- positions: int32 [8, 2048], P('dp', 'ctx'), may hold values from 0 to 2047, as said below
- cotangent: bfloat16 [8, 2048, 1024], P('dp', 'ctx'), may hold values from -6 to 6
Outputs:
- output: bfloat16 [8, 2048, 1024], P('dp', 'ctx')
- grad_tokens: float32 [8, 2048, 1024], P('dp', 'ctx')
- grad_w_query: float32 [1024, 2048], P(('dp', 'ctx'))
- grad_w_key: float32 [1024, 1024], P(('dp', 'ctx'))
- grad_w_value: float32 [1024, 1024], P(('dp', 'ctx'))
- grad_w_out: float32 [2048, 1024], P(('dp', 'ctx'))
- grad_w_gate: float32 [1024, 3072], P(('dp', 'ctx'))
- grad_w_up: float32 [1024, 3072], P(('dp', 'ctx'))
- grad_w_down: float32 [3072, 1024], P(('dp', 'ctx'))
- grad_gains: float32 [2304], P(('dp', 'ctx'))
Inputs may be any that keep to these rules, and one draw needn't show every extreme that they name: `segment_ids`: segment ids never fall along a sequence and start at 0. Document 0 holds 1 to 511 tokens, document 1 follows it and ends within the last 511 tokens, and one or two further documents (ids 2 and 3, or 3 alone) fill the rest. `positions`: positions rise by one from token to token inside a document; every document but document 0 starts at 0; document 0 continues an earlier document, and its last token has position 2047.
All inputs are finite; a program needn't handle non-finite values.
Results may differ from a plain program's by a relative error of at most 0.015.
Values may be sent and summed in bfloat16 or wider, within the bound.
No kernel may reach another device: no remote copies, remote signals or barrier semaphores. Data moves between devices by JAX's collectives and lax.ppermute only.
A program may use at most 256 MiB of HBM per device.

v0:
```python
import jax
import jax.numpy as jnp
from jax import lax
from jax.sharding import PartitionSpec as P

MODEL_WIDTH = 1024
QUERY_HEADS = 16
KEY_VALUE_HEADS = 8
HEAD_SIZE = 128


EPSILON = 1e-06
THETA = 1000000.0


def row_norm_apply(value_rows, gain_vec):
    return (
        value_rows
        * lax.rsqrt(jnp.mean(value_rows * value_rows, axis=-1, keepdims=True) + EPSILON)
        * gain_vec
    )


def rotary_embed(value_rows, token_positions):
    half_size = value_rows.shape[-1] // 2
    inverse_rates = THETA ** (
        -2.0 * jnp.arange(half_size, dtype=jnp.float32) / value_rows.shape[-1]
    )
    angles = token_positions.astype(jnp.float32)[:, None] * inverse_rates[None, :]
    cosine = jnp.cos(angles)[:, None, :]
    sine_part = jnp.sin(angles)[:, None, :]
    former = value_rows[..., :half_size]
    second = value_rows[..., half_size:]
    return jnp.concatenate(
        [former * cosine - second * sine_part, second * cosine + former * sine_part], axis=-1
    )


def heads_per_group(raw_rows, gain_vec, token_positions, head_count):
    return rotary_embed(
        row_norm_apply(raw_rows.reshape(raw_rows.shape[0], head_count, HEAD_SIZE), gain_vec),
        token_positions,
    )


def split_gains(packed):
    packed = packed.astype(jnp.float32)
    return (
        packed[:MODEL_WIDTH],
        packed[MODEL_WIDTH : 2 * MODEL_WIDTH],
        packed[2 * MODEL_WIDTH : 2 * MODEL_WIDTH + HEAD_SIZE],
        packed[2 * MODEL_WIDTH + HEAD_SIZE :],
    )


def owner_major(grad_full, owners):
    return grad_full.reshape(owners, -1)


def local(
    tokens,
    w_query,
    key_weight,
    value_weight,
    w_out,
    w_gate,
    w_up,
    w_down,
    gains,
    segment_ids,
    positions,
    cotangent,
):
    sequence_count = tokens.shape[0]
    device_local_rows = tokens.shape[1]
    every_row_set = sequence_count * device_local_rows
    inputs = tokens.reshape(every_row_set, MODEL_WIDTH).astype(jnp.float32)
    token_positions = positions.reshape(every_row_set)
    cot_rows = cotangent.reshape(every_row_set, MODEL_WIDTH)
    head_groups = QUERY_HEADS // KEY_VALUE_HEADS
    score_scale = HEAD_SIZE ** (-0.5)
    f32 = jnp.float32
    brain_float_half = jnp.bfloat16
    owners = lax.axis_size(("dp", "ctx"))
    shard_shapes = (
        w_query.shape,
        key_weight.shape,
        value_weight.shape,
        w_out.shape,
        w_gate.shape,
        w_up.shape,
        w_down.shape,
        gains.shape,
    )
    gathered = (
        lax.all_gather(w_query, ("dp", "ctx"), axis=0, tiled=True),
        lax.all_gather(key_weight, ("dp", "ctx"), axis=0, tiled=True),
        lax.all_gather(value_weight, ("dp", "ctx"), axis=0, tiled=True),
        lax.all_gather(w_out, ("dp", "ctx"), axis=0, tiled=True),
        lax.all_gather(w_gate, ("dp", "ctx"), axis=0, tiled=True),
        lax.all_gather(w_up, ("dp", "ctx"), axis=0, tiled=True),
        lax.all_gather(w_down, ("dp", "ctx"), axis=0, tiled=True),
        lax.all_gather(gains, ("dp", "ctx"), axis=0, tiled=True),
    )
    full_query, full_key, full_value, full_out, full_gate, full_up, full_down, full_gains = gathered
    gain_attn, gain_mlp, gain_query, key_norm_gain = split_gains(full_gains)
    normalized_input = row_norm_apply(inputs, gain_attn).astype(brain_float_half)
    query_raw = jnp.dot(normalized_input, full_query, preferred_element_type=f32)
    unrotated_keys = jnp.dot(normalized_input, full_key, preferred_element_type=f32)
    value_low = (
        jnp.dot(normalized_input, full_value, preferred_element_type=f32)
        .astype(brain_float_half)
        .reshape(sequence_count, device_local_rows, KEY_VALUE_HEADS * HEAD_SIZE)
    )
    reduced_queries = heads_per_group(query_raw, gain_query, token_positions, QUERY_HEADS).astype(
        brain_float_half
    )
    key_low = (
        heads_per_group(unrotated_keys, key_norm_gain, token_positions, KEY_VALUE_HEADS)
        .astype(brain_float_half)
        .reshape(sequence_count, device_local_rows, KEY_VALUE_HEADS * HEAD_SIZE)
    )
    segment_low = segment_ids.astype(brain_float_half)
    gathered_keys, gathered_values, segment_all = (
        lax.all_gather(key_low, "ctx", axis=1, tiled=True),
        lax.all_gather(value_low, "ctx", axis=1, tiled=True),
        lax.all_gather(segment_low, "ctx", axis=1, tiled=True),
    )
    overall_rows = gathered_keys.shape[1]
    query_index = lax.axis_index("ctx") * device_local_rows + jnp.arange(
        device_local_rows, dtype=jnp.int32
    )
    key_index = jnp.arange(overall_rows, dtype=jnp.int32)
    allowed = (segment_low[:, :, None] == segment_all[:, None, :]) & (
        query_index[None, :, None] >= key_index[None, None, :]
    )
    grouped_queries = reduced_queries.reshape(
        sequence_count, device_local_rows, KEY_VALUE_HEADS, head_groups, HEAD_SIZE
    ).transpose(0, 2, 3, 1, 4)
    grouped_keys = gathered_keys.reshape(
        sequence_count, overall_rows, KEY_VALUE_HEADS, HEAD_SIZE
    ).transpose(0, 2, 1, 3)
    grouped_values = gathered_values.reshape(
        sequence_count, overall_rows, KEY_VALUE_HEADS, HEAD_SIZE
    ).transpose(0, 2, 1, 3)

    def masked_scores(query_head, key_head, mask_rows):
        scores = (
            jnp.einsum("rld,kd->rlk", query_head, key_head, preferred_element_type=f32)
            * score_scale
        )
        return jnp.where(mask_rows[None], scores, -1e30)

    def forward_sequence(slices):
        query_seq, key_seq, value_seq, mask_rows = slices

        def forward_head(head_slices):
            query_head, key_head, value_head = head_slices
            scores = masked_scores(query_head, key_head, mask_rows)
            row_peak = jnp.max(scores, axis=-1, keepdims=True)
            exp_scores = jnp.exp(scores - row_peak)
            denominator = jnp.sum(exp_scores, axis=-1, keepdims=True)
            prob_low = (exp_scores / denominator).astype(brain_float_half)
            mixed_head = jnp.einsum("rlk,kd->rld", prob_low, value_head, preferred_element_type=f32)
            return (mixed_head, row_peak[..., 0] + jnp.log(denominator[..., 0]))

        return lax.map(forward_head, (query_seq, key_seq, value_seq))

    mixed_heads, log_totals = lax.map(
        forward_sequence, (grouped_queries, grouped_keys, grouped_values, allowed)
    )
    attended = (
        mixed_heads.transpose(0, 3, 1, 2, 4)
        .reshape(every_row_set, QUERY_HEADS * HEAD_SIZE)
        .astype(brain_float_half)
    )
    middle = inputs + jnp.dot(attended, full_out, preferred_element_type=f32)
    normed_mlp = row_norm_apply(middle, gain_mlp).astype(brain_float_half)
    gate_value = jnp.dot(normed_mlp, full_gate, preferred_element_type=f32)
    up_value = jnp.dot(normed_mlp, full_up, preferred_element_type=f32)
    hidden = (jax.nn.silu(gate_value) * up_value).astype(brain_float_half)
    output = (middle + jnp.dot(hidden, full_down, preferred_element_type=f32)).astype(
        brain_float_half
    )
    regathered = (
        lax.all_gather(w_query, ("dp", "ctx"), axis=0, tiled=True),
        lax.all_gather(key_weight, ("dp", "ctx"), axis=0, tiled=True),
        lax.all_gather(value_weight, ("dp", "ctx"), axis=0, tiled=True),
        lax.all_gather(w_out, ("dp", "ctx"), axis=0, tiled=True),
        lax.all_gather(w_gate, ("dp", "ctx"), axis=0, tiled=True),
        lax.all_gather(w_up, ("dp", "ctx"), axis=0, tiled=True),
        lax.all_gather(w_down, ("dp", "ctx"), axis=0, tiled=True),
        lax.all_gather(gains, ("dp", "ctx"), axis=0, tiled=True),
    )
    back_query, back_key, back_value, back_out, back_gate, back_up, back_down, back_gains = (
        regathered
    )
    gain_attn, gain_mlp, gain_query, key_norm_gain = split_gains(back_gains)
    d_hidden = jnp.einsum("ld,fd->lf", cot_rows, back_down, preferred_element_type=f32)
    grad_down = jnp.einsum("lf,ld->fd", hidden, cot_rows, preferred_element_type=f32)
    unused, swiglu_pull = jax.vjp(
        lambda gate_in, up_in: jax.nn.silu(gate_in) * up_in, gate_value, up_value
    )
    d_gate, d_up = swiglu_pull(d_hidden)
    d_gate = d_gate.astype(brain_float_half)
    d_up = d_up.astype(brain_float_half)
    grad_gate = jnp.einsum("ld,lf->df", normed_mlp, d_gate, preferred_element_type=f32)
    grad_up = jnp.einsum("ld,lf->df", normed_mlp, d_up, preferred_element_type=f32)
    d_normed = jnp.einsum("lf,df->ld", d_gate, back_gate, preferred_element_type=f32)
    d_normed = d_normed + jnp.einsum("lf,df->ld", d_up, back_up, preferred_element_type=f32)
    unused, norm_pull = jax.vjp(row_norm_apply, middle, gain_mlp)
    d_middle, d_gain_mlp = norm_pull(d_normed)
    d_middle = d_middle + cot_rows.astype(f32)
    d_branch = d_middle.astype(brain_float_half)
    grad_out = jnp.einsum("lh,ld->hd", attended, d_branch, preferred_element_type=f32)
    attended_gradient = jnp.einsum(
        "ld,hd->lh", d_branch, back_out, preferred_element_type=f32
    ).astype(brain_float_half)
    group_gradient = attended_gradient.reshape(
        sequence_count, device_local_rows, KEY_VALUE_HEADS, head_groups, HEAD_SIZE
    ).transpose(0, 2, 3, 1, 4)

    def backward_sequence(slices):
        query_seq, key_seq, value_seq, d_seq, log_seq, mask_rows = slices

        def backward_head(head_slices):
            query_head, key_head, value_head, d_head, log_total = head_slices
            scores = masked_scores(query_head, key_head, mask_rows)
            probs_full = jnp.exp(scores - log_total[..., None])
            prob_low = probs_full.astype(brain_float_half)
            d_value = jnp.einsum("rlk,rld->kd", prob_low, d_head, preferred_element_type=f32)
            d_probs = jnp.einsum("rld,kd->rlk", d_head, value_head, preferred_element_type=f32)
            d_scores = probs_full * (
                d_probs - jnp.sum(probs_full * d_probs, axis=-1, keepdims=True)
            )
            d_scores = d_scores.astype(brain_float_half)
            d_query = (
                jnp.einsum("rlk,kd->rld", d_scores, key_head, preferred_element_type=f32)
                * score_scale
            )
            d_key = (
                jnp.einsum("rlk,rld->kd", d_scores, query_head, preferred_element_type=f32)
                * score_scale
            )
            return (d_query, d_key, d_value)

        return lax.map(backward_head, (query_seq, key_seq, value_seq, d_seq, log_seq))

    d_queries, key_rows_gradient, value_rows_gradient = lax.map(
        backward_sequence,
        (grouped_queries, grouped_keys, grouped_values, group_gradient, log_totals, allowed),
    )
    gathered_key_gradient = key_rows_gradient.transpose(2, 0, 1, 3).reshape(
        overall_rows, sequence_count, KEY_VALUE_HEADS * HEAD_SIZE
    )
    gathered_value_gradient = value_rows_gradient.transpose(2, 0, 1, 3).reshape(
        overall_rows, sequence_count, KEY_VALUE_HEADS * HEAD_SIZE
    )
    local_key_gradient, local_value_gradient = (
        lax.psum_scatter(
            gathered_key_gradient.astype(jnp.bfloat16), "ctx", scatter_dimension=0, tiled=True
        ).astype(jnp.float32),
        lax.psum_scatter(
            gathered_value_gradient.astype(jnp.bfloat16), "ctx", scatter_dimension=0, tiled=True
        ).astype(jnp.float32),
    )
    local_key_gradient = local_key_gradient.transpose(1, 0, 2)
    local_value_gradient = local_value_gradient.transpose(1, 0, 2)
    d_query_heads = d_queries.transpose(0, 3, 1, 2, 4).reshape(
        every_row_set, QUERY_HEADS, HEAD_SIZE
    )
    unused, query_pull = jax.vjp(
        lambda unnormalized_input, input_gain_vector: heads_per_group(
            unnormalized_input, input_gain_vector, token_positions, QUERY_HEADS
        ),
        query_raw,
        gain_query,
    )
    d_query_raw, d_gain_query = query_pull(d_query_heads)
    unused, key_pullback = jax.vjp(
        lambda unnormalized_input, input_gain_vector: heads_per_group(
            unnormalized_input, input_gain_vector, token_positions, KEY_VALUE_HEADS
        ),
        unrotated_keys,
        key_norm_gain,
    )
    unrotated_key_gradient, key_gain_gradient = key_pullback(
        local_key_gradient.reshape(every_row_set, KEY_VALUE_HEADS, HEAD_SIZE)
    )
    d_query_low = d_query_raw.astype(brain_float_half)
    d_key_low = unrotated_key_gradient.astype(brain_float_half)
    reduced_value_gradient = local_value_gradient.reshape(
        every_row_set, KEY_VALUE_HEADS * HEAD_SIZE
    ).astype(brain_float_half)
    grad_query = jnp.einsum("ld,lh->dh", normalized_input, d_query_low, preferred_element_type=f32)
    grad_key = jnp.einsum("ld,lh->dh", normalized_input, d_key_low, preferred_element_type=f32)
    grad_value = jnp.einsum(
        "ld,lh->dh", normalized_input, reduced_value_gradient, preferred_element_type=f32
    )
    d_normed_attn = jnp.einsum("lh,dh->ld", d_query_low, back_query, preferred_element_type=f32)
    d_normed_attn = d_normed_attn + jnp.einsum(
        "lh,dh->ld", d_key_low, back_key, preferred_element_type=f32
    )
    d_normed_attn = d_normed_attn + jnp.einsum(
        "lh,dh->ld", reduced_value_gradient, back_value, preferred_element_type=f32
    )
    unused, first_pull = jax.vjp(row_norm_apply, inputs, gain_attn)
    d_inputs, d_gain_attn = first_pull(d_normed_attn)
    grad_tokens = (d_middle + d_inputs).reshape(sequence_count, device_local_rows, MODEL_WIDTH)
    grad_gains = jnp.concatenate([d_gain_attn, d_gain_mlp, d_gain_query, key_gain_gradient])
    summed = (
        lax.psum_scatter(
            owner_major(grad_query, owners), ("dp", "ctx"), scatter_dimension=0, tiled=True
        ),
        lax.psum_scatter(
            owner_major(grad_key, owners), ("dp", "ctx"), scatter_dimension=0, tiled=True
        ),
        lax.psum_scatter(
            owner_major(grad_value, owners), ("dp", "ctx"), scatter_dimension=0, tiled=True
        ),
        lax.psum_scatter(
            owner_major(grad_out, owners), ("dp", "ctx"), scatter_dimension=0, tiled=True
        ),
        lax.psum_scatter(
            owner_major(grad_gate, owners), ("dp", "ctx"), scatter_dimension=0, tiled=True
        ),
        lax.psum_scatter(
            owner_major(grad_up, owners), ("dp", "ctx"), scatter_dimension=0, tiled=True
        ),
        lax.psum_scatter(
            owner_major(grad_down, owners), ("dp", "ctx"), scatter_dimension=0, tiled=True
        ),
        lax.psum_scatter(
            owner_major(grad_gains, owners), ("dp", "ctx"), scatter_dimension=0, tiled=True
        ),
    )
    grad_query = summed[0].reshape(shard_shapes[0])
    grad_key = summed[1].reshape(shard_shapes[1])
    grad_value = summed[2].reshape(shard_shapes[2])
    grad_out = summed[3].reshape(shard_shapes[3])
    grad_gate = summed[4].reshape(shard_shapes[4])
    grad_up = summed[5].reshape(shard_shapes[5])
    grad_down = summed[6].reshape(shard_shapes[6])
    grad_gains = summed[7].reshape(shard_shapes[7])
    return (
        output.reshape(sequence_count, device_local_rows, MODEL_WIDTH),
        grad_tokens,
        grad_query,
        grad_key,
        grad_value,
        grad_out,
        grad_gate,
        grad_up,
        grad_down,
        grad_gains,
    )


def solution(mesh):
    return jax.shard_map(
        local,
        mesh=mesh,
        in_specs=(
            P("dp", "ctx", None),
            P(("dp", "ctx"), None),
            P(("dp", "ctx"), None),
            P(("dp", "ctx"), None),
            P(("dp", "ctx"), None),
            P(("dp", "ctx"), None),
            P(("dp", "ctx"), None),
            P(("dp", "ctx"), None),
            P(("dp", "ctx")),
            P("dp", "ctx"),
            P("dp", "ctx"),
            P("dp", "ctx", None),
        ),
        out_specs=(
            P("dp", "ctx", None),
            P("dp", "ctx", None),
            P(("dp", "ctx"), None),
            P(("dp", "ctx"), None),
            P(("dp", "ctx"), None),
            P(("dp", "ctx"), None),
            P(("dp", "ctx"), None),
            P(("dp", "ctx"), None),
            P(("dp", "ctx"), None),
            P(("dp", "ctx")),
        ),
        check_vma=False,
    )
```

profile of v0, /device:TPU:27, one launch (start us, length us, event | category | flops | bytes accessed | tf_op | source)
XLA Modules:
  0.0 1792.3 jit_solution(467685173860914227)
XLA Ops:
  10.3 38.4 %all-reduce.4 = bf16[2304]{0:T(1024)(128)(2,1)S(1)} all-reduce(bf16[2304]{0:T(1024)(128)(2,1)S(1)} %dynamic-update-slice), channel_id=1, replica_groups=mesh['dp'=8,'ctx'=4] {'dp','ctx'}, use_global_device_ids=true, to_apply=%add.4 | all-reduce | flops 2304 | bytes 9216
  50.8 16.7 all-gather.17.cloned.1.call-done
  67.5 4.2 convolution_convert_fusion.1
  72.4 53.2 %all-gather.13.cloned.1.call-done = bf16[1024,1024]{1,0:T(8,128)(2,1)} async-done(((bf16[32,1024]{1,0:T(8,128)(2,1)}), bf16[1024,1024]{1,0:T(8,128)(2,1)}) %all-gather.13.cloned.1.call-update) | async-done | bytes 2097168 | tf_op jit(solution)/shard_map/all_gather | solution.py:97
  135.5 5.5 all_gather.43
  141.1 47.9 %all-gather.11.cloned.1.call-done = bf16[1024,2048]{1,0:T(8,128)(2,1)} async-done(((bf16[32,2048]{1,0:T(8,128)(2,1)}), bf16[1024,2048]{1,0:T(8,128)(2,1)}) %all-gather.11.cloned.1.call-update) | async-done | bytes 4194320 | tf_op jit(solution)/shard_map/all_gather | solution.py:96
  188.9 6.4 copy.48
  195.3 4.9 multiply_reduce_fusion.3
  211.9 12.2 all-gather.27.cloned.1.call-done
  230.1 30.0 %all-gather.15.cloned.1.call-done = bf16[1,2048,1024]{1,2,0:T(8,128)(2,1)} async-done(((bf16[1,512,1024]{1,2,0:T(8,128)(2,1)}), bf16[1,2048,1024]{1,2,0:T(8,128)(2,1)}) %all-gather.15.cloned.1.call-update) | async-done | bytes 4194320 | tf_op jit(solution)/shard_map/all_gather | solution.py:125
  260.1 6.6 copy.53
  266.7 87.1 %while.48 = (s32[]{:T(128)}, bf16[8,2,512,128]{2,3,1,0:T(8,128)(2,1)S(1)}, f32[8,2,512]{2,1,0:T(2,128)S(1)}, bf16[8,2,512,128]{3,2,1,0:T(8,128)(2,1)}, bf16[8,20...) while((s32[]{:T(128)}, ...), condition=%wide.region_6.7_spmd.clone, body=%wide.region_3.6_spmd.clone.sunk | while | flops 1104149504 | bytes 31237232 | solution.py:167
  355.1 5.3 multiply_reduce_fusion.8
  360.6 34.6 %all-gather.23.cloned.1.call-done = bf16[1024,3072]{1,0:T(8,128)(2,1)} async-done(((bf16[32,3072]{1,0:T(8,128)(2,1)}), bf16[1024,3072]{1,0:T(8,128)(2,1)}) %all-gather.23.cloned.1.call-update) | async-done | bytes 6291472 | tf_op jit(solution)/shard_map/all_gather | solution.py:101
  395.3 8.1 fusion.118
  403.3 62.8 %all-gather.21.cloned.1.call-done = bf16[1024,3072]{1,0:T(8,128)(2,1)} async-done(((bf16[32,3072]{1,0:T(8,128)(2,1)}), bf16[1024,3072]{1,0:T(8,128)(2,1)}) %all-gather.21.cloned.1.call-update) | async-done | bytes 6291472 | tf_op jit(solution)/shard_map/all_gather | solution.py:100
  466.2 8.0 fusion.117
  474.2 62.9 %all-gather.25.cloned.1.call-done = bf16[3072,1024]{1,0:T(8,128)(2,1)} async-done(((bf16[96,1024]{1,0:T(8,128)(2,1)}), bf16[3072,1024]{1,0:T(8,128)(2,1)}) %all-gather.25.cloned.1.call-update) | async-done | bytes 6291472 | tf_op jit(solution)/shard_map/all_gather | solution.py:102
  537.1 12.2 multiply_convert_fusion.1
  552.8 6.6 multiply_reduce_fusion.5
  566.1 4.4 reshape.465
  574.0 168.3 %while.49 = (s32[]{:T(128)}, f32[8,2,512,128]{3,2,1,0:T(8,128)}, bf16[8,2048,128]{1,2,0:T(8,128)(2,1)}, bf16[8,2048,128]{1,2,0:T(8,128)(2,1)}, bf16[8,2,512,128]...) while((s32[]{:T(128)}, f32[8,2,512,128]{3,2,1,0:T(8,128)}, ...), condition=%wide.region_11.12_spmd.clone, body=%wide.region_9.11_spmd.clone.sunk | while | flops 2721709056 | bytes 73964688 | solution.py:247
  577.8 4.3 fusion.190
  598.8 4.3 fusion.190
  619.8 4.3 fusion.190
  640.8 4.3 fusion.190
  661.8 4.3 fusion.190
  682.9 4.3 fusion.190
  703.9 4.3 fusion.190
  724.9 4.3 fusion.190
  743.1 5.8 copy.57
  748.9 7.2 fusion.102
  756.1 7.9 reshape.474
  772.1 5.9 fusion.95
  778.0 7.7 reshape.468
  785.7 10.5 fusion.87
  796.2 10.2 reshape.480
  806.4 10.3 fusion.122
  816.7 9.9 reshape.478
  826.6 10.2 fusion.121
  836.8 10.2 reshape.476
  855.1 4.9 reshape.470
  860.0 4.7 fusion.83
  864.7 5.0 reshape.472
  869.7 8.8 fusion.81
  887.9 42.2 %all-reduce.12 = f32[32,72]{1,0:T(8,128)S(1)} all-reduce(f32[32,72]{1,0:T(8,128)S(1)} %reshape.482), channel_id=12, replica_groups=mesh['dp'=8,'ctx'=4] {'dp','ctx'}, use_global_device_ids=true, to_apply=%region_28.29.clone | all-reduce | flops 2304 | bytes 18432
  934.1 831.9 %all-reduce.16.cloned.1.call-done = (f32[32,65536]{1,0:T(8,128)}, f32[32,32768]{1,0:T(8,128)}, f32[32,32768]{1,0:T(8,128)}, f32[32,65536]{1,0:T(8,128)}, f32[32,...) async-done(((f32[32,65536]{1,0:T(8,128)}, f32[32,32768]{1,0:T(8,128)}, f32[32,32768]{1,0:T(8,128)}, f32[32,65536]{1,0:T(8,128)}, f32[32,98304]{1,0:T(8,128)}, ...) | async-done | bytes 62914576
  1777.6 5.0 dynamic-slice_reduce_fusion
  (304 shorter events, 312.1 us)
Async XLA Ops:
  7.2 60.3 %all-gather.17.cloned.1.call-start = ((), (), s32[]{:S(2)}) async-start(), calls=%async_computation.5 | async-start | bytes 2162688 | tf_op jit(solution)/shard_map/all_gather | solution.py:98
  7.9 117.7 %all-gather.13.cloned.1.call-start = ((), (), s32[]{:S(2)}) async-start(), calls=%async_computation.3 | async-start | bytes 2162688 | tf_op jit(solution)/shard_map/all_gather | solution.py:97
  8.7 180.3 %all-gather.11.cloned.1.call-start = ((), (), s32[]{:S(2)}) async-start(), calls=%async_computation.2 | async-start | bytes 4325376 | tf_op jit(solution)/shard_map/all_gather | solution.py:96
  9.4 214.8 %all-gather.27.cloned.1.call-start = ((), (), s32[]{:S(2)}) async-start(), calls=%async_computation.12 | async-start | bytes 5242880 | tf_op jit(solution)/shard_map/all_gather | solution.py:126
  50.8 144.5 %copy-start.34 = (f32[512]{0:T(512)}, f32[512]{0:T(512)S(1)}, u32[]{:S(2)}) copy-start(f32[512]{0:T(512)S(1)} %fusion.107) | copy-start | bytes 6148
  50.8 144.5 %copy-start.32 = (f32[1024]{0:T(1024)}, f32[1024]{0:T(1024)S(1)}, u32[]{:S(2)}) copy-start(f32[1024]{0:T(1024)S(1)} %get-tuple-element.325) | copy-start | bytes 12292
  67.5 4.3 copy-start.42
  71.7 56.7 %copy-start.6 = (bf16[1,512,1024]{2,1,0:T(8,128)(2,1)S(1)}, bf16[1,512,1024]{2,1,0:T(8,128)(2,1)}, u32[]{:S(2)}) copy-start(bf16[1,512,1024]{2,1,0:T(8,128)(2,1)} %param.16) | copy-start | bytes 3145732
  71.8 188.3 %all-gather.15.cloned.1.call-start = ((), (), s32[]{:S(2)}) async-start(), calls=%async_computation.4 | async-start | bytes 5242880 | tf_op jit(solution)/shard_map/all_gather | solution.py:125
  71.9 58.6 %copy-start.37 = (f32[128]{0:T(128)}, f32[128]{0:T(128)S(1)}, u32[]{:S(2)}) copy-start(f32[128]{0:T(128)S(1)} %get-tuple-element.326) | copy-start | bytes 1540
  71.9 128.5 %copy-start.39 = (f32[128]{0:T(128)}, f32[128]{0:T(128)S(1)}, u32[]{:S(2)}) copy-start(f32[128]{0:T(128)S(1)} %get-tuple-element.327) | copy-start | bytes 1540
  72.4 128.7 %copy-start.9 = (f32[512,64]{0,1:T(8,128)}, f32[512,64]{0,1:T(8,128)S(1)}, u32[]{:S(2)}) copy-start(f32[512,64]{0,1:T(8,128)S(1)} %get-tuple-element.328) | copy-start | bytes 393220
  72.4 128.7 %copy-start.11 = (f32[512,64]{0,1:T(8,128)}, f32[512,64]{0,1:T(8,128)S(1)}, u32[]{:S(2)}) copy-start(f32[512,64]{0,1:T(8,128)S(1)} %get-tuple-element.329) | copy-start | bytes 393220
  131.1 4.3 copy-start.36
  132.6 221.2 %all-gather.19.cloned.1.call-start = ((), (), s32[]{:S(2)}) async-start(), calls=%async_computation.6 | async-start | bytes 4325376 | tf_op jit(solution)/shard_map/all_gather | solution.py:99
  133.1 262.1 %all-gather.23.cloned.1.call-start = ((), (), s32[]{:S(2)}) async-start(), calls=%async_computation.8 | async-start | bytes 6488064 | tf_op jit(solution)/shard_map/all_gather | solution.py:101
  133.9 332.3 %all-gather.21.cloned.1.call-start = ((), (), s32[]{:S(2)}) async-start(), calls=%async_computation.7 | async-start | bytes 6488064 | tf_op jit(solution)/shard_map/all_gather | solution.py:100
  134.6 402.5 %all-gather.25.cloned.1.call-start = ((), (), s32[]{:S(2)}) async-start(), calls=%async_computation.9 | async-start | bytes 6488064 | tf_op jit(solution)/shard_map/all_gather | solution.py:102
  135.4 711.7 %reduce-scatter.3.cloned.1.call-start = ((), (), s32[]{:S(2)}) async-start(), calls=%async_computation.10 | async-start | bytes 5242880 | tf_op jit(solution)/shard_map/reduce_scatter | solution.py:260
  200.3 2.0 copy-start
  200.3 2.0 copy-start.26
  260.1 6.6 copy-start.13
  266.7 88.4 %copy-start.7 = (bf16[1,512,1024]{2,1,0:T(8,128)(2,1)S(1)}, bf16[1,512,1024]{2,1,0:T(8,128)(2,1)}, u32[]{:S(2)}) copy-start(bf16[1,512,1024]{2,1,0:T(8,128)(2,1)} %param.16) | copy-start | bytes 3145732
  360.4 192.5 %copy-start.4 = (f32[512,1024]{1,0:T(8,128)}, f32[512,1024]{1,0:T(8,128)S(1)}, u32[]{:S(2)}) copy-start(f32[512,1024]{1,0:T(8,128)S(1)} %get-tuple-element.335) | copy-start | bytes 6291460
  360.6 105.6 %copy-start.18 = (bf16[512,1024]{1,0:T(8,128)(2,1)}, bf16[512,1024]{1,0:T(8,128)(2,1)S(1)}, u32[]{:S(2)}) copy-start(bf16[512,1024]{1,0:T(8,128)(2,1)S(1)} %multiply_convert_fusion.3) | copy-start | bytes 3145732
  537.1 12.2 copy-start.43
  549.3 3.5 copy-start.47
  549.3 3.5 copy-start.48
  552.8 6.6 copy-start.19
  559.5 2.8 copy-start.44
  742.3 117.7 %reduce-scatter.5.cloned.1.call-start = ((), (), s32[]{:S(2)}) async-start(), calls=%async_computation.11 | async-start | bytes 5242880 | tf_op jit(solution)/shard_map/reduce_scatter | solution.py:263
  743.1 1022.9 %all-reduce.16.cloned.1.call-start = ((), (), s32[]{:S(2)}) async-start(), calls=%async_computation.13 | async-start | bytes 125829120
  756.1 7.9 copy-start.10
  756.1 7.9 copy-start.12
  764.1 3.5 copy-start.1
  764.1 3.5 copy-start.23
  764.1 3.4 copy-start.40
  769.5 2.6 copy-start.8
  769.5 2.6 copy-start.33
  769.5 2.6 copy-start.35
  847.1 2.0 copy-start.3
  847.1 2.0 copy-start.25
  869.7 8.9 copy-start.45
  869.7 8.8 copy-start.46
  880.5 2.3 copy-start.5
  880.5 3.0 copy-start.17
  883.6 4.2 copy-start.41
  883.6 47.0 %copy-start.31 = (f32[512]{0:T(512)S(1)}, f32[512]{0:T(512)}, u32[]{:S(2)}) copy-start(f32[512]{0:T(512)} %copy-done.30) | copy-start | bytes 6148
  (13 other events, 18.2 us)
Sparse Core Ops, SparseCore 0:
  10.9 56.5 all-gather.16
  70.4 55.2 all-gather.12
  128.5 60.4 all-gather.10
  190.3 33.7 all-gather.26
  225.6 34.4 all-gather.14
  262.8 61.3 all-gather.18
  327.0 68.2 all-gather.22
  398.1 68.0 all-gather.20
  469.1 68.0 all-gather.24
  742.4 43.2 reduce-scatter.2
  788.4 44.5 reduce-scatter.4
  869.8 896.0 all-reduce.15
where the time goes:
time: 1800 us; the launch traced here: 1790 us
  waiting for transfers between devices  1160 us (64%)
  matrix products  311 us (17%)
  local copies, waits for them, and re-layouts  133 us (7%)
  other arithmetic  87 us (5%)
  blocking collectives  86.1 us (5%)
    unnamed x13, waiting for transfers between devices  837 us
    unnamed x2, blocking collectives  80.6 us
    all_gather x1, waiting for transfers between devices, local(): lax.all_gather(w_down, ('dp', 'ctx'), axis=0, tiled=True)  62.9 us
    all_gather x1, waiting for transfers between devices, local(): lax.all_gather(w_gate, ('dp', 'ctx'), axis=0, tiled=True)  62.8 us
    reshape x8, local copies, waits for them, and re-layouts, owner_major(): return grad_full.reshape(owners, -1)  55.8 us
    all_gather x1, waiting for transfers between devices, local(): lax.all_gather(key_weight, ('dp', 'ctx'), axis=0, tiled=True)  53.2 us
    all_gather x1, waiting for transfers between devices, local(): lax.all_gather(w_query, ('dp', 'ctx'), axis=0, tiled=True)  47.9 us
    dot_general x16, matrix products, masked_scores(): jnp.einsum('rld,kd->rlk', query_head, key_head, preferred_element_type=f32)  44.2 us
  transfers between devices with their start and end apart: 12, of which 9 were waited for; matrix products, arithmetic and copies ran while one was open for 16% of the time, Pallas kernels for 0%

commit v1 on v0

--- a/solution.py
+++ b/solution.py
@@ -1,6 +1,10 @@
+import functools
+
 import jax
 import jax.numpy as jnp
 from jax import lax
+from jax.experimental import pallas as pl
+from jax.experimental.pallas import tpu as pltpu
 from jax.sharding import PartitionSpec as P
 
 MODEL_WIDTH = 1024
@@ -355,10 +359,602 @@
         grad_gains,
     )
 
+FEATURES = 128
+MASK_DEPTH = -4096.0
+LOG2_E = 1.4426950408889634
+VMEM_BYTES = 56 * 1024 * 1024
+bf16 = jnp.bfloat16
+f32 = jnp.float32
+
+
+def xor_permute(value, axis, offset):
+    size = lax.axis_size(axis)
+    return lax.ppermute(value, axis, [(i, i ^ offset) for i in range(size)])
+
+
+def pick(stacked, index):
+    return lax.dynamic_index_in_dim(stacked, index, 0, keepdims=False)
+
+
+def exchange(stacked, me):
+    size = stacked.shape[0]
+    relative = [pick(stacked, me)]
+    for offset in range(1, size):
+        relative.append(xor_permute(pick(stacked, me ^ offset), "ctx", offset))
+    relative = jnp.stack(relative)
+    return jnp.stack([pick(relative, me ^ source) for source in range(size)])
+
+
+def gather_blocks(value):
+    across = xor_permute(value, "ctx", 2)
+    beside = xor_permute(value, "ctx", 1)
+    corner = xor_permute(across, "ctx", 1)
+    return [value, beside, across, corner]
+
+
+def scatter_sum(part):
+    corner = xor_permute(part(3).astype(bf16), "ctx", 1)
+    toward = part(2) + corner.astype(f32)
+    across = xor_permute(toward.astype(bf16), "ctx", 2)
+    beside = xor_permute(part(1).astype(bf16), "ctx", 1)
+    return part(0) + beside.astype(f32) + across.astype(f32)
+
+
+def nt_dot(left, right):
+    return lax.dot_general(left, right, (((1,), (1,)), ((), ())), preferred_element_type=f32)
+
+
+def nn_dot(left, right):
+    return jnp.dot(left, right, preferred_element_type=f32)
+
+
+def project_kernel(
+    query_heads,
+    key_heads,
+    x_ref,
+    gain_ref,
+    weight_ref,
+    cos_ref,
+    sin_ref,
+    gain_q_ref,
+    gain_k_ref,
+    normed_ref,
+    raw_ref,
+    q_ref,
+    k_ref,
+    v_ref,
+):
+    x = x_ref[...].astype(f32)
+    scale = lax.rsqrt(jnp.mean(x * x, axis=-1, keepdims=True) + EPSILON)
+    normed = (x * scale * gain_ref[...]).astype(bf16)
+    normed_ref[...] = normed
+    raw = nn_dot(normed, weight_ref[...])
+    turned = (query_heads + key_heads) * HEAD_SIZE
+    raw_ref[...] = raw[:, :turned]
+    v_ref[...] = raw[:, turned:].astype(bf16)
+    cosine = cos_ref[...]
+    sine = sin_ref[...]
+    for head in range(query_heads + key_heads):
+        rows = raw[:, head * HEAD_SIZE : (head + 1) * HEAD_SIZE]
+        gain = gain_q_ref[...] if head < query_heads else gain_k_ref[...]
+        rows = rows * lax.rsqrt(jnp.mean(rows * rows, axis=-1, keepdims=True) + EPSILON) * gain
+        rows = (rows * cosine + pltpu.roll(rows, HEAD_SIZE // 2, 1) * sine).astype(bf16)
+        if head < query_heads:
+            q_ref[:, head * HEAD_SIZE : (head + 1) * HEAD_SIZE] = rows
+        else:
+            at = (head - query_heads) * HEAD_SIZE
+            k_ref[:, at : at + HEAD_SIZE] = rows
+
+
+def project(x, gain, weight, cosine, sine, gain_q, gain_k, query_heads, key_heads):
+    rows, width = x.shape
+    block = 256
+    turned = (query_heads + key_heads) * HEAD_SIZE
+    columns = weight.shape[1]
+
+    def tall(n):
+        return pl.BlockSpec((block, n), lambda i: (i, 0))
+
+    def whole(shape):
+        return pl.BlockSpec(shape, lambda i: (0, 0))
+
+    return pl.pallas_call(
+        functools.partial(project_kernel, query_heads, key_heads),
+        grid=(rows // block,),
+        in_specs=[
+            tall(width),
+            whole((1, width)),
+            whole(weight.shape),
+            tall(HEAD_SIZE),
+            tall(HEAD_SIZE),
+            whole((1, HEAD_SIZE)),
+            whole((1, HEAD_SIZE)),
+        ],
+        out_specs=[
+            tall(width),
+            tall(turned),
+            tall(query_heads * HEAD_SIZE),
+            tall(key_heads * HEAD_SIZE),
+            tall(key_heads * HEAD_SIZE),
+        ],
+        out_shape=[
+            jax.ShapeDtypeStruct((rows, width), bf16),
+            jax.ShapeDtypeStruct((rows, turned), f32),
+            jax.ShapeDtypeStruct((rows, query_heads * HEAD_SIZE), bf16),
+            jax.ShapeDtypeStruct((rows, key_heads * HEAD_SIZE), bf16),
+            jax.ShapeDtypeStruct((rows, key_heads * HEAD_SIZE), bf16),
+        ],
+        compiler_params=pltpu.CompilerParams(vmem_limit_bytes=VMEM_BYTES),
+        cost_estimate=pl.CostEstimate(
+            flops=2 * rows * width * columns,
+            bytes_accessed=rows * (4 * width + 4 * turned + 2 * columns) + 2 * width * columns,
+            transcendentals=0,
+        ),
+        name="project",
+    )(x, gain, weight, cosine, sine, gain_q, gain_k)
+
+
+def unproject_kernel(
+    query_heads,
+    key_heads,
+    dq_ref,
+    dk_ref,
+    dv_ref,
+    raw_ref,
+    cos_ref,
+    sin_ref,
+    gain_q_ref,
+    gain_k_ref,
+    low_ref,
+    dgain_ref,
+):
+    @pl.when(pl.program_id(0) == 0)
+    def _():
+        dgain_ref[...] = jnp.zeros_like(dgain_ref)
+
+    cosine = cos_ref[...]
+    sine = sin_ref[...]
+    total_q = jnp.zeros((1, HEAD_SIZE), f32)
+    total_k = jnp.zeros((1, HEAD_SIZE), f32)
+    for head in range(query_heads + key_heads):
+        at = head * HEAD_SIZE
+        raw = raw_ref[:, at : at + HEAD_SIZE]
+        if head < query_heads:
+            grad = dq_ref[:, at : at + HEAD_SIZE]
+            gain = gain_q_ref[...]
+        else:
+            back = (head - query_heads) * HEAD_SIZE
+            grad = dk_ref[:, back : back + HEAD_SIZE]
+            gain = gain_k_ref[...]
+        grad = grad * cosine - pltpu.roll(grad, HEAD_SIZE // 2, 1) * sine
+        scale = lax.rsqrt(jnp.mean(raw * raw, axis=-1, keepdims=True) + EPSILON)
+        unit = raw * scale
+        summed = jnp.sum(unit * grad, axis=0, keepdims=True)
+        if head < query_heads:
+            total_q += summed
+        else:
+            total_k += summed
+        grad = grad * gain
+        mean = jnp.mean(unit * grad, axis=-1, keepdims=True)
+        low_ref[:, at : at + HEAD_SIZE] = (scale * (grad - unit * mean)).astype(bf16)
+    low_ref[:, (query_heads + key_heads) * HEAD_SIZE :] = dv_ref[...].astype(bf16)
+    dgain_ref[0:1, :] += total_q
+    dgain_ref[1:2, :] += total_k
+
+
+def unproject(dq, dk, dv, raw, cosine, sine, gain_q, gain_k, query_heads, key_heads):
+    rows = dq.shape[0]
+    block = 256
+    columns = (query_heads + 2 * key_heads) * HEAD_SIZE
+
+    def tall(n):
+        return pl.BlockSpec((block, n), lambda i: (i, 0))
+
+    def whole(shape):
+        return pl.BlockSpec(shape, lambda i: (0, 0))
+
+    return pl.pallas_call(
+        functools.partial(unproject_kernel, query_heads, key_heads),
+        grid=(rows // block,),
+        in_specs=[
+            tall(dq.shape[1]),
+            tall(dk.shape[1]),
+            tall(dv.shape[1]),
+            tall(raw.shape[1]),
+            tall(HEAD_SIZE),
+            tall(HEAD_SIZE),
+            whole((1, HEAD_SIZE)),
+            whole((1, HEAD_SIZE)),
+        ],
+        out_specs=[tall(columns), whole((8, HEAD_SIZE))],
+        out_shape=[
+            jax.ShapeDtypeStruct((rows, columns), bf16),
+            jax.ShapeDtypeStruct((8, HEAD_SIZE), f32),
+        ],
+        compiler_params=pltpu.CompilerParams(vmem_limit_bytes=VMEM_BYTES),
+        cost_estimate=pl.CostEstimate(
+            flops=20 * rows * columns, bytes_accessed=10 * rows * columns, transcendentals=0
+        ),
+        name="unproject",
+    )(dq, dk, dv, raw, cosine, sine, gain_q, gain_k)
+
+
+def attend_kernel(
+    group, block, me_ref, q_ref, qf_ref, k_ref, kf_ref, v_ref, o_ref, log_ref, total_ref
+):
+    me = me_ref[0]
+    at_query = pl.program_id(1)
+    factor = HEAD_SIZE ** (-0.5) * LOG2_E
+    query_features = qf_ref[...]
+    ones = jnp.ones((block, HEAD_SIZE), bf16)
+    total_ref[...] = jnp.zeros_like(total_ref)
+
+    def step(at_key, diagonal):
+        rows = pl.ds(pl.multiple_of((at_key ^ me) * block, block), block)
+        keys = jnp.concatenate([k_ref[rows, :], kf_ref[rows, :]], axis=1)
+        values = jnp.concatenate([v_ref[rows, :], ones], axis=1)
+        for head in range(group):
+            query = q_ref[:, head * HEAD_SIZE : (head + 1) * HEAD_SIZE]
+            scores = nt_dot(jnp.concatenate([query, query_features], axis=1), keys)
+            probs = jnp.exp2(scores * factor)
+            if diagonal:
+                down = lax.broadcasted_iota(jnp.int32, probs.shape, 0)
+                right = lax.broadcasted_iota(jnp.int32, probs.shape, 1)
+                probs = jnp.where(down >= right, probs, 0.0)
+            total_ref[head] += nn_dot(probs.astype(bf16), values)
+
+    @pl.loop(0, at_query)
+    def _(at_key):
+        step(at_key, False)
+
+    step(at_query, True)
+    for head in range(group):
+        weighted = total_ref[head, :, :HEAD_SIZE]
+        summed = total_ref[head, :, HEAD_SIZE:]
+        o_ref[:, head * HEAD_SIZE : (head + 1) * HEAD_SIZE] = (weighted / summed).astype(bf16)
+        log_ref[0, head : head + 1, :] = jnp.log2(summed.T[0:1, :])
+
+
+def attend(me, q, qf, k, kf, v, block, group):
+    rows = q.shape[0]
+    key_heads = k.shape[1] // HEAD_SIZE
+    blocks = rows // block
+    pairs = key_heads * group * blocks * (blocks + 1) // 2 * block * block
+    return pl.pallas_call(
+        functools.partial(attend_kernel, group, block),
+        grid_spec=pltpu.PrefetchScalarGridSpec(
+            num_scalar_prefetch=1,
+            grid=(key_heads, blocks),
+            in_specs=[
+                pl.BlockSpec((block, group * HEAD_SIZE), lambda g, i, me: (i ^ me[0], g)),
+                pl.BlockSpec((block, FEATURES), lambda g, i, me: (i ^ me[0], 0)),
+                pl.BlockSpec((rows, HEAD_SIZE), lambda g, i, me: (0, g)),
+                pl.BlockSpec((rows, FEATURES), lambda g, i, me: (0, 0)),
+                pl.BlockSpec((rows, HEAD_SIZE), lambda g, i, me: (0, g)),
+            ],
+            out_specs=[
+                pl.BlockSpec((block, group * HEAD_SIZE), lambda g, i, me: (i ^ me[0], g)),
+                pl.BlockSpec((1, group, block), lambda g, i, me: (g, 0, i ^ me[0])),
+            ],
+            scratch_shapes=[pltpu.VMEM((group, block, 2 * HEAD_SIZE), f32)],
+        ),
+        out_shape=[
+            jax.ShapeDtypeStruct(q.shape, bf16),
+            jax.ShapeDtypeStruct((key_heads, group, rows), f32),
+        ],
+        compiler_params=pltpu.CompilerParams(vmem_limit_bytes=VMEM_BYTES),
+        cost_estimate=pl.CostEstimate(
+            flops=8 * pairs * HEAD_SIZE, bytes_accessed=10 * q.size, transcendentals=pairs
+        ),
+        name="attend",
+    )(me, q, qf, k, kf, v)
+
+
+def unattend_kernel(
+    group,
+    block,
+    me_ref,
+    q_ref,
+    qf_ref,
+    k_ref,
+    kf_ref,
+    v_ref,
+    o_ref,
+    do_ref,
+    log_ref,
+    dq_ref,
+    dk_ref,
+    dv_ref,
+    flipped_ref,
+    total_ref,
+):
+    me = me_ref[0]
+    at_query = pl.program_id(1)
+    scale = HEAD_SIZE ** (-0.5)
+    factor = scale * LOG2_E
+
+    @pl.when(at_query == 0)
+    def _():
+        dk_ref[...] = jnp.zeros_like(dk_ref)
+        dv_ref[...] = jnp.zeros_like(dv_ref)
+        flipped_ref[...] = k_ref[...].astype(f32).T.astype(bf16)
+
+    total_ref[...] = jnp.zeros_like(total_ref)
+    query_features = qf_ref[...]
+    deltas = []
+    for head in range(group):
+        lanes = slice(head * HEAD_SIZE, (head + 1) * HEAD_SIZE)
+        product = do_ref[:, lanes].astype(f32) * o_ref[:, lanes].astype(f32)
+        deltas.append(jnp.sum(product.T, axis=0, keepdims=True))
+
+    def step(at_key, diagonal):
+        start = pl.multiple_of((at_key ^ me) * block, block)
+        rows = pl.ds(start, block)
+        keys = jnp.concatenate([k_ref[rows, :], kf_ref[rows, :]], axis=1)
+        values = v_ref[rows, :]
+        for head in range(group):
+            lanes = slice(head * HEAD_SIZE, (head + 1) * HEAD_SIZE)
+            query = q_ref[:, lanes]
+            d_out = do_ref[:, lanes]
+            scores = nt_dot(keys, jnp.concatenate([query, query_features], axis=1))
+            probs = jnp.exp2(scores * factor - log_ref[0, head : head + 1, :])
+            if diagonal:
+                key_at = lax.broadcasted_iota(jnp.int32, probs.shape, 0)
+                query_at = lax.broadcasted_iota(jnp.int32, probs.shape, 1)
+                probs = jnp.where(query_at >= key_at, probs, 0.0)
+            d_scores = (probs * (nt_dot(values, d_out) - deltas[head])).astype(bf16)
+            dv_ref[rows, :] += nn_dot(probs.astype(bf16), d_out)
+            dk_ref[rows, :] += nn_dot(d_scores, query)
+            total_ref[head] += nn_dot(flipped_ref[:, rows], d_scores)
+
+    @pl.loop(0, at_query)
+    def _(at_key):
+        step(at_key, False)
+
+    step(at_query, True)
+    for head in range(group):
+        dq_ref[:, head * HEAD_SIZE : (head + 1) * HEAD_SIZE] = total_ref[head].T * scale
+
+    @pl.when(at_query == pl.num_programs(1) - 1)
+    def _():
+        dk_ref[...] = dk_ref[...] * scale
+
+
+def unattend(me, q, qf, k, kf, v, o, d_out, logs, block, group):
+    rows = q.shape[0]
+    key_heads = k.shape[1] // HEAD_SIZE
+    blocks = rows // block
+    pairs = key_heads * group * blocks * (blocks + 1) // 2 * block * block
+
+    def by_query(n):
+        return pl.BlockSpec((block, n), lambda g, i, me: (i ^ me[0], g))
+
+    by_key = pl.BlockSpec((rows, HEAD_SIZE), lambda g, i, me: (0, g))
+    return pl.pallas_call(
+        functools.partial(unattend_kernel, group, block),
+        grid_spec=pltpu.PrefetchScalarGridSpec(
+            num_scalar_prefetch=1,
+            grid=(key_heads, blocks),
+            in_specs=[
+                by_query(group * HEAD_SIZE),
+                pl.BlockSpec((block, FEATURES), lambda g, i, me: (i ^ me[0], 0)),
+                by_key,
+                pl.BlockSpec((rows, FEATURES), lambda g, i, me: (0, 0)),
+                by_key,
+                by_query(group * HEAD_SIZE),
+                by_query(group * HEAD_SIZE),
+                pl.BlockSpec((1, group, block), lambda g, i, me: (g, 0, i ^ me[0])),
+            ],
+            out_specs=[by_query(group * HEAD_SIZE), by_key, by_key],
+            scratch_shapes=[
+                pltpu.VMEM((HEAD_SIZE, rows), bf16),
+                pltpu.VMEM((group, HEAD_SIZE, block), f32),
+            ],
+        ),
+        out_shape=[
+            jax.ShapeDtypeStruct(q.shape, f32),
+            jax.ShapeDtypeStruct(k.shape, f32),
+            jax.ShapeDtypeStruct(v.shape, f32),
+        ],
+        compiler_params=pltpu.CompilerParams(vmem_limit_bytes=VMEM_BYTES),
+        cost_estimate=pl.CostEstimate(
+            flops=14 * pairs * HEAD_SIZE, bytes_accessed=20 * q.size, transcendentals=pairs
+        ),
+        name="unattend",
+    )(me, q, qf, k, kf, v, o, d_out, logs)
+
+
+def norm_back(value_rows, gain_vec, grad):
+    scale = lax.rsqrt(jnp.mean(value_rows * value_rows, axis=-1, keepdims=True) + EPSILON)
+    unit = value_rows * scale
+    d_gain = jnp.sum(unit * grad, axis=0)
+    grad = grad * gain_vec
+    return scale * (grad - unit * jnp.mean(unit * grad, axis=-1, keepdims=True)), d_gain
+
+
+def split_local(
+    tokens,
+    w_query,
+    key_weight,
+    value_weight,
+    w_out,
+    w_gate,
+    w_up,
+    w_down,
+    gains,
+    segment_ids,
+    positions,
+    cotangent,
+):
+    size = lax.axis_size("ctx")
+    copies = lax.axis_size("dp")
+    me = lax.axis_index("ctx")
+    me_row = me.reshape(1).astype(jnp.int32)
+    block = tokens.shape[1]
+    group = QUERY_HEADS // KEY_VALUE_HEADS
+    query_heads = QUERY_HEADS // size
+    key_heads = KEY_VALUE_HEADS // size
+    q_cols = query_heads * HEAD_SIZE
+    k_cols = key_heads * HEAD_SIZE
+    owned = w_query.shape[0]
+    hidden_cols = w_gate.shape[1] // size
+    gain_count = gains.shape[0]
+    pad_rows = 16
+    forward_owner = [
+        (b, (b % copies) * size + b // copies) for b in range(size * copies)
+    ]
+    backward_owner = [(target, source) for source, target in forward_owner]
+
+    def by_columns(weight):
+        return weight.reshape(weight.shape[0], size, -1).transpose(1, 0, 2)
+
+    x_own = tokens.reshape(block, MODEL_WIDTH)
+    x_blocks = gather_blocks(x_own)
+    x_all = jnp.concatenate(x_blocks)
+    places = jnp.concatenate([positions, segment_ids]).astype(jnp.int32)
+    places = jnp.concatenate(gather_blocks(places), axis=1)
+
+    first = jnp.concatenate(
+        [by_columns(w_query), by_columns(key_weight), by_columns(value_weight)], axis=2
+    )
+    gain_rows = jnp.zeros((pad_rows, first.shape[2]), bf16).at[0, :gain_count].set(gains)
+    first = jnp.concatenate(
+        [first, jnp.broadcast_to(gain_rows[None], (size,) + gain_rows.shape)], axis=1
+    )
+    first = exchange(first, me)
+    gain_rows = jnp.concatenate(
+        [first[:, owned], jnp.zeros((pad_rows - size, first.shape[2]), bf16)]
+    )
+    first = jnp.concatenate(
+        [first[:, :owned].reshape(size * owned, first.shape[2]), gain_rows]
+    )
+    first = lax.all_gather(first, "dp", axis=0, tiled=True)
+    first = first.reshape(copies, size * owned + pad_rows, -1)
+    w_first = first[:, : size * owned].reshape(MODEL_WIDTH, -1)
+    full_gains = first[:, size * owned : size * owned + size, :gain_count].reshape(-1)
+    gain_attn, gain_mlp, gain_query, gain_key = split_gains(full_gains)
+
+    out_rows = lax.ppermute(w_out, ("dp", "ctx"), forward_owner)
+    out_full = lax.all_gather(out_rows, "dp", axis=0, tiled=True)
+    gate_up = jnp.concatenate([by_columns(w_gate), by_columns(w_up)], axis=2)
+    gate_up = exchange(gate_up, me).reshape(size * owned, -1)
+    gate_up = lax.all_gather(gate_up, "dp", axis=0, tiled=True)
+    down_rows = lax.ppermute(w_down, ("dp", "ctx"), forward_owner)
+    down_full = lax.all_gather(down_rows, "dp", axis=0, tiled=True)
+
+    cot_own = cotangent.reshape(block, MODEL_WIDTH)
+    cot_tied, unused = lax.optimization_barrier((cot_own, x_blocks[2]))
+    cot_all = jnp.concatenate(gather_blocks(cot_tied))
+
+    half = HEAD_SIZE // 2
+    rates = THETA ** (-2.0 * jnp.arange(half, dtype=f32) / HEAD_SIZE)
+    angles = places[0].astype(f32)[:, None] * rates[None, :]
+    cosine, sine = jnp.cos(angles), jnp.sin(angles)
+    cosine = jnp.concatenate([cosine, cosine], axis=1)
+    sine = jnp.concatenate([-sine, sine], axis=1)
+    lane = jnp.arange(FEATURES, dtype=jnp.int32)[None, :]
+    same = places[1][:, None] == lane
+    key_features = same.astype(bf16)
+    query_features = jnp.where(same, 0.0, MASK_DEPTH).astype(bf16)
+    gain_q_row, gain_k_row = gain_query[None], gain_key[None]
+    normed, raw, q, k, v = project(
+        x_all, gain_attn[None], w_first, cosine, sine, gain_q_row, gain_k_row, query_heads, key_heads
+    )
+    attended, logs = attend(me_row, q, query_features, k, key_features, v, block, group)
+
+    def rows_of(value, r):
+        return value[r * block : (r + 1) * block]
+
+    branch = scatter_sum(lambda r: nn_dot(rows_of(attended, r), out_full))
+    middle = x_own.astype(f32) + branch
+    normed_mlp = jnp.concatenate(gather_blocks(row_norm_apply(middle, gain_mlp).astype(bf16)))
+    both = nn_dot(normed_mlp, gate_up)
+    gate_value, up_value = both[:, :hidden_cols], both[:, hidden_cols:]
+    d_hidden = nt_dot(cot_all, down_full)
+    sigmoid = 1.0 / (1.0 + jnp.exp(-gate_value))
+    silu = gate_value * sigmoid
+    hidden = (silu * up_value).astype(bf16)
+    d_gate = (d_hidden * up_value * sigmoid * (1.0 + gate_value * (1.0 - sigmoid))).astype(bf16)
+    d_up = (d_hidden * silu).astype(bf16)
+    d_both = jnp.concatenate([d_gate, d_up], axis=1)
+
+    d_normed = scatter_sum(lambda r: nt_dot(rows_of(d_both, r), gate_up))
+    d_middle, d_gain_mlp = norm_back(middle, gain_mlp, d_normed)
+    d_middle = d_middle + cot_own.astype(f32)
+    d_branch = jnp.concatenate(gather_blocks(d_middle.astype(bf16)))
+    d_attended = nt_dot(d_branch, out_full).astype(bf16)
+
+    down = scatter_sum(lambda r: nn_dot(rows_of(hidden, r), down_full))
+    output = (middle + down).astype(bf16)
+
+    def tn_dot(left, right):
+        return lax.dot_general(left, right, (((0,), (0,)), ((), ())), preferred_element_type=f32)
+
+    def reduce_rows(grad):
+        return lax.psum_scatter(grad.astype(bf16), "dp", scatter_dimension=0, tiled=True)
+
+    grad_down = reduce_rows(tn_dot(hidden, cot_all))
+    grad_both = reduce_rows(tn_dot(normed_mlp, d_both))
+    grad_out = reduce_rows(tn_dot(attended, d_branch))
+
+    dq, dk, dv = unattend(
+        me_row, q, query_features, k, key_features, v, attended, d_attended, logs, block, group
+    )
+    low, d_gain_heads = unproject(
+        dq, dk, dv, raw, cosine, sine, gain_q_row, gain_k_row, query_heads, key_heads
+    )
+    d_normed_attn = scatter_sum(lambda r: nt_dot(rows_of(low, r), w_first))
+    d_inputs, d_gain_attn = norm_back(x_own.astype(f32), gain_attn, d_normed_attn)
+    grad_tokens = (d_middle + d_inputs).reshape(tokens.shape)
+
+    grad_first = tn_dot(normed, low).astype(bf16)
+    grad_gains = jnp.concatenate(
+        [d_gain_attn, d_gain_mlp, d_gain_heads[0], d_gain_heads[1]]
+    ).reshape(copies, size, gain_count)
+    gain_block = jnp.zeros((copies, pad_rows, grad_first.shape[1]), bf16)
+    gain_block = gain_block.at[:, :size, :gain_count].set(grad_gains.astype(bf16))
+    grad_first = jnp.concatenate(
+        [grad_first.reshape(copies, size * owned, -1), gain_block], axis=1
+    ).reshape(-1, grad_first.shape[1])
+    grad_first = reduce_rows(grad_first)
+    gain_part = grad_first[size * owned :][:size]
+    gain_part = jnp.broadcast_to(gain_part[:, None], (size, pad_rows, gain_part.shape[1]))
+    grad_first = jnp.concatenate(
+        [grad_first[: size * owned].reshape(size, owned, -1), gain_part], axis=1
+    )
+    grad_first = exchange(grad_first, me).astype(f32)
+    grad_gains = jnp.sum(grad_first[:, owned, :gain_count], axis=0)
+    grad_first = grad_first[:, :owned]
+
+    def to_rows(pieces):
+        return pieces.transpose(1, 0, 2).reshape(owned, -1)
+
+    grad_query = to_rows(grad_first[:, :, :q_cols])
+    grad_key = to_rows(grad_first[:, :, q_cols : q_cols + k_cols])
+    grad_value = to_rows(grad_first[:, :, q_cols + k_cols :])
+    grad_both = exchange(grad_both.reshape(size, owned, -1), me).astype(f32)
+    grad_gate = to_rows(grad_both[:, :, :hidden_cols])
+    grad_up = to_rows(grad_both[:, :, hidden_cols:])
+    grad_out = lax.ppermute(grad_out, ("dp", "ctx"), backward_owner).astype(f32)
+    grad_down = lax.ppermute(grad_down, ("dp", "ctx"), backward_owner).astype(f32)
+    return (
+        output.reshape(tokens.shape),
+        grad_tokens,
+        grad_query,
+        grad_key,
+        grad_value,
+        grad_out,
+        grad_gate,
+        grad_up,
+        grad_down,
+        grad_gains,
+    )
+
 
 def solution(mesh):
+    small = mesh.shape["ctx"] == 4
     return jax.shard_map(
-        local,
+        split_local if small else local,
         mesh=mesh,
         in_specs=(
             P("dp", "ctx", None),

time: 1800 us -> 664 us (0.37)
  waiting for transfers between devices: 1160 us -> 337 us
  matrix products: 311 us -> 87.9 us
  local copies, waits for them, and re-layouts: 133 us -> 38.4 us
  blocking collectives: 86.1 us -> 0 us
  Pallas kernels: 0 us -> 85.1 us
  starting transfers between devices: 0.47 us -> 51.5 us
  other arithmetic: 87 us -> 38.4 us
    unnamed x13 -> x8, waiting for transfers between devices: 837 us -> 0.13 us
    all_gather x9 -> x4, waiting for transfers between devices: 320 us -> 45.3 us  [the longest x1 30.8 us: split_local(): down_full = lax.all_gather(down_rows, 'dp', axis=0, tiled=True)]
    dot_general x77 -> x23, matrix products: 311 us -> 87.9 us  [the longest x10 35.3 us: nt_dot(): lax.dot_general(left, right, (((1,), (1,)), ((), ())), preferred_element_...]
    ppermute x0 -> x43, waiting for transfers between devices: none -> 169 us  [the longest x39 145 us: xor_permute(): return lax.ppermute(value, axis, [(i, i ^ offset) for i in range(size)])]
    reduce_scatter x2 -> x4, waiting for transfers between devices: 0.02 us -> 122 us  [reduce_rows(): lax.psum_scatter(grad.astype(bf16), 'dp', scatter_dimension=0, tiled=True)]
    pallas_call x0 -> x4, Pallas kernels: none -> 85.1 us  [the longest x1 37.6 us: unattend(): pl.pallas_call(functools.partial(unattend_kernel, group, block), grid_spe...]
    unnamed x2 -> x0, blocking collectives: 80.6 us -> none
    reshape x19 -> x10, local copies, waits for them, and re-layouts: 72.2 us -> 6.59 us  [the longest x5 3.59 us: to_rows(): return pieces.transpose(1, 0, 2).reshape(owned, -1)]
  transfers between devices with their start and end apart: 12 -> 51, of which waited for: 9 -> 23; matrix products, arithmetic and copies ran while one was open for 16% -> 20% of each run, Pallas kernels for 0% -> 13%
where the time goes in v1:
time: 664 us; the launch traced here: 653 us
  waiting for transfers between devices  337 us (51%)
  matrix products  87.9 us (13%)
  Pallas kernels  85.1 us (13%)
  starting transfers between devices  51.5 us (8%)
  local copies, waits for them, and re-layouts  38.4 us (6%)
  other arithmetic  38.4 us (6%)
  between operations  15.1 us (2%)
    ppermute x39, waiting for transfers between devices, xor_permute(): return lax.ppermute(value, axis, [(i, i ^ offset) for i in range(size)])  145 us
    reduce_scatter x4, waiting for transfers between devices, reduce_rows(): lax.psum_scatter(grad.astype(bf16), 'dp', scatter_dimension=0, tiled=True)  122 us
    ppermute x39, starting transfers between devices, xor_permute(): return lax.ppermute(value, axis, [(i, i ^ offset) for i in range(size)])  40.2 us
    pallas_call x1, Pallas kernels, unattend(): pl.pallas_call(functools.partial(unattend_kernel, group, block), grid_spe...  37.6 us
    dot_general x10, matrix products, nt_dot(): lax.dot_general(left, right, (((1,), (1,)), ((), ())), preferred_element_...  35.3 us
    all_gather x1, waiting for transfers between devices, split_local(): down_full = lax.all_gather(down_rows, 'dp', axis=0, tiled=True)  30.8 us
    dot_general x4, matrix products, tn_dot(): lax.dot_general(left, right, (((0,), (0,)), ((), ())), preferred_element_...  30.1 us
    dot_general x9, matrix products, nn_dot(): return jnp.dot(left, right, preferred_element_type=f32)  22.5 us
  transfers between devices with their start and end apart: 51, of which 23 were waited for; matrix products, arithmetic and copies ran while one was open for 20% of the time, Pallas kernels for 13%

profile of v1, /device:TPU:27, one launch (start us, length us, event | category | flops | bytes accessed | tf_op | source)
XLA Modules:
  0.0 653.2 jit_solution(11175776503863312939)
XLA Ops:
  14.6 2.4 collective-permute-done.4
  25.7 2.9 collective-permute-start.9
  33.9 5.4 fusion.56
  39.2 6.3 collective-permute-start.16
  51.4 3.6 pad_maximum_fusion.7
  61.7 3.6 pad_maximum_fusion.2.x_ref
  65.3 13.4 %all-gather.5.cloned.1.call-done = bf16[1152,1024]{1,0:T(8,128)(2,1)} async-done(((bf16[144,1024]{1,0:T(8,128)(2,1)}), bf16[1152,1024]{1,0:T(8,128)(2,1)}) %all-gather.5.cloned.1.call-update) | async-done | bytes 2359312 | tf_op jit(solution)/shard_map/all_gather | solution.py:831
  79.4 3.1 slice.204
  83.7 13.0 %project.1 = (bf16[2048,1024]{1,0:T(8,128)(2,1)}, f32[2048,768]{1,0:T(8,128)}, bf16[2048,512]{1,0:T(8,128)(2,1)}, bf16[2048,256]{1,0:T(8,128)(2,1)}, bf16[2048,256]{1,0:T(8,128)(2,1)}) custom-call(bf16[2048,1024]{1,0:T(8,128)(2,1)} %pad_maximum_fusion.2.x_ref, f32[1,1024]{1,0:T(1,128)} %bitcast.171, bf16[1024,1024]{1,0:T(8,128)(2,1)} %bitcast.133, ...), custom_call_target="tpu_custom_call" | custom-call | flops 4294967296 | bytes 20971520 | tf_op jit(solution)/shard_map/project/pallas_call | solution.py:461
  96.7 20.7 %attend.1 = (bf16[2048,512]{1,0:T(8,128)(2,1)}, f32[2,2,2048]{2,1,0:T(2,128)}) custom-call(s32[1]{0:T(128)} %bitcast.1.me_ref, bf16[2048,512]{1,0:T(8,128)(2,1)} %get-tuple-element.47.q_ref, bf16[2048,128]{1,0:T(8,128)(2,1)} %select_convert_fusion.qf_ref, bf16[2048,256]{1,0:T(8,128)(2,1)} %get-tuple-element.48.k_ref, bf16[2048,128]{1,0:T(8,128)(2,1)} %fusion.44.kf_ref, ...), custom_call_target="tpu_custom_call" | custom-call | flops 10737418240 | bytes 10485760 | tf_op jit(solution)/shard_map/attend/pallas_call | solution.py:623
  120.7 2.6 collective-permute-start.11
  128.6 22.1 %collective-permute-done.12 = bf16[512,1024]{1,0:T(8,128)(2,1)S(1)} collective-permute-done((bf16[512,1024]{1,0:T(8,128)(2,1)S(1)}, bf16[512,1024]{1,0:T(8,128)(2,1)S(1)}, u32[]{:S(2)}, u32[]{:S(2)}) %collective-permute-start.12) | collective-permute-done | bytes 1048608 | tf_op jit(solution)/shard_map/ppermute | solution.py:372
  153.1 2.4 collective-permute-start.23
  155.4 17.9 %collective-permute-done.24 = bf16[512,1024]{1,0:T(8,128)(2,1)} collective-permute-done((bf16[512,1024]{1,0:T(8,128)(2,1)}, bf16[512,1024]{1,0:T(8,128)(2,1)}, u32[]{:S(2)}, u32[]{:S(2)}) %collective-permute-start.24) | collective-permute-done | bytes 1048608 | tf_op jit(solution)/shard_map/ppermute | solution.py:372
  175.4 20.3 %collective-permute-done.14 = bf16[512,1024]{1,0:T(8,128)(2,1)} collective-permute-done((bf16[512,1024]{1,0:T(8,128)(2,1)}, bf16[512,1024]{1,0:T(8,128)(2,1)}, u32[]{:S(2)}, u32[]{:S(2)}) %collective-permute-start.14) | collective-permute-done | bytes 1048608 | tf_op jit(solution)/shard_map/ppermute | solution.py:372
  197.0 2.4 collective-permute-start.19
  199.5 4.5 collective-permute-done.19
  204.9 2.4 constant_dynamic-update-slice_fusion.3
  207.3 2.4 constant_dynamic-update-slice_fusion.2
  209.7 2.3 constant_dynamic-update-slice_fusion.1
  212.0 2.3 constant_dynamic-update-slice_fusion
  214.3 12.8 %fusion.50 = f32[2048,1536]{0,1:T(8,128)} fusion(bf16[1024,1536]{1,0:T(8,128)(2,1)} %all-gather.9.cloned.1.call-done, bf16[512,1024]{1,0:T(8,128)(2,1)} %collective-permute-done.15, bf16[512,1024]{1,0:T(8,128)(2,1)} %collective-permute-done.14, bf16[512,1024]{1,0:T(8,128)(2,1)} %collective-permute-done.13, bf16[512,1024]{1,0:T(8,128)(2,1)} %multiply_convert_fusion.3), kind=kOutput, calls=%fused_computation.90 | convolution fusion | flops 6459228160 | bytes 19922944 | tf_op jit(solution)/shard_map/dot_general | solution.py:408
  227.0 30.8 %all-gather.11.cloned.1.call-done = bf16[768,1024]{1,0:T(8,128)(2,1)} async-done(((bf16[96,1024]{1,0:T(8,128)(2,1)}), bf16[768,1024]{1,0:T(8,128)(2,1)}) %all-gather.11.cloned.1.call-update) | async-done | bytes 1572880 | tf_op jit(solution)/shard_map/all_gather | solution.py:843
  257.8 12.2 %multiply_convert_fusion = (bf16[2048,768]{0,1:T(8,128)(2,1)S(1)}, bf16[2048,768]{0,1:T(8,128)(2,1)S(1)}, bf16[2048,768]{0,1:T(8,128)(2,1)}) fusion(f32[2048,1536]{0,1:T(8,128)} %fusion.50, bf16[2048,1024]{1,0:T(8,128)(2,1)} %constant_dynamic-update-slice_fusion, bf16[768,1024]{1,0:T(8,128)(2,1)} %all-gather.11.cloned.1.call-done), kind=kOutput, calls=%fused_computation.10 | convolution fusion | flops 3244818432 | bytes 27787264 | tf_op jit(solution)/shard_map/dot_general | solution.py:404
  278.3 3.0 add_convert_fusion.1
  286.8 18.9 %collective-permute-done.28 = bf16[512,1024]{1,0:T(8,128)(2,1)S(1)} collective-permute-done((bf16[512,1024]{1,0:T(8,128)(2,1)S(1)}, bf16[512,1024]{1,0:T(8,128)(2,1)S(1)}, u32[]{:S(2)}, u32[]{:S(2)}) %collective-permute-start.28) | collective-permute-done | bytes 1048608 | tf_op jit(solution)/shard_map/ppermute | solution.py:372
  305.7 2.5 multiply_reduce_fusion
  308.2 19.9 %collective-permute-done.22 = bf16[512,1024]{1,0:T(8,128)(2,1)S(1)} collective-permute-done((bf16[512,1024]{1,0:T(8,128)(2,1)S(1)}, bf16[512,1024]{1,0:T(8,128)(2,1)S(1)}, u32[]{:S(2)}, u32[]{:S(2)}) %collective-permute-start.22) | collective-permute-done | bytes 1048608 | tf_op jit(solution)/shard_map/ppermute | solution.py:372
  328.1 5.1 fusion.76
  333.5 6.9 %convolution_convert_fusion.2 = bf16[768,1024]{1,0:T(8,128)(2,1)} fusion(bf16[2048,768]{0,1:T(8,128)(2,1)S(1)} %copy-done.28, bf16[2048,1024]{1,0:T(8,128)(2,1)} %constant_dynamic-update-slice_fusion), kind=kOutput, calls=%fused_computation.49 | convolution fusion | flops 3222011904 | bytes 8912896 | tf_op jit(solution)/shard_map/dot_general | solution.py:891
  342.1 14.8 %collective-permute-done.30 = bf16[512,1024]{1,0:T(8,128)(2,1)} collective-permute-done((bf16[512,1024]{1,0:T(8,128)(2,1)}, bf16[512,1024]{1,0:T(8,128)(2,1)}, u32[]{:S(2)}, u32[]{:S(2)}) %collective-permute-start.30) | collective-permute-done | bytes 1048608 | tf_op jit(solution)/shard_map/ppermute | solution.py:372
  359.1 2.5 collective-permute-done.31
  362.7 5.0 convolution_convert_fusion.9
  367.7 12.5 %fusion.3 = bf16[1024,1536]{1,0:T(8,128)(2,1)} fusion(bf16[2048,768]{0,1:T(8,128)(2,1)} %copy-done.24, bf16[2048,768]{0,1:T(8,128)(2,1)} %copy-done.25, bf16[512,1024]{1,0:T(8,128)(2,1)} %collective-permute-done.15, bf16[512,1024]{1,0:T(8,128)(2,1)} %collective-permute-done.14, bf16[512,1024]{1,0:T(8,128)(2,1)} %collective-permute-done.13, ...), kind=kOutput, calls=%fused_computation.20 | convolution fusion | flops 6473383936 | bytes 13631488 | tf_op jit(solution)/shard_map/dot_general | solution.py:891
  381.8 5.6 convolution_convert_fusion.do_ref
  387.3 37.6 %unattend.1 = (f32[2048,512]{1,0:T(8,128)}, f32[2048,256]{1,0:T(8,128)}, f32[2048,256]{1,0:T(8,128)}) custom-call(s32[1]{0:T(128)} %bitcast.1.me_ref, bf16[2048,512]{1,0:T(8,128)(2,1)} %get-tuple-element.47.q_ref, bf16[2048,128]{1,0:T(8,128)(2,1)} %select_convert_fusion.qf_ref, bf16[2048,256]{1,0:T(8,128)(2,1)} %get-tuple-element.48.k_ref, ...), custom_call_target="tpu_custom_call" | custom-call | flops 18790481920 | bytes 20971520 | tf_op jit(solution)/shard_map/unattend/pallas_call | solution.py:733
  424.9 13.8 %unproject.1 = (bf16[2048,1024]{1,0:T(8,128)(2,1)}, f32[8,128]{1,0:T(8,128)}) custom-call(f32[2048,512]{1,0:T(8,128)} %get-tuple-element.53.dq_ref, f32[2048,256]{1,0:T(8,128)} %get-tuple-element.54.dk_ref, f32[2048,256]{1,0:T(8,128)} %get-tuple-element.55.dv_ref, f32[2048,768]{1,0:T(8,128)} %get-tuple-element.56.raw_ref, ...), custom_call_target="tpu_custom_call" | custom-call | flops 41943040 | bytes 20971520 | tf_op jit(solution)/shard_map/unproject/pallas_call | solution.py:556
  438.8 2.7 convolution_convert_fusion.5
  445.8 5.8 convolution_convert_fusion.1
  451.6 18.4 %collective-permute-done.34 = bf16[512,1024]{1,0:T(8,128)(2,1)S(1)} collective-permute-done((bf16[512,1024]{1,0:T(8,128)(2,1)S(1)}, bf16[512,1024]{1,0:T(8,128)(2,1)S(1)}, u32[]{:S(2)}, u32[]{:S(2)}) %collective-permute-start.34) | collective-permute-done | bytes 1048608 | tf_op jit(solution)/shard_map/ppermute | solution.py:372
  470.1 3.1 fusion.13
  473.3 3.4 fusion.7
  476.7 3.1 collective-permute-start.42
  479.8 19.7 %collective-permute-done.42 = bf16[96,1024]{1,0:T(8,128)(2,1)S(1)} collective-permute-done((bf16[96,1024]{1,0:T(8,128)(2,1)}, bf16[96,1024]{1,0:T(8,128)(2,1)S(1)}, u32[]{:S(2)}, u32[]{:S(2)}) %collective-permute-start.42) | collective-permute-done | bytes 196640 | tf_op jit(solution)/shard_map/ppermute | solution.py:939
  502.2 59.2 %reduce-scatter.9.cloned.1.call-done = bf16[128,1536]{1,0:T(8,128)(2,1)} async-done(((bf16[1024,1536]{1,0:T(8,128)(2,1)}), bf16[128,1536]{1,0:T(8,128)(2,1)}) %reduce-scatter.9.cloned.1.call-update) | async-done | bytes 393232 | tf_op jit(solution)/shard_map/reduce_scatter | solution.py:894
  565.2 4.3 fusion.12
  570.0 62.7 %reduce-scatter.5.cloned.1.call-done = bf16[144,1024]{1,0:T(8,128)(2,1)} async-done(((bf16[1152,1024]{1,0:T(8,128)(2,1)}), bf16[144,1024]{1,0:T(8,128)(2,1)}) %reduce-scatter.5.cloned.1.call-update) | async-done | bytes 294928 | tf_op jit(solution)/shard_map/reduce_scatter | solution.py:894
  641.1 2.3 collective-permute-done.37
  (237 shorter events, 93.9 us)
Async XLA Ops:
  7.2 71.5 %all-gather.5.cloned.1.call-start = ((), (), s32[]{:S(2)}) async-start(), calls=%async_computation.4 | async-start | bytes 2654208 | tf_op jit(solution)/shard_map/all_gather | solution.py:831
  12.5 4.5 collective-permute-start.4
  12.9 6.3 collective-permute-start.5
  23.2 95.3 %all-gather.7.cloned.1.call-start = ((), (), s32[]{:S(2)}) async-start(), calls=%async_computation.5 | async-start | bytes 1179648 | tf_op jit(solution)/shard_map/all_gather | solution.py:838
  23.3 6.6 %collective-permute-start.7 = (s32[2,512]{1,0:T(2,128)S(1)}, s32[2,512]{1,0:T(2,128)S(1)}, u32[]{:S(2)}, u32[]{:S(2)}) collective-permute-start(s32[2,512]{1,0:T(2,128)S(1)} %pad_add_fusion.1), channel_id=1, source_target_pairs={{0,2},{1,3},{2,0},{3,1},{4,6},{5,7},{6,4},{7,5},{8,10},{9,11},{10,... | collective-permute-start | bytes 12296 | tf_op jit(solution)/shard_map/ppermute | solution.py:372
  23.6 8.4 %collective-permute-start.6 = (s32[2,512]{1,0:T(2,128)S(1)}, s32[2,512]{1,0:T(2,128)S(1)}, u32[]{:S(2)}, u32[]{:S(2)}) collective-permute-start(s32[2,512]{1,0:T(2,128)S(1)} %pad_add_fusion.1), channel_id=1, source_target_pairs={{0,1},{1,0},{2,3},{3,2},{4,5},{5,4},{6,7},{7,6},{8,9},{9,8},{10,11... | collective-permute-start | bytes 12296 | tf_op jit(solution)/shard_map/ppermute | solution.py:372
  24.2 24.9 %collective-permute-start.1 = (bf16[512,1024]{1,0:T(8,128)(2,1)S(1)}, bf16[512,1024]{1,0:T(8,128)(2,1)}, u32[]{:S(2)}, u32[]{:S(2)}) collective-permute-start(bf16[512,1024]{1,0:T(8,128)(2,1)S(1)} %bitcast.130), channel_id=1, source_target_pairs={{0,2},{1,3},{2,0},{3,1},{4,6},{5,7},{6,4},{7,5},{8,10},{9,11},{10,... | collective-permute-start | bytes 3145736 | tf_op jit(solution)/shard_map/ppermute | solution.py:372
  25.4 36.3 %collective-permute-start = (bf16[512,1024]{1,0:T(8,128)(2,1)S(1)}, bf16[512,1024]{1,0:T(8,128)(2,1)}, u32[]{:S(2)}, u32[]{:S(2)}) collective-permute-start(bf16[512,1024]{1,0:T(8,128)(2,1)S(1)} %bitcast.131), channel_id=1, source_target_pairs={{0,1},{1,0},{2,3},{3,2},{4,5},{5,4},{6,7},{7,6},{8,9},{9,8},{10,11... | collective-permute-start | bytes 3145736 | tf_op jit(solution)/shard_map/ppermute | solution.py:372
  25.7 13.6 %collective-permute-start.9 = (bf16[64,1024]{1,0:T(8,128)(2,1)}, bf16[64,1024]{1,0:T(8,128)(2,1)S(1)}, u32[]{:S(2)}, u32[]{:S(2)}) collective-permute-start(bf16[64,1024]{1,0:T(8,128)(2,1)} %param.20), channel_id=1, source_target_pairs={{0,0},{1,4},{2,8},{3,12},{4,16},{5,20},{6,24},{7,28},{8,1},{9,5},{... | collective-permute-start | bytes 393224 | tf_op jit(solution)/shard_map/ppermute | solution.py:837
  29.9 3.5 collective-permute-start.8
  32.0 23.0 %collective-permute-start.18 = (bf16[32,1536]{1,0:T(8,128)(2,1)}, bf16[32,1536]{1,0:T(8,128)(2,1)}, u32[]{:S(2)}, u32[]{:S(2)}) collective-permute-start(bf16[32,1536]{1,0:T(8,128)(2,1)} %bitcast.123), channel_id=1, source_target_pairs={{0,3},{1,2},{2,1},{3,0},{4,7},{5,6},{6,5},{7,4},{8,11},{9,10},{10,... | collective-permute-start | bytes 294920 | tf_op jit(solution)/shard_map/ppermute | solution.py:372
  33.4 22.6 %collective-permute-start.17 = (bf16[32,1536]{1,0:T(8,128)(2,1)}, bf16[32,1536]{1,0:T(8,128)(2,1)}, u32[]{:S(2)}, u32[]{:S(2)}) collective-permute-start(bf16[32,1536]{1,0:T(8,128)(2,1)} %bitcast.124), channel_id=1, source_target_pairs={{0,2},{1,3},{2,0},{3,1},{4,6},{5,7},{6,4},{7,5},{8,10},{9,11},{10,... | collective-permute-start | bytes 294920 | tf_op jit(solution)/shard_map/ppermute | solution.py:372
  39.2 17.9 %collective-permute-start.16 = (bf16[32,1536]{1,0:T(8,128)(2,1)}, bf16[32,1536]{1,0:T(8,128)(2,1)}, u32[]{:S(2)}, u32[]{:S(2)}) collective-permute-start(bf16[32,1536]{1,0:T(8,128)(2,1)} %bitcast.161), channel_id=1, source_target_pairs={{0,1},{1,0},{2,3},{3,2},{4,5},{5,4},{6,7},{7,6},{8,9},{9,8},{10,11... | collective-permute-start | bytes 294920 | tf_op jit(solution)/shard_map/ppermute | solution.py:372
  45.5 168.7 %all-gather.9.cloned.1.call-start = ((), (), s32[]{:S(2)}) async-start(), calls=%async_computation.6 | async-start | bytes 3538944 | tf_op jit(solution)/shard_map/all_gather | solution.py:841
  49.1 12.7 %collective-permute-start.2 = (bf16[512,1024]{1,0:T(8,128)(2,1)}, bf16[512,1024]{1,0:T(8,128)(2,1)}, u32[]{:S(2)}, u32[]{:S(2)}) collective-permute-start(bf16[512,1024]{1,0:T(8,128)(2,1)} %collective-permute-done.1), channel_id=1, source_target_pairs={{0,1},{1,0},{2,3},{3,2},{4,5},{5,4},{6,7},{7,6},{8,9},{9,8},{10,11... | collective-permute-start | bytes 3145736 | tf_op jit(solution)/shard_map/ppermute | solution.py:372
  61.7 196.1 %all-gather.11.cloned.1.call-start = ((), (), s32[]{:S(2)}) async-start(), calls=%async_computation.7 | async-start | bytes 1769472 | tf_op jit(solution)/shard_map/all_gather | solution.py:843
  120.7 4.9 collective-permute-start.11
  126.4 24.4 %collective-permute-start.12 = (bf16[512,1024]{1,0:T(8,128)(2,1)S(1)}, bf16[512,1024]{1,0:T(8,128)(2,1)S(1)}, u32[]{:S(2)}, u32[]{:S(2)}) collective-permute-start(bf16[512,1024]{1,0:T(8,128)(2,1)S(1)} %add_convert_fusion.4), channel_id=1, source_target_pairs={{0,2},{1,3},{2,0},{3,1},{4,6},{5,7},{6,4},{7,5},{8,10},{9,11},{10,... | collective-permute-start | bytes 3145736 | tf_op jit(solution)/shard_map/ppermute | solution.py:372
  126.7 46.6 %collective-permute-start.24 = (bf16[512,1024]{1,0:T(8,128)(2,1)}, bf16[512,1024]{1,0:T(8,128)(2,1)}, u32[]{:S(2)}, u32[]{:S(2)}) collective-permute-start(bf16[512,1024]{1,0:T(8,128)(2,1)} %bitcast.25), channel_id=1, source_target_pairs={{0,2},{1,3},{2,0},{3,1},{4,6},{5,7},{6,4},{7,5},{8,10},{9,11},{10,... | collective-permute-start | bytes 3145736 | tf_op jit(solution)/shard_map/ppermute | solution.py:372
  152.7 43.0 %collective-permute-start.14 = (bf16[512,1024]{1,0:T(8,128)(2,1)}, bf16[512,1024]{1,0:T(8,128)(2,1)}, u32[]{:S(2)}, u32[]{:S(2)}) collective-permute-start(bf16[512,1024]{1,0:T(8,128)(2,1)} %multiply_convert_fusion.3), channel_id=1, source_target_pairs={{0,2},{1,3},{2,0},{3,1},{4,6},{5,7},{6,4},{7,5},{8,10},{9,11},{10,... | collective-permute-start | bytes 3145736 | tf_op jit(solution)/shard_map/ppermute | solution.py:372
  153.1 54.2 %collective-permute-start.23 = (bf16[512,1024]{1,0:T(8,128)(2,1)}, bf16[512,1024]{1,0:T(8,128)(2,1)}, u32[]{:S(2)}, u32[]{:S(2)}) collective-permute-start(bf16[512,1024]{1,0:T(8,128)(2,1)} %bitcast.25), channel_id=1, source_target_pairs={{0,1},{1,0},{2,3},{3,2},{4,5},{5,4},{6,7},{7,6},{8,9},{9,8},{10,11... | collective-permute-start | bytes 3145736 | tf_op jit(solution)/shard_map/ppermute | solution.py:372
  173.3 38.7 %collective-permute-start.25 = (bf16[512,1024]{1,0:T(8,128)(2,1)}, bf16[512,1024]{1,0:T(8,128)(2,1)}, u32[]{:S(2)}, u32[]{:S(2)}) collective-permute-start(bf16[512,1024]{1,0:T(8,128)(2,1)} %collective-permute-done.24), channel_id=1, source_target_pairs={{0,1},{1,0},{2,3},{3,2},{4,5},{5,4},{6,7},{7,6},{8,9},{9,8},{10,11... | collective-permute-start | bytes 3145736 | tf_op jit(solution)/shard_map/ppermute | solution.py:372
  175.4 38.8 %collective-permute-start.13 = (bf16[512,1024]{1,0:T(8,128)(2,1)}, bf16[512,1024]{1,0:T(8,128)(2,1)}, u32[]{:S(2)}, u32[]{:S(2)}) collective-permute-start(bf16[512,1024]{1,0:T(8,128)(2,1)} %multiply_convert_fusion.3), channel_id=1, source_target_pairs={{0,1},{1,0},{2,3},{3,2},{4,5},{5,4},{6,7},{7,6},{8,9},{9,8},{10,11... | collective-permute-start | bytes 3145736 | tf_op jit(solution)/shard_map/ppermute | solution.py:372
  195.8 18.5 %collective-permute-start.15 = (bf16[512,1024]{1,0:T(8,128)(2,1)}, bf16[512,1024]{1,0:T(8,128)(2,1)}, u32[]{:S(2)}, u32[]{:S(2)}) collective-permute-start(bf16[512,1024]{1,0:T(8,128)(2,1)} %collective-permute-done.14), channel_id=1, source_target_pairs={{0,1},{1,0},{2,3},{3,2},{4,5},{5,4},{6,7},{7,6},{8,9},{9,8},{10,11... | collective-permute-start | bytes 3145736 | tf_op jit(solution)/shard_map/ppermute | solution.py:372
  197.0 7.0 %collective-permute-start.19 = (bf16[96,1024]{1,0:T(8,128)(2,1)S(1)}, bf16[96,1024]{1,0:T(8,128)(2,1)S(1)}, u32[]{:S(2)}, u32[]{:S(2)}) collective-permute-start(bf16[96,1024]{1,0:T(8,128)(2,1)S(1)} %copy-done.23), channel_id=1, source_target_pairs={{0,0},{1,4},{2,8},{3,12},{4,16},{5,20},{6,24},{7,28},{8,1},{9,5},{... | collective-permute-start | bytes 589832 | tf_op jit(solution)/shard_map/ppermute | solution.py:842
  204.7 271.9 %reduce-scatter.11.cloned.1.call-start = ((), (), s32[]{:S(2)}) async-start(), calls=%async_computation.11 | async-start | bytes 1769472 | tf_op jit(solution)/shard_map/reduce_scatter | solution.py:894
  271.9 6.4 collective-permute-start.27
  275.7 7.9 %collective-permute-start.21 = (bf16[512,1024]{1,0:T(8,128)(2,1)S(1)}, bf16[512,1024]{1,0:T(8,128)(2,1)S(1)}, u32[]{:S(2)}, u32[]{:S(2)}) collective-permute-start(bf16[512,1024]{1,0:T(8,128)(2,1)S(1)} %convolution_convert_fusion.3), channel_id=1, source_target_pairs={{0,1},{1,0},{2,3},{3,2},{4,5},{5,4},{6,7},{7,6},{8,9},{9,8},{10,11... | collective-permute-start | bytes 3145736 | tf_op jit(solution)/shard_map/ppermute | solution.py:372
  278.2 8.6 %collective-permute-start.26 = (bf16[512,1024]{1,0:T(8,128)(2,1)S(1)}, bf16[512,1024]{1,0:T(8,128)(2,1)S(1)}, u32[]{:S(2)}, u32[]{:S(2)}) collective-permute-start(bf16[512,1024]{1,0:T(8,128)(2,1)S(1)} %fusion.30), channel_id=1, source_target_pairs={{0,1},{1,0},{2,3},{3,2},{4,5},{5,4},{6,7},{7,6},{8,9},{9,8},{10,11... | collective-permute-start | bytes 3145736 | tf_op jit(solution)/shard_map/ppermute | solution.py:372
  281.3 24.3 %collective-permute-start.28 = (bf16[512,1024]{1,0:T(8,128)(2,1)S(1)}, bf16[512,1024]{1,0:T(8,128)(2,1)S(1)}, u32[]{:S(2)}, u32[]{:S(2)}) collective-permute-start(bf16[512,1024]{1,0:T(8,128)(2,1)S(1)} %add_convert_fusion.1), channel_id=1, source_target_pairs={{0,2},{1,3},{2,0},{3,1},{4,6},{5,7},{6,4},{7,5},{8,10},{9,11},{10,... | collective-permute-start | bytes 3145736 | tf_op jit(solution)/shard_map/ppermute | solution.py:372
  282.7 25.5 %collective-permute-start.20 = (bf16[512,1024]{1,0:T(8,128)(2,1)S(1)}, bf16[512,1024]{1,0:T(8,128)(2,1)S(1)}, u32[]{:S(2)}, u32[]{:S(2)}) collective-permute-start(bf16[512,1024]{1,0:T(8,128)(2,1)S(1)} %convolution_convert_fusion.4), channel_id=1, source_target_pairs={{0,1},{1,0},{2,3},{3,2},{4,5},{5,4},{6,7},{7,6},{8,9},{9,8},{10,11... | collective-permute-start | bytes 3145736 | tf_op jit(solution)/shard_map/ppermute | solution.py:372
  284.5 43.6 %collective-permute-start.22 = (bf16[512,1024]{1,0:T(8,128)(2,1)S(1)}, bf16[512,1024]{1,0:T(8,128)(2,1)S(1)}, u32[]{:S(2)}, u32[]{:S(2)}) collective-permute-start(bf16[512,1024]{1,0:T(8,128)(2,1)S(1)} %add_convert_fusion.3), channel_id=1, source_target_pairs={{0,2},{1,3},{2,0},{3,1},{4,6},{5,7},{6,4},{7,5},{8,10},{9,11},{10,... | collective-permute-start | bytes 3145736 | tf_op jit(solution)/shard_map/ppermute | solution.py:372
  333.2 23.7 %collective-permute-start.30 = (bf16[512,1024]{1,0:T(8,128)(2,1)}, bf16[512,1024]{1,0:T(8,128)(2,1)}, u32[]{:S(2)}, u32[]{:S(2)}) collective-permute-start(bf16[512,1024]{1,0:T(8,128)(2,1)} %get-tuple-element.64), channel_id=1, source_target_pairs={{0,2},{1,3},{2,0},{3,1},{4,6},{5,7},{6,4},{7,5},{8,10},{9,11},{10,... | collective-permute-start | bytes 3145736 | tf_op jit(solution)/shard_map/ppermute | solution.py:372
  340.4 159.9 %reduce-scatter.7.cloned.1.call-start = ((), (), s32[]{:S(2)}) async-start(), calls=%async_computation.9 | async-start | bytes 1179648 | tf_op jit(solution)/shard_map/reduce_scatter | solution.py:894
  340.4 18.7 %collective-permute-start.29 = (bf16[512,1024]{1,0:T(8,128)(2,1)}, bf16[512,1024]{1,0:T(8,128)(2,1)S(1)}, u32[]{:S(2)}, u32[]{:S(2)}) collective-permute-start(bf16[512,1024]{1,0:T(8,128)(2,1)} %get-tuple-element.64), channel_id=1, source_target_pairs={{0,1},{1,0},{2,3},{3,2},{4,5},{5,4},{6,7},{7,6},{8,9},{9,8},{10,11... | collective-permute-start | bytes 3145736 | tf_op jit(solution)/shard_map/ppermute | solution.py:372
  356.9 4.7 collective-permute-start.31
  367.7 193.8 %reduce-scatter.9.cloned.1.call-start = ((), (), s32[]{:S(2)}) async-start(), calls=%async_computation.10 | async-start | bytes 3538944 | tf_op jit(solution)/shard_map/reduce_scatter | solution.py:894
  380.3 252.4 %reduce-scatter.5.cloned.1.call-start = ((), (), s32[]{:S(2)}) async-start(), calls=%async_computation.8 | async-start | bytes 2654208 | tf_op jit(solution)/shard_map/reduce_scatter | solution.py:894
  443.2 8.4 %collective-permute-start.32 = (bf16[512,1024]{1,0:T(8,128)(2,1)S(1)}, bf16[512,1024]{1,0:T(8,128)(2,1)S(1)}, u32[]{:S(2)}, u32[]{:S(2)}) collective-permute-start(bf16[512,1024]{1,0:T(8,128)(2,1)S(1)} %convolution_convert_fusion.6), channel_id=1, source_target_pairs={{0,1},{1,0},{2,3},{3,2},{4,5},{5,4},{6,7},{7,6},{8,9},{9,8},{10,11... | collective-permute-start | bytes 3145736 | tf_op jit(solution)/shard_map/ppermute | solution.py:372
  445.5 24.5 %collective-permute-start.34 = (bf16[512,1024]{1,0:T(8,128)(2,1)S(1)}, bf16[512,1024]{1,0:T(8,128)(2,1)S(1)}, u32[]{:S(2)}, u32[]{:S(2)}) collective-permute-start(bf16[512,1024]{1,0:T(8,128)(2,1)S(1)} %add_convert_fusion), channel_id=1, source_target_pairs={{0,2},{1,3},{2,0},{3,1},{4,6},{5,7},{6,4},{7,5},{8,10},{9,11},{10,... | collective-permute-start | bytes 3145736 | tf_op jit(solution)/shard_map/ppermute | solution.py:372
  476.7 22.9 %collective-permute-start.42 = (bf16[96,1024]{1,0:T(8,128)(2,1)}, bf16[96,1024]{1,0:T(8,128)(2,1)S(1)}, u32[]{:S(2)}, u32[]{:S(2)}) collective-permute-start(bf16[96,1024]{1,0:T(8,128)(2,1)} %reduce-scatter.11.cloned.1.call-done), channel_id=1, source_target_pairs={{0,0},{4,1},{8,2},{12,3},{16,4},{20,5},{24,6},{28,7},{1,8},{5,9},{... | collective-permute-start | bytes 589832 | tf_op jit(solution)/shard_map/ppermute | solution.py:939
  500.3 139.7 %collective-permute-start.38 = (bf16[64,1024]{1,0:T(8,128)(2,1)}, bf16[64,1024]{1,0:T(8,128)(2,1)S(1)}, u32[]{:S(2)}, u32[]{:S(2)}) collective-permute-start(bf16[64,1024]{1,0:T(8,128)(2,1)} %reduce-scatter.7.cloned.1.call-done), channel_id=1, source_target_pairs={{0,0},{4,1},{8,2},{12,3},{16,4},{20,5},{24,6},{28,7},{1,8},{5,9},{... | collective-permute-start | bytes 393224 | tf_op jit(solution)/shard_map/ppermute | solution.py:938
  562.5 6.9 %collective-permute-start.41 = (bf16[32,1536]{1,0:T(8,128)(2,1)S(1)}, bf16[32,1536]{1,0:T(8,128)(2,1)S(1)}, u32[]{:S(2)}, u32[]{:S(2)}) collective-permute-start(bf16[32,1536]{1,0:T(8,128)(2,1)S(1)} %get-tuple-element.80), channel_id=1, source_target_pairs={{0,3},{1,2},{2,1},{3,0},{4,7},{5,6},{6,5},{7,4},{8,11},{9,10},{10,... | collective-permute-start | bytes 294920 | tf_op jit(solution)/shard_map/ppermute | solution.py:372
  563.9 5.9 collective-permute-start.40
  565.1 4.7 collective-permute-start.39
  634.4 6.3 collective-permute-start.35
  636.7 4.4 collective-permute-start.36
  637.0 6.3 collective-permute-start.37
  (33 other events, 393.6 us)
Sparse Core Ops, SparseCore 0:
  23.3 55.3 all-gather.4
  81.4 37.0 all-gather.6
  121.3 61.0 all-gather.8
  204.8 52.9 all-gather.10
  340.5 63.5 reduce-scatter.10
  407.8 61.9 reduce-scatter.6
  473.3 88.0 reduce-scatter.8
  565.0 67.6 reduce-scatter.4

commit v2 on v1

--- a/solution.py
+++ b/solution.py
@@ -385,6 +385,87 @@
     return jnp.stack([pick(relative, me ^ source) for source in range(size)])
 
 
+def shift_z(value, offset):
+    size = lax.axis_size("dp")
+    return lax.ppermute(value, "dp", [(i, (i + 2 * offset) % size) for i in range(size)])
+
+
+def assemble_kernel(splits, count, places_ref, *refs):
+    pieces, results, sems = refs[:count], refs[count:-1], refs[-1]
+    copies = []
+    for n, piece in enumerate(pieces):
+        start = 0
+        for m, rows in enumerate(splits):
+            copy = pltpu.make_async_copy(
+                piece.at[pl.ds(start, rows)], results[m].at[places_ref[n]], sems.at[n, m]
+            )
+            copy.start()
+            copies.append(copy)
+            start += rows
+    for copy in copies:
+        copy.wait()
+
+
+def assemble(pieces, places, splits=None):
+    count = len(pieces)
+    rows, columns = pieces[0].shape
+    splits = (rows,) if splits is None else splits
+    anywhere = pl.BlockSpec(memory_space=pl.ANY)
+    results = pl.pallas_call(
+        functools.partial(assemble_kernel, splits, count),
+        in_specs=[pl.BlockSpec(memory_space=pltpu.SMEM)] + [anywhere] * count,
+        out_specs=[anywhere] * len(splits),
+        out_shape=[jax.ShapeDtypeStruct((count, n, columns), pieces[0].dtype) for n in splits],
+        scratch_shapes=[pltpu.SemaphoreType.DMA((count, len(splits)))],
+        cost_estimate=pl.CostEstimate(
+            flops=0, bytes_accessed=4 * count * rows * columns, transcendentals=0
+        ),
+        name="assemble",
+    )(places.astype(jnp.int32), *pieces)
+    return [result.reshape(-1, columns) for result in results]
+
+
+def join(blocks):
+    return assemble(blocks, jnp.arange(len(blocks)))[0]
+
+
+def gather_copies(value):
+    depth = lax.axis_size("dp") // 2
+    at = lax.axis_index("dp")
+    along = [value] + [shift_z(value, k) for k in range(1, depth)]
+    beside = [xor_permute(piece, "dp", 1) for piece in along]
+    rows = jnp.stack([(at // 2 - k) % depth for k in range(depth)])
+    places = jnp.concatenate([rows * 2 + at % 2, rows * 2 + 1 - at % 2])
+    return along + beside, places
+
+
+def reduce_beside(grad):
+    depth = grad.shape[0] // 2
+    y = lax.axis_index("dp") % 2
+    grad = grad.reshape((depth, 2) + grad.shape[1:])
+    away = lax.dynamic_index_in_dim(grad, 1 - y, 1, keepdims=False)
+    kept = lax.dynamic_index_in_dim(grad, y, 1, keepdims=False)
+    return (kept.astype(f32) + xor_permute(away, "dp", 1).astype(f32)).astype(bf16)
+
+
+def reduce_along(pair):
+    depth = pair.shape[0]
+    z = lax.axis_index("dp") // 2
+    sent = [shift_z(pick(pair, (z + k) % depth), k) for k in range(1, depth)]
+    return [pick(pair, z)] + sent
+
+
+def add_all(terms):
+    total = terms[0].astype(f32)
+    for term in terms[1:]:
+        total = total + term.astype(f32)
+    return total.astype(bf16)
+
+
+def after(value, *others):
+    return lax.optimization_barrier((value, *others))[0]
+
+
 def gather_blocks(value):
     across = xor_permute(value, "ctx", 2)
     beside = xor_permute(value, "ctx", 1)
@@ -392,12 +473,14 @@
     return [value, beside, across, corner]
 
 
-def scatter_sum(part):
+def scatter_sum(part, waits=()):
     corner = xor_permute(part(3).astype(bf16), "ctx", 1)
-    toward = part(2) + corner.astype(f32)
-    across = xor_permute(toward.astype(bf16), "ctx", 2)
+    toward = (part(2) + corner.astype(f32)).astype(bf16)
+    if waits:
+        toward = after(toward, *waits)
+    across = xor_permute(toward, "ctx", 2)
     beside = xor_permute(part(1).astype(bf16), "ctx", 1)
-    return part(0) + beside.astype(f32) + across.astype(f32)
+    return part(0) + beside.astype(f32) + across.astype(f32), across
 
 
 def nt_dot(left, right):
@@ -810,14 +893,14 @@
 
     x_own = tokens.reshape(block, MODEL_WIDTH)
     x_blocks = gather_blocks(x_own)
-    x_all = jnp.concatenate(x_blocks)
+    x_all = join(x_blocks)
     places = jnp.concatenate([positions, segment_ids]).astype(jnp.int32)
     places = jnp.concatenate(gather_blocks(places), axis=1)
 
     first = jnp.concatenate(
         [by_columns(w_query), by_columns(key_weight), by_columns(value_weight)], axis=2
     )
-    gain_rows = jnp.zeros((pad_rows, first.shape[2]), bf16).at[0, :gain_count].set(gains)
+    gain_rows = jnp.pad(gains[None], ((0, pad_rows - 1), (0, first.shape[2] - gain_count)))
     first = jnp.concatenate(
         [first, jnp.broadcast_to(gain_rows[None], (size,) + gain_rows.shape)], axis=1
     )
@@ -828,23 +911,26 @@
     first = jnp.concatenate(
         [first[:, :owned].reshape(size * owned, first.shape[2]), gain_rows]
     )
-    first = lax.all_gather(first, "dp", axis=0, tiled=True)
-    first = first.reshape(copies, size * owned + pad_rows, -1)
-    w_first = first[:, : size * owned].reshape(MODEL_WIDTH, -1)
-    full_gains = first[:, size * owned : size * owned + size, :gain_count].reshape(-1)
+    first_pieces, places_dp = gather_copies(first)
+    cot_own = cotangent.reshape(block, MODEL_WIDTH)
+    cot_blocks = gather_blocks(after(cot_own, x_blocks[2]))
+    w_first, gain_rows = assemble(first_pieces, places_dp, (size * owned, pad_rows))
+    w_first = after(w_first, *cot_blocks)
+    full_gains = gain_rows.reshape(copies, pad_rows, -1)[:, :size, :gain_count].reshape(-1)
     gain_attn, gain_mlp, gain_query, gain_key = split_gains(full_gains)
 
+    early = first_pieces[1:copies // 2]
     out_rows = lax.ppermute(w_out, ("dp", "ctx"), forward_owner)
-    out_full = lax.all_gather(out_rows, "dp", axis=0, tiled=True)
+    out_pieces, unused = gather_copies(after(out_rows, *early))
+    out_full = assemble(out_pieces, places_dp)[0]
     gate_up = jnp.concatenate([by_columns(w_gate), by_columns(w_up)], axis=2)
     gate_up = exchange(gate_up, me).reshape(size * owned, -1)
-    gate_up = lax.all_gather(gate_up, "dp", axis=0, tiled=True)
+    gate_up_pieces, unused = gather_copies(after(gate_up, *early))
+    gate_up = assemble(gate_up_pieces, places_dp)[0]
     down_rows = lax.ppermute(w_down, ("dp", "ctx"), forward_owner)
-    down_full = lax.all_gather(down_rows, "dp", axis=0, tiled=True)
-
-    cot_own = cotangent.reshape(block, MODEL_WIDTH)
-    cot_tied, unused = lax.optimization_barrier((cot_own, x_blocks[2]))
-    cot_all = jnp.concatenate(gather_blocks(cot_tied))
+    down_pieces, unused = gather_copies(after(down_rows, *early))
+    down_full = assemble(down_pieces, places_dp)[0]
+    cot_all = join(cot_blocks)
 
     half = HEAD_SIZE // 2
     rates = THETA ** (-2.0 * jnp.arange(half, dtype=f32) / HEAD_SIZE)
@@ -860,14 +946,17 @@
     normed, raw, q, k, v = project(
         x_all, gain_attn[None], w_first, cosine, sine, gain_q_row, gain_k_row, query_heads, key_heads
     )
+    q = after(q, *out_pieces[1:4], *gate_up_pieces[1:4])
     attended, logs = attend(me_row, q, query_features, k, key_features, v, block, group)
+
+    attended = after(attended, *out_pieces[4:], *gate_up_pieces[4:], *down_pieces[1:4])
 
     def rows_of(value, r):
         return value[r * block : (r + 1) * block]
 
-    branch = scatter_sum(lambda r: nn_dot(rows_of(attended, r), out_full))
+    branch, unused = scatter_sum(lambda r: nn_dot(rows_of(attended, r), out_full))
     middle = x_own.astype(f32) + branch
-    normed_mlp = jnp.concatenate(gather_blocks(row_norm_apply(middle, gain_mlp).astype(bf16)))
+    normed_mlp = join(gather_blocks(row_norm_apply(middle, gain_mlp).astype(bf16)))
     both = nn_dot(normed_mlp, gate_up)
     gate_value, up_value = both[:, :hidden_cols], both[:, hidden_cols:]
     d_hidden = nt_dot(cot_all, down_full)
@@ -878,45 +967,54 @@
     d_up = (d_hidden * silu).astype(bf16)
     d_both = jnp.concatenate([d_gate, d_up], axis=1)
 
-    d_normed = scatter_sum(lambda r: nt_dot(rows_of(d_both, r), gate_up))
+    d_normed, unused = scatter_sum(lambda r: nt_dot(rows_of(d_both, r), gate_up))
     d_middle, d_gain_mlp = norm_back(middle, gain_mlp, d_normed)
     d_middle = d_middle + cot_own.astype(f32)
-    d_branch = jnp.concatenate(gather_blocks(d_middle.astype(bf16)))
+    d_branch_blocks = gather_blocks(d_middle.astype(bf16))
+    d_branch = join(d_branch_blocks)
     d_attended = nt_dot(d_branch, out_full).astype(bf16)
 
-    down = scatter_sum(lambda r: nn_dot(rows_of(hidden, r), down_full))
+    down, down_across = scatter_sum(lambda r: nn_dot(rows_of(hidden, r), down_full), d_branch_blocks[2:3])
     output = (middle + down).astype(bf16)
 
     def tn_dot(left, right):
         return lax.dot_general(left, right, (((0,), (0,)), ((), ())), preferred_element_type=f32)
 
-    def reduce_rows(grad):
-        return lax.psum_scatter(grad.astype(bf16), "dp", scatter_dimension=0, tiled=True)
-
-    grad_down = reduce_rows(tn_dot(hidden, cot_all))
-    grad_both = reduce_rows(tn_dot(normed_mlp, d_both))
-    grad_out = reduce_rows(tn_dot(attended, d_branch))
+    def by_copy(grad):
+        return grad.astype(bf16).reshape(copies, -1, grad.shape[-1])
+
+    pair_down = reduce_beside(by_copy(tn_dot(hidden, cot_all)))
+    pair_both = reduce_beside(by_copy(tn_dot(normed_mlp, d_both)))
+    pair_out = reduce_beside(by_copy(tn_dot(attended, d_branch)))
+    terms_down = reduce_along(after(pair_down, d_branch_blocks[2]))
+    terms_both = reduce_along(after(pair_both, d_attended))
 
     dq, dk, dv = unattend(
         me_row, q, query_features, k, key_features, v, attended, d_attended, logs, block, group
     )
+    dq = after(dq, *terms_down, *terms_both, pair_out, down_across)
+    terms_out = reduce_along(after(pair_out, dq))
     low, d_gain_heads = unproject(
         dq, dk, dv, raw, cosine, sine, gain_q_row, gain_k_row, query_heads, key_heads
     )
-    d_normed_attn = scatter_sum(lambda r: nt_dot(rows_of(low, r), w_first))
-    d_inputs, d_gain_attn = norm_back(x_own.astype(f32), gain_attn, d_normed_attn)
+    d_normed_attn, unused = scatter_sum(lambda r: nt_dot(rows_of(low, r), w_first))
+    d_inputs, unused = norm_back(x_own.astype(f32), gain_attn, d_normed_attn)
     grad_tokens = (d_middle + d_inputs).reshape(tokens.shape)
 
     grad_first = tn_dot(normed, low).astype(bf16)
+    d_gain_attn = jnp.sum(w_first.astype(f32) * grad_first.astype(f32), axis=1) / gain_attn
     grad_gains = jnp.concatenate(
         [d_gain_attn, d_gain_mlp, d_gain_heads[0], d_gain_heads[1]]
     ).reshape(copies, size, gain_count)
-    gain_block = jnp.zeros((copies, pad_rows, grad_first.shape[1]), bf16)
-    gain_block = gain_block.at[:, :size, :gain_count].set(grad_gains.astype(bf16))
+    gain_block = jnp.pad(
+        grad_gains.astype(bf16),
+        ((0, 0), (0, pad_rows - size), (0, grad_first.shape[1] - gain_count)),
+    )
     grad_first = jnp.concatenate(
         [grad_first.reshape(copies, size * owned, -1), gain_block], axis=1
-    ).reshape(-1, grad_first.shape[1])
-    grad_first = reduce_rows(grad_first)
+    )
+    grad_first = add_all(reduce_along(reduce_beside(grad_first)))
+    grad_down, grad_both, grad_out = map(add_all, (terms_down, terms_both, terms_out))
     gain_part = grad_first[size * owned :][:size]
     gain_part = jnp.broadcast_to(gain_part[:, None], (size, pad_rows, gain_part.shape[1]))
     grad_first = jnp.concatenate(

time: 664 us -> 1330 us (2.00)
  Pallas kernels: 85.1 us -> 855 us
  waiting for transfers between devices: 337 us -> 189 us
  starting transfers between devices: 51.5 us -> 107 us
  local copies, waits for them, and re-layouts: 38.4 us -> 22.2 us
    pallas_call x0 -> x8, Pallas kernels: none -> 769 us  [assemble(): pl.pallas_call(functools.partial(assemble_kernel, splits, count), in_spec...]
    reduce_scatter x4 -> x0, waiting for transfers between devices: 122 us -> none  [reduce_rows(): lax.psum_scatter(grad.astype(bf16), 'dp', scatter_dimension=0, tiled=True)]
    all_gather x4 -> x0, waiting for transfers between devices: 45.3 us -> none  [the longest x1 30.8 us: split_local(): down_full = lax.all_gather(down_rows, 'dp', axis=0, tiled=True)]
    ppermute x0 -> x24, waiting for transfers between devices: none -> 42.2 us  [shift_z(): lax.ppermute(value, 'dp', [(i, (i + 2 * offset) % size) for i in range(si...]
    ppermute x0 -> x24, starting transfers between devices: none -> 32.2 us  [shift_z(): lax.ppermute(value, 'dp', [(i, (i + 2 * offset) % size) for i in range(si...]
    ppermute x39 -> x59, starting transfers between devices: 40.2 us -> 61.7 us  [xor_permute(): return lax.ppermute(value, axis, [(i, i ^ offset) for i in range(size)])]
    ppermute x1, waiting for transfers between devices: 19.7 us -> 5.48 us  [split_local(): lax.ppermute(grad_down, ('dp', 'ctx'), backward_owner).astype(f32)]
    ppermute x39 -> x59, waiting for transfers between devices: 145 us -> 140 us  [xor_permute(): return lax.ppermute(value, axis, [(i, i ^ offset) for i in range(size)])]
  transfers between devices with their start and end apart: 51 -> 87, of which waited for: 23 -> 29; matrix products, arithmetic and copies ran while one was open for 20% -> 7% of each run, Pallas kernels for 13% -> 54%
where the time goes in v2:
time: 1330 us; the launch traced here: 1310 us
  Pallas kernels  855 us (64%)
  waiting for transfers between devices  189 us (14%)
  starting transfers between devices  107 us (8%)
  matrix products  101 us (8%)
  other arithmetic  31.8 us (2%)
  local copies, waits for them, and re-layouts  22.2 us (2%)
    pallas_call x8, Pallas kernels, assemble(): pl.pallas_call(functools.partial(assemble_kernel, splits, count), in_spec...  769 us
    ppermute x59, waiting for transfers between devices, xor_permute(): return lax.ppermute(value, axis, [(i, i ^ offset) for i in range(size)])  140 us
    ppermute x59, starting transfers between devices, xor_permute(): return lax.ppermute(value, axis, [(i, i ^ offset) for i in range(size)])  61.7 us
    dot_general x10, matrix products, nt_dot(): lax.dot_general(left, right, (((1,), (1,)), ((), ())), preferred_element_...  43.1 us
    ppermute x24, waiting for transfers between devices, shift_z(): lax.ppermute(value, 'dp', [(i, (i + 2 * offset) % size) for i in range(si...  42.2 us
    pallas_call x1, Pallas kernels, unattend(): pl.pallas_call(functools.partial(unattend_kernel, group, block), grid_spe...  37.8 us
    ppermute x24, starting transfers between devices, shift_z(): lax.ppermute(value, 'dp', [(i, (i + 2 * offset) % size) for i in range(si...  32.2 us
    dot_general x9, matrix products, nn_dot(): return jnp.dot(left, right, preferred_element_type=f32)  30.6 us
  transfers between devices with their start and end apart: 87, of which 29 were waited for; matrix products, arithmetic and copies ran while one was open for 7% of the time, Pallas kernels for 54%

profile of v2, /device:TPU:27, one launch (start us, length us, event | category | flops | bytes accessed | tf_op | source)
XLA Modules:
  0.0 1308.0 jit_solution(17347970057866561087)
XLA Ops:
  20.6 3.7 fusion.58
  24.3 12.5 collective-permute-done.1.refs_2_
  39.0 7.9 collective-permute-done.7.refs_2_
  46.9 3.2 collective-permute-start.37
  51.7 3.6 collective-permute-start.20
  57.1 7.7 collective-permute-start.22
  68.1 5.2 collective-permute-start.10
  77.0 12.7 collective-permute-done.30.refs_5_
  98.5 33.6 %assemble.10 = bf16[8,64,1024]{2,1,0:T(8,128)(2,1)} custom-call(s32[8]{0:T(128)} %pad_add_fusion.2.places_ref, bf16[64,1024]{1,0:T(8,128)(2,1)} %copy-done.39, bf16[64,1024]{1,0:T(8,128)(2,1)} %copy-done.40, bf16[64,1024]{1,0:T(8,128)(2,1)} %copy-done.41, bf16[64,1024]{1,0:T(8,128)(2,1)} %copy-done.42, bf16[64,1024]{1,0:T(8,128)(2,1)} %copy-done.43, ...), custom_call_target="tpu_custom_call" | custom-call | bytes 2097152 | tf_op jit(solution)/shard_map/assemble/pallas_call | solution.py:414
  132.1 73.4 %assemble.9 = (bf16[8,128,1024]{2,1,0:T(8,128)(2,1)}, bf16[8,16,1024]{2,1,0:T(8,128)(2,1)}) custom-call(s32[8]{0:T(128)} %pad_add_fusion.2.places_ref, bf16[144,1024]{1,0:T(8,128)(2,1)} %copy-done.21, bf16[144,1024]{1,0:T(8,128)(2,1)} %copy-done.29, bf16[144,1024]{1,0:T(8,128)(2,1)} %copy-done.30, bf16[144,1024]{1,0:T(8,128)(2,1)} %collective-permute-done.8.refs_3_, ...), custom_call_target="tpu_custom_call" | custom-call | bytes 4718592 | tf_op jit(solution)/shard_map/assemble/pallas_call | solution.py:414
  211.6 128.9 %assemble.8 = bf16[4,512,1024]{2,1,0:T(8,128)(2,1)} custom-call(s32[4]{0:T(128)} %iota.21.places_ref, bf16[512,1024]{1,0:T(8,128)(2,1)} %bitcast.212, bf16[512,1024]{1,0:T(8,128)(2,1)} %collective-permute-done.refs_1_, bf16[512,1024]{1,0:T(8,128)(2,1)} %collective-permute-done.1.refs_2_, bf16[512,1024]{1,0:T(8,128)(2,1)} %collective-permute-done.2.refs_3_), custom_call_target="tpu_custom_call" | custom-call | bytes 8388608 | tf_op jit(solution)/shard_map/assemble/pallas_call | solution.py:414
  343.0 13.0 project.1
  360.5 20.8 %attend.1 = (bf16[2048,512]{1,0:T(8,128)(2,1)}, f32[2,2,2048]{2,1,0:T(2,128)}) custom-call(s32[1]{0:T(128)} %bitcast.1.me_ref, bf16[2048,512]{1,0:T(8,128)(2,1)} %get-tuple-element.43.q_ref, bf16[2048,128]{1,0:T(8,128)(2,1)} %select_convert_fusion.qf_ref, bf16[2048,256]{1,0:T(8,128)(2,1)} %get-tuple-element.44.k_ref, bf16[2048,128]{1,0:T(8,128)(2,1)} %fusion.46.kf_ref, ...), custom_call_target="tpu_custom_call" | custom-call | flops 10737418240 | bytes 10485760 | tf_op jit(solution)/shard_map/attend/pallas_call | solution.py:706
  382.4 8.4 collective-permute-done.36.refs_7_
  398.7 23.7 %collective-permute-done.43 = bf16[512,1024]{1,0:T(8,128)(2,1)S(1)} collective-permute-done((bf16[512,1024]{1,0:T(8,128)(2,1)S(1)}, bf16[512,1024]{1,0:T(8,128)(2,1)S(1)}, u32[]{:S(2)}, u32[]{:S(2)}) %collective-permute-start.43) | collective-permute-done | bytes 1048608 | tf_op jit(solution)/shard_map/ppermute | solution.py:372
  426.5 22.0 %collective-permute-done.45.refs_2_ = bf16[512,1024]{1,0:T(8,128)(2,1)} collective-permute-done((bf16[512,1024]{1,0:T(8,128)(2,1)}, bf16[512,1024]{1,0:T(8,128)(2,1)}, u32[]{:S(2)}, u32[]{:S(2)}) %collective-permute-start.45) | collective-permute-done | bytes 1048608 | tf_op jit(solution)/shard_map/ppermute | solution.py:372
  452.6 4.7 collective-permute-done.47.refs_4_
  457.9 3.7 collective-permute-done.48.refs_5_
  461.6 4.3 collective-permute-done.49.refs_6_
  465.9 4.2 collective-permute-done.50.refs_7_
  470.1 49.5 %assemble.13 = bf16[8,96,1024]{2,1,0:T(8,128)(2,1)} custom-call(s32[8]{0:T(128)} %pad_add_fusion.2.places_ref, bf16[96,1024]{1,0:T(8,128)(2,1)} %collective-permute-done.37.refs_0_, bf16[96,1024]{1,0:T(8,128)(2,1)} %collective-permute-done.38.refs_1_, bf16[96,1024]{1,0:T(8,128)(2,1)} %collective-permute-done.39.refs_2_, ...), custom_call_target="tpu_custom_call" | custom-call | bytes 3145728 | tf_op jit(solution)/shard_map/assemble/pallas_call | solution.py:414
  519.6 97.1 %assemble.12 = bf16[8,128,1536]{2,1,0:T(8,128)(2,1)} custom-call(s32[8]{0:T(128)} %pad_add_fusion.2.places_ref, bf16[128,1536]{1,0:T(8,128)(2,1)} %bitcast.247, bf16[128,1536]{1,0:T(8,128)(2,1)} %collective-permute-done.26.refs_1_, bf16[128,1536]{1,0:T(8,128)(2,1)} %copy-done.23, bf16[128,1536]{1,0:T(8,128)(2,1)} %copy-done.24, ...), custom_call_target="tpu_custom_call" | custom-call | bytes 6291456 | tf_op jit(solution)/shard_map/assemble/pallas_call | solution.py:414
  617.3 128.9 %assemble.14 = bf16[4,512,1024]{2,1,0:T(8,128)(2,1)} custom-call(s32[4]{0:T(128)} %iota.24.places_ref, bf16[512,1024]{1,0:T(8,128)(2,1)} %bitcast.215, bf16[512,1024]{1,0:T(8,128)(2,1)} %copy-done.22, bf16[512,1024]{1,0:T(8,128)(2,1)} %collective-permute-done.14.refs_2_, bf16[512,1024]{1,0:T(8,128)(2,1)} %collective-permute-done.15.refs_3_), custom_call_target="tpu_custom_call" | custom-call | bytes 8388608 | tf_op jit(solution)/shard_map/assemble/pallas_call | solution.py:414
  746.7 128.9 %assemble.11 = bf16[4,512,1024]{2,1,0:T(8,128)(2,1)} custom-call(s32[4]{0:T(128)} %iota.23.places_ref, bf16[512,1024]{1,0:T(8,128)(2,1)} %multiply_convert_fusion.3.refs_0_, bf16[512,1024]{1,0:T(8,128)(2,1)} %collective-permute-done.44.refs_1_, bf16[512,1024]{1,0:T(8,128)(2,1)} %collective-permute-done.45.refs_2_, ...), custom_call_target="tpu_custom_call" | custom-call | bytes 8388608 | tf_op jit(solution)/shard_map/assemble/pallas_call | solution.py:414
  875.5 12.5 fusion.84
  888.0 18.4 %multiply_convert_fusion = (bf16[2048,768]{0,1:T(8,128)(2,1)S(1)}, bf16[2048,768]{0,1:T(8,128)(2,1)S(1)}, bf16[2048,768]{0,1:T(8,128)(2,1)}) fusion(f32[2048,1536]{0,1:T(8,128)} %fusion.84, bf16[2048,1024]{1,0:T(8,128)(2,1)S(1)} %bitcast.229, bf16[768,1024]{1,0:T(8,128)(2,1)S(1)} %bitcast.249), kind=kOutput, calls=%fused_computation.10 | convolution fusion | flops 3244818432 | bytes 27787264 | tf_op jit(solution)/shard_map/dot_general | solution.py:487
  914.1 3.5 convolution_convert_fusion.2
  922.3 9.2 fusion.2
  931.6 13.5 %collective-permute-done.55 = bf16[512,1024]{1,0:T(8,128)(2,1)S(1)} collective-permute-done((bf16[512,1024]{1,0:T(8,128)(2,1)S(1)}, bf16[512,1024]{1,0:T(8,128)(2,1)S(1)}, u32[]{:S(2)}, u32[]{:S(2)}) %collective-permute-start.55) | collective-permute-done | bytes 1048608 | tf_op jit(solution)/shard_map/ppermute | solution.py:372
  945.1 4.2 multiply_reduce_fusion.1
  961.5 12.9 collective-permute-done.56.refs_2_
  984.9 3.5 add_convert_fusion.3
  988.4 8.5 collective-permute-done.62
  997.9 3.4 collective-permute-start.86
  1006.1 5.5 collective-permute-done.86
  1012.9 128.9 %assemble.15 = bf16[4,512,1024]{2,1,0:T(8,128)(2,1)} custom-call(s32[4]{0:T(128)} %iota.25.places_ref, bf16[512,1024]{1,0:T(8,128)(2,1)} %fusion.81.refs_0_, bf16[512,1024]{1,0:T(8,128)(2,1)} %collective-permute-done.58.refs_1_, bf16[512,1024]{1,0:T(8,128)(2,1)} %collective-permute-done.56.refs_2_, bf16[512,1024]{1,0:T(8,128)(2,1)} %collective-permute-done.59.refs_3_), custom_call_target="tpu_custom_call" | custom-call | bytes 8388608 | tf_op jit(solution)/shard_map/assemble/pallas_call | solution.py:414
  1141.8 6.3 convolution_convert_fusion.do_ref
  1150.5 37.8 %unattend.1 = (f32[2048,512]{1,0:T(8,128)}, f32[2048,256]{1,0:T(8,128)}, f32[2048,256]{1,0:T(8,128)}) custom-call(s32[1]{0:T(128)} %bitcast.1.me_ref, bf16[2048,512]{1,0:T(8,128)(2,1)} %get-tuple-element.43.q_ref, bf16[2048,128]{1,0:T(8,128)(2,1)} %select_convert_fusion.qf_ref, bf16[2048,256]{1,0:T(8,128)(2,1)} %get-tuple-element.44.k_ref, ...), custom_call_target="tpu_custom_call" | custom-call | flops 18790481920 | bytes 20971520 | tf_op jit(solution)/shard_map/unattend/pallas_call | solution.py:816
  1188.3 5.2 convolution_convert_fusion.9
  1198.0 3.9 fusion.36
  1207.5 13.9 %unproject.1 = (bf16[2048,1024]{1,0:T(8,128)(2,1)}, f32[8,128]{1,0:T(8,128)}) custom-call(f32[2048,512]{1,0:T(8,128)} %get-tuple-element.54.dq_ref, f32[2048,256]{1,0:T(8,128)} %get-tuple-element.55.dk_ref, f32[2048,256]{1,0:T(8,128)} %get-tuple-element.56.dv_ref, f32[2048,768]{1,0:T(8,128)} %get-tuple-element.57.raw_ref, ...), custom_call_target="tpu_custom_call" | custom-call | flops 41943040 | bytes 20971520 | tf_op jit(solution)/shard_map/unproject/pallas_call | solution.py:639
  1221.4 9.5 multiply_reduce_fusion
  1247.0 7.7 collective-permute-done.80
  1254.7 3.5 collective-permute-start.82
  1269.0 4.1 collective-permute-start.71
  1273.1 14.9 %collective-permute-done.74 = bf16[144,1024]{1,0:T(8,128)(2,1)S(1)} collective-permute-done((bf16[144,1024]{1,0:T(8,128)(2,1)S(1)}, bf16[144,1024]{1,0:T(8,128)(2,1)S(1)}, u32[]{:S(2)}, u32[]{:S(2)}) %collective-permute-start.74) | collective-permute-done | bytes 294944 | tf_op jit(solution)/shard_map/ppermute | solution.py:390
  1288.3 3.4 collective-permute-start.76
  1296.6 4.1 collective-permute-done.78
  (385 shorter events, 166.0 us)
Async XLA Ops:
  10.6 26.2 %collective-permute-start.1 = (bf16[512,1024]{1,0:T(8,128)(2,1)S(1)}, bf16[512,1024]{1,0:T(8,128)(2,1)}, u32[]{:S(2)}, u32[]{:S(2)}) collective-permute-start(bf16[512,1024]{1,0:T(8,128)(2,1)S(1)} %bitcast.213), channel_id=1, source_target_pairs={{0,2},{1,3},{2,0},{3,1},{4,6},{5,7},{6,4},{7,5},{8,10},{9,11},{10,... | collective-permute-start | bytes 3145736 | tf_op jit(solution)/shard_map/ppermute | solution.py:372
  11.8 25.5 %collective-permute-start.19 = (bf16[64,1024]{1,0:T(8,128)(2,1)S(1)}, bf16[64,1024]{1,0:T(8,128)(2,1)S(1)}, u32[]{:S(2)}, u32[]{:S(2)}) collective-permute-start(bf16[64,1024]{1,0:T(8,128)(2,1)S(1)} %copy-done.59), channel_id=1, source_target_pairs={{0,0},{1,4},{2,8},{3,12},{4,16},{5,20},{6,24},{7,28},{8,1},{9,5},{... | collective-permute-start | bytes 393224 | tf_op jit(solution)/shard_map/ppermute | solution.py:923
  18.4 20.1 %collective-permute-start.6 = (bf16[144,1024]{1,0:T(8,128)(2,1)S(1)}, bf16[144,1024]{1,0:T(8,128)(2,1)S(1)}, u32[]{:S(2)}, u32[]{:S(2)}) collective-permute-start(bf16[144,1024]{1,0:T(8,128)(2,1)S(1)} %maximum_maximum_fusion.refs_0_), channel_id=1, source_target_pairs={{0,8},{4,12},{8,16},{12,20},{16,24},{20,28},{24,0},{28,4},{1,9},{5... | collective-permute-start | bytes 884744 | tf_op jit(solution)/shard_map/ppermute | solution.py:390
  20.2 26.6 %collective-permute-start.7 = (bf16[144,1024]{1,0:T(8,128)(2,1)S(1)}, bf16[144,1024]{1,0:T(8,128)(2,1)S(1)}, u32[]{:S(2)}, u32[]{:S(2)}) collective-permute-start(bf16[144,1024]{1,0:T(8,128)(2,1)S(1)} %maximum_maximum_fusion.refs_0_), channel_id=1, source_target_pairs={{0,16},{4,20},{8,24},{12,28},{16,0},{20,4},{24,8},{28,12},{1,17},{... | collective-permute-start | bytes 884744 | tf_op jit(solution)/shard_map/ppermute | solution.py:390
  20.5 29.6 %collective-permute-start.8 = (bf16[144,1024]{1,0:T(8,128)(2,1)S(1)}, bf16[144,1024]{1,0:T(8,128)(2,1)}, u32[]{:S(2)}, u32[]{:S(2)}) collective-permute-start(bf16[144,1024]{1,0:T(8,128)(2,1)S(1)} %maximum_maximum_fusion.refs_0_), channel_id=1, source_target_pairs={{0,24},{4,28},{8,0},{12,4},{16,8},{20,12},{24,16},{28,20},{1,25},{... | collective-permute-start | bytes 884744 | tf_op jit(solution)/shard_map/ppermute | solution.py:390
  38.5 16.8 %collective-permute-start.25 = (bf16[32,1536]{1,0:T(8,128)(2,1)S(1)}, bf16[32,1536]{1,0:T(8,128)(2,1)S(1)}, u32[]{:S(2)}, u32[]{:S(2)}) collective-permute-start(bf16[32,1536]{1,0:T(8,128)(2,1)S(1)} %get-tuple-element.112), channel_id=1, source_target_pairs={{0,3},{1,2},{2,1},{3,0},{4,7},{5,6},{6,5},{7,4},{8,11},{9,10},{10,... | collective-permute-start | bytes 294920 | tf_op jit(solution)/shard_map/ppermute | solution.py:372
  50.1 47.7 %collective-permute-start.14 = (bf16[512,1024]{1,0:T(8,128)(2,1)S(1)}, bf16[512,1024]{1,0:T(8,128)(2,1)}, u32[]{:S(2)}, u32[]{:S(2)}) collective-permute-start(bf16[512,1024]{1,0:T(8,128)(2,1)S(1)} %bitcast.216), channel_id=1, source_target_pairs={{0,2},{1,3},{2,0},{3,1},{4,6},{5,7},{6,4},{7,5},{8,10},{9,11},{10,... | collective-permute-start | bytes 3145736 | tf_op jit(solution)/shard_map/ppermute | solution.py:372
  55.3 18.0 %collective-permute-start.21 = (bf16[64,1024]{1,0:T(8,128)(2,1)S(1)}, bf16[64,1024]{1,0:T(8,128)(2,1)S(1)}, u32[]{:S(2)}, u32[]{:S(2)}) collective-permute-start(bf16[64,1024]{1,0:T(8,128)(2,1)S(1)} %collective-permute-done.19.refs_0_), channel_id=1, source_target_pairs={{0,16},{4,20},{8,24},{12,28},{16,0},{20,4},{24,8},{28,12},{1,17},{... | collective-permute-start | bytes 393224 | tf_op jit(solution)/shard_map/ppermute | solution.py:390
  68.1 27.6 %collective-permute-start.10 = (bf16[144,1024]{1,0:T(8,128)(2,1)S(1)}, bf16[144,1024]{1,0:T(8,128)(2,1)S(1)}, u32[]{:S(2)}, u32[]{:S(2)}) collective-permute-start(bf16[144,1024]{1,0:T(8,128)(2,1)S(1)} %collective-permute-done.6.refs_1_), channel_id=1, source_target_pairs={{0,4},{4,0},{8,12},{12,8},{16,20},{20,16},{24,28},{28,24},{1,5},{5... | collective-permute-start | bytes 884744 | tf_op jit(solution)/shard_map/ppermute | solution.py:372
  73.3 24.5 %collective-permute-start.11 = (bf16[144,1024]{1,0:T(8,128)(2,1)S(1)}, bf16[144,1024]{1,0:T(8,128)(2,1)S(1)}, u32[]{:S(2)}, u32[]{:S(2)}) collective-permute-start(bf16[144,1024]{1,0:T(8,128)(2,1)S(1)} %collective-permute-done.7.refs_2_), channel_id=1, source_target_pairs={{0,4},{4,0},{8,12},{12,8},{16,20},{20,16},{24,28},{28,24},{1,5},{5... | collective-permute-start | bytes 884744 | tf_op jit(solution)/shard_map/ppermute | solution.py:372
  92.5 117.1 %collective-permute-start = (bf16[512,1024]{1,0:T(8,128)(2,1)S(1)}, bf16[512,1024]{1,0:T(8,128)(2,1)}, u32[]{:S(2)}, u32[]{:S(2)}) collective-permute-start(bf16[512,1024]{1,0:T(8,128)(2,1)S(1)} %bitcast.214), channel_id=1, source_target_pairs={{0,1},{1,0},{2,3},{3,2},{4,5},{5,4},{6,7},{7,6},{8,9},{9,8},{10,11... | collective-permute-start | bytes 3145736 | tf_op jit(solution)/shard_map/ppermute | solution.py:372
  94.5 37.6 %collective-permute-start.12 = (bf16[144,1024]{1,0:T(8,128)(2,1)}, bf16[144,1024]{1,0:T(8,128)(2,1)}, u32[]{:S(2)}, u32[]{:S(2)}) collective-permute-start(bf16[144,1024]{1,0:T(8,128)(2,1)} %collective-permute-done.8.refs_3_), channel_id=1, source_target_pairs={{0,4},{4,0},{8,12},{12,8},{16,20},{20,16},{24,28},{28,24},{1,5},{5... | collective-permute-start | bytes 884744 | tf_op jit(solution)/shard_map/ppermute | solution.py:372
  95.8 244.8 %collective-permute-start.13 = (bf16[512,1024]{1,0:T(8,128)(2,1)S(1)}, bf16[512,1024]{1,0:T(8,128)(2,1)S(1)}, u32[]{:S(2)}, u32[]{:S(2)}) collective-permute-start(bf16[512,1024]{1,0:T(8,128)(2,1)S(1)} %bitcast.217), channel_id=1, source_target_pairs={{0,1},{1,0},{2,3},{3,2},{4,5},{5,4},{6,7},{7,6},{8,9},{9,8},{10,11... | collective-permute-start | bytes 3145736 | tf_op jit(solution)/shard_map/ppermute | solution.py:372
  97.7 112.2 %collective-permute-start.2 = (bf16[512,1024]{1,0:T(8,128)(2,1)}, bf16[512,1024]{1,0:T(8,128)(2,1)}, u32[]{:S(2)}, u32[]{:S(2)}) collective-permute-start(bf16[512,1024]{1,0:T(8,128)(2,1)} %collective-permute-done.1.refs_2_), channel_id=1, source_target_pairs={{0,1},{1,0},{2,3},{3,2},{4,5},{5,4},{6,7},{7,6},{8,9},{9,8},{10,11... | collective-permute-start | bytes 3145736 | tf_op jit(solution)/shard_map/ppermute | solution.py:372
  97.8 244.8 %collective-permute-start.15 = (bf16[512,1024]{1,0:T(8,128)(2,1)}, bf16[512,1024]{1,0:T(8,128)(2,1)}, u32[]{:S(2)}, u32[]{:S(2)}) collective-permute-start(bf16[512,1024]{1,0:T(8,128)(2,1)} %collective-permute-done.14.refs_2_), channel_id=1, source_target_pairs={{0,1},{1,0},{2,3},{3,2},{4,5},{5,4},{6,7},{7,6},{8,9},{9,8},{10,11... | collective-permute-start | bytes 3145736 | tf_op jit(solution)/shard_map/ppermute | solution.py:372
  132.1 224.0 %collective-permute-start.26 = (bf16[128,1536]{1,0:T(8,128)(2,1)S(1)}, bf16[128,1536]{1,0:T(8,128)(2,1)}, u32[]{:S(2)}, u32[]{:S(2)}) collective-permute-start(bf16[128,1536]{1,0:T(8,128)(2,1)S(1)} %bitcast.243), channel_id=1, source_target_pairs={{0,8},{4,12},{8,16},{12,20},{16,24},{20,28},{24,0},{28,4},{1,9},{5... | collective-permute-start | bytes 1179656 | tf_op jit(solution)/shard_map/ppermute | solution.py:390
  209.6 146.5 %collective-permute-start.27 = (bf16[128,1536]{1,0:T(8,128)(2,1)S(1)}, bf16[128,1536]{1,0:T(8,128)(2,1)S(1)}, u32[]{:S(2)}, u32[]{:S(2)}) collective-permute-start(bf16[128,1536]{1,0:T(8,128)(2,1)S(1)} %bitcast.244), channel_id=1, source_target_pairs={{0,16},{4,20},{8,24},{12,28},{16,0},{20,4},{24,8},{28,12},{1,17},{... | collective-permute-start | bytes 1179656 | tf_op jit(solution)/shard_map/ppermute | solution.py:390
  209.9 147.7 %collective-permute-start.28 = (bf16[128,1536]{1,0:T(8,128)(2,1)S(1)}, bf16[128,1536]{1,0:T(8,128)(2,1)S(1)}, u32[]{:S(2)}, u32[]{:S(2)}) collective-permute-start(bf16[128,1536]{1,0:T(8,128)(2,1)S(1)} %bitcast.245), channel_id=1, source_target_pairs={{0,24},{4,28},{8,0},{12,4},{16,8},{20,12},{24,16},{28,20},{1,25},{... | collective-permute-start | bytes 1179656 | tf_op jit(solution)/shard_map/ppermute | solution.py:390
  340.5 18.5 %collective-permute-start.38 = (bf16[96,1024]{1,0:T(8,128)(2,1)}, bf16[96,1024]{1,0:T(8,128)(2,1)}, u32[]{:S(2)}, u32[]{:S(2)}) collective-permute-start(bf16[96,1024]{1,0:T(8,128)(2,1)} %collective-permute-done.37.refs_0_), channel_id=1, source_target_pairs={{0,8},{4,12},{8,16},{12,20},{16,24},{20,28},{24,0},{28,4},{1,9},{5... | collective-permute-start | bytes 589832 | tf_op jit(solution)/shard_map/ppermute | solution.py:390
  356.0 25.3 %collective-permute-start.33 = (bf16[128,1536]{1,0:T(8,128)(2,1)S(1)}, bf16[128,1536]{1,0:T(8,128)(2,1)S(1)}, u32[]{:S(2)}, u32[]{:S(2)}) collective-permute-start(bf16[128,1536]{1,0:T(8,128)(2,1)S(1)} %bitcast.246), channel_id=1, source_target_pairs={{0,4},{4,0},{8,12},{12,8},{16,20},{20,16},{24,28},{28,24},{1,5},{5... | collective-permute-start | bytes 1179656 | tf_op jit(solution)/shard_map/ppermute | solution.py:372
  356.1 25.1 %collective-permute-start.40 = (bf16[96,1024]{1,0:T(8,128)(2,1)}, bf16[96,1024]{1,0:T(8,128)(2,1)}, u32[]{:S(2)}, u32[]{:S(2)}) collective-permute-start(bf16[96,1024]{1,0:T(8,128)(2,1)} %collective-permute-done.37.refs_0_), channel_id=1, source_target_pairs={{0,24},{4,28},{8,0},{12,4},{16,8},{20,12},{24,16},{28,20},{1,25},{... | collective-permute-start | bytes 589832 | tf_op jit(solution)/shard_map/ppermute | solution.py:390
  357.6 23.7 %collective-permute-start.34 = (bf16[128,1536]{1,0:T(8,128)(2,1)}, bf16[128,1536]{1,0:T(8,128)(2,1)S(1)}, u32[]{:S(2)}, u32[]{:S(2)}) collective-permute-start(bf16[128,1536]{1,0:T(8,128)(2,1)} %collective-permute-done.26.refs_1_), channel_id=1, source_target_pairs={{0,4},{4,0},{8,12},{12,8},{16,20},{20,16},{24,28},{28,24},{1,5},{5... | collective-permute-start | bytes 1179656 | tf_op jit(solution)/shard_map/ppermute | solution.py:372
  359.0 23.4 %collective-permute-start.35 = (bf16[128,1536]{1,0:T(8,128)(2,1)S(1)}, bf16[128,1536]{1,0:T(8,128)(2,1)S(1)}, u32[]{:S(2)}, u32[]{:S(2)}) collective-permute-start(bf16[128,1536]{1,0:T(8,128)(2,1)S(1)} %collective-permute-done.27.refs_2_), channel_id=1, source_target_pairs={{0,4},{4,0},{8,12},{12,8},{16,20},{20,16},{24,28},{28,24},{1,5},{5... | collective-permute-start | bytes 1179656 | tf_op jit(solution)/shard_map/ppermute | solution.py:372
  359.1 31.7 %collective-permute-start.36 = (bf16[128,1536]{1,0:T(8,128)(2,1)S(1)}, bf16[128,1536]{1,0:T(8,128)(2,1)S(1)}, u32[]{:S(2)}, u32[]{:S(2)}) collective-permute-start(bf16[128,1536]{1,0:T(8,128)(2,1)S(1)} %collective-permute-done.28.refs_3_), channel_id=1, source_target_pairs={{0,4},{4,0},{8,12},{12,8},{16,20},{20,16},{24,28},{28,24},{1,5},{5... | collective-permute-start | bytes 1179656 | tf_op jit(solution)/shard_map/ppermute | solution.py:372
  397.9 24.4 %collective-permute-start.43 = (bf16[512,1024]{1,0:T(8,128)(2,1)S(1)}, bf16[512,1024]{1,0:T(8,128)(2,1)S(1)}, u32[]{:S(2)}, u32[]{:S(2)}) collective-permute-start(bf16[512,1024]{1,0:T(8,128)(2,1)S(1)} %add_convert_fusion.4), channel_id=1, source_target_pairs={{0,2},{1,3},{2,0},{3,1},{4,6},{5,7},{6,4},{7,5},{8,10},{9,11},{10,... | collective-permute-start | bytes 3145736 | tf_op jit(solution)/shard_map/ppermute | solution.py:372
  424.7 23.8 %collective-permute-start.45 = (bf16[512,1024]{1,0:T(8,128)(2,1)}, bf16[512,1024]{1,0:T(8,128)(2,1)}, u32[]{:S(2)}, u32[]{:S(2)}) collective-permute-start(bf16[512,1024]{1,0:T(8,128)(2,1)} %multiply_convert_fusion.3.refs_0_), channel_id=1, source_target_pairs={{0,2},{1,3},{2,0},{3,1},{4,6},{5,7},{6,4},{7,5},{8,10},{9,11},{10,... | collective-permute-start | bytes 3145736 | tf_op jit(solution)/shard_map/ppermute | solution.py:372
  425.0 321.1 %collective-permute-start.44 = (bf16[512,1024]{1,0:T(8,128)(2,1)}, bf16[512,1024]{1,0:T(8,128)(2,1)}, u32[]{:S(2)}, u32[]{:S(2)}) collective-permute-start(bf16[512,1024]{1,0:T(8,128)(2,1)} %multiply_convert_fusion.3.refs_0_), channel_id=1, source_target_pairs={{0,1},{1,0},{2,3},{3,2},{4,5},{5,4},{6,7},{7,6},{8,9},{9,8},{10,11... | collective-permute-start | bytes 3145736 | tf_op jit(solution)/shard_map/ppermute | solution.py:372
  448.5 297.6 %collective-permute-start.46 = (bf16[512,1024]{1,0:T(8,128)(2,1)}, bf16[512,1024]{1,0:T(8,128)(2,1)}, u32[]{:S(2)}, u32[]{:S(2)}) collective-permute-start(bf16[512,1024]{1,0:T(8,128)(2,1)} %collective-permute-done.45.refs_2_), channel_id=1, source_target_pairs={{0,1},{1,0},{2,3},{3,2},{4,5},{5,4},{6,7},{7,6},{8,9},{9,8},{10,11... | collective-permute-start | bytes 3145736 | tf_op jit(solution)/shard_map/ppermute | solution.py:372
  914.0 17.6 %collective-permute-start.53 = (bf16[512,1024]{1,0:T(8,128)(2,1)S(1)}, bf16[512,1024]{1,0:T(8,128)(2,1)S(1)}, u32[]{:S(2)}, u32[]{:S(2)}) collective-permute-start(bf16[512,1024]{1,0:T(8,128)(2,1)S(1)} %fusion.29), channel_id=1, source_target_pairs={{0,1},{1,0},{2,3},{3,2},{4,5},{5,4},{6,7},{7,6},{8,9},{9,8},{10,11... | collective-permute-start | bytes 3145736 | tf_op jit(solution)/shard_map/ppermute | solution.py:372
  918.6 41.2 %collective-permute-start.60 = (bf16[4,96,1024]{2,1,0:T(8,128)(2,1)}, bf16[4,96,1024]{2,1,0:T(8,128)(2,1)}, u32[]{:S(2)}, u32[]{:S(2)}) collective-permute-start(bf16[4,96,1024]{2,1,0:T(8,128)(2,1)} %dynamic-slice_bitcast_fusion.1), channel_id=1, source_target_pairs={{0,4},{4,0},{8,12},{12,8},{16,20},{20,16},{24,28},{28,24},{1,5},{5... | collective-permute-start | bytes 2359304 | tf_op jit(solution)/shard_map/ppermute | solution.py:372
  921.0 24.0 %collective-permute-start.55 = (bf16[512,1024]{1,0:T(8,128)(2,1)S(1)}, bf16[512,1024]{1,0:T(8,128)(2,1)S(1)}, u32[]{:S(2)}, u32[]{:S(2)}) collective-permute-start(bf16[512,1024]{1,0:T(8,128)(2,1)S(1)} %add_convert_fusion.2), channel_id=1, source_target_pairs={{0,2},{1,3},{2,0},{3,1},{4,6},{5,7},{6,4},{7,5},{8,10},{9,11},{10,... | collective-permute-start | bytes 3145736 | tf_op jit(solution)/shard_map/ppermute | solution.py:372
  951.0 23.4 %collective-permute-start.56 = (bf16[512,1024]{1,0:T(8,128)(2,1)}, bf16[512,1024]{1,0:T(8,128)(2,1)}, u32[]{:S(2)}, u32[]{:S(2)}) collective-permute-start(bf16[512,1024]{1,0:T(8,128)(2,1)} %fusion.81.refs_0_), channel_id=1, source_target_pairs={{0,2},{1,3},{2,0},{3,1},{4,6},{5,7},{6,4},{7,5},{8,10},{9,11},{10,... | collective-permute-start | bytes 3145736 | tf_op jit(solution)/shard_map/ppermute | solution.py:372
  953.5 47.7 %collective-permute-start.64 = (bf16[4,128,1536]{2,1,0:T(8,128)(2,1)}, bf16[4,128,1536]{2,1,0:T(8,128)(2,1)}, u32[]{:S(2)}, u32[]{:S(2)}) collective-permute-start(bf16[4,128,1536]{2,1,0:T(8,128)(2,1)} %dynamic-slice_bitcast_fusion), channel_id=1, source_target_pairs={{0,4},{4,0},{8,12},{12,8},{16,20},{20,16},{24,28},{28,24},{1,5},{5... | collective-permute-start | bytes 4718600 | tf_op jit(solution)/shard_map/ppermute | solution.py:372
  956.7 25.9 %collective-permute-start.52 = (bf16[512,1024]{1,0:T(8,128)(2,1)}, bf16[512,1024]{1,0:T(8,128)(2,1)}, u32[]{:S(2)}, u32[]{:S(2)}) collective-permute-start(bf16[512,1024]{1,0:T(8,128)(2,1)} %convolution_convert_fusion.3), channel_id=1, source_target_pairs={{0,1},{1,0},{2,3},{3,2},{4,5},{5,4},{6,7},{7,6},{8,9},{9,8},{10,11... | collective-permute-start | bytes 3145736 | tf_op jit(solution)/shard_map/ppermute | solution.py:372
  978.3 34.1 %collective-permute-start.58 = (bf16[512,1024]{1,0:T(8,128)(2,1)}, bf16[512,1024]{1,0:T(8,128)(2,1)}, u32[]{:S(2)}, u32[]{:S(2)}) collective-permute-start(bf16[512,1024]{1,0:T(8,128)(2,1)} %fusion.81.refs_0_), channel_id=1, source_target_pairs={{0,1},{1,0},{2,3},{3,2},{4,5},{5,4},{6,7},{7,6},{8,9},{9,8},{10,11... | collective-permute-start | bytes 3145736 | tf_op jit(solution)/shard_map/ppermute | solution.py:372
  984.4 28.0 %collective-permute-start.59 = (bf16[512,1024]{1,0:T(8,128)(2,1)}, bf16[512,1024]{1,0:T(8,128)(2,1)}, u32[]{:S(2)}, u32[]{:S(2)}) collective-permute-start(bf16[512,1024]{1,0:T(8,128)(2,1)} %collective-permute-done.56.refs_2_), channel_id=1, source_target_pairs={{0,1},{1,0},{2,3},{3,2},{4,5},{5,4},{6,7},{7,6},{8,9},{9,8},{10,11... | collective-permute-start | bytes 3145736 | tf_op jit(solution)/shard_map/ppermute | solution.py:372
  996.9 201.0 %collective-permute-start.51 = (bf16[512,1024]{1,0:T(8,128)(2,1)}, bf16[512,1024]{1,0:T(8,128)(2,1)}, u32[]{:S(2)}, u32[]{:S(2)}) collective-permute-start(bf16[512,1024]{1,0:T(8,128)(2,1)} %convolution_convert_fusion.4), channel_id=1, source_target_pairs={{0,1},{1,0},{2,3},{3,2},{4,5},{5,4},{6,7},{7,6},{8,9},{9,8},{10,11... | collective-permute-start | bytes 3145736 | tf_op jit(solution)/shard_map/ppermute | solution.py:372
  1004.2 193.8 %collective-permute-start.57 = (bf16[512,1024]{1,0:T(8,128)(2,1)}, bf16[512,1024]{1,0:T(8,128)(2,1)}, u32[]{:S(2)}, u32[]{:S(2)}) collective-permute-start(bf16[512,1024]{1,0:T(8,128)(2,1)} %add_convert_fusion.3), channel_id=1, source_target_pairs={{0,2},{1,3},{2,0},{3,1},{4,6},{5,7},{6,4},{7,5},{8,10},{9,11},{10,... | collective-permute-start | bytes 3145736 | tf_op jit(solution)/shard_map/ppermute | solution.py:372
  1149.0 44.5 %collective-permute-start.65 = (bf16[128,1536]{1,0:T(8,128)(2,1)}, bf16[128,1536]{1,0:T(8,128)(2,1)}, u32[]{:S(2)}, u32[]{:S(2)}) collective-permute-start(bf16[128,1536]{1,0:T(8,128)(2,1)} %get-tuple-element.73), channel_id=1, source_target_pairs={{0,8},{4,12},{8,16},{12,20},{16,24},{20,28},{24,0},{28,4},{1,9},{5... | collective-permute-start | bytes 1179656 | tf_op jit(solution)/shard_map/ppermute | solution.py:390
  1149.0 44.6 %collective-permute-start.66 = (bf16[128,1536]{1,0:T(8,128)(2,1)S(1)}, bf16[128,1536]{1,0:T(8,128)(2,1)}, u32[]{:S(2)}, u32[]{:S(2)}) collective-permute-start(bf16[128,1536]{1,0:T(8,128)(2,1)S(1)} %get-tuple-element.75), channel_id=1, source_target_pairs={{0,16},{4,20},{8,24},{12,28},{16,0},{20,4},{24,8},{28,12},{1,17},{... | collective-permute-start | bytes 1179656 | tf_op jit(solution)/shard_map/ppermute | solution.py:390
  1149.7 43.9 %collective-permute-start.67 = (bf16[128,1536]{1,0:T(8,128)(2,1)S(1)}, bf16[128,1536]{1,0:T(8,128)(2,1)}, u32[]{:S(2)}, u32[]{:S(2)}) collective-permute-start(bf16[128,1536]{1,0:T(8,128)(2,1)S(1)} %get-tuple-element.74), channel_id=1, source_target_pairs={{0,24},{4,28},{8,0},{12,4},{16,8},{20,12},{24,16},{28,20},{1,25},{... | collective-permute-start | bytes 1179656 | tf_op jit(solution)/shard_map/ppermute | solution.py:390
  1234.6 26.1 %collective-permute-start.72 = (bf16[4,144,1024]{2,1,0:T(8,128)(2,1)S(1)}, bf16[4,144,1024]{2,1,0:T(8,128)(2,1)S(1)}, u32[]{:S(2)}, u32[]{:S(2)}) collective-permute-start(bf16[4,144,1024]{2,1,0:T(8,128)(2,1)S(1)} %fusion.38), channel_id=1, source_target_pairs={{0,4},{4,0},{8,12},{12,8},{16,20},{20,16},{24,28},{28,24},{1,5},{5... | collective-permute-start | bytes 3538952 | tf_op jit(solution)/shard_map/ppermute | solution.py:372
  1238.7 25.1 %collective-permute-start.70 = (bf16[512,1024]{1,0:T(8,128)(2,1)S(1)}, bf16[512,1024]{1,0:T(8,128)(2,1)S(1)}, u32[]{:S(2)}, u32[]{:S(2)}) collective-permute-start(bf16[512,1024]{1,0:T(8,128)(2,1)S(1)} %convolution_convert_fusion.5), channel_id=1, source_target_pairs={{0,1},{1,0},{2,3},{3,2},{4,5},{5,4},{6,7},{7,6},{8,9},{9,8},{10,11... | collective-permute-start | bytes 3145736 | tf_op jit(solution)/shard_map/ppermute | solution.py:372
  1245.7 57.9 %collective-permute-start.69 = (bf16[512,1024]{1,0:T(8,128)(2,1)S(1)}, bf16[512,1024]{1,0:T(8,128)(2,1)S(1)}, u32[]{:S(2)}, u32[]{:S(2)}) collective-permute-start(bf16[512,1024]{1,0:T(8,128)(2,1)S(1)} %convolution_convert_fusion.6), channel_id=1, source_target_pairs={{0,1},{1,0},{2,3},{3,2},{4,5},{5,4},{6,7},{7,6},{8,9},{9,8},{10,11... | collective-permute-start | bytes 3145736 | tf_op jit(solution)/shard_map/ppermute | solution.py:372
  1254.7 37.0 %collective-permute-start.82 = (bf16[64,1024]{1,0:T(8,128)(2,1)S(1)}, bf16[64,1024]{1,0:T(8,128)(2,1)S(1)}, u32[]{:S(2)}, u32[]{:S(2)}) collective-permute-start(bf16[64,1024]{1,0:T(8,128)(2,1)S(1)} %fusion.61), channel_id=1, source_target_pairs={{0,0},{4,1},{8,2},{12,3},{16,4},{20,5},{24,6},{28,7},{1,8},{5,9},{... | collective-permute-start | bytes 393224 | tf_op jit(solution)/shard_map/ppermute | solution.py:1036
  1262.6 25.4 %collective-permute-start.74 = (bf16[144,1024]{1,0:T(8,128)(2,1)S(1)}, bf16[144,1024]{1,0:T(8,128)(2,1)S(1)}, u32[]{:S(2)}, u32[]{:S(2)}) collective-permute-start(bf16[144,1024]{1,0:T(8,128)(2,1)S(1)} %get-tuple-element.78), channel_id=1, source_target_pairs={{0,16},{4,20},{8,24},{12,28},{16,0},{20,4},{24,8},{28,12},{1,17},{... | collective-permute-start | bytes 884744 | tf_op jit(solution)/shard_map/ppermute | solution.py:390
  1263.7 24.3 %collective-permute-start.75 = (bf16[144,1024]{1,0:T(8,128)(2,1)S(1)}, bf16[144,1024]{1,0:T(8,128)(2,1)S(1)}, u32[]{:S(2)}, u32[]{:S(2)}) collective-permute-start(bf16[144,1024]{1,0:T(8,128)(2,1)S(1)} %get-tuple-element.77), channel_id=1, source_target_pairs={{0,24},{4,28},{8,0},{12,4},{16,8},{20,12},{24,16},{28,20},{1,25},{... | collective-permute-start | bytes 884744 | tf_op jit(solution)/shard_map/ppermute | solution.py:390
  1269.0 34.6 %collective-permute-start.71 = (bf16[512,1024]{1,0:T(8,128)(2,1)S(1)}, bf16[512,1024]{1,0:T(8,128)(2,1)S(1)}, u32[]{:S(2)}, u32[]{:S(2)}) collective-permute-start(bf16[512,1024]{1,0:T(8,128)(2,1)S(1)} %add_convert_fusion), channel_id=1, source_target_pairs={{0,2},{1,3},{2,0},{3,1},{4,6},{5,7},{6,4},{7,5},{8,10},{9,11},{10,... | collective-permute-start | bytes 3145736 | tf_op jit(solution)/shard_map/ppermute | solution.py:372
  (102 other events, 1425.2 us)

commit v3 on v2

--- a/solution.py
+++ b/solution.py
@@ -360,6 +360,7 @@
     )
 
 FEATURES = 128
+NARROW = 512
 MASK_DEPTH = -4096.0
 LOG2_E = 1.4426950408889634
 VMEM_BYTES = 56 * 1024 * 1024
@@ -413,10 +414,12 @@
     anywhere = pl.BlockSpec(memory_space=pl.ANY)
     results = pl.pallas_call(
         functools.partial(assemble_kernel, splits, count),
-        in_specs=[pl.BlockSpec(memory_space=pltpu.SMEM)] + [anywhere] * count,
+        in_specs=[pl.BlockSpec(memory_space=pltpu.SMEM)]
+        + [pl.BlockSpec(memory_space=pltpu.VMEM)] * count,
         out_specs=[anywhere] * len(splits),
         out_shape=[jax.ShapeDtypeStruct((count, n, columns), pieces[0].dtype) for n in splits],
         scratch_shapes=[pltpu.SemaphoreType.DMA((count, len(splits)))],
+        compiler_params=pltpu.CompilerParams(vmem_limit_bytes=VMEM_BYTES),
         cost_estimate=pl.CostEstimate(
             flops=0, bytes_accessed=4 * count * rows * columns, transcendentals=0
         ),
@@ -462,6 +465,17 @@
     return total.astype(bf16)
 
 
+def narrow(rows, parts):
+    pieces = rows.reshape(parts, rows.shape[0] // parts, -1, NARROW)
+    return pieces.transpose(0, 2, 1, 3).reshape(parts, -1, NARROW)
+
+
+def widen(pieces, height):
+    parts = pieces.shape[0]
+    pieces = pieces.reshape(parts, -1, height, NARROW).transpose(0, 2, 1, 3)
+    return pieces.reshape(parts * height, -1)
+
+
 def after(value, *others):
     return lax.optimization_barrier((value, *others))[0]
 
@@ -473,14 +487,25 @@
     return [value, beside, across, corner]
 
 
-def scatter_sum(part, waits=()):
-    corner = xor_permute(part(3).astype(bf16), "ctx", 1)
-    toward = (part(2) + corner.astype(f32)).astype(bf16)
-    if waits:
-        toward = after(toward, *waits)
-    across = xor_permute(toward, "ctx", 2)
-    beside = xor_permute(part(1).astype(bf16), "ctx", 1)
-    return part(0) + beside.astype(f32) + across.astype(f32), across
+def gather_near(value):
+    return [value, xor_permute(value, "ctx", 1)], xor_permute(value, "ctx", 2)
+
+
+def gather_far(across, *waits):
+    across = after(across, *waits)
+    return [across, xor_permute(across, "ctx", 1)]
+
+
+def send_across(part_corner, part_across, *waits):
+    corner = xor_permute(part_corner.astype(bf16), "ctx", 1)
+    toward = (part_across.astype(f32) + corner.astype(f32)).astype(bf16)
+    toward = after(toward, *waits) if waits else toward
+    return toward, xor_permute(toward, "ctx", 2)
+
+
+def sum_own(part_beside, part_own, across):
+    beside = xor_permute(part_beside.astype(bf16), "ctx", 1)
+    return part_own.astype(f32) + beside.astype(f32) + across.astype(f32)
 
 
 def nt_dot(left, right):
@@ -663,10 +688,10 @@
 
 
 def attend_kernel(
-    group, block, me_ref, q_ref, qf_ref, k_ref, kf_ref, v_ref, o_ref, log_ref, total_ref
+    group, block, first, me_ref, q_ref, qf_ref, k_ref, kf_ref, v_ref, o_ref, log_ref, total_ref
 ):
     me = me_ref[0]
-    at_query = pl.program_id(1)
+    at_query = (pl.program_id(1) + first) ^ me
     factor = HEAD_SIZE ** (-0.5) * LOG2_E
     query_features = qf_ref[...]
     ones = jnp.ones((block, HEAD_SIZE), bf16)
@@ -698,32 +723,31 @@
         log_ref[0, head : head + 1, :] = jnp.log2(summed.T[0:1, :])
 
 
-def attend(me, q, qf, k, kf, v, block, group):
-    rows = q.shape[0]
+def attend(me, q, qf, k, kf, v, block, group, first, count):
+    rows = k.shape[0]
     key_heads = k.shape[1] // HEAD_SIZE
-    blocks = rows // block
-    pairs = key_heads * group * blocks * (blocks + 1) // 2 * block * block
+    pairs = key_heads * group * count * block * rows * 5 // 8
     return pl.pallas_call(
-        functools.partial(attend_kernel, group, block),
+        functools.partial(attend_kernel, group, block, first),
         grid_spec=pltpu.PrefetchScalarGridSpec(
             num_scalar_prefetch=1,
-            grid=(key_heads, blocks),
+            grid=(key_heads, count),
             in_specs=[
-                pl.BlockSpec((block, group * HEAD_SIZE), lambda g, i, me: (i ^ me[0], g)),
-                pl.BlockSpec((block, FEATURES), lambda g, i, me: (i ^ me[0], 0)),
+                pl.BlockSpec((block, group * HEAD_SIZE), lambda g, i, me: (i + first, g)),
+                pl.BlockSpec((block, FEATURES), lambda g, i, me: (i + first, 0)),
                 pl.BlockSpec((rows, HEAD_SIZE), lambda g, i, me: (0, g)),
                 pl.BlockSpec((rows, FEATURES), lambda g, i, me: (0, 0)),
                 pl.BlockSpec((rows, HEAD_SIZE), lambda g, i, me: (0, g)),
             ],
             out_specs=[
-                pl.BlockSpec((block, group * HEAD_SIZE), lambda g, i, me: (i ^ me[0], g)),
-                pl.BlockSpec((1, group, block), lambda g, i, me: (g, 0, i ^ me[0])),
+                pl.BlockSpec((block, group * HEAD_SIZE), lambda g, i, me: (i, g)),
+                pl.BlockSpec((1, group, block), lambda g, i, me: (g, 0, i)),
             ],
             scratch_shapes=[pltpu.VMEM((group, block, 2 * HEAD_SIZE), f32)],
         ),
         out_shape=[
-            jax.ShapeDtypeStruct(q.shape, bf16),
-            jax.ShapeDtypeStruct((key_heads, group, rows), f32),
+            jax.ShapeDtypeStruct((count * block, q.shape[1]), bf16),
+            jax.ShapeDtypeStruct((key_heads, group, count * block), f32),
         ],
         compiler_params=pltpu.CompilerParams(vmem_limit_bytes=VMEM_BYTES),
         cost_estimate=pl.CostEstimate(
@@ -736,6 +760,8 @@
 def unattend_kernel(
     group,
     block,
+    first,
+    resumed,
     me_ref,
     q_ref,
     qf_ref,
@@ -745,21 +771,20 @@
     o_ref,
     do_ref,
     log_ref,
-    dq_ref,
-    dk_ref,
-    dv_ref,
-    flipped_ref,
-    total_ref,
+    *rest,
 ):
+    if resumed:
+        dk_in_ref, dv_in_ref, *rest = rest
+    dq_ref, dk_ref, dv_ref, flipped_ref, total_ref = rest
     me = me_ref[0]
-    at_query = pl.program_id(1)
+    at_query = (pl.program_id(1) + first) ^ me
     scale = HEAD_SIZE ** (-0.5)
     factor = scale * LOG2_E
 
-    @pl.when(at_query == 0)
+    @pl.when(pl.program_id(1) == 0)
     def _():
-        dk_ref[...] = jnp.zeros_like(dk_ref)
-        dv_ref[...] = jnp.zeros_like(dv_ref)
+        dk_ref[...] = dk_in_ref[...] if resumed else jnp.zeros_like(dk_ref)
+        dv_ref[...] = dv_in_ref[...] if resumed else jnp.zeros_like(dv_ref)
         flipped_ref[...] = k_ref[...].astype(f32).T.astype(bf16)
 
     total_ref[...] = jnp.zeros_like(total_ref)
@@ -798,36 +823,38 @@
     for head in range(group):
         dq_ref[:, head * HEAD_SIZE : (head + 1) * HEAD_SIZE] = total_ref[head].T * scale
 
-    @pl.when(at_query == pl.num_programs(1) - 1)
-    def _():
-        dk_ref[...] = dk_ref[...] * scale
-
-
-def unattend(me, q, qf, k, kf, v, o, d_out, logs, block, group):
-    rows = q.shape[0]
+    if resumed:
+
+        @pl.when(pl.program_id(1) == pl.num_programs(1) - 1)
+        def _():
+            dk_ref[...] = dk_ref[...] * scale
+
+
+def unattend(me, q, qf, k, kf, v, o, d_out, logs, block, group, first, count, earlier=()):
+    rows = k.shape[0]
     key_heads = k.shape[1] // HEAD_SIZE
-    blocks = rows // block
-    pairs = key_heads * group * blocks * (blocks + 1) // 2 * block * block
+    pairs = key_heads * group * count * block * rows * 5 // 8
 
     def by_query(n):
-        return pl.BlockSpec((block, n), lambda g, i, me: (i ^ me[0], g))
+        return pl.BlockSpec((block, n), lambda g, i, me: (i, g))
 
     by_key = pl.BlockSpec((rows, HEAD_SIZE), lambda g, i, me: (0, g))
     return pl.pallas_call(
-        functools.partial(unattend_kernel, group, block),
+        functools.partial(unattend_kernel, group, block, first, bool(earlier)),
         grid_spec=pltpu.PrefetchScalarGridSpec(
             num_scalar_prefetch=1,
-            grid=(key_heads, blocks),
+            grid=(key_heads, count),
             in_specs=[
-                by_query(group * HEAD_SIZE),
-                pl.BlockSpec((block, FEATURES), lambda g, i, me: (i ^ me[0], 0)),
+                pl.BlockSpec((block, group * HEAD_SIZE), lambda g, i, me: (i + first, g)),
+                pl.BlockSpec((block, FEATURES), lambda g, i, me: (i + first, 0)),
                 by_key,
                 pl.BlockSpec((rows, FEATURES), lambda g, i, me: (0, 0)),
                 by_key,
                 by_query(group * HEAD_SIZE),
                 by_query(group * HEAD_SIZE),
-                pl.BlockSpec((1, group, block), lambda g, i, me: (g, 0, i ^ me[0])),
-            ],
+                pl.BlockSpec((1, group, block), lambda g, i, me: (g, 0, i)),
+            ]
+            + [by_key] * len(earlier),
             out_specs=[by_query(group * HEAD_SIZE), by_key, by_key],
             scratch_shapes=[
                 pltpu.VMEM((HEAD_SIZE, rows), bf16),
@@ -835,7 +862,7 @@
             ],
         ),
         out_shape=[
-            jax.ShapeDtypeStruct(q.shape, f32),
+            jax.ShapeDtypeStruct((count * block, q.shape[1]), f32),
             jax.ShapeDtypeStruct(k.shape, f32),
             jax.ShapeDtypeStruct(v.shape, f32),
         ],
@@ -844,7 +871,54 @@
             flops=14 * pairs * HEAD_SIZE, bytes_accessed=20 * q.size, transcendentals=pairs
         ),
         name="unattend",
-    )(me, q, qf, k, kf, v, o, d_out, logs)
+    )(me, q, qf, k, kf, v, o, d_out, logs, *earlier)
+
+
+def feed_kernel(
+    units, h_ref, cot_ref, both_ref, down_ref, hidden_ref, d_both_ref, part_ref, d_part_ref
+):
+    both = nn_dot(h_ref[...], both_ref[...])
+    d_hidden = nt_dot(cot_ref[...], down_ref[...])
+    gate, up = both[:, :units], both[:, units:]
+    sigmoid = 1.0 / (1.0 + jnp.exp(-gate))
+    silu = gate * sigmoid
+    hidden = (silu * up).astype(bf16)
+    hidden_ref[...] = hidden
+    part_ref[...] = nn_dot(hidden, down_ref[...]).astype(bf16)
+    d_gate = (d_hidden * up * sigmoid * (1.0 + gate * (1.0 - sigmoid))).astype(bf16)
+    d_up = (d_hidden * silu).astype(bf16)
+    d_both = jnp.concatenate([d_gate, d_up], axis=1)
+    d_both_ref[...] = d_both
+    d_part_ref[...] = nt_dot(d_both, both_ref[...]).astype(bf16)
+
+
+def feed(h, cot, both, down):
+    rows, width = h.shape
+    units = down.shape[0]
+    block = 256
+
+    def tall(n):
+        return pl.BlockSpec((block, n), lambda i: (i, 0))
+
+    def whole(shape):
+        return pl.BlockSpec(shape, lambda i: (0, 0))
+
+    return pl.pallas_call(
+        functools.partial(feed_kernel, units),
+        grid=(rows // block,),
+        in_specs=[tall(width), tall(width), whole(both.shape), whole(down.shape)],
+        out_specs=[tall(units), tall(2 * units), tall(width), tall(width)],
+        out_shape=[
+            jax.ShapeDtypeStruct((rows, n), bf16) for n in (units, 2 * units, width, width)
+        ],
+        compiler_params=pltpu.CompilerParams(vmem_limit_bytes=VMEM_BYTES),
+        cost_estimate=pl.CostEstimate(
+            flops=12 * rows * width * units,
+            bytes_accessed=rows * (8 * width + 6 * units) + 6 * width * units,
+            transcendentals=rows * units,
+        ),
+        name="feed",
+    )(h, cot, both, down)
 
 
 def norm_back(value_rows, gain_vec, grad):
@@ -919,18 +993,22 @@
     full_gains = gain_rows.reshape(copies, pad_rows, -1)[:, :size, :gain_count].reshape(-1)
     gain_attn, gain_mlp, gain_query, gain_key = split_gains(full_gains)
 
-    early = first_pieces[1:copies // 2]
-    out_rows = lax.ppermute(w_out, ("dp", "ctx"), forward_owner)
-    out_pieces, unused = gather_copies(after(out_rows, *early))
-    out_full = assemble(out_pieces, places_dp)[0]
+    rows_out, rows_down, rows_both = w_out.shape[0], w_down.shape[0], size * owned
+    per_row = MODEL_WIDTH // NARROW
+    feed_rows = rows_both * (2 * hidden_cols // NARROW) + rows_down * per_row
+    moved = lax.ppermute(jnp.concatenate([w_out, w_down]), ("dp", "ctx"), forward_owner)
     gate_up = jnp.concatenate([by_columns(w_gate), by_columns(w_up)], axis=2)
-    gate_up = exchange(gate_up, me).reshape(size * owned, -1)
-    gate_up_pieces, unused = gather_copies(after(gate_up, *early))
-    gate_up = assemble(gate_up_pieces, places_dp)[0]
-    down_rows = lax.ppermute(w_down, ("dp", "ctx"), forward_owner)
-    down_pieces, unused = gather_copies(after(down_rows, *early))
-    down_full = assemble(down_pieces, places_dp)[0]
-    cot_all = join(cot_blocks)
+    gate_up = exchange(gate_up, me).reshape(rows_both, -1)
+    later = jnp.concatenate(
+        [narrow(gate_up, 1)[0], narrow(moved[rows_out:], 1)[0], narrow(moved[:rows_out], 1)[0]]
+    )
+    w_first = after(w_first, later)
+    later = lax.all_gather(later, "dp", axis=0, tiled=True).reshape(copies, -1, NARROW)
+    out_full = widen(later[:, feed_rows:], rows_out)
+    gate_up = widen(later[:, : rows_both * (2 * hidden_cols // NARROW)], rows_both)
+    down_full = widen(later[:, rows_both * (2 * hidden_cols // NARROW) : feed_rows], rows_down)
+    near, far = slice(0, 2), slice(2, 4)
+    cot_near, cot_far = join(cot_blocks[near]), join(cot_blocks[far])
 
     half = HEAD_SIZE // 2
     rates = THETA ** (-2.0 * jnp.arange(half, dtype=f32) / HEAD_SIZE)
@@ -946,36 +1024,36 @@
     normed, raw, q, k, v = project(
         x_all, gain_attn[None], w_first, cosine, sine, gain_q_row, gain_k_row, query_heads, key_heads
     )
-    q = after(q, *out_pieces[1:4], *gate_up_pieces[1:4])
-    attended, logs = attend(me_row, q, query_features, k, key_features, v, block, group)
-
-    attended = after(attended, *out_pieces[4:], *gate_up_pieces[4:], *down_pieces[1:4])
-
-    def rows_of(value, r):
-        return value[r * block : (r + 1) * block]
-
-    branch, unused = scatter_sum(lambda r: nn_dot(rows_of(attended, r), out_full))
-    middle = x_own.astype(f32) + branch
-    normed_mlp = join(gather_blocks(row_norm_apply(middle, gain_mlp).astype(bf16)))
-    both = nn_dot(normed_mlp, gate_up)
-    gate_value, up_value = both[:, :hidden_cols], both[:, hidden_cols:]
-    d_hidden = nt_dot(cot_all, down_full)
-    sigmoid = 1.0 / (1.0 + jnp.exp(-gate_value))
-    silu = gate_value * sigmoid
-    hidden = (silu * up_value).astype(bf16)
-    d_gate = (d_hidden * up_value * sigmoid * (1.0 + gate_value * (1.0 - sigmoid))).astype(bf16)
-    d_up = (d_hidden * silu).astype(bf16)
-    d_both = jnp.concatenate([d_gate, d_up], axis=1)
-
-    d_normed, unused = scatter_sum(lambda r: nt_dot(rows_of(d_both, r), gate_up))
+    def attend_half(query, first):
+        return attend(
+            me_row, query, query_features, k, key_features, v, block, group, first, 2
+        )
+
+    def halves(value):
+        return value[:block], value[block:]
+
+    att_far, logs_far = attend_half(q, 2)
+    att_across, att_corner = halves(att_far)
+    part_corner, part_across = nn_dot(att_corner, out_full), nn_dot(att_across, out_full)
+    toward, across = send_across(part_corner, part_across)
+    att_near, logs_near = attend_half(after(q, toward), 0)
+    att_own, att_beside = halves(att_near)
+    part_beside, part_own = nn_dot(att_beside, out_full), nn_dot(att_own, out_full)
+    middle = x_own.astype(f32) + sum_own(part_beside, part_own, across)
+    h_blocks, across = gather_near(row_norm_apply(middle, gain_mlp).astype(bf16))
+    h_near = join(h_blocks)
+    hidden_near, d_both_near, down_near, d_h_near = feed(h_near, cot_near, gate_up, down_full)
+    h_far = join(gather_far(across, hidden_near))
+    hidden_far, d_both_far, down_far, d_h_far = feed(h_far, cot_far, gate_up, down_full)
+
+    part_across, part_corner = halves(d_h_far)
+    unused, across = send_across(part_corner, part_across)
+    part_own, part_beside = halves(d_h_near)
+    d_normed = sum_own(part_beside, part_own, across)
     d_middle, d_gain_mlp = norm_back(middle, gain_mlp, d_normed)
     d_middle = d_middle + cot_own.astype(f32)
-    d_branch_blocks = gather_blocks(d_middle.astype(bf16))
-    d_branch = join(d_branch_blocks)
-    d_attended = nt_dot(d_branch, out_full).astype(bf16)
-
-    down, down_across = scatter_sum(lambda r: nn_dot(rows_of(hidden, r), down_full), d_branch_blocks[2:3])
-    output = (middle + down).astype(bf16)
+    d_branch_blocks, d_branch_across = gather_near(d_middle.astype(bf16))
+    d_branch_near = join(d_branch_blocks)
 
     def tn_dot(left, right):
         return lax.dot_general(left, right, (((0,), (0,)), ((), ())), preferred_element_type=f32)
@@ -983,21 +1061,55 @@
     def by_copy(grad):
         return grad.astype(bf16).reshape(copies, -1, grad.shape[-1])
 
-    pair_down = reduce_beside(by_copy(tn_dot(hidden, cot_all)))
-    pair_both = reduce_beside(by_copy(tn_dot(normed_mlp, d_both)))
-    pair_out = reduce_beside(by_copy(tn_dot(attended, d_branch)))
-    terms_down = reduce_along(after(pair_down, d_branch_blocks[2]))
-    terms_both = reduce_along(after(pair_both, d_attended))
-
-    dq, dk, dv = unattend(
-        me_row, q, query_features, k, key_features, v, attended, d_attended, logs, block, group
-    )
-    dq = after(dq, *terms_down, *terms_both, pair_out, down_across)
-    terms_out = reduce_along(after(pair_out, dq))
+    grad_down = tn_dot(hidden_near, cot_near) + tn_dot(hidden_far, cot_far)
+    grad_both = tn_dot(h_near, d_both_near) + tn_dot(h_far, d_both_far)
+    feed_parts = jnp.concatenate(
+        [narrow(grad_both.astype(bf16), copies), narrow(grad_down.astype(bf16), copies)], axis=1
+    ).reshape(-1, NARROW)
+    grad_feed = lax.psum_scatter(feed_parts, "dp", scatter_dimension=0, tiled=True)
+
+    def unattend_half(att, d_branch, logs, first, earlier, *waits):
+        d_att = after(nt_dot(d_branch, out_full).astype(bf16), *waits)
+        return unattend(
+            me_row,
+            q,
+            query_features,
+            k,
+            key_features,
+            v,
+            att,
+            d_att,
+            logs,
+            block,
+            group,
+            first,
+            2,
+            earlier,
+        )
+
+    dq_near, *earlier = unattend_half(att_near, d_branch_near, logs_near, 0, (), feed_parts)
+    d_branch_blocks = gather_far(d_branch_across, dq_near)
+    d_branch_far = join(d_branch_blocks)
+    part_across, part_corner = halves(down_far)
+    unused, down_across = send_across(part_corner, part_across, d_branch_blocks[0])
+    part_own, part_beside = halves(down_near)
+    output = (middle + sum_own(part_beside, part_own, down_across)).astype(bf16)
+
+    grad_out = tn_dot(att_near, d_branch_near) + tn_dot(att_far, d_branch_far)
+    pair_out = reduce_beside(by_copy(grad_out))
+    dq_far, dk, dv = unattend_half(att_far, d_branch_far, logs_far, 2, earlier)
+    dk = after(dk, pair_out, down_across)
+    dq = jnp.concatenate([dq_near, dq_far])
     low, d_gain_heads = unproject(
         dq, dk, dv, raw, cosine, sine, gain_q_row, gain_k_row, query_heads, key_heads
     )
-    d_normed_attn, unused = scatter_sum(lambda r: nt_dot(rows_of(low, r), w_first))
+    terms_out = reduce_along(after(pair_out, low))
+    low_own, low_beside, low_across, low_corner = (
+        low[r * block : (r + 1) * block] for r in range(size)
+    )
+    toward, across = send_across(nt_dot(low_corner, w_first), nt_dot(low_across, w_first))
+    part_beside, part_own = nt_dot(low_beside, w_first), nt_dot(low_own, w_first)
+    d_normed_attn = sum_own(part_beside, part_own, across)
     d_inputs, unused = norm_back(x_own.astype(f32), gain_attn, d_normed_attn)
     grad_tokens = (d_middle + d_inputs).reshape(tokens.shape)
 
@@ -1013,8 +1125,13 @@
     grad_first = jnp.concatenate(
         [grad_first.reshape(copies, size * owned, -1), gain_block], axis=1
     )
-    grad_first = add_all(reduce_along(reduce_beside(grad_first)))
-    grad_down, grad_both, grad_out = map(add_all, (terms_down, terms_both, terms_out))
+    terms_first = reduce_along(after(reduce_beside(grad_first), across))
+    grad_first = add_all(terms_first)
+    grad_out = add_all(after(terms_out, *terms_first))
+    grad_feed = after(grad_feed, *terms_first)
+    split = rows_both * (2 * hidden_cols // NARROW)
+    grad_both = widen(grad_feed[None, :split], rows_both)
+    grad_down = widen(grad_feed[None, split:], rows_down)
     gain_part = grad_first[size * owned :][:size]
     gain_part = jnp.broadcast_to(gain_part[:, None], (size, pad_rows, gain_part.shape[1]))
     grad_first = jnp.concatenate(

time: 1330 us -> 555 us (0.42)
  Pallas kernels: 855 us -> 146 us
  waiting for transfers between devices: 189 us -> 117 us
  matrix products: 101 us -> 48.5 us
  local copies, waits for them, and re-layouts: 22.2 us -> 64.2 us
  other arithmetic: 31.8 us -> 46.3 us
  between operations: 2.3 us -> 15.8 us
    pallas_call x8, Pallas kernels: 769 us -> 24.9 us  [assemble(): pl.pallas_call(functools.partial(assemble_kernel, splits, count), in_spec...]
    ppermute x59 -> x45, waiting for transfers between devices: 140 us -> 57.8 us  [xor_permute(): return lax.ppermute(value, axis, [(i, i ^ offset) for i in range(size)])]
    pallas_call x2 -> x6, Pallas kernels: 58.6 us -> 94.5 us  [the longest x2 42.2 us: unattend(): pl.pallas_call(functools.partial(unattend_kernel, group, block, first, bo...]
    dot_general x9 -> x4, matrix products: 30.6 us -> 3.97 us  [nn_dot(): return jnp.dot(left, right, preferred_element_type=f32)]
    dot_general x10 -> x6, matrix products: 43.1 us -> 17.5 us  [nt_dot(): lax.dot_general(left, right, (((1,), (1,)), ((), ())), preferred_element_...]
    ppermute x59 -> x45, starting transfers between devices: 61.7 us -> 85.9 us  [xor_permute(): return lax.ppermute(value, axis, [(i, i ^ offset) for i in range(size)])]
    ppermute x24 -> x9, starting transfers between devices: 32.2 us -> 13.1 us  [shift_z(): lax.ppermute(value, 'dp', [(i, (i + 2 * offset) % size) for i in range(si...]
    ppermute x24 -> x9, waiting for transfers between devices: 42.2 us -> 49.1 us  [shift_z(): lax.ppermute(value, 'dp', [(i, (i + 2 * offset) % size) for i in range(si...]
  transfers between devices with their start and end apart: 87 -> 59, of which waited for: 29 -> 18; matrix products, arithmetic and copies ran while one was open for 7% -> 26% of each run, Pallas kernels for 54% -> 24%
where the time goes in v3:
time: 555 us; the launch traced here: 545 us
  Pallas kernels  146 us (26%)
  waiting for transfers between devices  117 us (21%)
  starting transfers between devices  107 us (19%)
  local copies, waits for them, and re-layouts  64.2 us (12%)
  matrix products  48.5 us (9%)
  other arithmetic  46.3 us (8%)
  between operations  15.8 us (3%)
    ppermute x45, starting transfers between devices, xor_permute(): return lax.ppermute(value, axis, [(i, i ^ offset) for i in range(size)])  85.9 us
    ppermute x45, waiting for transfers between devices, xor_permute(): return lax.ppermute(value, axis, [(i, i ^ offset) for i in range(size)])  57.8 us
    ppermute x9, waiting for transfers between devices, shift_z(): lax.ppermute(value, 'dp', [(i, (i + 2 * offset) % size) for i in range(si...  49.1 us
    pallas_call x2, Pallas kernels, unattend(): pl.pallas_call(functools.partial(unattend_kernel, group, block, first, bo...  42.2 us
    pallas_call x2, Pallas kernels, feed(): pl.pallas_call(functools.partial(feed_kernel, units), grid=(rows // block...  29 us
    dot_general x7, matrix products, tn_dot(): lax.dot_general(left, right, (((0,), (0,)), ((), ())), preferred_element_...  27 us
    pallas_call x8, Pallas kernels, assemble(): pl.pallas_call(functools.partial(assemble_kernel, splits, count), in_spec...  24.9 us
    pallas_call x2, Pallas kernels, attend(): pl.pallas_call(functools.partial(attend_kernel, group, block, first), gri...  23.4 us
  transfers between devices with their start and end apart: 59, of which 18 were waited for; matrix products, arithmetic and copies ran while one was open for 26% of the time, Pallas kernels for 24%

profile of v3, /device:TPU:27, one launch (start us, length us, event | category | flops | bytes accessed | tf_op | source)
XLA Modules:
  0.0 545.2 jit_solution(14800046702057541739)
XLA Ops:
  24.7 11.5 %collective-permute-start.21 = (s32[2,512]{1,0:T(2,128)S(1)}, s32[2,512]{1,0:T(2,128)S(1)}, u32[]{:S(2)}, u32[]{:S(2)}) collective-permute-start(s32[2,512]{1,0:T(2,128)S(1)} %pad_add_fusion.1), channel_id=1, source_target_pairs={{0,2},{1,3},{2,0},{3,1},{4,6},{5,7},{6,4},{7,5},{8,10},{9,11},{10,... | collective-permute-start | bytes 12296 | tf_op jit(solution)/shard_map/ppermute | solution.py:373
  36.2 5.9 %collective-permute-start.20 = (s32[2,512]{1,0:T(2,128)S(1)}, s32[2,512]{1,0:T(2,128)S(1)}, u32[]{:S(2)}, u32[]{:S(2)}) collective-permute-start(s32[2,512]{1,0:T(2,128)S(1)} %pad_add_fusion.1), channel_id=1, source_target_pairs={{0,1},{1,0},{2,3},{3,2},{4,5},{5,4},{6,7},{7,6},{8,9},{9,8},{10,11... | collective-permute-start | bytes 12296 | tf_op jit(solution)/shard_map/ppermute | solution.py:373
  48.4 21.6 %collective-permute-done.5 = bf16[48,1024]{1,0:T(8,128)(2,1)S(1)} collective-permute-done((bf16[48,1024]{1,0:T(8,128)(2,1)S(1)}, bf16[48,1024]{1,0:T(8,128)(2,1)S(1)}, u32[]{:S(2)}, u32[]{:S(2)}) %collective-permute-start.5) | collective-permute-done | bytes 98336 | tf_op jit(solution)/shard_map/ppermute | solution.py:373
  76.5 3.7 fusion.34
  82.1 3.6 collective-permute-done.6.refs_1_
  85.7 31.5 %collective-permute-done.7.refs_2_ = bf16[144,1024]{1,0:T(8,128)(2,1)S(1)} collective-permute-done((bf16[144,1024]{1,0:T(8,128)(2,1)S(1)}, bf16[144,1024]{1,0:T(8,128)(2,1)S(1)}, u32[]{:S(2)}, u32[]{:S(2)}) %collective-permute-start.7) | collective-permute-done | bytes 294944 | tf_op jit(solution)/shard_map/ppermute | solution.py:391
  117.2 5.1 collective-permute-start.11
  123.5 7.3 %collective-permute-start = (bf16[512,1024]{1,0:T(8,128)(2,1)S(1)}, bf16[512,1024]{1,0:T(8,128)(2,1)}, u32[]{:S(2)}, u32[]{:S(2)}) collective-permute-start(bf16[512,1024]{1,0:T(8,128)(2,1)S(1)} %bitcast.221), channel_id=1, source_target_pairs={{0,1},{1,0},{2,3},{3,2},{4,5},{5,4},{6,7},{7,6},{8,9},{9,8},{10,11... | collective-permute-start | bytes 3145736 | tf_op jit(solution)/shard_map/ppermute | solution.py:373
  131.0 5.1 collective-permute-start.2
  140.7 3.1 assemble.9
  146.3 4.2 assemble.8
  150.5 13.0 %project.1 = (bf16[2048,1024]{1,0:T(8,128)(2,1)}, f32[2048,768]{1,0:T(8,128)}, bf16[2048,512]{1,0:T(8,128)(2,1)}, bf16[2048,256]{1,0:T(8,128)(2,1)}, bf16[2048,256]{1,0:T(8,128)(2,1)}) custom-call(bf16[2048,1024]{1,0:T(8,128)(2,1)} %bitcast.240, f32[1,1024]{1,0:T(1,128)} %bitcast.306, bf16[1024,1024]{1,0:T(8,128)(2,1)} %bitcast.308, ...), custom_call_target="tpu_custom_call" | custom-call | flops 4294967296 | bytes 20971520 | tf_op jit(solution)/shard_map/project/pallas_call | solution.py:569
  163.5 8.4 %attend.2 = (bf16[1024,512]{1,0:T(8,128)(2,1)}, f32[2,2,1024]{2,1,0:T(2,128)}) custom-call(s32[1]{0:T(128)} %bitcast.1.me_ref, bf16[2048,512]{1,0:T(8,128)(2,1)} %get-tuple-element.62.q_ref, bf16[2048,128]{1,0:T(8,128)(2,1)} %select_convert_fusion.qf_ref, bf16[2048,256]{1,0:T(8,128)(2,1)} %get-tuple-element.59.k_ref, bf16[2048,128]{1,0:T(8,128)(2,1)} %fusion.25.kf_ref, ...), custom_call_target="tpu_custom_call" | custom-call | flops 5368709120 | bytes 10485760 | tf_op jit(solution)/shard_map/attend/pallas_call | solution.py:730
  178.8 6.7 %collective-permute-start.25 = (bf16[512,1024]{1,0:T(8,128)(2,1)S(1)}, bf16[512,1024]{1,0:T(8,128)(2,1)S(1)}, u32[]{:S(2)}, u32[]{:S(2)}) collective-permute-start(bf16[512,1024]{1,0:T(8,128)(2,1)S(1)} %add_convert_fusion.7), channel_id=1, source_target_pairs={{0,2},{1,3},{2,0},{3,1},{4,6},{5,7},{6,4},{7,5},{8,10},{9,11},{10,... | collective-permute-start | bytes 3145736 | tf_op jit(solution)/shard_map/ppermute | solution.py:373
  185.5 15.0 %attend.3 = (bf16[1024,512]{1,0:T(8,128)(2,1)}, f32[2,2,1024]{2,1,0:T(2,128)}) custom-call(s32[1]{0:T(128)} %bitcast.1.me_ref, bf16[2048,512]{1,0:T(8,128)(2,1)} %get-tuple-element.62.q_ref, bf16[2048,128]{1,0:T(8,128)(2,1)} %select_convert_fusion.qf_ref, bf16[2048,256]{1,0:T(8,128)(2,1)} %get-tuple-element.59.k_ref, bf16[2048,128]{1,0:T(8,128)(2,1)} %fusion.25.kf_ref, ...), custom_call_target="tpu_custom_call" | custom-call | flops 5368709120 | bytes 10485760 | tf_op jit(solution)/shard_map/attend/pallas_call | solution.py:730
  203.8 4.9 collective-permute-done.25
  231.9 14.3 %feed.2 = (bf16[1024,768]{1,0:T(8,128)(2,1)}, bf16[1024,1536]{1,0:T(8,128)(2,1)}, bf16[1024,1024]{1,0:T(8,128)(2,1)}, bf16[1024,1024]{1,0:T(8,128)(2,1)}) custom-call(bf16[1024,1024]{1,0:T(8,128)(2,1)} %bitcast.254, bf16[1024,1024]{1,0:T(8,128)(2,1)} %bitcast.224, bf16[1024,1536]{1,0:T(8,128)(2,1)} %bitcast.246, bf16[768,1024]{1,0:T(8,128)(2,1)} %bitcast.260), custom_call_target="tpu_custom_call" | custom-call | flops 9663676416 | bytes 17825792 | tf_op jit(solution)/shard_map/feed/pallas_call | solution.py:906
  254.1 14.6 %feed.3 = (bf16[1024,768]{1,0:T(8,128)(2,1)}, bf16[1024,1536]{1,0:T(8,128)(2,1)}, bf16[1024,1024]{1,0:T(8,128)(2,1)}, bf16[1024,1024]{1,0:T(8,128)(2,1)}) custom-call(bf16[1024,1024]{1,0:T(8,128)(2,1)} %bitcast.256, bf16[1024,1024]{1,0:T(8,128)(2,1)} %bitcast.258, bf16[1024,1536]{1,0:T(8,128)(2,1)} %bitcast.247, bf16[768,1024]{1,0:T(8,128)(2,1)} %bitcast.261), custom_call_target="tpu_custom_call" | custom-call | flops 9663676416 | bytes 17825792 | tf_op jit(solution)/shard_map/feed/pallas_call | solution.py:906
  277.2 3.1 add_convert_fusion.1
  280.3 3.8 reshape.221
  284.1 3.0 copy.54
  287.1 5.6 %fusion.49 = f32[1024,1536]{1,0:T(8,128)S(1)} fusion(bf16[1024,1024]{1,0:T(8,128)(2,1)S(1)} %bitcast.257, bf16[1024,1536]{1,0:T(8,128)(2,1)} %get-tuple-element.71), kind=kOutput, calls=%fused_computation.179 | convolution fusion | flops 3221225472 | bytes 11534336 | tf_op jit(solution)/shard_map/dot_general | solution.py:1059
  292.8 9.3 %collective-permute-done.33 = bf16[512,1024]{1,0:T(8,128)(2,1)} collective-permute-done((bf16[512,1024]{1,0:T(8,128)(2,1)}, bf16[512,1024]{1,0:T(8,128)(2,1)}, u32[]{:S(2)}, u32[]{:S(2)}) %collective-permute-start.33) | collective-permute-done | bytes 1048608 | tf_op jit(solution)/shard_map/ppermute | solution.py:373
  304.5 4.3 fusion.46
  309.9 5.5 %add_convert_fusion = bf16[1024,1536]{1,0:T(8,128)(2,1)} fusion(f32[1024,1536]{1,0:T(8,128)S(1)} %fusion.49, bf16[1024,1024]{1,0:T(8,128)(2,1)S(1)} %bitcast.255, bf16[1024,1536]{1,0:T(8,128)(2,1)S(1)} %copy-done.55), kind=kOutput, calls=%fused_computation | convolution fusion | flops 3224371200 | bytes 14680064 | tf_op jit(solution)/shard_map/dot_general | solution.py:1059
  315.4 4.7 copy.52
  320.1 4.3 copy.78
  324.4 5.0 copy.53
  329.4 4.9 pad_maximum_fusion
  337.9 3.9 convolution_convert_fusion.4.do_ref
  341.7 26.4 %unattend.2 = (f32[1024,512]{1,0:T(8,128)}, f32[2048,256]{1,0:T(8,128)}, f32[2048,256]{1,0:T(8,128)}) custom-call(s32[1]{0:T(128)} %bitcast.1.me_ref, bf16[2048,512]{1,0:T(8,128)(2,1)} %get-tuple-element.62.q_ref, bf16[2048,128]{1,0:T(8,128)(2,1)} %select_convert_fusion.qf_ref, bf16[2048,256]{1,0:T(8,128)(2,1)} %get-tuple-element.59.k_ref, ...), custom_call_target="tpu_custom_call" | custom-call | flops 9395240960 | bytes 20971520 | tf_op jit(solution)/shard_map/unattend/pallas_call | solution.py:842
  373.6 3.0 assemble.15
  376.7 4.0 convolution_convert_fusion.3.do_ref
  386.5 15.7 %unattend.3 = (f32[1024,512]{1,0:T(8,128)}, f32[2048,256]{1,0:T(8,128)}, f32[2048,256]{1,0:T(8,128)}) custom-call(s32[1]{0:T(128)} %bitcast.1.me_ref, bf16[2048,512]{1,0:T(8,128)(2,1)} %get-tuple-element.62.q_ref, bf16[2048,128]{1,0:T(8,128)(2,1)} %select_convert_fusion.qf_ref, bf16[2048,256]{1,0:T(8,128)(2,1)} %get-tuple-element.59.k_ref, ...), custom_call_target="tpu_custom_call" | custom-call | flops 9395240960 | bytes 20971520 | tf_op jit(solution)/shard_map/unattend/pallas_call | solution.py:842
  402.2 4.1 pad_maximum_fusion.1.dq_ref
  407.3 13.8 %unproject.1 = (bf16[2048,1024]{1,0:T(8,128)(2,1)}, f32[8,128]{1,0:T(8,128)}) custom-call(f32[2048,512]{1,0:T(8,128)} %pad_maximum_fusion.1.dq_ref, f32[2048,256]{1,0:T(8,128)} %get-tuple-element.83.dk_ref, f32[2048,256]{1,0:T(8,128)} %get-tuple-element.84.dv_ref, f32[2048,768]{1,0:T(8,128)} %get-tuple-element.85.raw_ref, ...), custom_call_target="tpu_custom_call" | custom-call | flops 41943040 | bytes 20971520 | tf_op jit(solution)/shard_map/unproject/pallas_call | solution.py:664
  421.1 3.6 convolution_convert_fusion.1
  425.1 8.4 %multiply_reduce_fusion = (f32[1024]{0:T(1024)S(1)}, bf16[1024,1024]{1,0:T(8,128)(2,1)}) fusion(bf16[1024,1024]{1,0:T(8,128)(2,1)S(1)} %bitcast.310, bf16[2048,1024]{1,0:T(8,128)(2,1)} %get-tuple-element.87, bf16[2048,1024]{1,0:T(8,128)(2,1)S(1)} %copy-done.50), kind=kOutput, calls=%fused_computation.3 | convolution fusion | flops 4300209152 | bytes 12587008 | tf_op jit(solution)/shard_map/dot_general | solution.py:1059
  435.5 3.1 add_convert_fusion.2
  438.6 13.6 %collective-permute-start.41 = (bf16[512,1024]{1,0:T(8,128)(2,1)S(1)}, bf16[512,1024]{1,0:T(8,128)(2,1)S(1)}, u32[]{:S(2)}, u32[]{:S(2)}) collective-permute-start(bf16[512,1024]{1,0:T(8,128)(2,1)S(1)} %add_convert_fusion.2), channel_id=1, source_target_pairs={{0,2},{1,3},{2,0},{3,1},{4,6},{5,7},{6,4},{7,5},{8,10},{9,11},{10,... | collective-permute-start | bytes 3145736 | tf_op jit(solution)/shard_map/ppermute | solution.py:373
  454.1 3.4 fusion.13
  457.7 4.0 collective-permute-start.50
  461.6 7.4 %collective-permute-done.42 = bf16[4,144,1024]{2,1,0:T(8,128)(2,1)S(1)} collective-permute-done((bf16[4,144,1024]{2,1,0:T(8,128)(2,1)S(1)}, bf16[4,144,1024]{2,1,0:T(8,128)(2,1)S(1)}, u32[]{:S(2)}, u32[]{:S(2)}) %collective-permute-start.42) | collective-permute-done | bytes 1179680 | tf_op jit(solution)/shard_map/ppermute | solution.py:373
  469.6 6.1 %collective-permute-done.41 = bf16[512,1024]{1,0:T(8,128)(2,1)S(1)} collective-permute-done((bf16[512,1024]{1,0:T(8,128)(2,1)S(1)}, bf16[512,1024]{1,0:T(8,128)(2,1)S(1)}, u32[]{:S(2)}, u32[]{:S(2)}) %collective-permute-start.41) | collective-permute-done | bytes 1048608 | tf_op jit(solution)/shard_map/ppermute | solution.py:373
  486.5 13.7 %collective-permute-done.44 = bf16[144,1024]{1,0:T(8,128)(2,1)S(1)} collective-permute-done((bf16[144,1024]{1,0:T(8,128)(2,1)S(1)}, bf16[144,1024]{1,0:T(8,128)(2,1)S(1)}, u32[]{:S(2)}, u32[]{:S(2)}) %collective-permute-start.44) | collective-permute-done | bytes 294944 | tf_op jit(solution)/shard_map/ppermute | solution.py:391
  500.5 5.9 %collective-permute-start.48 = (bf16[48,1024]{1,0:T(8,128)(2,1)S(1)}, bf16[48,1024]{1,0:T(8,128)(2,1)S(1)}, u32[]{:S(2)}, u32[]{:S(2)}) collective-permute-start(bf16[48,1024]{1,0:T(8,128)(2,1)S(1)} %get-tuple-element.133), channel_id=1, source_target_pairs={{0,3},{1,2},{2,1},{3,0},{4,7},{5,6},{6,5},{7,4},{8,11},{9,10},{10,... | collective-permute-start | bytes 294920 | tf_op jit(solution)/shard_map/ppermute | solution.py:373
  513.9 5.0 collective-permute-start.55
  528.5 8.8 %collective-permute-done.56 = bf16[96,1024]{1,0:T(8,128)(2,1)S(1)} collective-permute-done((bf16[96,1024]{1,0:T(8,128)(2,1)S(1)}, bf16[96,1024]{1,0:T(8,128)(2,1)S(1)}, u32[]{:S(2)}, u32[]{:S(2)}) %collective-permute-start.56) | collective-permute-done | bytes 196640 | tf_op jit(solution)/shard_map/ppermute | solution.py:1154
  (359 shorter events, 142.3 us)
Async XLA Ops:
  7.2 164.7 %all-gather.2.cloned.1.call-start = ((), (), s32[]{:S(2)}) async-start(), calls=%async_computation.1 | async-start | bytes 6488064 | tf_op jit(solution)/shard_map/all_gather | solution.py:1006
  11.4 6.6 %collective-permute-start.17 = (bf16[32,1536]{1,0:T(8,128)(2,1)S(1)}, bf16[32,1536]{1,0:T(8,128)(2,1)S(1)}, u32[]{:S(2)}, u32[]{:S(2)}) collective-permute-start(bf16[32,1536]{1,0:T(8,128)(2,1)S(1)} %bitcast.299), channel_id=1, source_target_pairs={{0,2},{1,3},{2,0},{3,1},{4,6},{5,7},{6,4},{7,5},{8,10},{9,11},{10,... | collective-permute-start | bytes 294920 | tf_op jit(solution)/shard_map/ppermute | solution.py:373
  12.9 10.1 %collective-permute-start.19 = (bf16[160,1024]{1,0:T(8,128)(2,1)S(1)}, bf16[160,1024]{1,0:T(8,128)(2,1)S(1)}, u32[]{:S(2)}, u32[]{:S(2)}) collective-permute-start(bf16[160,1024]{1,0:T(8,128)(2,1)S(1)} %pad_maximum_fusion.12), channel_id=1, source_target_pairs={{0,0},{1,4},{2,8},{3,12},{4,16},{5,20},{6,24},{7,28},{8,1},{9,5},{... | collective-permute-start | bytes 983048 | tf_op jit(solution)/shard_map/ppermute | solution.py:999
  24.3 487.6 %reduce-scatter.2.cloned.1.call-start = ((), (), s32[]{:S(2)}) async-start(), calls=%async_computation.2 | async-start | bytes 5308416 | tf_op jit(solution)/shard_map/reduce_scatter | solution.py:1069
  24.7 22.2 %collective-permute-start.21 = (s32[2,512]{1,0:T(2,128)S(1)}, s32[2,512]{1,0:T(2,128)S(1)}, u32[]{:S(2)}, u32[]{:S(2)}) collective-permute-start(s32[2,512]{1,0:T(2,128)S(1)} %pad_add_fusion.1), channel_id=1, source_target_pairs={{0,2},{1,3},{2,0},{3,1},{4,6},{5,7},{6,4},{7,5},{8,10},{9,11},{10,... | collective-permute-start | bytes 12296 | tf_op jit(solution)/shard_map/ppermute | solution.py:373
  36.2 12.0 %collective-permute-start.20 = (s32[2,512]{1,0:T(2,128)S(1)}, s32[2,512]{1,0:T(2,128)S(1)}, u32[]{:S(2)}, u32[]{:S(2)}) collective-permute-start(s32[2,512]{1,0:T(2,128)S(1)} %pad_add_fusion.1), channel_id=1, source_target_pairs={{0,1},{1,0},{2,3},{3,2},{4,5},{5,4},{6,7},{7,6},{8,9},{9,8},{10,11... | collective-permute-start | bytes 12296 | tf_op jit(solution)/shard_map/ppermute | solution.py:373
  42.1 32.7 %collective-permute-start.1 = (bf16[512,1024]{1,0:T(8,128)(2,1)S(1)}, bf16[512,1024]{1,0:T(8,128)(2,1)S(1)}, u32[]{:S(2)}, u32[]{:S(2)}) collective-permute-start(bf16[512,1024]{1,0:T(8,128)(2,1)S(1)} %bitcast.220), channel_id=1, source_target_pairs={{0,2},{1,3},{2,0},{3,1},{4,6},{5,7},{6,4},{7,5},{8,10},{9,11},{10,... | collective-permute-start | bytes 3145736 | tf_op jit(solution)/shard_map/ppermute | solution.py:373
  45.0 25.0 %collective-permute-start.5 = (bf16[48,1024]{1,0:T(8,128)(2,1)S(1)}, bf16[48,1024]{1,0:T(8,128)(2,1)S(1)}, u32[]{:S(2)}, u32[]{:S(2)}) collective-permute-start(bf16[48,1024]{1,0:T(8,128)(2,1)S(1)} %bitcast.291), channel_id=1, source_target_pairs={{0,3},{1,2},{2,1},{3,0},{4,7},{5,6},{6,5},{7,4},{8,11},{9,10},{10,... | collective-permute-start | bytes 294920 | tf_op jit(solution)/shard_map/ppermute | solution.py:373
  45.2 26.3 %collective-permute-start.4 = (bf16[48,1024]{1,0:T(8,128)(2,1)S(1)}, bf16[48,1024]{1,0:T(8,128)(2,1)S(1)}, u32[]{:S(2)}, u32[]{:S(2)}) collective-permute-start(bf16[48,1024]{1,0:T(8,128)(2,1)S(1)} %bitcast.293), channel_id=1, source_target_pairs={{0,2},{1,3},{2,0},{3,1},{4,6},{5,7},{6,4},{7,5},{8,10},{9,11},{10,... | collective-permute-start | bytes 294920 | tf_op jit(solution)/shard_map/ppermute | solution.py:373
  48.2 23.4 %collective-permute-start.3 = (bf16[48,1024]{1,0:T(8,128)(2,1)S(1)}, bf16[48,1024]{1,0:T(8,128)(2,1)S(1)}, u32[]{:S(2)}, u32[]{:S(2)}) collective-permute-start(bf16[48,1024]{1,0:T(8,128)(2,1)S(1)} %bitcast.295), channel_id=1, source_target_pairs={{0,1},{1,0},{2,3},{3,2},{4,5},{5,4},{6,7},{7,6},{8,9},{9,8},{10,11... | collective-permute-start | bytes 294920 | tf_op jit(solution)/shard_map/ppermute | solution.py:373
  74.8 61.3 %collective-permute-start.14 = (bf16[512,1024]{1,0:T(8,128)(2,1)S(1)}, bf16[512,1024]{1,0:T(8,128)(2,1)}, u32[]{:S(2)}, u32[]{:S(2)}) collective-permute-start(bf16[512,1024]{1,0:T(8,128)(2,1)S(1)} %bitcast.244), channel_id=1, source_target_pairs={{0,2},{1,3},{2,0},{3,1},{4,6},{5,7},{6,4},{7,5},{8,10},{9,11},{10,... | collective-permute-start | bytes 3145736 | tf_op jit(solution)/shard_map/ppermute | solution.py:373
  76.3 9.4 %collective-permute-start.6 = (bf16[144,1024]{1,0:T(8,128)(2,1)S(1)}, bf16[144,1024]{1,0:T(8,128)(2,1)S(1)}, u32[]{:S(2)}, u32[]{:S(2)}) collective-permute-start(bf16[144,1024]{1,0:T(8,128)(2,1)S(1)} %maximum_maximum_fusion.refs_0_), channel_id=1, source_target_pairs={{0,8},{4,12},{8,16},{12,20},{16,24},{20,28},{24,0},{28,4},{1,9},{5... | collective-permute-start | bytes 884744 | tf_op jit(solution)/shard_map/ppermute | solution.py:391
  76.4 40.9 %collective-permute-start.7 = (bf16[144,1024]{1,0:T(8,128)(2,1)S(1)}, bf16[144,1024]{1,0:T(8,128)(2,1)S(1)}, u32[]{:S(2)}, u32[]{:S(2)}) collective-permute-start(bf16[144,1024]{1,0:T(8,128)(2,1)S(1)} %maximum_maximum_fusion.refs_0_), channel_id=1, source_target_pairs={{0,16},{4,20},{8,24},{12,28},{16,0},{20,4},{24,8},{28,12},{1,17},{... | collective-permute-start | bytes 884744 | tf_op jit(solution)/shard_map/ppermute | solution.py:391
  80.2 43.3 %collective-permute-start.8 = (bf16[144,1024]{1,0:T(8,128)(2,1)S(1)}, bf16[144,1024]{1,0:T(8,128)(2,1)S(1)}, u32[]{:S(2)}, u32[]{:S(2)}) collective-permute-start(bf16[144,1024]{1,0:T(8,128)(2,1)S(1)} %maximum_maximum_fusion.refs_0_), channel_id=1, source_target_pairs={{0,24},{4,28},{8,0},{12,4},{16,8},{20,12},{24,16},{28,20},{1,25},{... | collective-permute-start | bytes 884744 | tf_op jit(solution)/shard_map/ppermute | solution.py:391
  82.1 48.7 %collective-permute-start.9 = (bf16[144,1024]{1,0:T(8,128)(2,1)S(1)}, bf16[144,1024]{1,0:T(8,128)(2,1)S(1)}, u32[]{:S(2)}, u32[]{:S(2)}) collective-permute-start(bf16[144,1024]{1,0:T(8,128)(2,1)S(1)} %maximum_maximum_fusion.refs_0_), channel_id=1, source_target_pairs={{0,4},{4,0},{8,12},{12,8},{16,20},{20,16},{24,28},{28,24},{1,5},{5... | collective-permute-start | bytes 884744 | tf_op jit(solution)/shard_map/ppermute | solution.py:373
  85.7 45.1 %collective-permute-start.10 = (bf16[144,1024]{1,0:T(8,128)(2,1)S(1)}, bf16[144,1024]{1,0:T(8,128)(2,1)S(1)}, u32[]{:S(2)}, u32[]{:S(2)}) collective-permute-start(bf16[144,1024]{1,0:T(8,128)(2,1)S(1)} %collective-permute-done.6.refs_1_), channel_id=1, source_target_pairs={{0,4},{4,0},{8,12},{12,8},{16,20},{20,16},{24,28},{28,24},{1,5},{5... | collective-permute-start | bytes 884744 | tf_op jit(solution)/shard_map/ppermute | solution.py:373
  117.2 13.8 %collective-permute-start.11 = (bf16[144,1024]{1,0:T(8,128)(2,1)S(1)}, bf16[144,1024]{1,0:T(8,128)(2,1)S(1)}, u32[]{:S(2)}, u32[]{:S(2)}) collective-permute-start(bf16[144,1024]{1,0:T(8,128)(2,1)S(1)} %collective-permute-done.7.refs_2_), channel_id=1, source_target_pairs={{0,4},{4,0},{8,12},{12,8},{16,20},{20,16},{24,28},{28,24},{1,5},{5... | collective-permute-start | bytes 884744 | tf_op jit(solution)/shard_map/ppermute | solution.py:373
  123.5 22.3 %collective-permute-start = (bf16[512,1024]{1,0:T(8,128)(2,1)S(1)}, bf16[512,1024]{1,0:T(8,128)(2,1)}, u32[]{:S(2)}, u32[]{:S(2)}) collective-permute-start(bf16[512,1024]{1,0:T(8,128)(2,1)S(1)} %bitcast.221), channel_id=1, source_target_pairs={{0,1},{1,0},{2,3},{3,2},{4,5},{5,4},{6,7},{7,6},{8,9},{9,8},{10,11... | collective-permute-start | bytes 3145736 | tf_op jit(solution)/shard_map/ppermute | solution.py:373
  130.8 9.2 %collective-permute-start.12 = (bf16[144,1024]{1,0:T(8,128)(2,1)S(1)}, bf16[144,1024]{1,0:T(8,128)(2,1)S(1)}, u32[]{:S(2)}, u32[]{:S(2)}) collective-permute-start(bf16[144,1024]{1,0:T(8,128)(2,1)S(1)} %collective-permute-done.8.refs_3_), channel_id=1, source_target_pairs={{0,4},{4,0},{8,12},{12,8},{16,20},{20,16},{24,28},{28,24},{1,5},{5... | collective-permute-start | bytes 884744 | tf_op jit(solution)/shard_map/ppermute | solution.py:373
  130.8 19.7 %collective-permute-start.13 = (bf16[512,1024]{1,0:T(8,128)(2,1)S(1)}, bf16[512,1024]{1,0:T(8,128)(2,1)}, u32[]{:S(2)}, u32[]{:S(2)}) collective-permute-start(bf16[512,1024]{1,0:T(8,128)(2,1)S(1)} %bitcast.245), channel_id=1, source_target_pairs={{0,1},{1,0},{2,3},{3,2},{4,5},{5,4},{6,7},{7,6},{8,9},{9,8},{10,11... | collective-permute-start | bytes 3145736 | tf_op jit(solution)/shard_map/ppermute | solution.py:373
  131.0 14.8 %collective-permute-start.2 = (bf16[512,1024]{1,0:T(8,128)(2,1)S(1)}, bf16[512,1024]{1,0:T(8,128)(2,1)}, u32[]{:S(2)}, u32[]{:S(2)}) collective-permute-start(bf16[512,1024]{1,0:T(8,128)(2,1)S(1)} %collective-permute-done.1.refs_2_), channel_id=1, source_target_pairs={{0,1},{1,0},{2,3},{3,2},{4,5},{5,4},{6,7},{7,6},{8,9},{9,8},{10,11... | collective-permute-start | bytes 3145736 | tf_op jit(solution)/shard_map/ppermute | solution.py:373
  136.1 14.4 %collective-permute-start.15 = (bf16[512,1024]{1,0:T(8,128)(2,1)}, bf16[512,1024]{1,0:T(8,128)(2,1)}, u32[]{:S(2)}, u32[]{:S(2)}) collective-permute-start(bf16[512,1024]{1,0:T(8,128)(2,1)} %collective-permute-done.14.refs_0_), channel_id=1, source_target_pairs={{0,1},{1,0},{2,3},{3,2},{4,5},{5,4},{6,7},{7,6},{8,9},{9,8},{10,11... | collective-permute-start | bytes 3145736 | tf_op jit(solution)/shard_map/ppermute | solution.py:373
  178.8 29.9 %collective-permute-start.25 = (bf16[512,1024]{1,0:T(8,128)(2,1)S(1)}, bf16[512,1024]{1,0:T(8,128)(2,1)S(1)}, u32[]{:S(2)}, u32[]{:S(2)}) collective-permute-start(bf16[512,1024]{1,0:T(8,128)(2,1)S(1)} %add_convert_fusion.7), channel_id=1, source_target_pairs={{0,2},{1,3},{2,0},{3,1},{4,6},{5,7},{6,4},{7,5},{8,10},{9,11},{10,... | collective-permute-start | bytes 3145736 | tf_op jit(solution)/shard_map/ppermute | solution.py:373
  209.8 18.3 %collective-permute-start.26 = (bf16[512,1024]{1,0:T(8,128)(2,1)S(1)}, bf16[512,1024]{1,0:T(8,128)(2,1)S(1)}, u32[]{:S(2)}, u32[]{:S(2)}) collective-permute-start(bf16[512,1024]{1,0:T(8,128)(2,1)S(1)} %multiply_convert_fusion.refs_0_), channel_id=1, source_target_pairs={{0,1},{1,0},{2,3},{3,2},{4,5},{5,4},{6,7},{7,6},{8,9},{9,8},{10,11... | collective-permute-start | bytes 3145736 | tf_op jit(solution)/shard_map/ppermute | solution.py:373
  210.7 35.6 %collective-permute-start.28 = (bf16[512,1024]{1,0:T(8,128)(2,1)S(1)}, bf16[512,1024]{1,0:T(8,128)(2,1)S(1)}, u32[]{:S(2)}, u32[]{:S(2)}) collective-permute-start(bf16[512,1024]{1,0:T(8,128)(2,1)S(1)} %multiply_convert_fusion.refs_0_), channel_id=1, source_target_pairs={{0,2},{1,3},{2,0},{3,1},{4,6},{5,7},{6,4},{7,5},{8,10},{9,11},{10,... | collective-permute-start | bytes 3145736 | tf_op jit(solution)/shard_map/ppermute | solution.py:373
  271.7 21.1 %collective-permute-start.31 = (bf16[512,1024]{1,0:T(8,128)(2,1)}, bf16[512,1024]{1,0:T(8,128)(2,1)}, u32[]{:S(2)}, u32[]{:S(2)}) collective-permute-start(bf16[512,1024]{1,0:T(8,128)(2,1)} %slice.157), channel_id=1, source_target_pairs={{0,1},{1,0},{2,3},{3,2},{4,5},{5,4},{6,7},{7,6},{8,9},{9,8},{10,11... | collective-permute-start | bytes 3145736 | tf_op jit(solution)/shard_map/ppermute | solution.py:373
  274.9 96.1 %collective-permute-start.30 = (bf16[512,1024]{1,0:T(8,128)(2,1)}, bf16[512,1024]{1,0:T(8,128)(2,1)}, u32[]{:S(2)}, u32[]{:S(2)}) collective-permute-start(bf16[512,1024]{1,0:T(8,128)(2,1)} %slice.155), channel_id=1, source_target_pairs={{0,1},{1,0},{2,3},{3,2},{4,5},{5,4},{6,7},{7,6},{8,9},{9,8},{10,11... | collective-permute-start | bytes 3145736 | tf_op jit(solution)/shard_map/ppermute | solution.py:373
  277.2 24.8 %collective-permute-start.33 = (bf16[512,1024]{1,0:T(8,128)(2,1)}, bf16[512,1024]{1,0:T(8,128)(2,1)}, u32[]{:S(2)}, u32[]{:S(2)}) collective-permute-start(bf16[512,1024]{1,0:T(8,128)(2,1)} %add_convert_fusion.5), channel_id=1, source_target_pairs={{0,2},{1,3},{2,0},{3,1},{4,6},{5,7},{6,4},{7,5},{8,10},{9,11},{10,... | collective-permute-start | bytes 3145736 | tf_op jit(solution)/shard_map/ppermute | solution.py:373
  308.8 25.5 %collective-permute-start.35 = (bf16[512,1024]{1,0:T(8,128)(2,1)}, bf16[512,1024]{1,0:T(8,128)(2,1)}, u32[]{:S(2)}, u32[]{:S(2)}) collective-permute-start(bf16[512,1024]{1,0:T(8,128)(2,1)} %get-tuple-element.100.refs_0_), channel_id=1, source_target_pairs={{0,1},{1,0},{2,3},{3,2},{4,5},{5,4},{6,7},{7,6},{8,9},{9,8},{10,11... | collective-permute-start | bytes 3145736 | tf_op jit(solution)/shard_map/ppermute | solution.py:373
  334.3 33.8 %collective-permute-start.34 = (bf16[512,1024]{1,0:T(8,128)(2,1)}, bf16[512,1024]{1,0:T(8,128)(2,1)}, u32[]{:S(2)}, u32[]{:S(2)}) collective-permute-start(bf16[512,1024]{1,0:T(8,128)(2,1)} %get-tuple-element.100.refs_0_), channel_id=1, source_target_pairs={{0,2},{1,3},{2,0},{3,1},{4,6},{5,7},{6,4},{7,5},{8,10},{9,11},{10,... | collective-permute-start | bytes 3145736 | tf_op jit(solution)/shard_map/ppermute | solution.py:373
  370.9 83.2 %collective-permute-start.27 = (bf16[512,1024]{1,0:T(8,128)(2,1)}, bf16[512,1024]{1,0:T(8,128)(2,1)}, u32[]{:S(2)}, u32[]{:S(2)}) collective-permute-start(bf16[512,1024]{1,0:T(8,128)(2,1)} %slice.153), channel_id=1, source_target_pairs={{0,1},{1,0},{2,3},{3,2},{4,5},{5,4},{6,7},{7,6},{8,9},{9,8},{10,11... | collective-permute-start | bytes 3145736 | tf_op jit(solution)/shard_map/ppermute | solution.py:373
  373.0 34.2 %collective-permute-start.36 = (bf16[512,1024]{1,0:T(8,128)(2,1)S(1)}, bf16[512,1024]{1,0:T(8,128)(2,1)}, u32[]{:S(2)}, u32[]{:S(2)}) collective-permute-start(bf16[512,1024]{1,0:T(8,128)(2,1)S(1)} %add_convert_fusion.6), channel_id=1, source_target_pairs={{0,2},{1,3},{2,0},{3,1},{4,6},{5,7},{6,4},{7,5},{8,10},{9,11},{10,... | collective-permute-start | bytes 3145736 | tf_op jit(solution)/shard_map/ppermute | solution.py:373
  384.9 21.3 %collective-permute-start.38 = (bf16[4,64,1024]{2,1,0:T(8,128)(2,1)}, bf16[4,64,1024]{2,1,0:T(8,128)(2,1)S(1)}, u32[]{:S(2)}, u32[]{:S(2)}) collective-permute-start(bf16[4,64,1024]{2,1,0:T(8,128)(2,1)} %dynamic-slice_bitcast_fusion), channel_id=1, source_target_pairs={{0,4},{4,0},{8,12},{12,8},{16,20},{20,16},{24,28},{28,24},{1,5},{5... | collective-permute-start | bytes 1572872 | tf_op jit(solution)/shard_map/ppermute | solution.py:373
  424.7 10.5 %collective-permute-start.40 = (bf16[512,1024]{1,0:T(8,128)(2,1)}, bf16[512,1024]{1,0:T(8,128)(2,1)}, u32[]{:S(2)}, u32[]{:S(2)}) collective-permute-start(bf16[512,1024]{1,0:T(8,128)(2,1)} %convolution_convert_fusion.1), channel_id=1, source_target_pairs={{0,1},{1,0},{2,3},{3,2},{4,5},{5,4},{6,7},{7,6},{8,9},{9,8},{10,11... | collective-permute-start | bytes 3145736 | tf_op jit(solution)/shard_map/ppermute | solution.py:373
  435.2 33.9 %collective-permute-start.42 = (bf16[4,144,1024]{2,1,0:T(8,128)(2,1)S(1)}, bf16[4,144,1024]{2,1,0:T(8,128)(2,1)S(1)}, u32[]{:S(2)}, u32[]{:S(2)}) collective-permute-start(bf16[4,144,1024]{2,1,0:T(8,128)(2,1)S(1)} %fusion.10), channel_id=1, source_target_pairs={{0,4},{4,0},{8,12},{12,8},{16,20},{20,16},{24,28},{28,24},{1,5},{5... | collective-permute-start | bytes 3538952 | tf_op jit(solution)/shard_map/ppermute | solution.py:373
  438.6 37.1 %collective-permute-start.41 = (bf16[512,1024]{1,0:T(8,128)(2,1)S(1)}, bf16[512,1024]{1,0:T(8,128)(2,1)S(1)}, u32[]{:S(2)}, u32[]{:S(2)}) collective-permute-start(bf16[512,1024]{1,0:T(8,128)(2,1)S(1)} %add_convert_fusion.2), channel_id=1, source_target_pairs={{0,2},{1,3},{2,0},{3,1},{4,6},{5,7},{6,4},{7,5},{8,10},{9,11},{10,... | collective-permute-start | bytes 3145736 | tf_op jit(solution)/shard_map/ppermute | solution.py:373
  453.5 26.1 %collective-permute-start.39 = (bf16[512,1024]{1,0:T(8,128)(2,1)S(1)}, bf16[512,1024]{1,0:T(8,128)(2,1)S(1)}, u32[]{:S(2)}, u32[]{:S(2)}) collective-permute-start(bf16[512,1024]{1,0:T(8,128)(2,1)S(1)} %convolution_convert_fusion.2), channel_id=1, source_target_pairs={{0,1},{1,0},{2,3},{3,2},{4,5},{5,4},{6,7},{7,6},{8,9},{9,8},{10,11... | collective-permute-start | bytes 3145736 | tf_op jit(solution)/shard_map/ppermute | solution.py:373
  457.6 48.8 %collective-permute-start.49 = (bf16[64,1024]{1,0:T(8,128)(2,1)S(1)}, bf16[64,1024]{1,0:T(8,128)(2,1)S(1)}, u32[]{:S(2)}, u32[]{:S(2)}) collective-permute-start(bf16[64,1024]{1,0:T(8,128)(2,1)S(1)} %get-tuple-element.114), channel_id=1, source_target_pairs={{0,8},{4,12},{8,16},{12,20},{16,24},{20,28},{24,0},{28,4},{1,9},{5... | collective-permute-start | bytes 393224 | tf_op jit(solution)/shard_map/ppermute | solution.py:391
  457.7 49.2 %collective-permute-start.50 = (bf16[64,1024]{1,0:T(8,128)(2,1)S(1)}, bf16[64,1024]{1,0:T(8,128)(2,1)S(1)}, u32[]{:S(2)}, u32[]{:S(2)}) collective-permute-start(bf16[64,1024]{1,0:T(8,128)(2,1)S(1)} %get-tuple-element.113), channel_id=1, source_target_pairs={{0,16},{4,20},{8,24},{12,28},{16,0},{20,4},{24,8},{28,12},{1,17},{... | collective-permute-start | bytes 393224 | tf_op jit(solution)/shard_map/ppermute | solution.py:391
  475.8 9.9 %collective-permute-start.45 = (bf16[144,1024]{1,0:T(8,128)(2,1)S(1)}, bf16[144,1024]{1,0:T(8,128)(2,1)S(1)}, u32[]{:S(2)}, u32[]{:S(2)}) collective-permute-start(bf16[144,1024]{1,0:T(8,128)(2,1)S(1)} %get-tuple-element.107), channel_id=1, source_target_pairs={{0,24},{4,28},{8,0},{12,4},{16,8},{20,12},{24,16},{28,20},{1,25},{... | collective-permute-start | bytes 884744 | tf_op jit(solution)/shard_map/ppermute | solution.py:391
  477.1 23.1 %collective-permute-start.44 = (bf16[144,1024]{1,0:T(8,128)(2,1)S(1)}, bf16[144,1024]{1,0:T(8,128)(2,1)S(1)}, u32[]{:S(2)}, u32[]{:S(2)}) collective-permute-start(bf16[144,1024]{1,0:T(8,128)(2,1)S(1)} %get-tuple-element.108), channel_id=1, source_target_pairs={{0,16},{4,20},{8,24},{12,28},{16,0},{20,4},{24,8},{28,12},{1,17},{... | collective-permute-start | bytes 884744 | tf_op jit(solution)/shard_map/ppermute | solution.py:391
  479.6 20.6 %collective-permute-start.43 = (bf16[144,1024]{1,0:T(8,128)(2,1)S(1)}, bf16[144,1024]{1,0:T(8,128)(2,1)S(1)}, u32[]{:S(2)}, u32[]{:S(2)}) collective-permute-start(bf16[144,1024]{1,0:T(8,128)(2,1)S(1)} %get-tuple-element.106), channel_id=1, source_target_pairs={{0,8},{4,12},{8,16},{12,20},{16,24},{20,28},{24,0},{28,4},{1,9},{5... | collective-permute-start | bytes 884744 | tf_op jit(solution)/shard_map/ppermute | solution.py:391
  485.6 21.3 %collective-permute-start.51 = (bf16[64,1024]{1,0:T(8,128)(2,1)S(1)}, bf16[64,1024]{1,0:T(8,128)(2,1)S(1)}, u32[]{:S(2)}, u32[]{:S(2)}) collective-permute-start(bf16[64,1024]{1,0:T(8,128)(2,1)S(1)} %get-tuple-element.112), channel_id=1, source_target_pairs={{0,24},{4,28},{8,0},{12,4},{16,8},{20,12},{24,16},{28,20},{1,25},{... | collective-permute-start | bytes 393224 | tf_op jit(solution)/shard_map/ppermute | solution.py:391
  500.5 8.6 %collective-permute-start.48 = (bf16[48,1024]{1,0:T(8,128)(2,1)S(1)}, bf16[48,1024]{1,0:T(8,128)(2,1)S(1)}, u32[]{:S(2)}, u32[]{:S(2)}) collective-permute-start(bf16[48,1024]{1,0:T(8,128)(2,1)S(1)} %get-tuple-element.133), channel_id=1, source_target_pairs={{0,3},{1,2},{2,1},{3,0},{4,7},{5,6},{6,5},{7,4},{8,11},{9,10},{10,... | collective-permute-start | bytes 294920 | tf_op jit(solution)/shard_map/ppermute | solution.py:373
  507.0 16.1 %collective-permute-start.52 = (bf16[64,1024]{1,0:T(8,128)(2,1)S(1)}, bf16[64,1024]{1,0:T(8,128)(2,1)S(1)}, u32[]{:S(2)}, u32[]{:S(2)}) collective-permute-start(bf16[64,1024]{1,0:T(8,128)(2,1)S(1)} %add_convert_fusion.9), channel_id=1, source_target_pairs={{0,0},{4,1},{8,2},{12,3},{16,4},{20,5},{24,6},{28,7},{1,8},{5,9},{... | collective-permute-start | bytes 393224 | tf_op jit(solution)/shard_map/ppermute | solution.py:1153
  513.9 12.8 %collective-permute-start.55 = (bf16[32,1536]{1,0:T(8,128)(2,1)S(1)}, bf16[32,1536]{1,0:T(8,128)(2,1)S(1)}, u32[]{:S(2)}, u32[]{:S(2)}) collective-permute-start(bf16[32,1536]{1,0:T(8,128)(2,1)S(1)} %get-tuple-element.121), channel_id=1, source_target_pairs={{0,3},{1,2},{2,1},{3,0},{4,7},{5,6},{6,5},{7,4},{8,11},{9,10},{10,... | collective-permute-start | bytes 294920 | tf_op jit(solution)/shard_map/ppermute | solution.py:373
  518.9 7.8 %collective-permute-start.54 = (bf16[32,1536]{1,0:T(8,128)(2,1)S(1)}, bf16[32,1536]{1,0:T(8,128)(2,1)S(1)}, u32[]{:S(2)}, u32[]{:S(2)}) collective-permute-start(bf16[32,1536]{1,0:T(8,128)(2,1)S(1)} %get-tuple-element.122), channel_id=1, source_target_pairs={{0,2},{1,3},{2,0},{3,1},{4,6},{5,7},{6,4},{7,5},{8,10},{9,11},{10,... | collective-permute-start | bytes 294920 | tf_op jit(solution)/shard_map/ppermute | solution.py:373
  524.0 13.3 %collective-permute-start.56 = (bf16[96,1024]{1,0:T(8,128)(2,1)S(1)}, bf16[96,1024]{1,0:T(8,128)(2,1)S(1)}, u32[]{:S(2)}, u32[]{:S(2)}) collective-permute-start(bf16[96,1024]{1,0:T(8,128)(2,1)S(1)} %bitcast.282), channel_id=1, source_target_pairs={{0,0},{4,1},{8,2},{12,3},{16,4},{20,5},{24,6},{28,7},{1,8},{5,9},{... | collective-permute-start | bytes 589832 | tf_op jit(solution)/shard_map/ppermute | solution.py:1154
  (68 other events, 687.9 us)
Sparse Core Ops, SparseCore 0:
  24.5 122.4 all-gather.1
  371.2 107.6 reduce-scatter.1

commit v4 on v3

--- a/solution.py
+++ b/solution.py
@@ -360,7 +360,6 @@
     )
 
 FEATURES = 128
-NARROW = 512
 MASK_DEPTH = -4096.0
 LOG2_E = 1.4426950408889634
 VMEM_BYTES = 56 * 1024 * 1024
@@ -382,8 +381,9 @@
     relative = [pick(stacked, me)]
     for offset in range(1, size):
         relative.append(xor_permute(pick(stacked, me ^ offset), "ctx", offset))
+    arrived = relative[1:]
     relative = jnp.stack(relative)
-    return jnp.stack([pick(relative, me ^ source) for source in range(size)])
+    return jnp.stack([pick(relative, me ^ source) for source in range(size)]), arrived
 
 
 def shift_z(value, offset):
@@ -465,17 +465,6 @@
     return total.astype(bf16)
 
 
-def narrow(rows, parts):
-    pieces = rows.reshape(parts, rows.shape[0] // parts, -1, NARROW)
-    return pieces.transpose(0, 2, 1, 3).reshape(parts, -1, NARROW)
-
-
-def widen(pieces, height):
-    parts = pieces.shape[0]
-    pieces = pieces.reshape(parts, -1, height, NARROW).transpose(0, 2, 1, 3)
-    return pieces.reshape(parts * height, -1)
-
-
 def after(value, *others):
     return lax.optimization_barrier((value, *others))[0]
 
@@ -519,7 +508,8 @@
 def project_kernel(
     query_heads,
     key_heads,
-    x_ref,
+    per_block,
+    x_refs,
     gain_ref,
     weight_ref,
     cos_ref,
@@ -531,8 +521,15 @@
     q_ref,
     k_ref,
     v_ref,
+    held_ref,
 ):
-    x = x_ref[...].astype(f32)
+    for r, x_ref in enumerate(x_refs):
+
+        @pl.when(pl.program_id(0) // per_block == r)
+        def _():
+            held_ref[...] = x_ref[...]
+
+    x = held_ref[...].astype(f32)
     scale = lax.rsqrt(jnp.mean(x * x, axis=-1, keepdims=True) + EPSILON)
     normed = (x * scale * gain_ref[...]).astype(bf16)
     normed_ref[...] = normed
@@ -554,9 +551,11 @@
             k_ref[:, at : at + HEAD_SIZE] = rows
 
 
-def project(x, gain, weight, cosine, sine, gain_q, gain_k, query_heads, key_heads):
-    rows, width = x.shape
+def project(x_blocks, gain, weight, cosine, sine, gain_q, gain_k, query_heads, key_heads):
+    rows, width = x_blocks[0].shape
     block = 256
+    per_block = rows // block
+    rows = rows * len(x_blocks)
     turned = (query_heads + key_heads) * HEAD_SIZE
     columns = weight.shape[1]
 
@@ -566,11 +565,16 @@
     def whole(shape):
         return pl.BlockSpec(shape, lambda i: (0, 0))
 
+    def part(r):
+        return pl.BlockSpec(
+            (block, width), lambda i: (jnp.clip(i - r * per_block, 0, per_block - 1), 0)
+        )
+
     return pl.pallas_call(
-        functools.partial(project_kernel, query_heads, key_heads),
+        functools.partial(project_kernel, query_heads, key_heads, per_block),
         grid=(rows // block,),
         in_specs=[
-            tall(width),
+            [part(r) for r in range(len(x_blocks))],
             whole((1, width)),
             whole(weight.shape),
             tall(HEAD_SIZE),
@@ -592,6 +596,7 @@
             jax.ShapeDtypeStruct((rows, key_heads * HEAD_SIZE), bf16),
             jax.ShapeDtypeStruct((rows, key_heads * HEAD_SIZE), bf16),
         ],
+        scratch_shapes=[pltpu.VMEM((block, width), bf16)],
         compiler_params=pltpu.CompilerParams(vmem_limit_bytes=VMEM_BYTES),
         cost_estimate=pl.CostEstimate(
             flops=2 * rows * width * columns,
@@ -599,13 +604,15 @@
             transcendentals=0,
         ),
         name="project",
-    )(x, gain, weight, cosine, sine, gain_q, gain_k)
+    )(list(x_blocks), gain, weight, cosine, sine, gain_q, gain_k)
 
 
 def unproject_kernel(
     query_heads,
     key_heads,
-    dq_ref,
+    half,
+    dq_near_ref,
+    dq_far_ref,
     dk_ref,
     dv_ref,
     raw_ref,
@@ -628,7 +635,8 @@
         at = head * HEAD_SIZE
         raw = raw_ref[:, at : at + HEAD_SIZE]
         if head < query_heads:
-            grad = dq_ref[:, at : at + HEAD_SIZE]
+            lanes = slice(at, at + HEAD_SIZE)
+            grad = jnp.where(pl.program_id(0) < half, dq_near_ref[:, lanes], dq_far_ref[:, lanes])
             gain = gain_q_ref[...]
         else:
             back = (head - query_heads) * HEAD_SIZE
@@ -650,9 +658,10 @@
     dgain_ref[1:2, :] += total_k
 
 
-def unproject(dq, dk, dv, raw, cosine, sine, gain_q, gain_k, query_heads, key_heads):
-    rows = dq.shape[0]
+def unproject(dq_near, dq_far, dk, dv, raw, cosine, sine, gain_q, gain_k, query_heads, key_heads):
+    rows = dk.shape[0]
     block = 256
+    half = rows // block // 2
     columns = (query_heads + 2 * key_heads) * HEAD_SIZE
 
     def tall(n):
@@ -662,10 +671,11 @@
         return pl.BlockSpec(shape, lambda i: (0, 0))
 
     return pl.pallas_call(
-        functools.partial(unproject_kernel, query_heads, key_heads),
+        functools.partial(unproject_kernel, query_heads, key_heads, half),
         grid=(rows // block,),
         in_specs=[
-            tall(dq.shape[1]),
+            pl.BlockSpec((block, dq_near.shape[1]), lambda i: (jnp.minimum(i, half - 1), 0)),
+            pl.BlockSpec((block, dq_far.shape[1]), lambda i: (jnp.maximum(i - half, 0), 0)),
             tall(dk.shape[1]),
             tall(dv.shape[1]),
             tall(raw.shape[1]),
@@ -684,7 +694,7 @@
             flops=20 * rows * columns, bytes_accessed=10 * rows * columns, transcendentals=0
         ),
         name="unproject",
-    )(dq, dk, dv, raw, cosine, sine, gain_q, gain_k)
+    )(dq_near, dq_far, dk, dv, raw, cosine, sine, gain_q, gain_k)
 
 
 def attend_kernel(
@@ -769,13 +779,15 @@
     kf_ref,
     v_ref,
     o_ref,
-    do_ref,
+    branch_first_ref,
+    branch_second_ref,
+    out_ref,
     log_ref,
     *rest,
 ):
     if resumed:
-        dk_in_ref, dv_in_ref, *rest = rest
-    dq_ref, dk_ref, dv_ref, flipped_ref, total_ref = rest
+        dk_in_ref, dv_in_ref, d_weight_in_ref, *rest = rest
+    dq_ref, dk_ref, dv_ref, d_weight_ref, flipped_ref, total_ref, do_ref = rest
     me = me_ref[0]
     at_query = (pl.program_id(1) + first) ^ me
     scale = HEAD_SIZE ** (-0.5)
@@ -785,7 +797,21 @@
     def _():
         dk_ref[...] = dk_in_ref[...] if resumed else jnp.zeros_like(dk_ref)
         dv_ref[...] = dv_in_ref[...] if resumed else jnp.zeros_like(dv_ref)
+        d_weight_ref[...] = d_weight_in_ref[...] if resumed else jnp.zeros_like(d_weight_ref)
         flipped_ref[...] = k_ref[...].astype(f32).T.astype(bf16)
+
+    def take(branch_ref):
+        do_ref[...] = nt_dot(branch_ref[...], out_ref[...]).astype(bf16)
+        turned = o_ref[...].astype(f32).T.astype(bf16)
+        d_weight_ref[...] += nn_dot(turned, branch_ref[...])
+
+    @pl.when(pl.program_id(1) == 0)
+    def _():
+        take(branch_first_ref)
+
+    @pl.when(pl.program_id(1) == 1)
+    def _():
+        take(branch_second_ref)
 
     total_ref[...] = jnp.zeros_like(total_ref)
     query_features = qf_ref[...]
@@ -830,53 +856,85 @@
             dk_ref[...] = dk_ref[...] * scale
 
 
-def unattend(me, q, qf, k, kf, v, o, d_out, logs, block, group, first, count, earlier=()):
+def unattend(me, q, qf, k, kf, v, o, branches, out, logs, block, group, first, earlier=()):
+    count = len(branches)
     rows = k.shape[0]
     key_heads = k.shape[1] // HEAD_SIZE
+    width = out.shape[1]
+    lanes = group * HEAD_SIZE
     pairs = key_heads * group * count * block * rows * 5 // 8
 
     def by_query(n):
         return pl.BlockSpec((block, n), lambda g, i, me: (i, g))
 
     by_key = pl.BlockSpec((rows, HEAD_SIZE), lambda g, i, me: (0, g))
+    by_head = pl.BlockSpec((lanes, width), lambda g, i, me: (g, 0))
+    whole = pl.BlockSpec((block, width), lambda g, i, me: (0, 0))
     return pl.pallas_call(
         functools.partial(unattend_kernel, group, block, first, bool(earlier)),
         grid_spec=pltpu.PrefetchScalarGridSpec(
             num_scalar_prefetch=1,
             grid=(key_heads, count),
             in_specs=[
-                pl.BlockSpec((block, group * HEAD_SIZE), lambda g, i, me: (i + first, g)),
+                pl.BlockSpec((block, lanes), lambda g, i, me: (i + first, g)),
                 pl.BlockSpec((block, FEATURES), lambda g, i, me: (i + first, 0)),
                 by_key,
                 pl.BlockSpec((rows, FEATURES), lambda g, i, me: (0, 0)),
                 by_key,
-                by_query(group * HEAD_SIZE),
-                by_query(group * HEAD_SIZE),
+                by_query(lanes),
+                whole,
+                whole,
+                by_head,
                 pl.BlockSpec((1, group, block), lambda g, i, me: (g, 0, i)),
             ]
-            + [by_key] * len(earlier),
-            out_specs=[by_query(group * HEAD_SIZE), by_key, by_key],
+            + ([by_key, by_key, by_head] if earlier else []),
+            out_specs=[by_query(lanes), by_key, by_key, by_head],
             scratch_shapes=[
                 pltpu.VMEM((HEAD_SIZE, rows), bf16),
                 pltpu.VMEM((group, HEAD_SIZE, block), f32),
+                pltpu.VMEM((block, lanes), bf16),
             ],
         ),
         out_shape=[
             jax.ShapeDtypeStruct((count * block, q.shape[1]), f32),
             jax.ShapeDtypeStruct(k.shape, f32),
             jax.ShapeDtypeStruct(v.shape, f32),
+            jax.ShapeDtypeStruct(out.shape, f32),
         ],
         compiler_params=pltpu.CompilerParams(vmem_limit_bytes=VMEM_BYTES),
         cost_estimate=pl.CostEstimate(
             flops=14 * pairs * HEAD_SIZE, bytes_accessed=20 * q.size, transcendentals=pairs
         ),
         name="unattend",
-    )(me, q, qf, k, kf, v, o, d_out, logs, *earlier)
+    )(me, q, qf, k, kf, v, o, *branches, out, logs, *earlier)
 
 
 def feed_kernel(
-    units, h_ref, cot_ref, both_ref, down_ref, hidden_ref, d_both_ref, part_ref, d_part_ref
+    units,
+    half,
+    first_ref,
+    second_ref,
+    cot_ref,
+    both_ref,
+    down_ref,
+    h_ref,
+    hidden_ref,
+    d_both_ref,
+    part_first_ref,
+    part_second_ref,
+    d_part_first_ref,
+    d_part_second_ref,
 ):
+    in_first = pl.program_id(0) < half
+
+    @pl.when(in_first)
+    def _():
+        h_ref[...] = first_ref[...]
+
+    @pl.when(jnp.logical_not(in_first))
+    def _():
+        h_ref[...] = second_ref[...]
+
     both = nn_dot(h_ref[...], both_ref[...])
     d_hidden = nt_dot(cot_ref[...], down_ref[...])
     gate, up = both[:, :units], both[:, units:]
@@ -884,18 +942,29 @@
     silu = gate * sigmoid
     hidden = (silu * up).astype(bf16)
     hidden_ref[...] = hidden
-    part_ref[...] = nn_dot(hidden, down_ref[...]).astype(bf16)
+    part = nn_dot(hidden, down_ref[...]).astype(bf16)
     d_gate = (d_hidden * up * sigmoid * (1.0 + gate * (1.0 - sigmoid))).astype(bf16)
     d_up = (d_hidden * silu).astype(bf16)
     d_both = jnp.concatenate([d_gate, d_up], axis=1)
     d_both_ref[...] = d_both
-    d_part_ref[...] = nt_dot(d_both, both_ref[...]).astype(bf16)
-
-
-def feed(h, cot, both, down):
-    rows, width = h.shape
+    d_part = nt_dot(d_both, both_ref[...]).astype(bf16)
+
+    @pl.when(in_first)
+    def _():
+        part_first_ref[...] = part
+        d_part_first_ref[...] = d_part
+
+    @pl.when(jnp.logical_not(in_first))
+    def _():
+        part_second_ref[...] = part
+        d_part_second_ref[...] = d_part
+
+
+def feed(h_first, h_second, cot, both, down):
+    rows, width = cot.shape
     units = down.shape[0]
     block = 256
+    half = rows // block // 2
 
     def tall(n):
         return pl.BlockSpec((block, n), lambda i: (i, 0))
@@ -903,22 +972,23 @@
     def whole(shape):
         return pl.BlockSpec(shape, lambda i: (0, 0))
 
+    of_first = pl.BlockSpec((block, width), lambda i: (jnp.minimum(i, half - 1), 0))
+    of_second = pl.BlockSpec((block, width), lambda i: (jnp.maximum(i - half, 0), 0))
+    shapes = [(rows, width), (rows, units), (rows, 2 * units)] + [(rows // 2, width)] * 4
     return pl.pallas_call(
-        functools.partial(feed_kernel, units),
+        functools.partial(feed_kernel, units, half),
         grid=(rows // block,),
-        in_specs=[tall(width), tall(width), whole(both.shape), whole(down.shape)],
-        out_specs=[tall(units), tall(2 * units), tall(width), tall(width)],
-        out_shape=[
-            jax.ShapeDtypeStruct((rows, n), bf16) for n in (units, 2 * units, width, width)
-        ],
+        in_specs=[of_first, of_second, tall(width), whole(both.shape), whole(down.shape)],
+        out_specs=[tall(width), tall(units), tall(2 * units)] + [of_first, of_second] * 2,
+        out_shape=[jax.ShapeDtypeStruct(shape, bf16) for shape in shapes],
         compiler_params=pltpu.CompilerParams(vmem_limit_bytes=VMEM_BYTES),
         cost_estimate=pl.CostEstimate(
             flops=12 * rows * width * units,
-            bytes_accessed=rows * (8 * width + 6 * units) + 6 * width * units,
+            bytes_accessed=rows * (10 * width + 6 * units) + 6 * width * units,
             transcendentals=rows * units,
         ),
         name="feed",
-    )(h, cot, both, down)
+    )(h_first, h_second, cot, both, down)
 
 
 def norm_back(value_rows, gain_vec, grad):
@@ -965,12 +1035,6 @@
     def by_columns(weight):
         return weight.reshape(weight.shape[0], size, -1).transpose(1, 0, 2)
 
-    x_own = tokens.reshape(block, MODEL_WIDTH)
-    x_blocks = gather_blocks(x_own)
-    x_all = join(x_blocks)
-    places = jnp.concatenate([positions, segment_ids]).astype(jnp.int32)
-    places = jnp.concatenate(gather_blocks(places), axis=1)
-
     first = jnp.concatenate(
         [by_columns(w_query), by_columns(key_weight), by_columns(value_weight)], axis=2
     )
@@ -978,7 +1042,7 @@
     first = jnp.concatenate(
         [first, jnp.broadcast_to(gain_rows[None], (size,) + gain_rows.shape)], axis=1
     )
-    first = exchange(first, me)
+    first, arrived = exchange(first, me)
     gain_rows = jnp.concatenate(
         [first[:, owned], jnp.zeros((pad_rows - size, first.shape[2]), bf16)]
     )
@@ -986,29 +1050,27 @@
         [first[:, :owned].reshape(size * owned, first.shape[2]), gain_rows]
     )
     first_pieces, places_dp = gather_copies(first)
+    early = first_pieces[1 : copies // 2]
+
+    gate_up = jnp.concatenate([by_columns(w_gate), by_columns(w_up)], axis=2)
+    gate_up, arrived = exchange(after(gate_up, *arrived), me)
+    moved = after(jnp.concatenate([w_out, w_down]), *arrived)
+    moved = lax.ppermute(moved, ("dp", "ctx"), forward_owner)
+    places = jnp.concatenate([positions, segment_ids]).astype(jnp.int32)
+    places = jnp.concatenate(gather_blocks(after(places, *arrived)), axis=1)
+    x_own = tokens.reshape(block, MODEL_WIDTH)
+    x_blocks = gather_blocks(after(x_own, *arrived))
     cot_own = cotangent.reshape(block, MODEL_WIDTH)
     cot_blocks = gather_blocks(after(cot_own, x_blocks[2]))
+    cot_near, cot_far = join(cot_blocks[:2]), join(cot_blocks[2:])
+
+    gate_up_rows = after(gate_up.reshape(size * owned, -1), *early)
+    gate_up = lax.all_gather(gate_up_rows, "dp", axis=0, tiled=True)
+    moved_pieces, unused = gather_copies(after(moved, *early))
     w_first, gain_rows = assemble(first_pieces, places_dp, (size * owned, pad_rows))
-    w_first = after(w_first, *cot_blocks)
+    w_first = after(w_first, gate_up_rows, *moved_pieces[1 : copies // 2])
     full_gains = gain_rows.reshape(copies, pad_rows, -1)[:, :size, :gain_count].reshape(-1)
     gain_attn, gain_mlp, gain_query, gain_key = split_gains(full_gains)
-
-    rows_out, rows_down, rows_both = w_out.shape[0], w_down.shape[0], size * owned
-    per_row = MODEL_WIDTH // NARROW
-    feed_rows = rows_both * (2 * hidden_cols // NARROW) + rows_down * per_row
-    moved = lax.ppermute(jnp.concatenate([w_out, w_down]), ("dp", "ctx"), forward_owner)
-    gate_up = jnp.concatenate([by_columns(w_gate), by_columns(w_up)], axis=2)
-    gate_up = exchange(gate_up, me).reshape(rows_both, -1)
-    later = jnp.concatenate(
-        [narrow(gate_up, 1)[0], narrow(moved[rows_out:], 1)[0], narrow(moved[:rows_out], 1)[0]]
-    )
-    w_first = after(w_first, later)
-    later = lax.all_gather(later, "dp", axis=0, tiled=True).reshape(copies, -1, NARROW)
-    out_full = widen(later[:, feed_rows:], rows_out)
-    gate_up = widen(later[:, : rows_both * (2 * hidden_cols // NARROW)], rows_both)
-    down_full = widen(later[:, rows_both * (2 * hidden_cols // NARROW) : feed_rows], rows_down)
-    near, far = slice(0, 2), slice(2, 4)
-    cot_near, cot_far = join(cot_blocks[near]), join(cot_blocks[far])
 
     half = HEAD_SIZE // 2
     rates = THETA ** (-2.0 * jnp.arange(half, dtype=f32) / HEAD_SIZE)
@@ -1022,7 +1084,7 @@
     query_features = jnp.where(same, 0.0, MASK_DEPTH).astype(bf16)
     gain_q_row, gain_k_row = gain_query[None], gain_key[None]
     normed, raw, q, k, v = project(
-        x_all, gain_attn[None], w_first, cosine, sine, gain_q_row, gain_k_row, query_heads, key_heads
+        x_blocks, gain_attn[None], w_first, cosine, sine, gain_q_row, gain_k_row, query_heads, key_heads
     )
     def attend_half(query, first):
         return attend(
@@ -1032,28 +1094,36 @@
     def halves(value):
         return value[:block], value[block:]
 
+    q, cot_near, cot_far, *moved_pieces = lax.optimization_barrier(
+        (q, cot_near, cot_far, *moved_pieces)
+    )
     att_far, logs_far = attend_half(q, 2)
+    out_full, down_full = assemble(moved_pieces, places_dp, (w_out.shape[0], w_down.shape[0]))
     att_across, att_corner = halves(att_far)
     part_corner, part_across = nn_dot(att_corner, out_full), nn_dot(att_across, out_full)
     toward, across = send_across(part_corner, part_across)
-    att_near, logs_near = attend_half(after(q, toward), 0)
+    att_near, logs_near = attend_half(after(q, toward, gate_up), 0)
     att_own, att_beside = halves(att_near)
-    part_beside, part_own = nn_dot(att_beside, out_full), nn_dot(att_own, out_full)
-    middle = x_own.astype(f32) + sum_own(part_beside, part_own, across)
+    beside = [
+        xor_permute(nn_dot(piece, out_full).astype(bf16), "ctx", 1)
+        for piece in jnp.split(att_beside, 2)
+    ]
+    part_own = nn_dot(att_own, out_full) + jnp.concatenate(beside).astype(f32)
+    middle = x_own.astype(f32) + part_own + across.astype(f32)
     h_blocks, across = gather_near(row_norm_apply(middle, gain_mlp).astype(bf16))
-    h_near = join(h_blocks)
-    hidden_near, d_both_near, down_near, d_h_near = feed(h_near, cot_near, gate_up, down_full)
-    h_far = join(gather_far(across, hidden_near))
-    hidden_far, d_both_far, down_far, d_h_far = feed(h_far, cot_far, gate_up, down_full)
-
-    part_across, part_corner = halves(d_h_far)
-    unused, across = send_across(part_corner, part_across)
-    part_own, part_beside = halves(d_h_near)
-    d_normed = sum_own(part_beside, part_own, across)
+    h_near, hidden_near, d_both_near, down_own, down_beside, d_own, d_beside = feed(
+        *h_blocks, cot_near, gate_up, down_full
+    )
+    h_blocks = gather_far(across, hidden_near)
+    h_far, hidden_far, d_both_far, down_across, down_corner, d_across, d_corner = feed(
+        *h_blocks, cot_far, gate_up, down_full
+    )
+
+    unused, across = send_across(d_corner, d_across)
+    d_normed = sum_own(d_beside, d_own, across)
     d_middle, d_gain_mlp = norm_back(middle, gain_mlp, d_normed)
     d_middle = d_middle + cot_own.astype(f32)
-    d_branch_blocks, d_branch_across = gather_near(d_middle.astype(bf16))
-    d_branch_near = join(d_branch_blocks)
+    branches_near, branch_across = gather_near(d_middle.astype(bf16))
 
     def tn_dot(left, right):
         return lax.dot_general(left, right, (((0,), (0,)), ((), ())), preferred_element_type=f32)
@@ -1063,13 +1133,12 @@
 
     grad_down = tn_dot(hidden_near, cot_near) + tn_dot(hidden_far, cot_far)
     grad_both = tn_dot(h_near, d_both_near) + tn_dot(h_far, d_both_far)
-    feed_parts = jnp.concatenate(
-        [narrow(grad_both.astype(bf16), copies), narrow(grad_down.astype(bf16), copies)], axis=1
-    ).reshape(-1, NARROW)
-    grad_feed = lax.psum_scatter(feed_parts, "dp", scatter_dimension=0, tiled=True)
-
-    def unattend_half(att, d_branch, logs, first, earlier, *waits):
-        d_att = after(nt_dot(d_branch, out_full).astype(bf16), *waits)
+    grad_both = grad_both.astype(bf16)
+    grad_down = grad_down.astype(bf16)
+    d_both_sum = lax.psum_scatter(grad_both, "dp", scatter_dimension=0, tiled=True)
+    d_down_sum = lax.psum_scatter(grad_down, "dp", scatter_dimension=0, tiled=True)
+
+    def unattend_half(att, branches, logs, first, earlier=()):
         return unattend(
             me_row,
             q,
@@ -1078,30 +1147,25 @@
             key_features,
             v,
             att,
-            d_att,
+            branches,
+            out_full,
             logs,
             block,
             group,
             first,
-            2,
             earlier,
         )
 
-    dq_near, *earlier = unattend_half(att_near, d_branch_near, logs_near, 0, (), feed_parts)
-    d_branch_blocks = gather_far(d_branch_across, dq_near)
-    d_branch_far = join(d_branch_blocks)
-    part_across, part_corner = halves(down_far)
-    unused, down_across = send_across(part_corner, part_across, d_branch_blocks[0])
-    part_own, part_beside = halves(down_near)
-    output = (middle + sum_own(part_beside, part_own, down_across)).astype(bf16)
-
-    grad_out = tn_dot(att_near, d_branch_near) + tn_dot(att_far, d_branch_far)
+    branches_near = [after(branches_near[0], grad_both, grad_down), branches_near[1]]
+    dq_near, *earlier = unattend_half(att_near, branches_near, logs_near, 0)
+    branches_far = gather_far(branch_across, dq_near)
+    unused, across = send_across(down_corner, down_across, branches_far[0])
+    output = (middle + sum_own(down_beside, down_own, across)).astype(bf16)
+    dq_far, dk, dv, grad_out = unattend_half(att_far, branches_far, logs_far, 2, earlier)
     pair_out = reduce_beside(by_copy(grad_out))
-    dq_far, dk, dv = unattend_half(att_far, d_branch_far, logs_far, 2, earlier)
-    dk = after(dk, pair_out, down_across)
-    dq = jnp.concatenate([dq_near, dq_far])
+    dk = after(dk, across)
     low, d_gain_heads = unproject(
-        dq, dk, dv, raw, cosine, sine, gain_q_row, gain_k_row, query_heads, key_heads
+        dq_near, dq_far, dk, dv, raw, cosine, sine, gain_q_row, gain_k_row, query_heads, key_heads
     )
     terms_out = reduce_along(after(pair_out, low))
     low_own, low_beside, low_across, low_corner = (
@@ -1125,19 +1189,18 @@
     grad_first = jnp.concatenate(
         [grad_first.reshape(copies, size * owned, -1), gain_block], axis=1
     )
-    terms_first = reduce_along(after(reduce_beside(grad_first), across))
+    pair_first = reduce_beside(grad_first)
+    d_both_sum = after(d_both_sum, pair_first)
+    terms_first = reduce_along(after(pair_first, across))
+    d_down_sum = after(d_down_sum, *terms_first)
     grad_first = add_all(terms_first)
     grad_out = add_all(after(terms_out, *terms_first))
-    grad_feed = after(grad_feed, *terms_first)
-    split = rows_both * (2 * hidden_cols // NARROW)
-    grad_both = widen(grad_feed[None, :split], rows_both)
-    grad_down = widen(grad_feed[None, split:], rows_down)
     gain_part = grad_first[size * owned :][:size]
     gain_part = jnp.broadcast_to(gain_part[:, None], (size, pad_rows, gain_part.shape[1]))
     grad_first = jnp.concatenate(
         [grad_first[: size * owned].reshape(size, owned, -1), gain_part], axis=1
     )
-    grad_first = exchange(grad_first, me).astype(f32)
+    grad_first = exchange(grad_first, me)[0].astype(f32)
     grad_gains = jnp.sum(grad_first[:, owned, :gain_count], axis=0)
     grad_first = grad_first[:, :owned]
 
@@ -1147,11 +1210,11 @@
     grad_query = to_rows(grad_first[:, :, :q_cols])
     grad_key = to_rows(grad_first[:, :, q_cols : q_cols + k_cols])
     grad_value = to_rows(grad_first[:, :, q_cols + k_cols :])
-    grad_both = exchange(grad_both.reshape(size, owned, -1), me).astype(f32)
+    grad_both = exchange(d_both_sum.reshape(size, owned, -1), me)[0].astype(f32)
     grad_gate = to_rows(grad_both[:, :, :hidden_cols])
     grad_up = to_rows(grad_both[:, :, hidden_cols:])
     grad_out = lax.ppermute(grad_out, ("dp", "ctx"), backward_owner).astype(f32)
-    grad_down = lax.ppermute(grad_down, ("dp", "ctx"), backward_owner).astype(f32)
+    grad_down = lax.ppermute(d_down_sum, ("dp", "ctx"), backward_owner).astype(f32)
     return (
         output.reshape(tokens.shape),
         grad_tokens,

time: 555 us -> 553 us (level)
  waiting for transfers between devices: 117 us -> 174 us
  local copies, waits for them, and re-layouts: 64.2 us -> 21.8 us
  starting transfers between devices: 107 us -> 98.4 us
    ppermute x9 -> x12, waiting for transfers between devices: 49.1 us -> 80.2 us  [shift_z(): lax.ppermute(value, 'dp', [(i, (i + 2 * offset) % size) for i in range(si...]
    ppermute x45 -> x50, waiting for transfers between devices: 57.8 us -> 82.9 us  [xor_permute(): return lax.ppermute(value, axis, [(i, i ^ offset) for i in range(size)])]
    pallas_call x8 -> x4, Pallas kernels: 24.9 us -> 12.2 us  [assemble(): pl.pallas_call(functools.partial(assemble_kernel, splits, count), in_spec...]
    slice x12 -> x0, local copies, waits for them, and re-layouts: 12.1 us -> none  [the longest x4 5.88 us: halves(): return (value[:block], value[block:])]
    ppermute x1, waiting for transfers between devices: 0.01 us -> 10.9 us  [split_local(): grad_out = lax.ppermute(grad_out, ('dp', 'ctx'), backward_owner).astype(f32)]
    reshape x6 -> x0, local copies, waits for them, and re-layouts: 10.8 us -> none  [the longest x4 7.05 us: narrow(): pieces = rows.reshape(parts, rows.shape[0] // parts, -1, NARROW)]
    ppermute x2, waiting for transfers between devices: 10.2 us -> 0.01 us  [the longest x1 0.01 us: split_local(): moved = lax.ppermute(moved, ('dp', 'ctx'), forward_owner)]
    concatenate x5 -> x2, other arithmetic: 9.93 us -> 2.08 us  [the longest x1 1.34 us: split_local(): sine = jnp.concatenate([-sine, sine], axis=1)]
  transfers between devices with their start and end apart: 59 -> 68, of which waited for: 18 -> 28; matrix products, arithmetic and copies ran while one was open for 26% -> 17% of each run, Pallas kernels for 24% -> 24%
where the time goes in v4:
time: 553 us; the launch traced here: 543 us
  waiting for transfers between devices  174 us (31%)
  Pallas kernels  146 us (26%)
  starting transfers between devices  98.4 us (18%)
  matrix products  47.3 us (9%)
  other arithmetic  40.9 us (7%)
  local copies, waits for them, and re-layouts  21.8 us (4%)
  between operations  15.1 us (3%)
    ppermute x50, waiting for transfers between devices, xor_permute(): return lax.ppermute(value, axis, [(i, i ^ offset) for i in range(size)])  82.9 us
    ppermute x12, waiting for transfers between devices, shift_z(): lax.ppermute(value, 'dp', [(i, (i + 2 * offset) % size) for i in range(si...  80.2 us
    ppermute x50, starting transfers between devices, xor_permute(): return lax.ppermute(value, axis, [(i, i ^ offset) for i in range(size)])  79.5 us
    pallas_call x2, Pallas kernels, unattend(): pl.pallas_call(functools.partial(unattend_kernel, group, block, first, bo...  49.7 us
    pallas_call x2, Pallas kernels, feed(): pl.pallas_call(functools.partial(feed_kernel, units, half), grid=(rows //...  32.9 us
    dot_general x5, matrix products, tn_dot(): lax.dot_general(left, right, (((0,), (0,)), ((), ())), preferred_element_...  23.8 us
    pallas_call x2, Pallas kernels, attend(): pl.pallas_call(functools.partial(attend_kernel, group, block, first), gri...  23.3 us
    dot_general x4, matrix products, nt_dot(): lax.dot_general(left, right, (((1,), (1,)), ((), ())), preferred_element_...  14.7 us
  transfers between devices with their start and end apart: 68, of which 28 were waited for; matrix products, arithmetic and copies ran while one was open for 17% of the time, Pallas kernels for 24%

profile of v4, /device:TPU:27, one launch (start us, length us, event | category | flops | bytes accessed | tf_op | source)
XLA Modules:
  0.0 543.4 jit_solution(899842879281781596)
XLA Ops:
  25.2 3.1 collective-permute-start.9
  35.1 12.2 %collective-permute-done.10.refs_2_ = bf16[144,1024]{1,0:T(8,128)(2,1)S(1)} collective-permute-done((bf16[144,1024]{1,0:T(8,128)(2,1)S(1)}, bf16[144,1024]{1,0:T(8,128)(2,1)S(1)}, u32[]{:S(2)}, u32[]{:S(2)}) %collective-permute-start.10) | collective-permute-done | bytes 294944 | tf_op jit(solution)/shard_map/ppermute | solution.py:391
  51.1 3.7 fusion.30
  54.8 4.2 collective-permute-done.7.x_refs_2_
  61.8 15.0 %collective-permute-start.13 = (bf16[144,1024]{1,0:T(8,128)(2,1)S(1)}, bf16[144,1024]{1,0:T(8,128)(2,1)S(1)}, u32[]{:S(2)}, u32[]{:S(2)}) collective-permute-start(bf16[144,1024]{1,0:T(8,128)(2,1)S(1)} %copy-done.29), channel_id=1, source_target_pairs={{0,4},{4,0},{8,12},{12,8},{16,20},{20,16},{24,28},{28,24},{1,5},{5... | collective-permute-start | bytes 884744 | tf_op jit(solution)/shard_map/ppermute | solution.py:372
  79.8 4.0 collective-permute-done.13.refs_5_
  83.8 3.0 collective-permute-start.6
  86.8 3.3 collective-permute-done.14.refs_6_
  90.1 3.0 collective-permute-start.23
  93.1 3.2 collective-permute-done.15.refs_7_
  100.8 3.1 assemble.4
  104.9 27.9 %collective-permute-done.18.refs_2_ = bf16[160,1024]{1,0:T(8,128)(2,1)} collective-permute-done((bf16[160,1024]{1,0:T(8,128)(2,1)}, bf16[160,1024]{1,0:T(8,128)(2,1)}, u32[]{:S(2)}, u32[]{:S(2)}) %collective-permute-start.18) | collective-permute-done | bytes 327712 | tf_op jit(solution)/shard_map/ppermute | solution.py:391
  134.0 11.3 %collective-permute-done.19.refs_3_ = bf16[160,1024]{1,0:T(8,128)(2,1)S(1)} collective-permute-done((bf16[160,1024]{1,0:T(8,128)(2,1)}, bf16[160,1024]{1,0:T(8,128)(2,1)S(1)}, u32[]{:S(2)}, u32[]{:S(2)}) %collective-permute-start.19) | collective-permute-done | bytes 327712 | tf_op jit(solution)/shard_map/ppermute | solution.py:391
  147.3 3.0 assemble.5
  151.8 13.5 %project.1 = (bf16[2048,1024]{1,0:T(8,128)(2,1)}, f32[2048,768]{1,0:T(8,128)}, bf16[2048,512]{1,0:T(8,128)(2,1)}, bf16[2048,256]{1,0:T(8,128)(2,1)}, bf16[2048,256]{1,0:T(8,128)(2,1)}) custom-call(bf16[512,1024]{1,0:T(8,128)(2,1)} %bitcast.167, bf16[512,1024]{1,0:T(8,128)(2,1)} %collective-permute-done.6.x_refs_1_, bf16[512,1024]{1,0:T(8,128)(2,1)} %copy-done.46, ...), custom_call_target="tpu_custom_call" | custom-call | flops 4294967296 | bytes 20971520 | tf_op jit(solution)/shard_map/project/pallas_call | solution.py:573
  165.9 2.9 assemble.6
  168.8 6.1 %collective-permute-done.29.refs_7_ = bf16[160,1024]{1,0:T(8,128)(2,1)S(1)} collective-permute-done((bf16[160,1024]{1,0:T(8,128)(2,1)S(1)}, bf16[160,1024]{1,0:T(8,128)(2,1)S(1)}, u32[]{:S(2)}, u32[]{:S(2)}) %collective-permute-start.29) | collective-permute-done | bytes 327712 | tf_op jit(solution)/shard_map/ppermute | solution.py:372
  175.7 3.3 assemble.7
  179.0 8.4 %attend.2 = (bf16[1024,512]{1,0:T(8,128)(2,1)}, f32[2,2,1024]{2,1,0:T(2,128)}) custom-call(s32[1]{0:T(128)} %bitcast.1.me_ref, bf16[2048,512]{1,0:T(8,128)(2,1)} %get-tuple-element.104.q_ref, bf16[2048,128]{1,0:T(8,128)(2,1)} %select_convert_fusion.qf_ref, bf16[2048,256]{1,0:T(8,128)(2,1)} %get-tuple-element.92.k_ref, bf16[2048,128]{1,0:T(8,128)(2,1)} %fusion.20.kf_ref, ...), custom_call_target="tpu_custom_call" | custom-call | flops 5368709120 | bytes 10485760 | tf_op jit(solution)/shard_map/attend/pallas_call | solution.py:740
  194.8 6.9 %collective-permute-start.33 = (bf16[512,1024]{1,0:T(8,128)(2,1)}, bf16[512,1024]{1,0:T(8,128)(2,1)S(1)}, u32[]{:S(2)}, u32[]{:S(2)}) collective-permute-start(bf16[512,1024]{1,0:T(8,128)(2,1)} %add_convert_fusion.6), channel_id=1, source_target_pairs={{0,2},{1,3},{2,0},{3,1},{4,6},{5,7},{6,4},{7,5},{8,10},{9,11},{10,... | collective-permute-start | bytes 3145736 | tf_op jit(solution)/shard_map/ppermute | solution.py:372
  201.7 14.8 %attend.3 = (bf16[1024,512]{1,0:T(8,128)(2,1)}, f32[2,2,1024]{2,1,0:T(2,128)}) custom-call(s32[1]{0:T(128)} %bitcast.1.me_ref, bf16[2048,512]{1,0:T(8,128)(2,1)} %get-tuple-element.104.q_ref, bf16[2048,128]{1,0:T(8,128)(2,1)} %select_convert_fusion.qf_ref, bf16[2048,256]{1,0:T(8,128)(2,1)} %get-tuple-element.92.k_ref, bf16[2048,128]{1,0:T(8,128)(2,1)} %fusion.20.kf_ref, ...), custom_call_target="tpu_custom_call" | custom-call | flops 5368709120 | bytes 10485760 | tf_op jit(solution)/shard_map/attend/pallas_call | solution.py:740
  220.2 4.8 collective-permute-done.33
  232.9 16.4 %feed.2 = (bf16[1024,1024]{1,0:T(8,128)(2,1)}, bf16[1024,768]{1,0:T(8,128)(2,1)}, bf16[1024,1536]{1,0:T(8,128)(2,1)}, bf16[512,1024]{1,0:T(8,128)(2,1)}, bf16[51...) custom-call(bf16[512,1024]{1,0:T(8,128)(2,1)} %copy-done.17, ...), custom_call_target="tpu_custom_call" | custom-call | flops 9663676416 | bytes 19922944 | tf_op jit(solution)/shard_map/feed/pallas_call | solution.py:978
  249.2 5.1 collective-permute-done.36.first_ref
  258.5 16.5 %feed.3 = (bf16[1024,1024]{1,0:T(8,128)(2,1)}, bf16[1024,768]{1,0:T(8,128)(2,1)}, bf16[1024,1536]{1,0:T(8,128)(2,1)}, bf16[512,1024]{1,0:T(8,128)(2,1)}, bf16[51...) custom-call(bf16[512,1024]{1,0:T(8,128)(2,1)} %copy-done.47, ...), custom_call_target="tpu_custom_call" | custom-call | flops 9663676416 | bytes 19922944 | tf_op jit(solution)/shard_map/feed/pallas_call | solution.py:978
  282.0 5.3 fusion.43
  287.4 5.2 add_convert_fusion
  292.6 12.7 %collective-permute-done.41 = bf16[512,1024]{1,0:T(8,128)(2,1)} collective-permute-done((bf16[512,1024]{1,0:T(8,128)(2,1)}, bf16[512,1024]{1,0:T(8,128)(2,1)}, u32[]{:S(2)}, u32[]{:S(2)}) %collective-permute-start.41) | collective-permute-done | bytes 1048608 | tf_op jit(solution)/shard_map/ppermute | solution.py:372
  305.4 2.9 multiply_reduce_fusion.1
  308.3 4.3 fusion.40
  317.1 3.1 add_convert_fusion.1
  320.6 30.3 %unattend.2 = (f32[1024,512]{1,0:T(8,128)}, f32[2048,256]{1,0:T(8,128)}, f32[2048,256]{1,0:T(8,128)}, f32[512,1024]{1,0:T(8,128)}) custom-call(s32[1]{0:T(128)} %bitcast.1.me_ref, bf16[2048,512]{1,0:T(8,128)(2,1)} %get-tuple-element.104.q_ref, bf16[2048,128]{1,0:T(8,128)(2,1)} %select_convert_fusion.qf_ref, bf16[2048,256]{1,0:T(8,128)(2,1)} %get-tuple-element.92.k_ref, ...), custom_call_target="tpu_custom_call" | custom-call | flops 9395240960 | bytes 20971520 | tf_op jit(solution)/shard_map/unattend/pallas_call | solution.py:873
  354.0 19.5 %unattend.3 = (f32[1024,512]{1,0:T(8,128)}, f32[2048,256]{1,0:T(8,128)}, f32[2048,256]{1,0:T(8,128)}, f32[512,1024]{1,0:T(8,128)}) custom-call(s32[1]{0:T(128)} %bitcast.1.me_ref, bf16[2048,512]{1,0:T(8,128)(2,1)} %get-tuple-element.104.q_ref, bf16[2048,128]{1,0:T(8,128)(2,1)} %select_convert_fusion.qf_ref, bf16[2048,256]{1,0:T(8,128)(2,1)} %get-tuple-element.92.k_ref, ...), custom_call_target="tpu_custom_call" | custom-call | flops 9395240960 | bytes 20971520 | tf_op jit(solution)/shard_map/unattend/pallas_call | solution.py:873
  373.4 4.3 collective-permute-done.44
  377.7 14.0 %unproject.1 = (bf16[2048,1024]{1,0:T(8,128)(2,1)}, f32[8,128]{1,0:T(8,128)}) custom-call(f32[1024,512]{1,0:T(8,128)} %get-tuple-element.126.dq_near_ref, f32[1024,512]{1,0:T(8,128)} %get-tuple-element.133.dq_far_ref, f32[2048,256]{1,0:T(8,128)} %get-tuple-element.135.dk_ref, f32[2048,256]{1,0:T(8,128)} %get-tuple-element.136.dv_ref, ...), custom_call_target="tpu_custom_call" | custom-call | flops 41943040 | bytes 20971520 | tf_op jit(solution)/shard_map/unproject/pallas_call | solution.py:673
  392.4 3.7 convolution_convert_fusion.1
  397.2 8.3 %multiply_reduce_fusion = (f32[1024]{0:T(1024)S(1)}, bf16[1024,1024]{1,0:T(8,128)(2,1)}) fusion(bf16[1024,1024]{1,0:T(8,128)(2,1)S(1)} %bitcast.223, bf16[2048,1024]{1,0:T(8,128)(2,1)} %get-tuple-element.139, bf16[2048,1024]{1,0:T(8,128)(2,1)S(1)} %copy-done.41), kind=kOutput, calls=%fused_computation.1 | convolution fusion | flops 4300209152 | bytes 12587008 | tf_op jit(solution)/shard_map/dot_general | solution.py:1129
  412.0 3.9 convolution_convert_fusion.2
  416.1 3.5 add_convert_fusion.2
  419.6 8.6 %collective-permute-start.48 = (bf16[512,1024]{1,0:T(8,128)(2,1)}, bf16[512,1024]{1,0:T(8,128)(2,1)}, u32[]{:S(2)}, u32[]{:S(2)}) collective-permute-start(bf16[512,1024]{1,0:T(8,128)(2,1)} %add_convert_fusion.2), channel_id=1, source_target_pairs={{0,2},{1,3},{2,0},{3,1},{4,6},{5,7},{6,4},{7,5},{8,10},{9,11},{10,... | collective-permute-start | bytes 3145736 | tf_op jit(solution)/shard_map/ppermute | solution.py:372
  428.4 3.7 fusion.14
  432.0 18.6 %collective-permute-done.56 = bf16[4,64,1024]{2,1,0:T(8,128)(2,1)} collective-permute-done((bf16[4,64,1024]{2,1,0:T(8,128)(2,1)}, bf16[4,64,1024]{2,1,0:T(8,128)(2,1)}, u32[]{:S(2)}, u32[]{:S(2)}) %collective-permute-start.56) | collective-permute-done | bytes 524320 | tf_op jit(solution)/shard_map/ppermute | solution.py:372
  452.0 3.9 collective-permute-start.57
  457.8 3.6 fusion.3
  465.6 10.0 %collective-permute-start.62 = (bf16[32,1536]{1,0:T(8,128)(2,1)S(1)}, bf16[32,1536]{1,0:T(8,128)(2,1)S(1)}, u32[]{:S(2)}, u32[]{:S(2)}) collective-permute-start(bf16[32,1536]{1,0:T(8,128)(2,1)S(1)} %get-tuple-element.173), channel_id=1, source_target_pairs={{0,2},{1,3},{2,0},{3,1},{4,6},{5,7},{6,4},{7,5},{8,10},{9,11},{10,... | collective-permute-start | bytes 294920 | tf_op jit(solution)/shard_map/ppermute | solution.py:372
  475.8 2.9 collective-permute-done.62
  485.6 27.8 %collective-permute-done.51 = bf16[144,1024]{1,0:T(8,128)(2,1)S(1)} collective-permute-done((bf16[144,1024]{1,0:T(8,128)(2,1)S(1)}, bf16[144,1024]{1,0:T(8,128)(2,1)S(1)}, u32[]{:S(2)}, u32[]{:S(2)}) %collective-permute-start.51) | collective-permute-done | bytes 294944 | tf_op jit(solution)/shard_map/ppermute | solution.py:391
  524.3 10.9 %collective-permute-done.60 = bf16[64,1024]{1,0:T(8,128)(2,1)S(1)} collective-permute-done((bf16[64,1024]{1,0:T(8,128)(2,1)S(1)}, bf16[64,1024]{1,0:T(8,128)(2,1)S(1)}, u32[]{:S(2)}, u32[]{:S(2)}) %collective-permute-start.60) | collective-permute-done | bytes 131104 | tf_op jit(solution)/shard_map/ppermute | solution.py:1216
  (328 shorter events, 118.4 us)
Async XLA Ops:
  7.2 194.5 %all-gather.2.cloned.1.call-start = ((), (), s32[]{:S(2)}) async-start(), calls=%async_computation.2 | async-start | bytes 3538944 | tf_op jit(solution)/shard_map/all_gather | solution.py:1068
  24.9 22.5 %collective-permute-start.10 = (bf16[144,1024]{1,0:T(8,128)(2,1)S(1)}, bf16[144,1024]{1,0:T(8,128)(2,1)S(1)}, u32[]{:S(2)}, u32[]{:S(2)}) collective-permute-start(bf16[144,1024]{1,0:T(8,128)(2,1)S(1)} %maximum_maximum_fusion.refs_0_), channel_id=1, source_target_pairs={{0,16},{4,20},{8,24},{12,28},{16,0},{20,4},{24,8},{28,12},{1,17},{... | collective-permute-start | bytes 884744 | tf_op jit(solution)/shard_map/ppermute | solution.py:391
  25.0 24.5 %collective-permute-start.11 = (bf16[144,1024]{1,0:T(8,128)(2,1)S(1)}, bf16[144,1024]{1,0:T(8,128)(2,1)S(1)}, u32[]{:S(2)}, u32[]{:S(2)}) collective-permute-start(bf16[144,1024]{1,0:T(8,128)(2,1)S(1)} %maximum_maximum_fusion.refs_0_), channel_id=1, source_target_pairs={{0,24},{4,28},{8,0},{12,4},{16,8},{20,12},{24,16},{28,20},{1,25},{... | collective-permute-start | bytes 884744 | tf_op jit(solution)/shard_map/ppermute | solution.py:391
  25.2 24.4 %collective-permute-start.9 = (bf16[144,1024]{1,0:T(8,128)(2,1)S(1)}, bf16[144,1024]{1,0:T(8,128)(2,1)S(1)}, u32[]{:S(2)}, u32[]{:S(2)}) collective-permute-start(bf16[144,1024]{1,0:T(8,128)(2,1)S(1)} %maximum_maximum_fusion.refs_0_), channel_id=1, source_target_pairs={{0,8},{4,12},{8,16},{12,20},{16,24},{20,28},{24,0},{28,4},{1,9},{5... | collective-permute-start | bytes 884744 | tf_op jit(solution)/shard_map/ppermute | solution.py:391
  30.8 47.4 %collective-permute-start.12 = (bf16[144,1024]{1,0:T(8,128)(2,1)S(1)}, bf16[144,1024]{1,0:T(8,128)(2,1)}, u32[]{:S(2)}, u32[]{:S(2)}) collective-permute-start(bf16[144,1024]{1,0:T(8,128)(2,1)S(1)} %maximum_maximum_fusion.refs_0_), channel_id=1, source_target_pairs={{0,4},{4,0},{8,12},{12,8},{16,20},{20,16},{24,28},{28,24},{1,5},{5... | collective-permute-start | bytes 884744 | tf_op jit(solution)/shard_map/ppermute | solution.py:372
  34.5 24.5 %collective-permute-start.7 = (bf16[512,1024]{1,0:T(8,128)(2,1)S(1)}, bf16[512,1024]{1,0:T(8,128)(2,1)S(1)}, u32[]{:S(2)}, u32[]{:S(2)}) collective-permute-start(bf16[512,1024]{1,0:T(8,128)(2,1)S(1)} %bitcast.168), channel_id=1, source_target_pairs={{0,2},{1,3},{2,0},{3,1},{4,6},{5,7},{6,4},{7,5},{8,10},{9,11},{10,... | collective-permute-start | bytes 3145736 | tf_op jit(solution)/shard_map/ppermute | solution.py:372
  47.4 29.4 %collective-permute-start.16 = (bf16[160,1024]{1,0:T(8,128)(2,1)}, bf16[160,1024]{1,0:T(8,128)(2,1)}, u32[]{:S(2)}, u32[]{:S(2)}) collective-permute-start(bf16[160,1024]{1,0:T(8,128)(2,1)} %pad_maximum_fusion.10), channel_id=1, source_target_pairs={{0,0},{1,4},{2,8},{3,12},{4,16},{5,20},{6,24},{7,28},{8,1},{9,5},{... | collective-permute-start | bytes 983048 | tf_op jit(solution)/shard_map/ppermute | solution.py:1058
  51.0 412.3 %reduce-scatter.3.cloned.1.call-start = ((), (), s32[]{:S(2)}) async-start(), calls=%async_computation.3 | async-start | bytes 3538944 | tf_op jit(solution)/shard_map/reduce_scatter | solution.py:1138
  60.0 43.9 %collective-permute-start.24 = (bf16[512,1024]{1,0:T(8,128)(2,1)S(1)}, bf16[512,1024]{1,0:T(8,128)(2,1)S(1)}, u32[]{:S(2)}, u32[]{:S(2)}) collective-permute-start(bf16[512,1024]{1,0:T(8,128)(2,1)S(1)} %bitcast.180), channel_id=1, source_target_pairs={{0,2},{1,3},{2,0},{3,1},{4,6},{5,7},{6,4},{7,5},{8,10},{9,11},{10,... | collective-permute-start | bytes 3145736 | tf_op jit(solution)/shard_map/ppermute | solution.py:372
  61.8 22.1 %collective-permute-start.13 = (bf16[144,1024]{1,0:T(8,128)(2,1)S(1)}, bf16[144,1024]{1,0:T(8,128)(2,1)S(1)}, u32[]{:S(2)}, u32[]{:S(2)}) collective-permute-start(bf16[144,1024]{1,0:T(8,128)(2,1)S(1)} %copy-done.29), channel_id=1, source_target_pairs={{0,4},{4,0},{8,12},{12,8},{16,20},{20,16},{24,28},{28,24},{1,5},{5... | collective-permute-start | bytes 884744 | tf_op jit(solution)/shard_map/ppermute | solution.py:372
  76.7 13.4 %collective-permute-start.14 = (bf16[144,1024]{1,0:T(8,128)(2,1)S(1)}, bf16[144,1024]{1,0:T(8,128)(2,1)S(1)}, u32[]{:S(2)}, u32[]{:S(2)}) collective-permute-start(bf16[144,1024]{1,0:T(8,128)(2,1)S(1)} %copy-done.25), channel_id=1, source_target_pairs={{0,4},{4,0},{8,12},{12,8},{16,20},{20,16},{24,28},{28,24},{1,5},{5... | collective-permute-start | bytes 884744 | tf_op jit(solution)/shard_map/ppermute | solution.py:372
  76.8 19.6 %collective-permute-start.15 = (bf16[144,1024]{1,0:T(8,128)(2,1)S(1)}, bf16[144,1024]{1,0:T(8,128)(2,1)S(1)}, u32[]{:S(2)}, u32[]{:S(2)}) collective-permute-start(bf16[144,1024]{1,0:T(8,128)(2,1)S(1)} %copy-done.27), channel_id=1, source_target_pairs={{0,4},{4,0},{8,12},{12,8},{16,20},{20,16},{24,28},{28,24},{1,5},{5... | collective-permute-start | bytes 884744 | tf_op jit(solution)/shard_map/ppermute | solution.py:372
  78.2 21.2 %collective-permute-start.17 = (bf16[160,1024]{1,0:T(8,128)(2,1)}, bf16[160,1024]{1,0:T(8,128)(2,1)}, u32[]{:S(2)}, u32[]{:S(2)}) collective-permute-start(bf16[160,1024]{1,0:T(8,128)(2,1)} %collective-permute-done.16.refs_0_), channel_id=1, source_target_pairs={{0,8},{4,12},{8,16},{12,20},{16,24},{20,28},{24,0},{28,4},{1,9},{5... | collective-permute-start | bytes 983048 | tf_op jit(solution)/shard_map/ppermute | solution.py:391
  83.8 66.4 %collective-permute-start.6 = (bf16[512,1024]{1,0:T(8,128)(2,1)S(1)}, bf16[512,1024]{1,0:T(8,128)(2,1)}, u32[]{:S(2)}, u32[]{:S(2)}) collective-permute-start(bf16[512,1024]{1,0:T(8,128)(2,1)S(1)} %bitcast.169), channel_id=1, source_target_pairs={{0,1},{1,0},{2,3},{3,2},{4,5},{5,4},{6,7},{7,6},{8,9},{9,8},{10,11... | collective-permute-start | bytes 3145736 | tf_op jit(solution)/shard_map/ppermute | solution.py:372
  90.1 56.1 %collective-permute-start.23 = (bf16[512,1024]{1,0:T(8,128)(2,1)S(1)}, bf16[512,1024]{1,0:T(8,128)(2,1)}, u32[]{:S(2)}, u32[]{:S(2)}) collective-permute-start(bf16[512,1024]{1,0:T(8,128)(2,1)S(1)} %bitcast.181), channel_id=1, source_target_pairs={{0,1},{1,0},{2,3},{3,2},{4,5},{5,4},{6,7},{7,6},{8,9},{9,8},{10,11... | collective-permute-start | bytes 3145736 | tf_op jit(solution)/shard_map/ppermute | solution.py:372
  96.4 54.9 %collective-permute-start.8 = (bf16[512,1024]{1,0:T(8,128)(2,1)}, bf16[512,1024]{1,0:T(8,128)(2,1)}, u32[]{:S(2)}, u32[]{:S(2)}) collective-permute-start(bf16[512,1024]{1,0:T(8,128)(2,1)} %copy-done.46), channel_id=1, source_target_pairs={{0,1},{1,0},{2,3},{3,2},{4,5},{5,4},{6,7},{7,6},{8,9},{9,8},{10,11... | collective-permute-start | bytes 3145736 | tf_op jit(solution)/shard_map/ppermute | solution.py:372
  99.4 33.4 %collective-permute-start.18 = (bf16[160,1024]{1,0:T(8,128)(2,1)}, bf16[160,1024]{1,0:T(8,128)(2,1)}, u32[]{:S(2)}, u32[]{:S(2)}) collective-permute-start(bf16[160,1024]{1,0:T(8,128)(2,1)} %collective-permute-done.16.refs_0_), channel_id=1, source_target_pairs={{0,16},{4,20},{8,24},{12,28},{16,0},{20,4},{24,8},{28,12},{1,17},{... | collective-permute-start | bytes 983048 | tf_op jit(solution)/shard_map/ppermute | solution.py:391
  103.9 61.4 %collective-permute-start.25 = (bf16[512,1024]{1,0:T(8,128)(2,1)S(1)}, bf16[512,1024]{1,0:T(8,128)(2,1)}, u32[]{:S(2)}, u32[]{:S(2)}) collective-permute-start(bf16[512,1024]{1,0:T(8,128)(2,1)S(1)} %collective-permute-done.24.refs_0_), channel_id=1, source_target_pairs={{0,1},{1,0},{2,3},{3,2},{4,5},{5,4},{6,7},{7,6},{8,9},{9,8},{10,11... | collective-permute-start | bytes 3145736 | tf_op jit(solution)/shard_map/ppermute | solution.py:372
  132.8 12.5 %collective-permute-start.19 = (bf16[160,1024]{1,0:T(8,128)(2,1)}, bf16[160,1024]{1,0:T(8,128)(2,1)S(1)}, u32[]{:S(2)}, u32[]{:S(2)}) collective-permute-start(bf16[160,1024]{1,0:T(8,128)(2,1)} %collective-permute-done.16.refs_0_), channel_id=1, source_target_pairs={{0,24},{4,28},{8,0},{12,4},{16,8},{20,12},{24,16},{28,20},{1,25},{... | collective-permute-start | bytes 983048 | tf_op jit(solution)/shard_map/ppermute | solution.py:391
  145.3 23.4 %collective-permute-start.26 = (bf16[160,1024]{1,0:T(8,128)(2,1)}, bf16[160,1024]{1,0:T(8,128)(2,1)S(1)}, u32[]{:S(2)}, u32[]{:S(2)}) collective-permute-start(bf16[160,1024]{1,0:T(8,128)(2,1)} %collective-permute-done.16.refs_0_), channel_id=1, source_target_pairs={{0,4},{4,0},{8,12},{12,8},{16,20},{20,16},{24,28},{28,24},{1,5},{5... | collective-permute-start | bytes 983048 | tf_op jit(solution)/shard_map/ppermute | solution.py:372
  146.3 22.5 %collective-permute-start.27 = (bf16[160,1024]{1,0:T(8,128)(2,1)}, bf16[160,1024]{1,0:T(8,128)(2,1)S(1)}, u32[]{:S(2)}, u32[]{:S(2)}) collective-permute-start(bf16[160,1024]{1,0:T(8,128)(2,1)} %collective-permute-done.17.refs_1_), channel_id=1, source_target_pairs={{0,4},{4,0},{8,12},{12,8},{16,20},{20,16},{24,28},{28,24},{1,5},{5... | collective-permute-start | bytes 983048 | tf_op jit(solution)/shard_map/ppermute | solution.py:372
  150.3 18.5 %collective-permute-start.28 = (bf16[160,1024]{1,0:T(8,128)(2,1)}, bf16[160,1024]{1,0:T(8,128)(2,1)S(1)}, u32[]{:S(2)}, u32[]{:S(2)}) collective-permute-start(bf16[160,1024]{1,0:T(8,128)(2,1)} %collective-permute-done.18.refs_2_), channel_id=1, source_target_pairs={{0,4},{4,0},{8,12},{12,8},{16,20},{20,16},{24,28},{28,24},{1,5},{5... | collective-permute-start | bytes 983048 | tf_op jit(solution)/shard_map/ppermute | solution.py:372
  151.3 23.6 %collective-permute-start.29 = (bf16[160,1024]{1,0:T(8,128)(2,1)S(1)}, bf16[160,1024]{1,0:T(8,128)(2,1)S(1)}, u32[]{:S(2)}, u32[]{:S(2)}) collective-permute-start(bf16[160,1024]{1,0:T(8,128)(2,1)S(1)} %collective-permute-done.19.refs_3_), channel_id=1, source_target_pairs={{0,4},{4,0},{8,12},{12,8},{16,20},{20,16},{24,28},{28,24},{1,5},{5... | collective-permute-start | bytes 983048 | tf_op jit(solution)/shard_map/ppermute | solution.py:372
  194.8 30.3 %collective-permute-start.33 = (bf16[512,1024]{1,0:T(8,128)(2,1)}, bf16[512,1024]{1,0:T(8,128)(2,1)S(1)}, u32[]{:S(2)}, u32[]{:S(2)}) collective-permute-start(bf16[512,1024]{1,0:T(8,128)(2,1)} %add_convert_fusion.6), channel_id=1, source_target_pairs={{0,2},{1,3},{2,0},{3,1},{4,6},{5,7},{6,4},{7,5},{8,10},{9,11},{10,... | collective-permute-start | bytes 3145736 | tf_op jit(solution)/shard_map/ppermute | solution.py:372
  229.6 24.7 %collective-permute-start.36 = (bf16[512,1024]{1,0:T(8,128)(2,1)S(1)}, bf16[512,1024]{1,0:T(8,128)(2,1)S(1)}, u32[]{:S(2)}, u32[]{:S(2)}) collective-permute-start(bf16[512,1024]{1,0:T(8,128)(2,1)S(1)} %multiply_convert_fusion.first_ref), channel_id=1, source_target_pairs={{0,2},{1,3},{2,0},{3,1},{4,6},{5,7},{6,4},{7,5},{8,10},{9,11},{10,... | collective-permute-start | bytes 3145736 | tf_op jit(solution)/shard_map/ppermute | solution.py:372
  275.4 17.2 %collective-permute-start.39 = (bf16[512,1024]{1,0:T(8,128)(2,1)}, bf16[512,1024]{1,0:T(8,128)(2,1)}, u32[]{:S(2)}, u32[]{:S(2)}) collective-permute-start(bf16[512,1024]{1,0:T(8,128)(2,1)} %get-tuple-element.116), channel_id=1, source_target_pairs={{0,1},{1,0},{2,3},{3,2},{4,5},{5,4},{6,7},{7,6},{8,9},{9,8},{10,11... | collective-permute-start | bytes 3145736 | tf_op jit(solution)/shard_map/ppermute | solution.py:372
  280.7 24.7 %collective-permute-start.41 = (bf16[512,1024]{1,0:T(8,128)(2,1)}, bf16[512,1024]{1,0:T(8,128)(2,1)}, u32[]{:S(2)}, u32[]{:S(2)}) collective-permute-start(bf16[512,1024]{1,0:T(8,128)(2,1)} %add_convert_fusion.4), channel_id=1, source_target_pairs={{0,2},{1,3},{2,0},{3,1},{4,6},{5,7},{6,4},{7,5},{8,10},{9,11},{10,... | collective-permute-start | bytes 3145736 | tf_op jit(solution)/shard_map/ppermute | solution.py:372
  292.6 223.7 %reduce-scatter.5.cloned.1.call-start = ((), (), s32[]{:S(2)}) async-start(), calls=%async_computation.4 | async-start | bytes 1769472 | tf_op jit(solution)/shard_map/reduce_scatter | solution.py:1139
  312.6 8.0 %collective-permute-start.43 = (bf16[512,1024]{1,0:T(8,128)(2,1)}, bf16[512,1024]{1,0:T(8,128)(2,1)}, u32[]{:S(2)}, u32[]{:S(2)}) collective-permute-start(bf16[512,1024]{1,0:T(8,128)(2,1)} %get-tuple-element.124.branch_first_ref), channel_id=1, source_target_pairs={{0,1},{1,0},{2,3},{3,2},{4,5},{5,4},{6,7},{7,6},{8,9},{9,8},{10,11... | collective-permute-start | bytes 3145736 | tf_op jit(solution)/shard_map/ppermute | solution.py:372
  315.7 35.2 %collective-permute-start.42 = (bf16[512,1024]{1,0:T(8,128)(2,1)}, bf16[512,1024]{1,0:T(8,128)(2,1)}, u32[]{:S(2)}, u32[]{:S(2)}) collective-permute-start(bf16[512,1024]{1,0:T(8,128)(2,1)} %get-tuple-element.124.branch_first_ref), channel_id=1, source_target_pairs={{0,2},{1,3},{2,0},{3,1},{4,6},{5,7},{6,4},{7,5},{8,10},{9,11},{10,... | collective-permute-start | bytes 3145736 | tf_op jit(solution)/shard_map/ppermute | solution.py:372
  320.3 30.9 %collective-permute-start.38 = (bf16[512,1024]{1,0:T(8,128)(2,1)}, bf16[512,1024]{1,0:T(8,128)(2,1)}, u32[]{:S(2)}, u32[]{:S(2)}) collective-permute-start(bf16[512,1024]{1,0:T(8,128)(2,1)} %get-tuple-element.114), channel_id=1, source_target_pairs={{0,1},{1,0},{2,3},{3,2},{4,5},{5,4},{6,7},{7,6},{8,9},{9,8},{10,11... | collective-permute-start | bytes 3145736 | tf_op jit(solution)/shard_map/ppermute | solution.py:372
  353.2 24.5 %collective-permute-start.44 = (bf16[512,1024]{1,0:T(8,128)(2,1)S(1)}, bf16[512,1024]{1,0:T(8,128)(2,1)S(1)}, u32[]{:S(2)}, u32[]{:S(2)}) collective-permute-start(bf16[512,1024]{1,0:T(8,128)(2,1)S(1)} %add_convert_fusion.5), channel_id=1, source_target_pairs={{0,2},{1,3},{2,0},{3,1},{4,6},{5,7},{6,4},{7,5},{8,10},{9,11},{10,... | collective-permute-start | bytes 3145736 | tf_op jit(solution)/shard_map/ppermute | solution.py:372
  353.5 74.8 %collective-permute-start.35 = (bf16[512,1024]{1,0:T(8,128)(2,1)}, bf16[512,1024]{1,0:T(8,128)(2,1)}, u32[]{:S(2)}, u32[]{:S(2)}) collective-permute-start(bf16[512,1024]{1,0:T(8,128)(2,1)} %get-tuple-element.109), channel_id=1, source_target_pairs={{0,1},{1,0},{2,3},{3,2},{4,5},{5,4},{6,7},{7,6},{8,9},{9,8},{10,11... | collective-permute-start | bytes 3145736 | tf_op jit(solution)/shard_map/ppermute | solution.py:372
  396.1 20.1 %collective-permute-start.47 = (bf16[512,1024]{1,0:T(8,128)(2,1)}, bf16[512,1024]{1,0:T(8,128)(2,1)}, u32[]{:S(2)}, u32[]{:S(2)}) collective-permute-start(bf16[512,1024]{1,0:T(8,128)(2,1)} %convolution_convert_fusion.1), channel_id=1, source_target_pairs={{0,1},{1,0},{2,3},{3,2},{4,5},{5,4},{6,7},{7,6},{8,9},{9,8},{10,11... | collective-permute-start | bytes 3145736 | tf_op jit(solution)/shard_map/ppermute | solution.py:372
  408.2 47.6 %collective-permute-start.49 = (bf16[4,144,1024]{2,1,0:T(8,128)(2,1)}, bf16[4,144,1024]{2,1,0:T(8,128)(2,1)}, u32[]{:S(2)}, u32[]{:S(2)}) collective-permute-start(bf16[4,144,1024]{2,1,0:T(8,128)(2,1)} %fusion.11), channel_id=1, source_target_pairs={{0,4},{4,0},{8,12},{12,8},{16,20},{20,16},{24,28},{28,24},{1,5},{5... | collective-permute-start | bytes 3538952 | tf_op jit(solution)/shard_map/ppermute | solution.py:372
  411.2 39.5 %collective-permute-start.56 = (bf16[4,64,1024]{2,1,0:T(8,128)(2,1)}, bf16[4,64,1024]{2,1,0:T(8,128)(2,1)}, u32[]{:S(2)}, u32[]{:S(2)}) collective-permute-start(bf16[4,64,1024]{2,1,0:T(8,128)(2,1)} %dynamic-slice_bitcast_fusion), channel_id=1, source_target_pairs={{0,4},{4,0},{8,12},{12,8},{16,20},{20,16},{24,28},{28,24},{1,5},{5... | collective-permute-start | bytes 1572872 | tf_op jit(solution)/shard_map/ppermute | solution.py:372
  415.8 41.9 %collective-permute-start.46 = (bf16[512,1024]{1,0:T(8,128)(2,1)}, bf16[512,1024]{1,0:T(8,128)(2,1)}, u32[]{:S(2)}, u32[]{:S(2)}) collective-permute-start(bf16[512,1024]{1,0:T(8,128)(2,1)} %convolution_convert_fusion.2), channel_id=1, source_target_pairs={{0,1},{1,0},{2,3},{3,2},{4,5},{5,4},{6,7},{7,6},{8,9},{9,8},{10,11... | collective-permute-start | bytes 3145736 | tf_op jit(solution)/shard_map/ppermute | solution.py:372
  419.6 38.1 %collective-permute-start.48 = (bf16[512,1024]{1,0:T(8,128)(2,1)}, bf16[512,1024]{1,0:T(8,128)(2,1)}, u32[]{:S(2)}, u32[]{:S(2)}) collective-permute-start(bf16[512,1024]{1,0:T(8,128)(2,1)} %add_convert_fusion.2), channel_id=1, source_target_pairs={{0,2},{1,3},{2,0},{3,1},{4,6},{5,7},{6,4},{7,5},{8,10},{9,11},{10,... | collective-permute-start | bytes 3145736 | tf_op jit(solution)/shard_map/ppermute | solution.py:372
  452.0 64.3 %collective-permute-start.57 = (bf16[64,1024]{1,0:T(8,128)(2,1)S(1)}, bf16[64,1024]{1,0:T(8,128)(2,1)S(1)}, u32[]{:S(2)}, u32[]{:S(2)}) collective-permute-start(bf16[64,1024]{1,0:T(8,128)(2,1)S(1)} %get-tuple-element.165), channel_id=1, source_target_pairs={{0,8},{4,12},{8,16},{12,20},{16,24},{20,28},{24,0},{28,4},{1,9},{5... | collective-permute-start | bytes 393224 | tf_op jit(solution)/shard_map/ppermute | solution.py:391
  455.8 60.6 %collective-permute-start.58 = (bf16[64,1024]{1,0:T(8,128)(2,1)S(1)}, bf16[64,1024]{1,0:T(8,128)(2,1)S(1)}, u32[]{:S(2)}, u32[]{:S(2)}) collective-permute-start(bf16[64,1024]{1,0:T(8,128)(2,1)S(1)} %get-tuple-element.164), channel_id=1, source_target_pairs={{0,16},{4,20},{8,24},{12,28},{16,0},{20,4},{24,8},{28,12},{1,17},{... | collective-permute-start | bytes 393224 | tf_op jit(solution)/shard_map/ppermute | solution.py:391
  464.4 11.3 %collective-permute-start.61 = (bf16[32,1536]{1,0:T(8,128)(2,1)S(1)}, bf16[32,1536]{1,0:T(8,128)(2,1)S(1)}, u32[]{:S(2)}, u32[]{:S(2)}) collective-permute-start(bf16[32,1536]{1,0:T(8,128)(2,1)S(1)} %get-tuple-element.174), channel_id=1, source_target_pairs={{0,1},{1,0},{2,3},{3,2},{4,5},{5,4},{6,7},{7,6},{8,9},{9,8},{10,11... | collective-permute-start | bytes 294920 | tf_op jit(solution)/shard_map/ppermute | solution.py:372
  465.6 13.1 %collective-permute-start.62 = (bf16[32,1536]{1,0:T(8,128)(2,1)S(1)}, bf16[32,1536]{1,0:T(8,128)(2,1)S(1)}, u32[]{:S(2)}, u32[]{:S(2)}) collective-permute-start(bf16[32,1536]{1,0:T(8,128)(2,1)S(1)} %get-tuple-element.173), channel_id=1, source_target_pairs={{0,2},{1,3},{2,0},{3,1},{4,6},{5,7},{6,4},{7,5},{8,10},{9,11},{10,... | collective-permute-start | bytes 294920 | tf_op jit(solution)/shard_map/ppermute | solution.py:372
  475.7 8.3 %collective-permute-start.50 = (bf16[144,1024]{1,0:T(8,128)(2,1)S(1)}, bf16[144,1024]{1,0:T(8,128)(2,1)S(1)}, u32[]{:S(2)}, u32[]{:S(2)}) collective-permute-start(bf16[144,1024]{1,0:T(8,128)(2,1)S(1)} %get-tuple-element.158), channel_id=1, source_target_pairs={{0,8},{4,12},{8,16},{12,20},{16,24},{20,28},{24,0},{28,4},{1,9},{5... | collective-permute-start | bytes 884744 | tf_op jit(solution)/shard_map/ppermute | solution.py:391
  478.6 34.7 %collective-permute-start.51 = (bf16[144,1024]{1,0:T(8,128)(2,1)S(1)}, bf16[144,1024]{1,0:T(8,128)(2,1)S(1)}, u32[]{:S(2)}, u32[]{:S(2)}) collective-permute-start(bf16[144,1024]{1,0:T(8,128)(2,1)S(1)} %get-tuple-element.160), channel_id=1, source_target_pairs={{0,16},{4,20},{8,24},{12,28},{16,0},{20,4},{24,8},{28,12},{1,17},{... | collective-permute-start | bytes 884744 | tf_op jit(solution)/shard_map/ppermute | solution.py:391
  481.1 32.3 %collective-permute-start.52 = (bf16[144,1024]{1,0:T(8,128)(2,1)S(1)}, bf16[144,1024]{1,0:T(8,128)(2,1)S(1)}, u32[]{:S(2)}, u32[]{:S(2)}) collective-permute-start(bf16[144,1024]{1,0:T(8,128)(2,1)S(1)} %get-tuple-element.159), channel_id=1, source_target_pairs={{0,24},{4,28},{8,0},{12,4},{16,8},{20,12},{24,16},{28,20},{1,25},{... | collective-permute-start | bytes 884744 | tf_op jit(solution)/shard_map/ppermute | solution.py:391
  484.0 35.3 %collective-permute-start.59 = (bf16[64,1024]{1,0:T(8,128)(2,1)S(1)}, bf16[64,1024]{1,0:T(8,128)(2,1)S(1)}, u32[]{:S(2)}, u32[]{:S(2)}) collective-permute-start(bf16[64,1024]{1,0:T(8,128)(2,1)S(1)} %get-tuple-element.163), channel_id=1, source_target_pairs={{0,24},{4,28},{8,0},{12,4},{16,8},{20,12},{24,16},{28,20},{1,25},{... | collective-permute-start | bytes 393224 | tf_op jit(solution)/shard_map/ppermute | solution.py:391
  516.4 19.5 %collective-permute-start.64 = (bf16[96,1024]{1,0:T(8,128)(2,1)}, bf16[96,1024]{1,0:T(8,128)(2,1)S(1)}, u32[]{:S(2)}, u32[]{:S(2)}) collective-permute-start(bf16[96,1024]{1,0:T(8,128)(2,1)} %reduce-scatter.5.cloned.1.call-done), channel_id=1, source_target_pairs={{0,0},{4,1},{8,2},{12,3},{16,4},{20,5},{24,6},{28,7},{1,8},{5,9},{... | collective-permute-start | bytes 589832 | tf_op jit(solution)/shard_map/ppermute | solution.py:1217
  519.4 15.8 %collective-permute-start.60 = (bf16[64,1024]{1,0:T(8,128)(2,1)S(1)}, bf16[64,1024]{1,0:T(8,128)(2,1)S(1)}, u32[]{:S(2)}, u32[]{:S(2)}) collective-permute-start(bf16[64,1024]{1,0:T(8,128)(2,1)S(1)} %add_convert_fusion.8), channel_id=1, source_target_pairs={{0,0},{4,1},{8,2},{12,3},{16,4},{20,5},{24,6},{28,7},{1,8},{5,9},{... | collective-permute-start | bytes 393224 | tf_op jit(solution)/shard_map/ppermute | solution.py:1216
  (76 other events, 554.2 us)
Sparse Core Ops, SparseCore 0:
  51.1 90.1 all-gather.1
  292.7 72.5 reduce-scatter.2
  428.5 86.4 reduce-scatter.4

commit v5 on v4

--- a/solution.py
+++ b/solution.py
@@ -363,6 +363,7 @@
 MASK_DEPTH = -4096.0
 LOG2_E = 1.4426950408889634
 VMEM_BYTES = 56 * 1024 * 1024
+SMALL_COST = pl.CostEstimate(flops=1, bytes_accessed=1, transcendentals=0)
 bf16 = jnp.bfloat16
 f32 = jnp.float32
 
@@ -394,52 +395,67 @@
 def assemble_kernel(splits, count, places_ref, *refs):
     pieces, results, sems = refs[:count], refs[count:-1], refs[-1]
     copies = []
-    for n, piece in enumerate(pieces):
-        start = 0
-        for m, rows in enumerate(splits):
-            copy = pltpu.make_async_copy(
-                piece.at[pl.ds(start, rows)], results[m].at[places_ref[n]], sems.at[n, m]
-            )
-            copy.start()
-            copies.append(copy)
-            start += rows
+    for piece in pieces:
+        for slot in range(piece.shape[0]):
+            n = len(copies) // len(splits)
+            start = 0
+            for m, rows in enumerate(splits):
+                copy = pltpu.make_async_copy(
+                    piece.at[slot, pl.ds(start, rows)],
+                    results[m].at[places_ref[n]],
+                    sems.at[n, m],
+                )
+                copy.start()
+                copies.append(copy)
+                start += rows
     for copy in copies:
         copy.wait()
 
 
 def assemble(pieces, places, splits=None):
-    count = len(pieces)
-    rows, columns = pieces[0].shape
+    slots = sum(piece.shape[0] for piece in pieces)
+    rows, columns = pieces[0].shape[1:]
     splits = (rows,) if splits is None else splits
     anywhere = pl.BlockSpec(memory_space=pl.ANY)
-    results = pl.pallas_call(
-        functools.partial(assemble_kernel, splits, count),
+    return pl.pallas_call(
+        functools.partial(assemble_kernel, splits, len(pieces)),
         in_specs=[pl.BlockSpec(memory_space=pltpu.SMEM)]
-        + [pl.BlockSpec(memory_space=pltpu.VMEM)] * count,
+        + [pl.BlockSpec(memory_space=pltpu.VMEM)] * len(pieces),
         out_specs=[anywhere] * len(splits),
-        out_shape=[jax.ShapeDtypeStruct((count, n, columns), pieces[0].dtype) for n in splits],
-        scratch_shapes=[pltpu.SemaphoreType.DMA((count, len(splits)))],
+        out_shape=[jax.ShapeDtypeStruct((slots, n, columns), pieces[0].dtype) for n in splits],
+        scratch_shapes=[pltpu.SemaphoreType.DMA((slots, len(splits)))],
         compiler_params=pltpu.CompilerParams(vmem_limit_bytes=VMEM_BYTES),
         cost_estimate=pl.CostEstimate(
-            flops=0, bytes_accessed=4 * count * rows * columns, transcendentals=0
+            flops=0, bytes_accessed=4 * slots * rows * columns, transcendentals=0
         ),
         name="assemble",
     )(places.astype(jnp.int32), *pieces)
-    return [result.reshape(-1, columns) for result in results]
 
 
 def join(blocks):
-    return assemble(blocks, jnp.arange(len(blocks)))[0]
-
-
-def gather_copies(value):
-    depth = lax.axis_size("dp") // 2
-    at = lax.axis_index("dp")
-    along = [value] + [shift_z(value, k) for k in range(1, depth)]
-    beside = [xor_permute(piece, "dp", 1) for piece in along]
-    rows = jnp.stack([(at // 2 - k) % depth for k in range(depth)])
-    places = jnp.concatenate([rows * 2 + at % 2, rows * 2 + 1 - at % 2])
-    return along + beside, places
+    joined = assemble([block[None] for block in blocks], jnp.arange(len(blocks)))[0]
+    return joined.reshape(-1, joined.shape[-1])
+
+
+def gather_along(value):
+    return [value] + [shift_z(value, k) for k in range(1, lax.axis_size("dp") // 2)]
+
+
+def gather_beside(along, *waits):
+    depth = len(along)
+    z = lax.axis_index("dp") // 2
+    places = jnp.stack([(z - k) % depth for k in range(depth)])
+    stack = assemble([piece[None] for piece in along], places)[0]
+    stack = after(stack, *waits)
+    return [stack, xor_permute(stack, "dp", 1)]
+
+
+def interleave(stacks, splits):
+    depth = stacks[0].shape[0]
+    y = lax.axis_index("dp") % 2
+    rows = 2 * jnp.arange(depth)
+    results = assemble(stacks, jnp.concatenate([rows + y, rows + 1 - y]), splits)
+    return [result.reshape(-1, result.shape[-1]) for result in results]
 
 
 def reduce_beside(grad):
@@ -467,6 +483,10 @@
 
 def after(value, *others):
     return lax.optimization_barrier((value, *others))[0]
+
+
+def after_all(values, *others):
+    return lax.optimization_barrier((*values, *others))[: len(values)]
 
 
 def gather_blocks(value):
@@ -691,7 +711,7 @@
         ],
         compiler_params=pltpu.CompilerParams(vmem_limit_bytes=VMEM_BYTES),
         cost_estimate=pl.CostEstimate(
-            flops=20 * rows * columns, bytes_accessed=10 * rows * columns, transcendentals=0
+            flops=20 * rows * columns, bytes_accessed=20 * rows * columns, transcendentals=0
         ),
         name="unproject",
     )(dq_near, dq_far, dk, dv, raw, cosine, sine, gain_q, gain_k)
@@ -862,7 +882,6 @@
     key_heads = k.shape[1] // HEAD_SIZE
     width = out.shape[1]
     lanes = group * HEAD_SIZE
-    pairs = key_heads * group * count * block * rows * 5 // 8
 
     def by_query(n):
         return pl.BlockSpec((block, n), lambda g, i, me: (i, g))
@@ -902,9 +921,7 @@
             jax.ShapeDtypeStruct(out.shape, f32),
         ],
         compiler_params=pltpu.CompilerParams(vmem_limit_bytes=VMEM_BYTES),
-        cost_estimate=pl.CostEstimate(
-            flops=14 * pairs * HEAD_SIZE, bytes_accessed=20 * q.size, transcendentals=pairs
-        ),
+        cost_estimate=SMALL_COST,
         name="unattend",
     )(me, q, qf, k, kf, v, o, *branches, out, logs, *earlier)
 
@@ -1049,8 +1066,8 @@
     first = jnp.concatenate(
         [first[:, :owned].reshape(size * owned, first.shape[2]), gain_rows]
     )
-    first_pieces, places_dp = gather_copies(first)
-    early = first_pieces[1 : copies // 2]
+    first_along = gather_along(first)
+    first_stacks = gather_beside(first_along)
 
     gate_up = jnp.concatenate([by_columns(w_gate), by_columns(w_up)], axis=2)
     gate_up, arrived = exchange(after(gate_up, *arrived), me)
@@ -1059,16 +1076,18 @@
     places = jnp.concatenate([positions, segment_ids]).astype(jnp.int32)
     places = jnp.concatenate(gather_blocks(after(places, *arrived)), axis=1)
     x_own = tokens.reshape(block, MODEL_WIDTH)
-    x_blocks = gather_blocks(after(x_own, *arrived))
+    x_near, across = gather_near(after(x_own, *arrived))
+    x_blocks = x_near + gather_far(across, first_stacks[0])
     cot_own = cotangent.reshape(block, MODEL_WIDTH)
-    cot_blocks = gather_blocks(after(cot_own, x_blocks[2]))
+    cot_blocks = gather_blocks(after(cot_own, first_stacks[1]))
     cot_near, cot_far = join(cot_blocks[:2]), join(cot_blocks[2:])
 
-    gate_up_rows = after(gate_up.reshape(size * owned, -1), *early)
+    moved_along = gather_along(after(moved, *first_along[1:]))
+    moved_stacks = gather_beside(moved_along, first_stacks[1])
+    gate_up_rows = after(gate_up.reshape(size * owned, -1), *moved_along[1:])
     gate_up = lax.all_gather(gate_up_rows, "dp", axis=0, tiled=True)
-    moved_pieces, unused = gather_copies(after(moved, *early))
-    w_first, gain_rows = assemble(first_pieces, places_dp, (size * owned, pad_rows))
-    w_first = after(w_first, gate_up_rows, *moved_pieces[1 : copies // 2])
+    w_first, gain_rows = interleave(first_stacks, (size * owned, pad_rows))
+    w_first = after(w_first, gate_up_rows)
     full_gains = gain_rows.reshape(copies, pad_rows, -1)[:, :size, :gain_count].reshape(-1)
     gain_attn, gain_mlp, gain_query, gain_key = split_gains(full_gains)
 
@@ -1091,18 +1110,23 @@
             me_row, query, query_features, k, key_features, v, block, group, first, 2
         )
 
+    def tn_dot(left, right):
+        return lax.dot_general(left, right, (((0,), (0,)), ((), ())), preferred_element_type=f32)
+
+    def by_copy(grad):
+        return grad.astype(bf16).reshape(copies, -1, grad.shape[-1])
+
     def halves(value):
         return value[:block], value[block:]
 
-    q, cot_near, cot_far, *moved_pieces = lax.optimization_barrier(
-        (q, cot_near, cot_far, *moved_pieces)
-    )
     att_far, logs_far = attend_half(q, 2)
-    out_full, down_full = assemble(moved_pieces, places_dp, (w_out.shape[0], w_down.shape[0]))
+    att_far, *moved_stacks = lax.optimization_barrier((att_far, *moved_stacks))
+    out_full, down_full = interleave(moved_stacks, (w_out.shape[0], w_down.shape[0]))
     att_across, att_corner = halves(att_far)
     part_corner, part_across = nn_dot(att_corner, out_full), nn_dot(att_across, out_full)
     toward, across = send_across(part_corner, part_across)
-    att_near, logs_near = attend_half(after(q, toward, gate_up), 0)
+    att_near, logs_near = attend_half(after(q, toward, cot_near, cot_far), 0)
+    att_near = after(att_near, gate_up)
     att_own, att_beside = halves(att_near)
     beside = [
         xor_permute(nn_dot(piece, out_full).astype(bf16), "ctx", 1)
@@ -1120,23 +1144,15 @@
     )
 
     unused, across = send_across(d_corner, d_across)
-    d_normed = sum_own(d_beside, d_own, across)
+    grad_down = (tn_dot(hidden_near, cot_near) + tn_dot(hidden_far, cot_far)).astype(bf16)
+    grad_both = (tn_dot(h_near, d_both_near) + tn_dot(h_far, d_both_far)).astype(bf16)
+    d_normed = sum_own(d_beside, d_own, after(across, grad_down, grad_both))
     d_middle, d_gain_mlp = norm_back(middle, gain_mlp, d_normed)
     d_middle = d_middle + cot_own.astype(f32)
     branches_near, branch_across = gather_near(d_middle.astype(bf16))
 
-    def tn_dot(left, right):
-        return lax.dot_general(left, right, (((0,), (0,)), ((), ())), preferred_element_type=f32)
-
-    def by_copy(grad):
-        return grad.astype(bf16).reshape(copies, -1, grad.shape[-1])
-
-    grad_down = tn_dot(hidden_near, cot_near) + tn_dot(hidden_far, cot_far)
-    grad_both = tn_dot(h_near, d_both_near) + tn_dot(h_far, d_both_far)
-    grad_both = grad_both.astype(bf16)
-    grad_down = grad_down.astype(bf16)
-    d_both_sum = lax.psum_scatter(grad_both, "dp", scatter_dimension=0, tiled=True)
-    d_down_sum = lax.psum_scatter(grad_down, "dp", scatter_dimension=0, tiled=True)
+    pair_both = reduce_beside(by_copy(grad_both))
+    pair_down = reduce_beside(by_copy(grad_down))
 
     def unattend_half(att, branches, logs, first, earlier=()):
         return unattend(
@@ -1156,17 +1172,23 @@
             earlier,
         )
 
-    branches_near = [after(branches_near[0], grad_both, grad_down), branches_near[1]]
     dq_near, *earlier = unattend_half(att_near, branches_near, logs_near, 0)
+    terms_down = reduce_along(pair_down)
+    dq_near, pair_both, *terms_down = lax.optimization_barrier((dq_near, pair_both, *terms_down))
+    terms_both = reduce_along(pair_both)
     branches_far = gather_far(branch_across, dq_near)
-    unused, across = send_across(down_corner, down_across, branches_far[0])
-    output = (middle + sum_own(down_beside, down_own, across)).astype(bf16)
     dq_far, dk, dv, grad_out = unattend_half(att_far, branches_far, logs_far, 2, earlier)
     pair_out = reduce_beside(by_copy(grad_out))
-    dk = after(dk, across)
+    dk, *terms_both = lax.optimization_barrier((dk, *terms_both))
+    unused, down_across = send_across(down_corner, down_across, dk)
+    grad_both = exchange(add_all(terms_both).reshape(size, owned, -1), me)[0]
     low, d_gain_heads = unproject(
         dq_near, dq_far, dk, dv, raw, cosine, sine, gain_q_row, gain_k_row, query_heads, key_heads
     )
+    low, d_gain_heads, pair_out, grad_both = lax.optimization_barrier(
+        (low, d_gain_heads, pair_out, grad_both)
+    )
+    terms_down = after_all(terms_down, low)
     terms_out = reduce_along(after(pair_out, low))
     low_own, low_beside, low_across, low_corner = (
         low[r * block : (r + 1) * block] for r in range(size)
@@ -1189,12 +1211,12 @@
     grad_first = jnp.concatenate(
         [grad_first.reshape(copies, size * owned, -1), gain_block], axis=1
     )
-    pair_first = reduce_beside(grad_first)
-    d_both_sum = after(d_both_sum, pair_first)
-    terms_first = reduce_along(after(pair_first, across))
-    d_down_sum = after(d_down_sum, *terms_first)
+    pair_first = after(reduce_beside(grad_first), *terms_out, down_across)
+    output = sum_own(down_beside, down_own, down_across)
+    output = (middle + output).astype(bf16)
+    terms_first = lax.optimization_barrier((*reduce_along(pair_first), across))[:-1]
     grad_first = add_all(terms_first)
-    grad_out = add_all(after(terms_out, *terms_first))
+    grad_out = add_all(after_all(terms_out, *terms_first))
     gain_part = grad_first[size * owned :][:size]
     gain_part = jnp.broadcast_to(gain_part[:, None], (size, pad_rows, gain_part.shape[1]))
     grad_first = jnp.concatenate(
@@ -1210,11 +1232,11 @@
     grad_query = to_rows(grad_first[:, :, :q_cols])
     grad_key = to_rows(grad_first[:, :, q_cols : q_cols + k_cols])
     grad_value = to_rows(grad_first[:, :, q_cols + k_cols :])
-    grad_both = exchange(d_both_sum.reshape(size, owned, -1), me)[0].astype(f32)
+    grad_both = grad_both.astype(f32)
     grad_gate = to_rows(grad_both[:, :, :hidden_cols])
     grad_up = to_rows(grad_both[:, :, hidden_cols:])
     grad_out = lax.ppermute(grad_out, ("dp", "ctx"), backward_owner).astype(f32)
-    grad_down = lax.ppermute(d_down_sum, ("dp", "ctx"), backward_owner).astype(f32)
+    grad_down = lax.ppermute(add_all(terms_down), ("dp", "ctx"), backward_owner).astype(f32)
     return (
         output.reshape(tokens.shape),
         grad_tokens,

time: 553 us -> 535 us (0.967)
  starting transfers between devices: 98.4 us -> 75.4 us
  waiting for transfers between devices: 174 us -> 188 us
  matrix products: 47.3 us -> 36.7 us
    ppermute x50 -> x46, starting transfers between devices: 79.5 us -> 35 us  [xor_permute(): return lax.ppermute(value, axis, [(i, i ^ offset) for i in range(size)])]
    ppermute x1, waiting for transfers between devices: 0.01 us -> 20 us  [split_local(): lax.ppermute(add_all(terms_down), ('dp', 'ctx'), backward_owner).astype(f32)]
    ppermute x12 -> x18, starting transfers between devices: 12 us -> 30.2 us  [shift_z(): lax.ppermute(value, 'dp', [(i, (i + 2 * offset) % size) for i in range(si...]
    ppermute x1, waiting for transfers between devices: 10.9 us -> 2.65 us  [split_local(): grad_out = lax.ppermute(grad_out, ('dp', 'ctx'), backward_owner).astype(f32)]
    pallas_call x4 -> x6, Pallas kernels: 12.2 us -> 17.1 us  [assemble(): pl.pallas_call(functools.partial(assemble_kernel, splits, len(pieces)), i...]
    ppermute x50 -> x46, waiting for transfers between devices: 82.9 us -> 84.4 us  [xor_permute(): return lax.ppermute(value, axis, [(i, i ^ offset) for i in range(size)])]
    ppermute x12 -> x18, waiting for transfers between devices: 80.2 us -> 80.5 us  [shift_z(): lax.ppermute(value, 'dp', [(i, (i + 2 * offset) % size) for i in range(si...]
  transfers between devices with their start and end apart: 68 -> 68, of which waited for: 28 -> 22; matrix products, arithmetic and copies ran while one was open for 17% -> 16% of each run, Pallas kernels for 24% -> 29%
where the time goes in v5:
time: 535 us; the launch traced here: 526 us
  waiting for transfers between devices  188 us (35%)
  Pallas kernels  151 us (28%)
  starting transfers between devices  75.4 us (14%)
  other arithmetic  39.1 us (7%)
  matrix products  36.7 us (7%)
  local copies, waits for them, and re-layouts  21.2 us (4%)
  between operations  15.7 us (3%)
    ppermute x46, waiting for transfers between devices, xor_permute(): return lax.ppermute(value, axis, [(i, i ^ offset) for i in range(size)])  84.4 us
    ppermute x18, waiting for transfers between devices, shift_z(): lax.ppermute(value, 'dp', [(i, (i + 2 * offset) % size) for i in range(si...  80.5 us
    pallas_call x2, Pallas kernels, unattend(): pl.pallas_call(functools.partial(unattend_kernel, group, block, first, bo...  49.8 us
    ppermute x46, starting transfers between devices, xor_permute(): return lax.ppermute(value, axis, [(i, i ^ offset) for i in range(size)])  35 us
    pallas_call x2, Pallas kernels, feed(): pl.pallas_call(functools.partial(feed_kernel, units, half), grid=(rows //...  32.9 us
    ppermute x18, starting transfers between devices, shift_z(): lax.ppermute(value, 'dp', [(i, (i + 2 * offset) % size) for i in range(si...  30.2 us
    pallas_call x2, Pallas kernels, attend(): pl.pallas_call(functools.partial(attend_kernel, group, block, first), gri...  23.2 us
    ppermute x1, waiting for transfers between devices, split_local(): lax.ppermute(add_all(terms_down), ('dp', 'ctx'), backward_owner).astype(f32)  20 us
  transfers between devices with their start and end apart: 68, of which 22 were waited for; matrix products, arithmetic and copies ran while one was open for 16% of the time, Pallas kernels for 29%

profile of v5, /device:TPU:27, one launch (start us, length us, event | category | flops | bytes accessed | tf_op | source)
XLA Modules:
  0.0 526.3 jit_solution(11642514113840727660)
XLA Ops:
  25.7 3.1 collective-permute-start.8
  30.8 5.3 %collective-permute-start.13 = (bf16[160,1024]{1,0:T(8,128)(2,1)S(1)}, bf16[160,1024]{1,0:T(8,128)(2,1)S(1)}, u32[]{:S(2)}, u32[]{:S(2)}) collective-permute-start(bf16[160,1024]{1,0:T(8,128)(2,1)S(1)} %pad_maximum_fusion.11), channel_id=1, source_target_pairs={{0,0},{1,4},{2,8},{3,12},{4,16},{5,20},{6,24},{7,28},{8,1},{9,5},{... | collective-permute-start | bytes 983048 | tf_op jit(solution)/shard_map/ppermute | solution.py:1075
  37.5 2.9 collective-permute-done.8
  40.5 12.4 %collective-permute-done.9 = bf16[144,1024]{1,0:T(8,128)(2,1)S(1)} collective-permute-done((bf16[144,1024]{1,0:T(8,128)(2,1)S(1)}, bf16[144,1024]{1,0:T(8,128)(2,1)S(1)}, u32[]{:S(2)}, u32[]{:S(2)}) %collective-permute-start.9) | collective-permute-done | bytes 294944 | tf_op jit(solution)/shard_map/ppermute | solution.py:392
  52.9 8.3 %collective-permute-start.14 = (bf16[160,1024]{1,0:T(8,128)(2,1)S(1)}, bf16[160,1024]{1,0:T(8,128)(2,1)S(1)}, u32[]{:S(2)}, u32[]{:S(2)}) collective-permute-start(bf16[160,1024]{1,0:T(8,128)(2,1)S(1)} %collective-permute-done.13), channel_id=1, source_target_pairs={{0,8},{4,12},{8,16},{12,20},{16,24},{20,28},{24,0},{28,4},{1,9},{5... | collective-permute-start | bytes 983048 | tf_op jit(solution)/shard_map/ppermute | solution.py:392
  61.2 8.8 %collective-permute-start.15 = (bf16[160,1024]{1,0:T(8,128)(2,1)S(1)}, bf16[160,1024]{1,0:T(8,128)(2,1)S(1)}, u32[]{:S(2)}, u32[]{:S(2)}) collective-permute-start(bf16[160,1024]{1,0:T(8,128)(2,1)S(1)} %collective-permute-done.13), channel_id=1, source_target_pairs={{0,16},{4,20},{8,24},{12,28},{16,0},{20,4},{24,8},{28,12},{1,17},{... | collective-permute-start | bytes 983048 | tf_op jit(solution)/shard_map/ppermute | solution.py:392
  70.3 3.0 collective-permute-done.14
  73.3 25.0 %collective-permute-done.15 = bf16[160,1024]{1,0:T(8,128)(2,1)S(1)} collective-permute-done((bf16[160,1024]{1,0:T(8,128)(2,1)S(1)}, bf16[160,1024]{1,0:T(8,128)(2,1)S(1)}, u32[]{:S(2)}, u32[]{:S(2)}) %collective-permute-start.15) | collective-permute-done | bytes 327712 | tf_op jit(solution)/shard_map/ppermute | solution.py:392
  98.3 3.7 fusion.33
  113.3 22.6 %collective-permute-done.12.refs_1_ = bf16[4,144,1024]{2,1,0:T(8,128)(2,1)S(1)} collective-permute-done((bf16[4,144,1024]{2,1,0:T(8,128)(2,1)}, bf16[4,144,1024]{2,1,0:T(8,128)(2,1)S(1)}, u32[]{:S(2)}, u32[]{:S(2)}) %collective-permute-start.12) | collective-permute-done | bytes 1179680 | tf_op jit(solution)/shard_map/ppermute | solution.py:373
  135.8 2.7 collective-permute-start.23
  138.5 5.6 %collective-permute-start.22 = (bf16[512,1024]{1,0:T(8,128)(2,1)S(1)}, bf16[512,1024]{1,0:T(8,128)(2,1)}, u32[]{:S(2)}, u32[]{:S(2)}) collective-permute-start(bf16[512,1024]{1,0:T(8,128)(2,1)S(1)} %bitcast.221), channel_id=1, source_target_pairs={{0,1},{1,0},{2,3},{3,2},{4,5},{5,4},{6,7},{7,6},{8,9},{9,8},{10,11... | collective-permute-start | bytes 3145736 | tf_op jit(solution)/shard_map/ppermute | solution.py:373
  144.1 3.2 assemble.7
  149.3 14.1 %project.1 = (bf16[2048,1024]{1,0:T(8,128)(2,1)}, f32[2048,768]{1,0:T(8,128)}, bf16[2048,512]{1,0:T(8,128)(2,1)}, bf16[2048,256]{1,0:T(8,128)(2,1)}, bf16[2048,256]{1,0:T(8,128)(2,1)}) custom-call(bf16[512,1024]{1,0:T(8,128)(2,1)} %bitcast.215, bf16[512,1024]{1,0:T(8,128)(2,1)} %collective-permute-done.6.x_refs_1_, ...), custom_call_target="tpu_custom_call" | custom-call | flops 4294967296 | bytes 20971520 | tf_op jit(solution)/shard_map/project/pallas_call | solution.py:593
  163.4 8.4 %attend.2 = (bf16[1024,512]{1,0:T(8,128)(2,1)}, f32[2,2,1024]{2,1,0:T(2,128)}) custom-call(s32[1]{0:T(128)} %bitcast.1.me_ref, bf16[2048,512]{1,0:T(8,128)(2,1)} %get-tuple-element.115.q_ref, bf16[2048,128]{1,0:T(8,128)(2,1)} %select_convert_fusion.qf_ref, bf16[2048,256]{1,0:T(8,128)(2,1)} %get-tuple-element.106.k_ref, bf16[2048,128]{1,0:T(8,128)(2,1)} %fusion.28.kf_ref, ...), custom_call_target="tpu_custom_call" | custom-call | flops 5368709120 | bytes 10485760 | tf_op jit(solution)/shard_map/attend/pallas_call | solution.py:760
  171.8 9.9 %collective-permute-done.20.refs_1_ = bf16[4,160,1024]{2,1,0:T(8,128)(2,1)S(1)} collective-permute-done((bf16[4,160,1024]{2,1,0:T(8,128)(2,1)}, bf16[4,160,1024]{2,1,0:T(8,128)(2,1)S(1)}, u32[]{:S(2)}, u32[]{:S(2)}) %collective-permute-start.20) | collective-permute-done | bytes 1310752 | tf_op jit(solution)/shard_map/ppermute | solution.py:373
  182.8 3.3 assemble.9
  189.2 3.0 assemble.10
  193.2 3.0 assemble.11
  199.1 14.8 %attend.3 = (bf16[1024,512]{1,0:T(8,128)(2,1)}, f32[2,2,1024]{2,1,0:T(2,128)}) custom-call(s32[1]{0:T(128)} %bitcast.1.me_ref, bf16[2048,512]{1,0:T(8,128)(2,1)} %get-tuple-element.115.q_ref, bf16[2048,128]{1,0:T(8,128)(2,1)} %select_convert_fusion.qf_ref, bf16[2048,256]{1,0:T(8,128)(2,1)} %get-tuple-element.106.k_ref, bf16[2048,128]{1,0:T(8,128)(2,1)} %fusion.28.kf_ref, ...), custom_call_target="tpu_custom_call" | custom-call | flops 5368709120 | bytes 10485760 | tf_op jit(solution)/shard_map/attend/pallas_call | solution.py:760
  218.1 4.9 collective-permute-done.27
  229.4 16.3 %feed.2 = (bf16[1024,1024]{1,0:T(8,128)(2,1)}, bf16[1024,768]{1,0:T(8,128)(2,1)}, bf16[1024,1536]{1,0:T(8,128)(2,1)}, bf16[512,1024]{1,0:T(8,128)(2,1)}, bf16[51...) custom-call(bf16[512,1024]{1,0:T(8,128)(2,1)} %copy-done.20, ...), custom_call_target="tpu_custom_call" | custom-call | flops 9663676416 | bytes 19922944 | tf_op jit(solution)/shard_map/feed/pallas_call | solution.py:995
  245.7 5.3 %collective-permute-done.30.first_ref = bf16[512,1024]{1,0:T(8,128)(2,1)} collective-permute-done((bf16[512,1024]{1,0:T(8,128)(2,1)S(1)}, bf16[512,1024]{1,0:T(8,128)(2,1)}, u32[]{:S(2)}, u32[]{:S(2)}) %collective-permute-start.30) | collective-permute-done | bytes 1048608 | tf_op jit(solution)/shard_map/ppermute | solution.py:373
  251.8 4.1 collective-permute-done.31.second_ref
  255.9 16.6 %feed.3 = (bf16[1024,1024]{1,0:T(8,128)(2,1)}, bf16[1024,768]{1,0:T(8,128)(2,1)}, bf16[1024,1536]{1,0:T(8,128)(2,1)}, bf16[512,1024]{1,0:T(8,128)(2,1)}, bf16[51...) custom-call(bf16[512,1024]{1,0:T(8,128)(2,1)} %collective-permute-done.30.first_ref, ...), custom_call_target="tpu_custom_call" | custom-call | flops 9663676416 | bytes 19922944 | tf_op jit(solution)/shard_map/feed/pallas_call | solution.py:995
  272.5 3.4 fusion.49
  279.4 3.5 fusion.50
  284.8 4.2 add_convert_fusion
  291.7 16.1 %collective-permute-done.35 = bf16[512,1024]{1,0:T(8,128)(2,1)S(1)} collective-permute-done((bf16[512,1024]{1,0:T(8,128)(2,1)S(1)}, bf16[512,1024]{1,0:T(8,128)(2,1)S(1)}, u32[]{:S(2)}, u32[]{:S(2)}) %collective-permute-start.35) | collective-permute-done | bytes 1048608 | tf_op jit(solution)/shard_map/ppermute | solution.py:373
  309.3 2.6 fusion.45
  317.0 15.4 %collective-permute-done.38 = bf16[4,128,1536]{2,1,0:T(8,128)(2,1)} collective-permute-done((bf16[4,128,1536]{2,1,0:T(8,128)(2,1)}, bf16[4,128,1536]{2,1,0:T(8,128)(2,1)}, u32[]{:S(2)}, u32[]{:S(2)}) %collective-permute-start.38) | collective-permute-done | bytes 1572896 | tf_op jit(solution)/shard_map/ppermute | solution.py:373
  334.3 30.0 %unattend.2 = (f32[1024,512]{1,0:T(8,128)}, f32[2048,256]{1,0:T(8,128)}, f32[2048,256]{1,0:T(8,128)}, f32[512,1024]{1,0:T(8,128)}) custom-call(s32[1]{0:T(128)} %bitcast.1.me_ref, bf16[2048,512]{1,0:T(8,128)(2,1)} %get-tuple-element.115.q_ref, bf16[2048,128]{1,0:T(8,128)(2,1)} %select_convert_fusion.qf_ref, bf16[2048,256]{1,0:T(8,128)(2,1)} %get-tuple-element.106.k_ref, ...), custom_call_target="tpu_custom_call" | custom-call | flops 1 | bytes 1 | tf_op jit(solution)/shard_map/unattend/pallas_call | solution.py:892
  366.4 3.6 collective-permute-start.44
  371.7 2.6 add_convert_fusion.5
  374.3 19.8 %unattend.3 = (f32[1024,512]{1,0:T(8,128)}, f32[2048,256]{1,0:T(8,128)}, f32[2048,256]{1,0:T(8,128)}, f32[512,1024]{1,0:T(8,128)}) custom-call(s32[1]{0:T(128)} %bitcast.1.me_ref, bf16[2048,512]{1,0:T(8,128)(2,1)} %get-tuple-element.115.q_ref, bf16[2048,128]{1,0:T(8,128)(2,1)} %select_convert_fusion.qf_ref, bf16[2048,256]{1,0:T(8,128)(2,1)} %get-tuple-element.106.k_ref, ...), custom_call_target="tpu_custom_call" | custom-call | flops 1 | bytes 1 | tf_op jit(solution)/shard_map/unattend/pallas_call | solution.py:892
  394.1 10.9 %collective-permute-done.45 = bf16[128,1536]{1,0:T(8,128)(2,1)S(1)} collective-permute-done((bf16[128,1536]{1,0:T(8,128)(2,1)S(1)}, bf16[128,1536]{1,0:T(8,128)(2,1)S(1)}, u32[]{:S(2)}, u32[]{:S(2)}) %collective-permute-start.45) | collective-permute-done | bytes 393248 | tf_op jit(solution)/shard_map/ppermute | solution.py:392
  408.2 13.6 %unproject.1 = (bf16[2048,1024]{1,0:T(8,128)(2,1)}, f32[8,128]{1,0:T(8,128)}) custom-call(f32[1024,512]{1,0:T(8,128)} %get-tuple-element.137.dq_near_ref, f32[1024,512]{1,0:T(8,128)} %get-tuple-element.147.dq_far_ref, f32[2048,256]{1,0:T(8,128)} %get-tuple-element.145.dk_ref, f32[2048,256]{1,0:T(8,128)} %get-tuple-element.148.dv_ref, ...), custom_call_target="tpu_custom_call" | custom-call | flops 41943040 | bytes 41943040 | tf_op jit(solution)/shard_map/unproject/pallas_call | solution.py:693
  423.4 3.7 convolution_convert_fusion.1
  428.0 5.9 %multiply_reduce_fusion = (f32[1024]{0:T(1024)S(1)}, bf16[1024,1024]{1,0:T(8,128)(2,1)}) fusion(bf16[1024,1024]{1,0:T(8,128)(2,1)S(1)} %bitcast.274, bf16[2048,1024]{1,0:T(8,128)(2,1)S(1)} %copy-done.58, bf16[2048,1024]{1,0:T(8,128)(2,1)S(1)} %copy-done.50), kind=kOutput, calls=%fused_computation.1 | convolution fusion | flops 4300209152 | bytes 12587008 | tf_op jit(solution)/shard_map/dot_general | solution.py:1114
  437.5 2.7 convolution_convert_fusion.2
  442.8 2.5 add_convert_fusion.2
  445.4 20.0 %collective-permute-done.66 = bf16[96,1024]{1,0:T(8,128)(2,1)S(1)} collective-permute-done((bf16[96,1024]{1,0:T(8,128)(2,1)S(1)}, bf16[96,1024]{1,0:T(8,128)(2,1)S(1)}, u32[]{:S(2)}, u32[]{:S(2)}) %collective-permute-start.66) | collective-permute-done | bytes 196640 | tf_op jit(solution)/shard_map/ppermute | solution.py:1239
  467.8 3.7 collective-permute-start.58
  472.1 4.7 collective-permute-done.57
  478.5 3.3 fusion.16
  481.7 4.5 collective-permute-done.59
  486.3 17.1 %collective-permute-done.60 = bf16[144,1024]{1,0:T(8,128)(2,1)S(1)} collective-permute-done((bf16[144,1024]{1,0:T(8,128)(2,1)S(1)}, bf16[144,1024]{1,0:T(8,128)(2,1)S(1)}, u32[]{:S(2)}, u32[]{:S(2)}) %collective-permute-start.60) | collective-permute-done | bytes 294944 | tf_op jit(solution)/shard_map/ppermute | solution.py:392
  515.9 2.7 collective-permute-done.65
  (349 shorter events, 104.2 us)
Async XLA Ops:
  7.2 206.7 %all-gather.2.cloned.1.call-start = ((), (), s32[]{:S(2)}) async-start(), calls=%async_computation | async-start | bytes 3538944 | tf_op jit(solution)/shard_map/all_gather | solution.py:1088
  25.5 11.8 %collective-permute-start.10 = (bf16[144,1024]{1,0:T(8,128)(2,1)S(1)}, bf16[144,1024]{1,0:T(8,128)(2,1)S(1)}, u32[]{:S(2)}, u32[]{:S(2)}) collective-permute-start(bf16[144,1024]{1,0:T(8,128)(2,1)S(1)} %get-tuple-element.239), channel_id=1, source_target_pairs={{0,24},{4,28},{8,0},{12,4},{16,8},{20,12},{24,16},{28,20},{1,25},{... | collective-permute-start | bytes 884744 | tf_op jit(solution)/shard_map/ppermute | solution.py:392
  25.7 14.7 %collective-permute-start.8 = (bf16[144,1024]{1,0:T(8,128)(2,1)S(1)}, bf16[144,1024]{1,0:T(8,128)(2,1)S(1)}, u32[]{:S(2)}, u32[]{:S(2)}) collective-permute-start(bf16[144,1024]{1,0:T(8,128)(2,1)S(1)} %get-tuple-element.239), channel_id=1, source_target_pairs={{0,8},{4,12},{8,16},{12,20},{16,24},{20,28},{24,0},{28,4},{1,9},{5... | collective-permute-start | bytes 884744 | tf_op jit(solution)/shard_map/ppermute | solution.py:392
  28.8 24.1 %collective-permute-start.9 = (bf16[144,1024]{1,0:T(8,128)(2,1)S(1)}, bf16[144,1024]{1,0:T(8,128)(2,1)S(1)}, u32[]{:S(2)}, u32[]{:S(2)}) collective-permute-start(bf16[144,1024]{1,0:T(8,128)(2,1)S(1)} %get-tuple-element.239), channel_id=1, source_target_pairs={{0,16},{4,20},{8,24},{12,28},{16,0},{20,4},{24,8},{28,12},{1,17},{... | collective-permute-start | bytes 884744 | tf_op jit(solution)/shard_map/ppermute | solution.py:392
  30.8 22.1 %collective-permute-start.13 = (bf16[160,1024]{1,0:T(8,128)(2,1)S(1)}, bf16[160,1024]{1,0:T(8,128)(2,1)S(1)}, u32[]{:S(2)}, u32[]{:S(2)}) collective-permute-start(bf16[160,1024]{1,0:T(8,128)(2,1)S(1)} %pad_maximum_fusion.11), channel_id=1, source_target_pairs={{0,0},{1,4},{2,8},{3,12},{4,16},{5,20},{6,24},{7,28},{8,1},{9,5},{... | collective-permute-start | bytes 983048 | tf_op jit(solution)/shard_map/ppermute | solution.py:1075
  37.3 71.0 %collective-permute-start.7 = (bf16[512,1024]{1,0:T(8,128)(2,1)S(1)}, bf16[512,1024]{1,0:T(8,128)(2,1)}, u32[]{:S(2)}, u32[]{:S(2)}) collective-permute-start(bf16[512,1024]{1,0:T(8,128)(2,1)S(1)} %bitcast.216), channel_id=1, source_target_pairs={{0,2},{1,3},{2,0},{3,1},{4,6},{5,7},{6,4},{7,5},{8,10},{9,11},{10,... | collective-permute-start | bytes 3145736 | tf_op jit(solution)/shard_map/ppermute | solution.py:373
  37.3 112.0 %collective-permute-start.6 = (bf16[512,1024]{1,0:T(8,128)(2,1)S(1)}, bf16[512,1024]{1,0:T(8,128)(2,1)}, u32[]{:S(2)}, u32[]{:S(2)}) collective-permute-start(bf16[512,1024]{1,0:T(8,128)(2,1)S(1)} %bitcast.217), channel_id=1, source_target_pairs={{0,1},{1,0},{2,3},{3,2},{4,5},{5,4},{6,7},{7,6},{8,9},{9,8},{10,11... | collective-permute-start | bytes 3145736 | tf_op jit(solution)/shard_map/ppermute | solution.py:373
  52.9 20.4 %collective-permute-start.14 = (bf16[160,1024]{1,0:T(8,128)(2,1)S(1)}, bf16[160,1024]{1,0:T(8,128)(2,1)S(1)}, u32[]{:S(2)}, u32[]{:S(2)}) collective-permute-start(bf16[160,1024]{1,0:T(8,128)(2,1)S(1)} %collective-permute-done.13), channel_id=1, source_target_pairs={{0,8},{4,12},{8,16},{12,20},{16,24},{20,28},{24,0},{28,4},{1,9},{5... | collective-permute-start | bytes 983048 | tf_op jit(solution)/shard_map/ppermute | solution.py:392
  61.2 37.1 %collective-permute-start.15 = (bf16[160,1024]{1,0:T(8,128)(2,1)S(1)}, bf16[160,1024]{1,0:T(8,128)(2,1)S(1)}, u32[]{:S(2)}, u32[]{:S(2)}) collective-permute-start(bf16[160,1024]{1,0:T(8,128)(2,1)S(1)} %collective-permute-done.13), channel_id=1, source_target_pairs={{0,16},{4,20},{8,24},{12,28},{16,0},{20,4},{24,8},{28,12},{1,17},{... | collective-permute-start | bytes 983048 | tf_op jit(solution)/shard_map/ppermute | solution.py:392
  70.0 28.3 %collective-permute-start.16 = (bf16[160,1024]{1,0:T(8,128)(2,1)S(1)}, bf16[160,1024]{1,0:T(8,128)(2,1)S(1)}, u32[]{:S(2)}, u32[]{:S(2)}) collective-permute-start(bf16[160,1024]{1,0:T(8,128)(2,1)S(1)} %collective-permute-done.13), channel_id=1, source_target_pairs={{0,24},{4,28},{8,0},{12,4},{16,8},{20,12},{24,16},{28,20},{1,25},{... | collective-permute-start | bytes 983048 | tf_op jit(solution)/shard_map/ppermute | solution.py:392
  104.4 31.4 %collective-permute-start.12 = (bf16[4,144,1024]{2,1,0:T(8,128)(2,1)}, bf16[4,144,1024]{2,1,0:T(8,128)(2,1)S(1)}, u32[]{:S(2)}, u32[]{:S(2)}) collective-permute-start(bf16[4,144,1024]{2,1,0:T(8,128)(2,1)} %assemble.6.refs_0_), channel_id=1, source_target_pairs={{0,4},{4,0},{8,12},{12,8},{16,20},{20,16},{24,28},{28,24},{1,5},{5... | collective-permute-start | bytes 3538952 | tf_op jit(solution)/shard_map/ppermute | solution.py:373
  108.3 41.0 %collective-permute-start.11 = (bf16[512,1024]{1,0:T(8,128)(2,1)}, bf16[512,1024]{1,0:T(8,128)(2,1)}, u32[]{:S(2)}, u32[]{:S(2)}) collective-permute-start(bf16[512,1024]{1,0:T(8,128)(2,1)} %collective-permute-done.7.x_refs_2_), channel_id=1, source_target_pairs={{0,1},{1,0},{2,3},{3,2},{4,5},{5,4},{6,7},{7,6},{8,9},{9,8},{10,11... | collective-permute-start | bytes 3145736 | tf_op jit(solution)/shard_map/ppermute | solution.py:373
  135.8 35.9 %collective-permute-start.23 = (bf16[512,1024]{1,0:T(8,128)(2,1)S(1)}, bf16[512,1024]{1,0:T(8,128)(2,1)}, u32[]{:S(2)}, u32[]{:S(2)}) collective-permute-start(bf16[512,1024]{1,0:T(8,128)(2,1)S(1)} %bitcast.220), channel_id=1, source_target_pairs={{0,2},{1,3},{2,0},{3,1},{4,6},{5,7},{6,4},{7,5},{8,10},{9,11},{10,... | collective-permute-start | bytes 3145736 | tf_op jit(solution)/shard_map/ppermute | solution.py:373
  138.5 50.2 %collective-permute-start.22 = (bf16[512,1024]{1,0:T(8,128)(2,1)S(1)}, bf16[512,1024]{1,0:T(8,128)(2,1)}, u32[]{:S(2)}, u32[]{:S(2)}) collective-permute-start(bf16[512,1024]{1,0:T(8,128)(2,1)S(1)} %bitcast.221), channel_id=1, source_target_pairs={{0,1},{1,0},{2,3},{3,2},{4,5},{5,4},{6,7},{7,6},{8,9},{9,8},{10,11... | collective-permute-start | bytes 3145736 | tf_op jit(solution)/shard_map/ppermute | solution.py:373
  144.1 37.6 %collective-permute-start.20 = (bf16[4,160,1024]{2,1,0:T(8,128)(2,1)}, bf16[4,160,1024]{2,1,0:T(8,128)(2,1)S(1)}, u32[]{:S(2)}, u32[]{:S(2)}) collective-permute-start(bf16[4,160,1024]{2,1,0:T(8,128)(2,1)} %assemble.8.refs_0_), channel_id=1, source_target_pairs={{0,4},{4,0},{8,12},{12,8},{16,20},{20,16},{24,28},{28,24},{1,5},{5... | collective-permute-start | bytes 3932168 | tf_op jit(solution)/shard_map/ppermute | solution.py:373
  171.8 20.4 %collective-permute-start.24 = (bf16[512,1024]{1,0:T(8,128)(2,1)}, bf16[512,1024]{1,0:T(8,128)(2,1)S(1)}, u32[]{:S(2)}, u32[]{:S(2)}) collective-permute-start(bf16[512,1024]{1,0:T(8,128)(2,1)} %collective-permute-done.23), channel_id=1, source_target_pairs={{0,1},{1,0},{2,3},{3,2},{4,5},{5,4},{6,7},{7,6},{8,9},{9,8},{10,11... | collective-permute-start | bytes 3145736 | tf_op jit(solution)/shard_map/ppermute | solution.py:373
  197.9 25.1 %collective-permute-start.27 = (bf16[512,1024]{1,0:T(8,128)(2,1)}, bf16[512,1024]{1,0:T(8,128)(2,1)}, u32[]{:S(2)}, u32[]{:S(2)}) collective-permute-start(bf16[512,1024]{1,0:T(8,128)(2,1)} %add_convert_fusion.6), channel_id=1, source_target_pairs={{0,2},{1,3},{2,0},{3,1},{4,6},{5,7},{6,4},{7,5},{8,10},{9,11},{10,... | collective-permute-start | bytes 3145736 | tf_op jit(solution)/shard_map/ppermute | solution.py:373
  226.1 24.8 %collective-permute-start.30 = (bf16[512,1024]{1,0:T(8,128)(2,1)S(1)}, bf16[512,1024]{1,0:T(8,128)(2,1)}, u32[]{:S(2)}, u32[]{:S(2)}) collective-permute-start(bf16[512,1024]{1,0:T(8,128)(2,1)S(1)} %multiply_convert_fusion.first_ref), channel_id=1, source_target_pairs={{0,2},{1,3},{2,0},{3,1},{4,6},{5,7},{6,4},{7,5},{8,10},{9,11},{10,... | collective-permute-start | bytes 3145736 | tf_op jit(solution)/shard_map/ppermute | solution.py:373
  251.8 56.1 %collective-permute-start.33 = (bf16[512,1024]{1,0:T(8,128)(2,1)}, bf16[512,1024]{1,0:T(8,128)(2,1)S(1)}, u32[]{:S(2)}, u32[]{:S(2)}) collective-permute-start(bf16[512,1024]{1,0:T(8,128)(2,1)} %get-tuple-element.126), channel_id=1, source_target_pairs={{0,1},{1,0},{2,3},{3,2},{4,5},{5,4},{6,7},{7,6},{8,9},{9,8},{10,11... | collective-permute-start | bytes 3145736 | tf_op jit(solution)/shard_map/ppermute | solution.py:373
  279.4 35.0 %collective-permute-start.39 = (bf16[4,96,1024]{2,1,0:T(8,128)(2,1)}, bf16[4,96,1024]{2,1,0:T(8,128)(2,1)}, u32[]{:S(2)}, u32[]{:S(2)}) collective-permute-start(bf16[4,96,1024]{2,1,0:T(8,128)(2,1)} %dynamic-slice_bitcast_fusion.1), channel_id=1, source_target_pairs={{0,4},{4,0},{8,12},{12,8},{16,20},{20,16},{24,28},{28,24},{1,5},{5... | collective-permute-start | bytes 2359304 | tf_op jit(solution)/shard_map/ppermute | solution.py:373
  283.4 24.5 %collective-permute-start.35 = (bf16[512,1024]{1,0:T(8,128)(2,1)S(1)}, bf16[512,1024]{1,0:T(8,128)(2,1)S(1)}, u32[]{:S(2)}, u32[]{:S(2)}) collective-permute-start(bf16[512,1024]{1,0:T(8,128)(2,1)S(1)} %add_convert_fusion.4), channel_id=1, source_target_pairs={{0,2},{1,3},{2,0},{3,1},{4,6},{5,7},{6,4},{7,5},{8,10},{9,11},{10,... | collective-permute-start | bytes 3145736 | tf_op jit(solution)/shard_map/ppermute | solution.py:373
  290.3 42.1 %collective-permute-start.38 = (bf16[4,128,1536]{2,1,0:T(8,128)(2,1)}, bf16[4,128,1536]{2,1,0:T(8,128)(2,1)}, u32[]{:S(2)}, u32[]{:S(2)}) collective-permute-start(bf16[4,128,1536]{2,1,0:T(8,128)(2,1)} %dynamic-slice_bitcast_fusion), channel_id=1, source_target_pairs={{0,4},{4,0},{8,12},{12,8},{16,20},{20,16},{24,28},{28,24},{1,5},{5... | collective-permute-start | bytes 4718600 | tf_op jit(solution)/shard_map/ppermute | solution.py:373
  311.8 20.7 %collective-permute-start.37 = (bf16[512,1024]{1,0:T(8,128)(2,1)}, bf16[512,1024]{1,0:T(8,128)(2,1)}, u32[]{:S(2)}, u32[]{:S(2)}) collective-permute-start(bf16[512,1024]{1,0:T(8,128)(2,1)} %get-tuple-element.182.branch_first_ref), channel_id=1, source_target_pairs={{0,1},{1,0},{2,3},{3,2},{4,5},{5,4},{6,7},{7,6},{8,9},{9,8},{10,11... | collective-permute-start | bytes 3145736 | tf_op jit(solution)/shard_map/ppermute | solution.py:373
  313.0 51.4 %collective-permute-start.36 = (bf16[512,1024]{1,0:T(8,128)(2,1)}, bf16[512,1024]{1,0:T(8,128)(2,1)}, u32[]{:S(2)}, u32[]{:S(2)}) collective-permute-start(bf16[512,1024]{1,0:T(8,128)(2,1)} %get-tuple-element.182.branch_first_ref), channel_id=1, source_target_pairs={{0,2},{1,3},{2,0},{3,1},{4,6},{5,7},{6,4},{7,5},{8,10},{9,11},{10,... | collective-permute-start | bytes 3145736 | tf_op jit(solution)/shard_map/ppermute | solution.py:373
  314.1 57.0 %collective-permute-start.32 = (bf16[512,1024]{1,0:T(8,128)(2,1)}, bf16[512,1024]{1,0:T(8,128)(2,1)}, u32[]{:S(2)}, u32[]{:S(2)}) collective-permute-start(bf16[512,1024]{1,0:T(8,128)(2,1)} %get-tuple-element.124), channel_id=1, source_target_pairs={{0,1},{1,0},{2,3},{3,2},{4,5},{5,4},{6,7},{7,6},{8,9},{9,8},{10,11... | collective-permute-start | bytes 3145736 | tf_op jit(solution)/shard_map/ppermute | solution.py:373
  317.0 47.3 %collective-permute-start.40 = (bf16[96,1024]{1,0:T(8,128)(2,1)S(1)}, bf16[96,1024]{1,0:T(8,128)(2,1)S(1)}, u32[]{:S(2)}, u32[]{:S(2)}) collective-permute-start(bf16[96,1024]{1,0:T(8,128)(2,1)S(1)} %get-tuple-element.199), channel_id=1, source_target_pairs={{0,8},{4,12},{8,16},{12,20},{16,24},{20,28},{24,0},{28,4},{1,9},{5... | collective-permute-start | bytes 589832 | tf_op jit(solution)/shard_map/ppermute | solution.py:392
  332.4 31.9 %collective-permute-start.41 = (bf16[96,1024]{1,0:T(8,128)(2,1)S(1)}, bf16[96,1024]{1,0:T(8,128)(2,1)S(1)}, u32[]{:S(2)}, u32[]{:S(2)}) collective-permute-start(bf16[96,1024]{1,0:T(8,128)(2,1)S(1)} %get-tuple-element.198), channel_id=1, source_target_pairs={{0,16},{4,20},{8,24},{12,28},{16,0},{20,4},{24,8},{28,12},{1,17},{... | collective-permute-start | bytes 589832 | tf_op jit(solution)/shard_map/ppermute | solution.py:392
  332.5 31.8 %collective-permute-start.42 = (bf16[96,1024]{1,0:T(8,128)(2,1)S(1)}, bf16[96,1024]{1,0:T(8,128)(2,1)S(1)}, u32[]{:S(2)}, u32[]{:S(2)}) collective-permute-start(bf16[96,1024]{1,0:T(8,128)(2,1)S(1)} %get-tuple-element.197), channel_id=1, source_target_pairs={{0,24},{4,28},{8,0},{12,4},{16,8},{20,12},{24,16},{28,20},{1,25},{... | collective-permute-start | bytes 589832 | tf_op jit(solution)/shard_map/ppermute | solution.py:392
  365.1 9.2 %collective-permute-start.43 = (bf16[512,1024]{1,0:T(8,128)(2,1)}, bf16[512,1024]{1,0:T(8,128)(2,1)}, u32[]{:S(2)}, u32[]{:S(2)}) collective-permute-start(bf16[512,1024]{1,0:T(8,128)(2,1)} %collective-permute-done.36.branch_first_ref), channel_id=1, source_target_pairs={{0,1},{1,0},{2,3},{3,2},{4,5},{5,4},{6,7},{7,6},{8,9},{9,8},{10,11... | collective-permute-start | bytes 3145736 | tf_op jit(solution)/shard_map/ppermute | solution.py:373
  366.4 27.8 %collective-permute-start.44 = (bf16[128,1536]{1,0:T(8,128)(2,1)S(1)}, bf16[128,1536]{1,0:T(8,128)(2,1)S(1)}, u32[]{:S(2)}, u32[]{:S(2)}) collective-permute-start(bf16[128,1536]{1,0:T(8,128)(2,1)S(1)} %get-tuple-element.188), channel_id=1, source_target_pairs={{0,8},{4,12},{8,16},{12,20},{16,24},{20,28},{24,0},{28,4},{1,9},{5... | collective-permute-start | bytes 1179656 | tf_op jit(solution)/shard_map/ppermute | solution.py:392
  370.0 35.1 %collective-permute-start.45 = (bf16[128,1536]{1,0:T(8,128)(2,1)S(1)}, bf16[128,1536]{1,0:T(8,128)(2,1)S(1)}, u32[]{:S(2)}, u32[]{:S(2)}) collective-permute-start(bf16[128,1536]{1,0:T(8,128)(2,1)S(1)} %get-tuple-element.187), channel_id=1, source_target_pairs={{0,16},{4,20},{8,24},{12,28},{16,0},{20,4},{24,8},{28,12},{1,17},{... | collective-permute-start | bytes 1179656 | tf_op jit(solution)/shard_map/ppermute | solution.py:392
  370.5 34.6 %collective-permute-start.46 = (bf16[128,1536]{1,0:T(8,128)(2,1)S(1)}, bf16[128,1536]{1,0:T(8,128)(2,1)S(1)}, u32[]{:S(2)}, u32[]{:S(2)}) collective-permute-start(bf16[128,1536]{1,0:T(8,128)(2,1)S(1)} %get-tuple-element.186), channel_id=1, source_target_pairs={{0,24},{4,28},{8,0},{12,4},{16,8},{20,12},{24,16},{28,20},{1,25},{... | collective-permute-start | bytes 1179656 | tf_op jit(solution)/shard_map/ppermute | solution.py:392
  371.1 105.9 %collective-permute-start.29 = (bf16[512,1024]{1,0:T(8,128)(2,1)}, bf16[512,1024]{1,0:T(8,128)(2,1)}, u32[]{:S(2)}, u32[]{:S(2)}) collective-permute-start(bf16[512,1024]{1,0:T(8,128)(2,1)} %get-tuple-element.120), channel_id=1, source_target_pairs={{0,1},{1,0},{2,3},{3,2},{4,5},{5,4},{6,7},{7,6},{8,9},{9,8},{10,11... | collective-permute-start | bytes 3145736 | tf_op jit(solution)/shard_map/ppermute | solution.py:373
  405.3 16.5 %collective-permute-start.49 = (bf16[32,1536]{1,0:T(8,128)(2,1)S(1)}, bf16[32,1536]{1,0:T(8,128)(2,1)S(1)}, u32[]{:S(2)}, u32[]{:S(2)}) collective-permute-start(bf16[32,1536]{1,0:T(8,128)(2,1)S(1)} %get-tuple-element.222), channel_id=1, source_target_pairs={{0,1},{1,0},{2,3},{3,2},{4,5},{5,4},{6,7},{7,6},{8,9},{9,8},{10,11... | collective-permute-start | bytes 294920 | tf_op jit(solution)/shard_map/ppermute | solution.py:373
  406.2 15.7 %collective-permute-start.50 = (bf16[32,1536]{1,0:T(8,128)(2,1)S(1)}, bf16[32,1536]{1,0:T(8,128)(2,1)S(1)}, u32[]{:S(2)}, u32[]{:S(2)}) collective-permute-start(bf16[32,1536]{1,0:T(8,128)(2,1)S(1)} %get-tuple-element.221), channel_id=1, source_target_pairs={{0,2},{1,3},{2,0},{3,1},{4,6},{5,7},{6,4},{7,5},{8,10},{9,11},{10,... | collective-permute-start | bytes 294920 | tf_op jit(solution)/shard_map/ppermute | solution.py:373
  406.2 15.7 %collective-permute-start.51 = (bf16[32,1536]{1,0:T(8,128)(2,1)S(1)}, bf16[32,1536]{1,0:T(8,128)(2,1)S(1)}, u32[]{:S(2)}, u32[]{:S(2)}) collective-permute-start(bf16[32,1536]{1,0:T(8,128)(2,1)S(1)} %get-tuple-element.220), channel_id=1, source_target_pairs={{0,3},{1,2},{2,1},{3,0},{4,7},{5,6},{6,5},{7,4},{8,11},{9,10},{10,... | collective-permute-start | bytes 294920 | tf_op jit(solution)/shard_map/ppermute | solution.py:373
  408.1 14.0 %collective-permute-start.48 = (bf16[4,64,1024]{2,1,0:T(8,128)(2,1)S(1)}, bf16[4,64,1024]{2,1,0:T(8,128)(2,1)S(1)}, u32[]{:S(2)}, u32[]{:S(2)}) collective-permute-start(bf16[4,64,1024]{2,1,0:T(8,128)(2,1)S(1)} %dynamic-slice_bitcast_fusion.2), channel_id=1, source_target_pairs={{0,4},{4,0},{8,12},{12,8},{16,20},{20,16},{24,28},{28,24},{1,5},{5... | collective-permute-start | bytes 1572872 | tf_op jit(solution)/shard_map/ppermute | solution.py:373
  421.8 54.9 %collective-permute-start.47 = (bf16[512,1024]{1,0:T(8,128)(2,1)}, bf16[512,1024]{1,0:T(8,128)(2,1)}, u32[]{:S(2)}, u32[]{:S(2)}) collective-permute-start(bf16[512,1024]{1,0:T(8,128)(2,1)} %add_convert_fusion.5), channel_id=1, source_target_pairs={{0,2},{1,3},{2,0},{3,1},{4,6},{5,7},{6,4},{7,5},{8,10},{9,11},{10,... | collective-permute-start | bytes 3145736 | tf_op jit(solution)/shard_map/ppermute | solution.py:373
  428.0 39.9 %collective-permute-start.56 = (bf16[64,1024]{1,0:T(8,128)(2,1)}, bf16[64,1024]{1,0:T(8,128)(2,1)}, u32[]{:S(2)}, u32[]{:S(2)}) collective-permute-start(bf16[64,1024]{1,0:T(8,128)(2,1)} %get-tuple-element.203), channel_id=1, source_target_pairs={{0,8},{4,12},{8,16},{12,20},{16,24},{20,28},{24,0},{28,4},{1,9},{5... | collective-permute-start | bytes 393224 | tf_op jit(solution)/shard_map/ppermute | solution.py:392
  436.0 31.8 %collective-permute-start.55 = (bf16[4,144,1024]{2,1,0:T(8,128)(2,1)S(1)}, bf16[4,144,1024]{2,1,0:T(8,128)(2,1)S(1)}, u32[]{:S(2)}, u32[]{:S(2)}) collective-permute-start(bf16[4,144,1024]{2,1,0:T(8,128)(2,1)S(1)} %fusion.13), channel_id=1, source_target_pairs={{0,4},{4,0},{8,12},{12,8},{16,20},{20,16},{24,28},{28,24},{1,5},{5... | collective-permute-start | bytes 3538952 | tf_op jit(solution)/shard_map/ppermute | solution.py:373
  440.5 25.0 %collective-permute-start.66 = (bf16[96,1024]{1,0:T(8,128)(2,1)S(1)}, bf16[96,1024]{1,0:T(8,128)(2,1)S(1)}, u32[]{:S(2)}, u32[]{:S(2)}) collective-permute-start(bf16[96,1024]{1,0:T(8,128)(2,1)S(1)} %add_convert_fusion.9), channel_id=1, source_target_pairs={{0,0},{4,1},{8,2},{12,3},{16,4},{20,5},{24,6},{28,7},{1,8},{5,9},{... | collective-permute-start | bytes 589832 | tf_op jit(solution)/shard_map/ppermute | solution.py:1239
  465.4 38.0 %collective-permute-start.54 = (bf16[512,1024]{1,0:T(8,128)(2,1)S(1)}, bf16[512,1024]{1,0:T(8,128)(2,1)S(1)}, u32[]{:S(2)}, u32[]{:S(2)}) collective-permute-start(bf16[512,1024]{1,0:T(8,128)(2,1)S(1)} %add_convert_fusion.2), channel_id=1, source_target_pairs={{0,2},{1,3},{2,0},{3,1},{4,6},{5,7},{6,4},{7,5},{8,10},{9,11},{10,... | collective-permute-start | bytes 3145736 | tf_op jit(solution)/shard_map/ppermute | solution.py:373
  476.8 32.8 %collective-permute-start.52 = (bf16[512,1024]{1,0:T(8,128)(2,1)S(1)}, bf16[512,1024]{1,0:T(8,128)(2,1)S(1)}, u32[]{:S(2)}, u32[]{:S(2)}) collective-permute-start(bf16[512,1024]{1,0:T(8,128)(2,1)S(1)} %convolution_convert_fusion.2), channel_id=1, source_target_pairs={{0,1},{1,0},{2,3},{3,2},{4,5},{5,4},{6,7},{7,6},{8,9},{9,8},{10,11... | collective-permute-start | bytes 3145736 | tf_op jit(solution)/shard_map/ppermute | solution.py:373
  476.9 9.4 %collective-permute-start.59 = (bf16[144,1024]{1,0:T(8,128)(2,1)S(1)}, bf16[144,1024]{1,0:T(8,128)(2,1)S(1)}, u32[]{:S(2)}, u32[]{:S(2)}) collective-permute-start(bf16[144,1024]{1,0:T(8,128)(2,1)S(1)} %get-tuple-element.192), channel_id=1, source_target_pairs={{0,8},{4,12},{8,16},{12,20},{16,24},{20,28},{24,0},{28,4},{1,9},{5... | collective-permute-start | bytes 884744 | tf_op jit(solution)/shard_map/ppermute | solution.py:392
  476.9 26.5 %collective-permute-start.60 = (bf16[144,1024]{1,0:T(8,128)(2,1)S(1)}, bf16[144,1024]{1,0:T(8,128)(2,1)S(1)}, u32[]{:S(2)}, u32[]{:S(2)}) collective-permute-start(bf16[144,1024]{1,0:T(8,128)(2,1)S(1)} %get-tuple-element.191), channel_id=1, source_target_pairs={{0,16},{4,20},{8,24},{12,28},{16,0},{20,4},{24,8},{28,12},{1,17},{... | collective-permute-start | bytes 884744 | tf_op jit(solution)/shard_map/ppermute | solution.py:392
  477.1 26.3 %collective-permute-start.61 = (bf16[144,1024]{1,0:T(8,128)(2,1)S(1)}, bf16[144,1024]{1,0:T(8,128)(2,1)S(1)}, u32[]{:S(2)}, u32[]{:S(2)}) collective-permute-start(bf16[144,1024]{1,0:T(8,128)(2,1)S(1)} %get-tuple-element.190), channel_id=1, source_target_pairs={{0,24},{4,28},{8,0},{12,4},{16,8},{20,12},{24,16},{28,20},{1,25},{... | collective-permute-start | bytes 884744 | tf_op jit(solution)/shard_map/ppermute | solution.py:392
  503.7 9.3 %collective-permute-start.62 = (bf16[48,1024]{1,0:T(8,128)(2,1)S(1)}, bf16[48,1024]{1,0:T(8,128)(2,1)S(1)}, u32[]{:S(2)}, u32[]{:S(2)}) collective-permute-start(bf16[48,1024]{1,0:T(8,128)(2,1)S(1)} %get-tuple-element.212), channel_id=1, source_target_pairs={{0,1},{1,0},{2,3},{3,2},{4,5},{5,4},{6,7},{7,6},{8,9},{9,8},{10,11... | collective-permute-start | bytes 294920 | tf_op jit(solution)/shard_map/ppermute | solution.py:373
  507.0 11.5 %collective-permute-start.65 = (bf16[64,1024]{1,0:T(8,128)(2,1)S(1)}, bf16[64,1024]{1,0:T(8,128)(2,1)S(1)}, u32[]{:S(2)}, u32[]{:S(2)}) collective-permute-start(bf16[64,1024]{1,0:T(8,128)(2,1)S(1)} %add_convert_fusion.10), channel_id=1, source_target_pairs={{0,0},{4,1},{8,2},{12,3},{16,4},{20,5},{24,6},{28,7},{1,8},{5,9},{... | collective-permute-start | bytes 393224 | tf_op jit(solution)/shard_map/ppermute | solution.py:1238
  (82 other events, 847.7 us)
Sparse Core Ops, SparseCore 0:
  98.4 70.8 all-gather.1

commit v6 on v5

--- a/solution.py
+++ b/solution.py
@@ -363,7 +363,6 @@
 MASK_DEPTH = -4096.0
 LOG2_E = 1.4426950408889634
 VMEM_BYTES = 56 * 1024 * 1024
-SMALL_COST = pl.CostEstimate(flops=1, bytes_accessed=1, transcendentals=0)
 bf16 = jnp.bfloat16
 f32 = jnp.float32
 
@@ -432,11 +431,6 @@
     )(places.astype(jnp.int32), *pieces)
 
 
-def join(blocks):
-    joined = assemble([block[None] for block in blocks], jnp.arange(len(blocks)))[0]
-    return joined.reshape(-1, joined.shape[-1])
-
-
 def gather_along(value):
     return [value] + [shift_z(value, k) for k in range(1, lax.axis_size("dp") // 2)]
 
@@ -458,13 +452,17 @@
     return [result.reshape(-1, result.shape[-1]) for result in results]
 
 
-def reduce_beside(grad):
+def send_beside(grad):
     depth = grad.shape[0] // 2
     y = lax.axis_index("dp") % 2
     grad = grad.reshape((depth, 2) + grad.shape[1:])
     away = lax.dynamic_index_in_dim(grad, 1 - y, 1, keepdims=False)
     kept = lax.dynamic_index_in_dim(grad, y, 1, keepdims=False)
-    return (kept.astype(f32) + xor_permute(away, "dp", 1).astype(f32)).astype(bf16)
+    return kept, away, xor_permute(away, "dp", 1)
+
+
+def add_beside(kept, away, arrived):
+    return (kept.astype(f32) + arrived.astype(f32)).astype(bf16)
 
 
 def reduce_along(pair):
@@ -921,7 +919,11 @@
             jax.ShapeDtypeStruct(out.shape, f32),
         ],
         compiler_params=pltpu.CompilerParams(vmem_limit_bytes=VMEM_BYTES),
-        cost_estimate=SMALL_COST,
+        cost_estimate=pl.CostEstimate(
+            flops=70 * count * block * rows * key_heads * group * HEAD_SIZE // 8,
+            bytes_accessed=20 * q.size,
+            transcendentals=0,
+        ),
         name="unattend",
     )(me, q, qf, k, kf, v, o, *branches, out, logs, *earlier)
 
@@ -931,10 +933,12 @@
     half,
     first_ref,
     second_ref,
-    cot_ref,
+    cot_first_ref,
+    cot_second_ref,
     both_ref,
     down_ref,
     h_ref,
+    cot_ref,
     hidden_ref,
     d_both_ref,
     part_first_ref,
@@ -947,10 +951,12 @@
     @pl.when(in_first)
     def _():
         h_ref[...] = first_ref[...]
+        cot_ref[...] = cot_first_ref[...]
 
     @pl.when(jnp.logical_not(in_first))
     def _():
         h_ref[...] = second_ref[...]
+        cot_ref[...] = cot_second_ref[...]
 
     both = nn_dot(h_ref[...], both_ref[...])
     d_hidden = nt_dot(cot_ref[...], down_ref[...])
@@ -977,8 +983,8 @@
         d_part_second_ref[...] = d_part
 
 
-def feed(h_first, h_second, cot, both, down):
-    rows, width = cot.shape
+def feed(h_first, h_second, cot_first, cot_second, both, down):
+    rows, width = 2 * cot_first.shape[0], cot_first.shape[1]
     units = down.shape[0]
     block = 256
     half = rows // block // 2
@@ -991,12 +997,12 @@
 
     of_first = pl.BlockSpec((block, width), lambda i: (jnp.minimum(i, half - 1), 0))
     of_second = pl.BlockSpec((block, width), lambda i: (jnp.maximum(i - half, 0), 0))
-    shapes = [(rows, width), (rows, units), (rows, 2 * units)] + [(rows // 2, width)] * 4
+    shapes = [(rows, width), (rows, width), (rows, units), (rows, 2 * units)] + [(rows // 2, width)] * 4
     return pl.pallas_call(
         functools.partial(feed_kernel, units, half),
         grid=(rows // block,),
-        in_specs=[of_first, of_second, tall(width), whole(both.shape), whole(down.shape)],
-        out_specs=[tall(width), tall(units), tall(2 * units)] + [of_first, of_second] * 2,
+        in_specs=[of_first, of_second] * 2 + [whole(both.shape), whole(down.shape)],
+        out_specs=[tall(width), tall(width), tall(units), tall(2 * units)] + [of_first, of_second] * 2,
         out_shape=[jax.ShapeDtypeStruct(shape, bf16) for shape in shapes],
         compiler_params=pltpu.CompilerParams(vmem_limit_bytes=VMEM_BYTES),
         cost_estimate=pl.CostEstimate(
@@ -1005,7 +1011,7 @@
             transcendentals=rows * units,
         ),
         name="feed",
-    )(h_first, h_second, cot, both, down)
+    )(h_first, h_second, cot_first, cot_second, both, down)
 
 
 def norm_back(value_rows, gain_vec, grad):
@@ -1078,11 +1084,11 @@
     x_own = tokens.reshape(block, MODEL_WIDTH)
     x_near, across = gather_near(after(x_own, *arrived))
     x_blocks = x_near + gather_far(across, first_stacks[0])
+
+    moved_along = gather_along(after(moved, first_stacks[0], x_near[1]))
+    first_stacks = [first_stacks[0], after(first_stacks[1], *moved_along[1:])]
     cot_own = cotangent.reshape(block, MODEL_WIDTH)
-    cot_blocks = gather_blocks(after(cot_own, first_stacks[1]))
-    cot_near, cot_far = join(cot_blocks[:2]), join(cot_blocks[2:])
-
-    moved_along = gather_along(after(moved, *first_along[1:]))
+    cot_near, cot_across = gather_near(after(cot_own, first_stacks[1]))
     moved_stacks = gather_beside(moved_along, first_stacks[1])
     gate_up_rows = after(gate_up.reshape(size * owned, -1), *moved_along[1:])
     gate_up = lax.all_gather(gate_up_rows, "dp", axis=0, tiled=True)
@@ -1119,13 +1125,15 @@
     def halves(value):
         return value[:block], value[block:]
 
+    cot_blocks = cot_near + gather_far(cot_across, q)
     att_far, logs_far = attend_half(q, 2)
-    att_far, *moved_stacks = lax.optimization_barrier((att_far, *moved_stacks))
+    att_far, *both = lax.optimization_barrier((att_far, *moved_stacks, *cot_blocks))
+    moved_stacks, cot_blocks = both[:2], both[2:]
     out_full, down_full = interleave(moved_stacks, (w_out.shape[0], w_down.shape[0]))
     att_across, att_corner = halves(att_far)
     part_corner, part_across = nn_dot(att_corner, out_full), nn_dot(att_across, out_full)
     toward, across = send_across(part_corner, part_across)
-    att_near, logs_near = attend_half(after(q, toward, cot_near, cot_far), 0)
+    att_near, logs_near = attend_half(after(q, toward), 0)
     att_near = after(att_near, gate_up)
     att_own, att_beside = halves(att_near)
     beside = [
@@ -1135,15 +1143,16 @@
     part_own = nn_dot(att_own, out_full) + jnp.concatenate(beside).astype(f32)
     middle = x_own.astype(f32) + part_own + across.astype(f32)
     h_blocks, across = gather_near(row_norm_apply(middle, gain_mlp).astype(bf16))
-    h_near, hidden_near, d_both_near, down_own, down_beside, d_own, d_beside = feed(
-        *h_blocks, cot_near, gate_up, down_full
+    h_near, cot_near, hidden_near, d_both_near, down_own, down_beside, d_own, d_beside = feed(
+        *h_blocks, *cot_blocks[:2], gate_up, down_full
     )
     h_blocks = gather_far(across, hidden_near)
-    h_far, hidden_far, d_both_far, down_across, down_corner, d_across, d_corner = feed(
-        *h_blocks, cot_far, gate_up, down_full
-    )
-
-    unused, across = send_across(d_corner, d_across)
+    h_far, cot_far, hidden_far, d_both_far, down_across, down_corner, d_across, d_corner = feed(
+        *h_blocks, *cot_blocks[2:], gate_up, down_full
+    )
+
+    toward, across = send_across(d_corner, d_across)
+    d_both_far, cot_far = lax.optimization_barrier((d_both_far, cot_far, toward))[:2]
     grad_down = (tn_dot(hidden_near, cot_near) + tn_dot(hidden_far, cot_far)).astype(bf16)
     grad_both = (tn_dot(h_near, d_both_near) + tn_dot(h_far, d_both_far)).astype(bf16)
     d_normed = sum_own(d_beside, d_own, after(across, grad_down, grad_both))
@@ -1151,8 +1160,9 @@
     d_middle = d_middle + cot_own.astype(f32)
     branches_near, branch_across = gather_near(d_middle.astype(bf16))
 
-    pair_both = reduce_beside(by_copy(grad_both))
-    pair_down = reduce_beside(by_copy(grad_down))
+    grad_down = grad_down.reshape(copies, -1, 2 * hidden_cols)
+    grad_feed = jnp.concatenate([by_copy(grad_both), grad_down], axis=1)
+    pair_feed = add_beside(*send_beside(grad_feed))
 
     def unattend_half(att, branches, logs, first, earlier=()):
         return unattend(
@@ -1173,32 +1183,20 @@
         )
 
     dq_near, *earlier = unattend_half(att_near, branches_near, logs_near, 0)
-    terms_down = reduce_along(pair_down)
-    dq_near, pair_both, *terms_down = lax.optimization_barrier((dq_near, pair_both, *terms_down))
-    terms_both = reduce_along(pair_both)
+    dq_near, pair_feed = lax.optimization_barrier((dq_near, pair_feed))
+    terms_both = reduce_along(pair_feed[:, : size * owned])
     branches_far = gather_far(branch_across, dq_near)
     dq_far, dk, dv, grad_out = unattend_half(att_far, branches_far, logs_far, 2, earlier)
-    pair_out = reduce_beside(by_copy(grad_out))
+    pair_out = add_beside(*send_beside(by_copy(grad_out)))
     dk, *terms_both = lax.optimization_barrier((dk, *terms_both))
+    terms_down = reduce_along(after(pair_feed[:, size * owned :], dk))
     unused, down_across = send_across(down_corner, down_across, dk)
-    grad_both = exchange(add_all(terms_both).reshape(size, owned, -1), me)[0]
     low, d_gain_heads = unproject(
         dq_near, dq_far, dk, dv, raw, cosine, sine, gain_q_row, gain_k_row, query_heads, key_heads
     )
-    low, d_gain_heads, pair_out, grad_both = lax.optimization_barrier(
-        (low, d_gain_heads, pair_out, grad_both)
-    )
-    terms_down = after_all(terms_down, low)
-    terms_out = reduce_along(after(pair_out, low))
-    low_own, low_beside, low_across, low_corner = (
-        low[r * block : (r + 1) * block] for r in range(size)
-    )
-    toward, across = send_across(nt_dot(low_corner, w_first), nt_dot(low_across, w_first))
-    part_beside, part_own = nt_dot(low_beside, w_first), nt_dot(low_own, w_first)
-    d_normed_attn = sum_own(part_beside, part_own, across)
-    d_inputs, unused = norm_back(x_own.astype(f32), gain_attn, d_normed_attn)
-    grad_tokens = (d_middle + d_inputs).reshape(tokens.shape)
-
+    low, d_gain_heads, pair_out, *terms_down = lax.optimization_barrier(
+        (low, d_gain_heads, pair_out, *terms_down)
+    )
     grad_first = tn_dot(normed, low).astype(bf16)
     d_gain_attn = jnp.sum(w_first.astype(f32) * grad_first.astype(f32), axis=1) / gain_attn
     grad_gains = jnp.concatenate(
@@ -1211,7 +1209,22 @@
     grad_first = jnp.concatenate(
         [grad_first.reshape(copies, size * owned, -1), gain_block], axis=1
     )
-    pair_first = after(reduce_beside(grad_first), *terms_out, down_across)
+    first_sent = send_beside(grad_first)
+    low = after(low, first_sent[1])
+    low_own, low_beside, low_across, low_corner = (
+        low[r * block : (r + 1) * block] for r in range(size)
+    )
+    toward, across = send_across(nt_dot(low_corner, w_first), nt_dot(low_across, w_first))
+    part_beside, part_own = nt_dot(low_beside, w_first), nt_dot(low_own, w_first)
+    d_normed_attn = sum_own(part_beside, part_own, across)
+    d_inputs, unused = norm_back(x_own.astype(f32), gain_attn, d_normed_attn)
+    grad_tokens = (d_middle + d_inputs).reshape(tokens.shape)
+
+    terms_out = reduce_along(after(pair_out, toward))
+    grad_both = add_all(after_all(terms_both, toward)).reshape(size, owned, -1)
+    grad_both = exchange(grad_both, me)[0].astype(f32)
+    grad_down = add_all(after_all(terms_down, toward)).reshape(w_down.shape)
+    pair_first = after(add_beside(*first_sent), *terms_out, down_across)
     output = sum_own(down_beside, down_own, down_across)
     output = (middle + output).astype(bf16)
     terms_first = lax.optimization_barrier((*reduce_along(pair_first), across))[:-1]
@@ -1232,11 +1245,10 @@
     grad_query = to_rows(grad_first[:, :, :q_cols])
     grad_key = to_rows(grad_first[:, :, q_cols : q_cols + k_cols])
     grad_value = to_rows(grad_first[:, :, q_cols + k_cols :])
-    grad_both = grad_both.astype(f32)
     grad_gate = to_rows(grad_both[:, :, :hidden_cols])
     grad_up = to_rows(grad_both[:, :, hidden_cols:])
     grad_out = lax.ppermute(grad_out, ("dp", "ctx"), backward_owner).astype(f32)
-    grad_down = lax.ppermute(add_all(terms_down), ("dp", "ctx"), backward_owner).astype(f32)
+    grad_down = lax.ppermute(grad_down, ("dp", "ctx"), backward_owner).astype(f32)
     return (
         output.reshape(tokens.shape),
         grad_tokens,

time: 535 us -> 522 us (0.976)
  waiting for transfers between devices: 188 us -> 138 us
  starting transfers between devices: 75.4 us -> 95 us
  other arithmetic: 39.1 us -> 49.6 us
  matrix products: 36.7 us -> 45.1 us
    ppermute x46 -> x45, starting transfers between devices: 35 us -> 61 us  [xor_permute(): return lax.ppermute(value, axis, [(i, i ^ offset) for i in range(size)])]
    ppermute x46 -> x45, waiting for transfers between devices: 84.4 us -> 66.1 us  [xor_permute(): return lax.ppermute(value, axis, [(i, i ^ offset) for i in range(size)])]
    ppermute x18, waiting for transfers between devices: 80.5 us -> 63 us  [shift_z(): lax.ppermute(value, 'dp', [(i, (i + 2 * offset) % size) for i in range(si...]
    ppermute x1, waiting for transfers between devices: 20 us -> 8.71 us  [split_local(): lax.ppermute(grad_down, ('dp', 'ctx'), backward_owner).astype(f32)]
    dot_general x5, matrix products: 18.9 us -> 27.2 us  [tn_dot(): lax.dot_general(left, right, (((0,), (0,)), ((), ())), preferred_element_...]
    ppermute x18, starting transfers between devices: 30.2 us -> 23.4 us  [shift_z(): lax.ppermute(value, 'dp', [(i, (i + 2 * offset) % size) for i in range(si...]
    pallas_call x6 -> x4, Pallas kernels: 17.1 us -> 11.3 us  [assemble(): pl.pallas_call(functools.partial(assemble_kernel, splits, len(pieces)), i...]
  transfers between devices with their start and end apart: 68 -> 67, of which waited for: 22 -> 23; matrix products, arithmetic and copies ran while one was open for 16% -> 20% of each run, Pallas kernels for 29% -> 25%
where the time goes in v6:
time: 522 us; the launch traced here: 513 us
  Pallas kernels  146 us (28%)
  waiting for transfers between devices  138 us (26%)
  starting transfers between devices  95 us (18%)
  other arithmetic  49.6 us (10%)
  matrix products  45.1 us (9%)
  local copies, waits for them, and re-layouts  23.8 us (5%)
  between operations  15.7 us (3%)
    ppermute x45, waiting for transfers between devices, xor_permute(): return lax.ppermute(value, axis, [(i, i ^ offset) for i in range(size)])  66.1 us
    ppermute x18, waiting for transfers between devices, shift_z(): lax.ppermute(value, 'dp', [(i, (i + 2 * offset) % size) for i in range(si...  63 us
    ppermute x45, starting transfers between devices, xor_permute(): return lax.ppermute(value, axis, [(i, i ^ offset) for i in range(size)])  61 us
    pallas_call x2, Pallas kernels, unattend(): pl.pallas_call(functools.partial(unattend_kernel, group, block, first, bo...  49.5 us
    pallas_call x2, Pallas kernels, feed(): pl.pallas_call(functools.partial(feed_kernel, units, half), grid=(rows //...  34.2 us
    dot_general x5, matrix products, tn_dot(): lax.dot_general(left, right, (((0,), (0,)), ((), ())), preferred_element_...  27.2 us
    ppermute x18, starting transfers between devices, shift_z(): lax.ppermute(value, 'dp', [(i, (i + 2 * offset) % size) for i in range(si...  23.4 us
    pallas_call x2, Pallas kernels, attend(): pl.pallas_call(functools.partial(attend_kernel, group, block, first), gri...  23.2 us
  transfers between devices with their start and end apart: 67, of which 23 were waited for; matrix products, arithmetic and copies ran while one was open for 20% of the time, Pallas kernels for 25%

profile of v6, /device:TPU:27, one launch (start us, length us, event | category | flops | bytes accessed | tf_op | source)
XLA Modules:
  0.0 512.9 jit_solution(3518152684806504335)
XLA Ops:
  26.9 2.7 collective-permute-done.5
  34.5 2.9 collective-permute-start.13
  37.5 3.6 collective-permute-start.7
  41.2 11.9 %collective-permute-done.9 = bf16[144,1024]{1,0:T(8,128)(2,1)S(1)} collective-permute-done((bf16[144,1024]{1,0:T(8,128)(2,1)S(1)}, bf16[144,1024]{1,0:T(8,128)(2,1)S(1)}, u32[]{:S(2)}, u32[]{:S(2)}) %collective-permute-start.9) | collective-permute-done | bytes 294944 | tf_op jit(solution)/shard_map/ppermute | solution.py:391
  56.2 8.4 %collective-permute-start.12 = (bf16[4,144,1024]{2,1,0:T(8,128)(2,1)}, bf16[4,144,1024]{2,1,0:T(8,128)(2,1)}, u32[]{:S(2)}, u32[]{:S(2)}) collective-permute-start(bf16[4,144,1024]{2,1,0:T(8,128)(2,1)} %assemble.4.refs_0_), channel_id=1, source_target_pairs={{0,4},{4,0},{8,12},{12,8},{16,20},{20,16},{24,28},{28,24},{1,5},{5... | collective-permute-start | bytes 3538952 | tf_op jit(solution)/shard_map/ppermute | solution.py:372
  64.7 3.0 collective-permute-start.15
  67.9 3.5 collective-permute-done.14
  71.4 23.8 %collective-permute-done.15 = bf16[160,1024]{1,0:T(8,128)(2,1)S(1)} collective-permute-done((bf16[160,1024]{1,0:T(8,128)(2,1)S(1)}, bf16[160,1024]{1,0:T(8,128)(2,1)S(1)}, u32[]{:S(2)}, u32[]{:S(2)}) %collective-permute-start.15) | collective-permute-done | bytes 327712 | tf_op jit(solution)/shard_map/ppermute | solution.py:391
  95.2 3.7 fusion.36
  107.9 3.2 assemble.5
  111.9 5.4 %collective-permute-start.20 = (bf16[4,160,1024]{2,1,0:T(8,128)(2,1)S(1)}, bf16[4,160,1024]{2,1,0:T(8,128)(2,1)S(1)}, u32[]{:S(2)}, u32[]{:S(2)}) collective-permute-start(bf16[4,160,1024]{2,1,0:T(8,128)(2,1)S(1)} %copy-done.7), channel_id=1, source_target_pairs={{0,4},{4,0},{8,12},{12,8},{16,20},{20,16},{24,28},{28,24},{1,5},{5... | collective-permute-start | bytes 3932168 | tf_op jit(solution)/shard_map/ppermute | solution.py:372
  118.5 13.8 %project.1 = (bf16[2048,1024]{1,0:T(8,128)(2,1)}, f32[2048,768]{1,0:T(8,128)}, bf16[2048,512]{1,0:T(8,128)(2,1)}, bf16[2048,256]{1,0:T(8,128)(2,1)}, bf16[2048,256]{1,0:T(8,128)(2,1)}) custom-call(bf16[512,1024]{1,0:T(8,128)(2,1)} %bitcast.205, bf16[512,1024]{1,0:T(8,128)(2,1)} %copy-done.53, bf16[512,1024]{1,0:T(8,128)(2,1)} %collective-permute-done.7.x_refs_2_, ...), custom_call_target="tpu_custom_call" | custom-call | flops 4294967296 | bytes 20971520 | tf_op jit(solution)/shard_map/project/pallas_call | solution.py:591
  135.4 8.4 %attend.2 = (bf16[1024,512]{1,0:T(8,128)(2,1)}, f32[2,2,1024]{2,1,0:T(2,128)}) custom-call(s32[1]{0:T(128)} %bitcast.1.me_ref, bf16[2048,512]{1,0:T(8,128)(2,1)} %get-tuple-element.132.q_ref, bf16[2048,128]{1,0:T(8,128)(2,1)} %select_convert_fusion.qf_ref, bf16[2048,256]{1,0:T(8,128)(2,1)} %get-tuple-element.122.k_ref, bf16[2048,128]{1,0:T(8,128)(2,1)} %fusion.31.kf_ref, ...), custom_call_target="tpu_custom_call" | custom-call | flops 5368709120 | bytes 10485760 | tf_op jit(solution)/shard_map/attend/pallas_call | solution.py:758
  143.8 11.8 %collective-permute-done.20.refs_1_ = bf16[4,160,1024]{2,1,0:T(8,128)(2,1)S(1)} collective-permute-done((bf16[4,160,1024]{2,1,0:T(8,128)(2,1)S(1)}, bf16[4,160,1024]{2,1,0:T(8,128)(2,1)S(1)}, u32[]{:S(2)}, u32[]{:S(2)}) %collective-permute-start.20) | collective-permute-done | bytes 1310752 | tf_op jit(solution)/shard_map/ppermute | solution.py:372
  156.6 3.3 assemble.7
  171.1 14.8 %attend.3 = (bf16[1024,512]{1,0:T(8,128)(2,1)}, f32[2,2,1024]{2,1,0:T(2,128)}) custom-call(s32[1]{0:T(128)} %bitcast.1.me_ref, bf16[2048,512]{1,0:T(8,128)(2,1)} %get-tuple-element.132.q_ref, bf16[2048,128]{1,0:T(8,128)(2,1)} %select_convert_fusion.qf_ref, bf16[2048,256]{1,0:T(8,128)(2,1)} %get-tuple-element.122.k_ref, bf16[2048,128]{1,0:T(8,128)(2,1)} %fusion.31.kf_ref, ...), custom_call_target="tpu_custom_call" | custom-call | flops 5368709120 | bytes 10485760 | tf_op jit(solution)/shard_map/attend/pallas_call | solution.py:758
  190.3 4.3 collective-permute-done.27
  201.1 17.4 %feed.2 = (bf16[1024,1024]{1,0:T(8,128)(2,1)}, bf16[1024,1024]{1,0:T(8,128)(2,1)}, bf16[1024,768]{1,0:T(8,128)(2,1)}, bf16[1024,1536]{1,0:T(8,128)(2,1)}, bf16[5...) custom-call(bf16[512,1024]{1,0:T(8,128)(2,1)} %copy-done.17, ...), custom_call_target="tpu_custom_call" | custom-call | flops 9663676416 | bytes 19922944 | tf_op jit(solution)/shard_map/feed/pallas_call | solution.py:1001
  218.5 4.1 collective-permute-done.30.first_ref
  226.7 16.8 %feed.3 = (bf16[1024,1024]{1,0:T(8,128)(2,1)}, bf16[1024,1024]{1,0:T(8,128)(2,1)}, bf16[1024,768]{1,0:T(8,128)(2,1)}, bf16[1024,1536]{1,0:T(8,128)(2,1)}, bf16[5...) custom-call(bf16[512,1024]{1,0:T(8,128)(2,1)} %copy-done.55, ...), custom_call_target="tpu_custom_call" | custom-call | flops 9663676416 | bytes 19922944 | tf_op jit(solution)/shard_map/feed/pallas_call | solution.py:1001
  246.6 2.9 add_convert_fusion.4
  251.0 3.4 fusion.52
  254.5 3.2 add_convert_fusion.1
  257.7 3.7 concatenate.69
  261.4 6.2 %fusion.53 = f32[1024,1536]{1,0:T(8,128)S(1)} fusion(bf16[1024,1024]{1,0:T(8,128)(2,1)} %get-tuple-element.157, bf16[1024,1536]{1,0:T(8,128)(2,1)} %get-tuple-element.158), kind=kOutput, calls=%fused_computation.192 | convolution fusion | flops 3221225472 | bytes 11534336 | tf_op jit(solution)/shard_map/dot_general | solution.py:1120
  267.6 4.1 add_convert_fusion
  276.4 3.0 multiply_reduce_fusion.1
  279.5 4.2 fusion.48
  287.2 30.1 %unattend.2 = (f32[1024,512]{1,0:T(8,128)}, f32[2048,256]{1,0:T(8,128)}, f32[2048,256]{1,0:T(8,128)}, f32[512,1024]{1,0:T(8,128)}) custom-call(s32[1]{0:T(128)} %bitcast.1.me_ref, bf16[2048,512]{1,0:T(8,128)(2,1)} %get-tuple-element.132.q_ref, bf16[2048,128]{1,0:T(8,128)(2,1)} %select_convert_fusion.qf_ref, bf16[2048,256]{1,0:T(8,128)(2,1)} %get-tuple-element.122.k_ref, ...), custom_call_target="tpu_custom_call" | custom-call | flops 9395240960 | bytes 20971520 | tf_op jit(solution)/shard_map/unattend/pallas_call | solution.py:890
  317.3 10.4 %collective-permute-done.38 = bf16[4,192,1536]{2,1,0:T(8,128)(2,1)} collective-permute-done((bf16[4,192,1536]{2,1,0:T(8,128)(2,1)}, bf16[4,192,1536]{2,1,0:T(8,128)(2,1)}, u32[]{:S(2)}, u32[]{:S(2)}) %collective-permute-start.38) | collective-permute-done | bytes 2359328 | tf_op jit(solution)/shard_map/ppermute | solution.py:372
  327.7 3.6 fusion
  336.6 19.5 %unattend.3 = (f32[1024,512]{1,0:T(8,128)}, f32[2048,256]{1,0:T(8,128)}, f32[2048,256]{1,0:T(8,128)}, f32[512,1024]{1,0:T(8,128)}) custom-call(s32[1]{0:T(128)} %bitcast.1.me_ref, bf16[2048,512]{1,0:T(8,128)(2,1)} %get-tuple-element.132.q_ref, bf16[2048,128]{1,0:T(8,128)(2,1)} %select_convert_fusion.qf_ref, bf16[2048,256]{1,0:T(8,128)(2,1)} %get-tuple-element.122.k_ref, ...), custom_call_target="tpu_custom_call" | custom-call | flops 9395240960 | bytes 20971520 | tf_op jit(solution)/shard_map/unattend/pallas_call | solution.py:890
  360.9 7.7 %collective-permute-done.41 = bf16[128,1536]{1,0:T(8,128)(2,1)S(1)} collective-permute-done((bf16[128,1536]{1,0:T(8,128)(2,1)}, bf16[128,1536]{1,0:T(8,128)(2,1)S(1)}, u32[]{:S(2)}, u32[]{:S(2)}) %collective-permute-start.41) | collective-permute-done | bytes 393248 | tf_op jit(solution)/shard_map/ppermute | solution.py:391
  369.4 4.1 collective-permute-start.46
  375.0 13.8 %unproject.1 = (bf16[2048,1024]{1,0:T(8,128)(2,1)}, f32[8,128]{1,0:T(8,128)}) custom-call(f32[1024,512]{1,0:T(8,128)} %get-tuple-element.162.dq_near_ref, f32[1024,512]{1,0:T(8,128)} %get-tuple-element.172.dq_far_ref, f32[2048,256]{1,0:T(8,128)} %get-tuple-element.170.dk_ref, f32[2048,256]{1,0:T(8,128)} %get-tuple-element.173.dv_ref, ...), custom_call_target="tpu_custom_call" | custom-call | flops 41943040 | bytes 41943040 | tf_op jit(solution)/shard_map/unproject/pallas_call | solution.py:691
  392.4 10.3 %multiply_reduce_fusion = (f32[1024]{0:T(1024)S(1)}, bf16[1024,1024]{1,0:T(8,128)(2,1)}) fusion(bf16[1024,1024]{1,0:T(8,128)(2,1)} %bitcast.257, bf16[2048,1024]{1,0:T(8,128)(2,1)} %get-tuple-element.180, bf16[2048,1024]{1,0:T(8,128)(2,1)} %get-tuple-element.182), kind=kOutput, calls=%fused_computation.7 | convolution fusion | flops 4300209152 | bytes 12587008 | tf_op jit(solution)/shard_map/dot_general | solution.py:1120
  405.4 2.7 convolution_convert_fusion.1
  413.1 3.3 fusion.19
  422.2 3.2 collective-permute-start.62
  429.0 14.2 %collective-permute-done.63 = bf16[32,1536]{1,0:T(8,128)(2,1)S(1)} collective-permute-done((bf16[32,1536]{1,0:T(8,128)(2,1)S(1)}, bf16[32,1536]{1,0:T(8,128)(2,1)S(1)}, u32[]{:S(2)}, u32[]{:S(2)}) %collective-permute-start.63) | collective-permute-done | bytes 98336 | tf_op jit(solution)/shard_map/ppermute | solution.py:372
  445.0 3.1 collective-permute-done.64
  449.4 4.4 collective-permute-start.65
  456.4 2.7 collective-permute-start.55
  459.2 8.7 %collective-permute-done.65 = bf16[96,1024]{1,0:T(8,128)(2,1)S(1)} collective-permute-done((bf16[96,1024]{1,0:T(8,128)(2,1)S(1)}, bf16[96,1024]{1,0:T(8,128)(2,1)S(1)}, u32[]{:S(2)}, u32[]{:S(2)}) %collective-permute-start.65) | collective-permute-done | bytes 196640 | tf_op jit(solution)/shard_map/ppermute | solution.py:1251
  467.9 4.2 collective-permute-start.57
  474.5 16.2 %collective-permute-done.56 = bf16[144,1024]{1,0:T(8,128)(2,1)S(1)} collective-permute-done((bf16[144,1024]{1,0:T(8,128)(2,1)S(1)}, bf16[144,1024]{1,0:T(8,128)(2,1)S(1)}, u32[]{:S(2)}, u32[]{:S(2)}) %collective-permute-start.56) | collective-permute-done | bytes 294944 | tf_op jit(solution)/shard_map/ppermute | solution.py:391
  493.7 3.3 collective-permute-start.61
  497.0 3.2 fusion.8
  (348 shorter events, 131.0 us)
Async XLA Ops:
  7.2 178.7 %all-gather.2.cloned.1.call-start = ((), (), s32[]{:S(2)}) async-start(), calls=%async_computation | async-start | bytes 3538944 | tf_op jit(solution)/shard_map/all_gather | solution.py:1094
  25.6 11.9 %collective-permute-start.8 = (bf16[144,1024]{1,0:T(8,128)(2,1)S(1)}, bf16[144,1024]{1,0:T(8,128)(2,1)S(1)}, u32[]{:S(2)}, u32[]{:S(2)}) collective-permute-start(bf16[144,1024]{1,0:T(8,128)(2,1)S(1)} %get-tuple-element.269), channel_id=1, source_target_pairs={{0,8},{4,12},{8,16},{12,20},{16,24},{20,28},{24,0},{28,4},{1,9},{5... | collective-permute-start | bytes 884744 | tf_op jit(solution)/shard_map/ppermute | solution.py:391
  25.6 27.5 %collective-permute-start.9 = (bf16[144,1024]{1,0:T(8,128)(2,1)S(1)}, bf16[144,1024]{1,0:T(8,128)(2,1)S(1)}, u32[]{:S(2)}, u32[]{:S(2)}) collective-permute-start(bf16[144,1024]{1,0:T(8,128)(2,1)S(1)} %get-tuple-element.269), channel_id=1, source_target_pairs={{0,16},{4,20},{8,24},{12,28},{16,0},{20,4},{24,8},{28,12},{1,17},{... | collective-permute-start | bytes 884744 | tf_op jit(solution)/shard_map/ppermute | solution.py:391
  29.9 34.8 %collective-permute-start.6 = (bf16[512,1024]{1,0:T(8,128)(2,1)S(1)}, bf16[512,1024]{1,0:T(8,128)(2,1)S(1)}, u32[]{:S(2)}, u32[]{:S(2)}) collective-permute-start(bf16[512,1024]{1,0:T(8,128)(2,1)S(1)} %bitcast.206), channel_id=1, source_target_pairs={{0,1},{1,0},{2,3},{3,2},{4,5},{5,4},{6,7},{7,6},{8,9},{9,8},{10,11... | collective-permute-start | bytes 3145736 | tf_op jit(solution)/shard_map/ppermute | solution.py:372
  33.7 19.3 %collective-permute-start.10 = (bf16[144,1024]{1,0:T(8,128)(2,1)S(1)}, bf16[144,1024]{1,0:T(8,128)(2,1)S(1)}, u32[]{:S(2)}, u32[]{:S(2)}) collective-permute-start(bf16[144,1024]{1,0:T(8,128)(2,1)S(1)} %get-tuple-element.269), channel_id=1, source_target_pairs={{0,24},{4,28},{8,0},{12,4},{16,8},{20,12},{24,16},{28,20},{1,25},{... | collective-permute-start | bytes 884744 | tf_op jit(solution)/shard_map/ppermute | solution.py:391
  34.5 30.1 %collective-permute-start.13 = (bf16[160,1024]{1,0:T(8,128)(2,1)S(1)}, bf16[160,1024]{1,0:T(8,128)(2,1)S(1)}, u32[]{:S(2)}, u32[]{:S(2)}) collective-permute-start(bf16[160,1024]{1,0:T(8,128)(2,1)S(1)} %pad_maximum_fusion.10), channel_id=1, source_target_pairs={{0,0},{1,4},{2,8},{3,12},{4,16},{5,20},{6,24},{7,28},{8,1},{9,5},{... | collective-permute-start | bytes 983048 | tf_op jit(solution)/shard_map/ppermute | solution.py:1081
  37.5 61.4 %collective-permute-start.7 = (bf16[512,1024]{1,0:T(8,128)(2,1)S(1)}, bf16[512,1024]{1,0:T(8,128)(2,1)}, u32[]{:S(2)}, u32[]{:S(2)}) collective-permute-start(bf16[512,1024]{1,0:T(8,128)(2,1)S(1)} %bitcast.207), channel_id=1, source_target_pairs={{0,2},{1,3},{2,0},{3,1},{4,6},{5,7},{6,4},{7,5},{8,10},{9,11},{10,... | collective-permute-start | bytes 3145736 | tf_op jit(solution)/shard_map/ppermute | solution.py:372
  56.2 50.2 %collective-permute-start.12 = (bf16[4,144,1024]{2,1,0:T(8,128)(2,1)}, bf16[4,144,1024]{2,1,0:T(8,128)(2,1)}, u32[]{:S(2)}, u32[]{:S(2)}) collective-permute-start(bf16[4,144,1024]{2,1,0:T(8,128)(2,1)} %assemble.4.refs_0_), channel_id=1, source_target_pairs={{0,4},{4,0},{8,12},{12,8},{16,20},{20,16},{24,28},{28,24},{1,5},{5... | collective-permute-start | bytes 3538952 | tf_op jit(solution)/shard_map/ppermute | solution.py:372
  64.7 30.4 %collective-permute-start.15 = (bf16[160,1024]{1,0:T(8,128)(2,1)S(1)}, bf16[160,1024]{1,0:T(8,128)(2,1)S(1)}, u32[]{:S(2)}, u32[]{:S(2)}) collective-permute-start(bf16[160,1024]{1,0:T(8,128)(2,1)S(1)} %collective-permute-done.13), channel_id=1, source_target_pairs={{0,16},{4,20},{8,24},{12,28},{16,0},{20,4},{24,8},{28,12},{1,17},{... | collective-permute-start | bytes 983048 | tf_op jit(solution)/shard_map/ppermute | solution.py:391
  67.7 27.4 %collective-permute-start.16 = (bf16[160,1024]{1,0:T(8,128)(2,1)S(1)}, bf16[160,1024]{1,0:T(8,128)(2,1)S(1)}, u32[]{:S(2)}, u32[]{:S(2)}) collective-permute-start(bf16[160,1024]{1,0:T(8,128)(2,1)S(1)} %collective-permute-done.13), channel_id=1, source_target_pairs={{0,24},{4,28},{8,0},{12,4},{16,8},{20,12},{24,16},{28,20},{1,25},{... | collective-permute-start | bytes 983048 | tf_op jit(solution)/shard_map/ppermute | solution.py:391
  98.9 19.6 %collective-permute-start.11 = (bf16[512,1024]{1,0:T(8,128)(2,1)}, bf16[512,1024]{1,0:T(8,128)(2,1)}, u32[]{:S(2)}, u32[]{:S(2)}) collective-permute-start(bf16[512,1024]{1,0:T(8,128)(2,1)} %collective-permute-done.7.x_refs_2_), channel_id=1, source_target_pairs={{0,1},{1,0},{2,3},{3,2},{4,5},{5,4},{6,7},{7,6},{8,9},{9,8},{10,11... | collective-permute-start | bytes 3145736 | tf_op jit(solution)/shard_map/ppermute | solution.py:372
  106.4 25.9 %collective-permute-start.22 = (bf16[512,1024]{1,0:T(8,128)(2,1)S(1)}, bf16[512,1024]{1,0:T(8,128)(2,1)}, u32[]{:S(2)}, u32[]{:S(2)}) collective-permute-start(bf16[512,1024]{1,0:T(8,128)(2,1)S(1)} %bitcast.217), channel_id=1, source_target_pairs={{0,2},{1,3},{2,0},{3,1},{4,6},{5,7},{6,4},{7,5},{8,10},{9,11},{10,... | collective-permute-start | bytes 3145736 | tf_op jit(solution)/shard_map/ppermute | solution.py:372
  107.2 36.6 %collective-permute-start.21 = (bf16[512,1024]{1,0:T(8,128)(2,1)S(1)}, bf16[512,1024]{1,0:T(8,128)(2,1)}, u32[]{:S(2)}, u32[]{:S(2)}) collective-permute-start(bf16[512,1024]{1,0:T(8,128)(2,1)S(1)} %bitcast.218), channel_id=1, source_target_pairs={{0,1},{1,0},{2,3},{3,2},{4,5},{5,4},{6,7},{7,6},{8,9},{9,8},{10,11... | collective-permute-start | bytes 3145736 | tf_op jit(solution)/shard_map/ppermute | solution.py:372
  111.9 43.6 %collective-permute-start.20 = (bf16[4,160,1024]{2,1,0:T(8,128)(2,1)S(1)}, bf16[4,160,1024]{2,1,0:T(8,128)(2,1)S(1)}, u32[]{:S(2)}, u32[]{:S(2)}) collective-permute-start(bf16[4,160,1024]{2,1,0:T(8,128)(2,1)S(1)} %copy-done.7), channel_id=1, source_target_pairs={{0,4},{4,0},{8,12},{12,8},{16,20},{20,16},{24,28},{28,24},{1,5},{5... | collective-permute-start | bytes 3932168 | tf_op jit(solution)/shard_map/ppermute | solution.py:372
  132.3 23.2 %collective-permute-start.23 = (bf16[512,1024]{1,0:T(8,128)(2,1)}, bf16[512,1024]{1,0:T(8,128)(2,1)S(1)}, u32[]{:S(2)}, u32[]{:S(2)}) collective-permute-start(bf16[512,1024]{1,0:T(8,128)(2,1)} %collective-permute-done.22.cot_first_ref), channel_id=1, source_target_pairs={{0,1},{1,0},{2,3},{3,2},{4,5},{5,4},{6,7},{7,6},{8,9},{9,8},{10,11... | collective-permute-start | bytes 3145736 | tf_op jit(solution)/shard_map/ppermute | solution.py:372
  168.7 25.9 %collective-permute-start.27 = (bf16[512,1024]{1,0:T(8,128)(2,1)}, bf16[512,1024]{1,0:T(8,128)(2,1)}, u32[]{:S(2)}, u32[]{:S(2)}) collective-permute-start(bf16[512,1024]{1,0:T(8,128)(2,1)} %add_convert_fusion.6), channel_id=1, source_target_pairs={{0,2},{1,3},{2,0},{3,1},{4,6},{5,7},{6,4},{7,5},{8,10},{9,11},{10,... | collective-permute-start | bytes 3145736 | tf_op jit(solution)/shard_map/ppermute | solution.py:372
  197.8 24.7 %collective-permute-start.30 = (bf16[512,1024]{1,0:T(8,128)(2,1)S(1)}, bf16[512,1024]{1,0:T(8,128)(2,1)S(1)}, u32[]{:S(2)}, u32[]{:S(2)}) collective-permute-start(bf16[512,1024]{1,0:T(8,128)(2,1)S(1)} %multiply_convert_fusion.first_ref), channel_id=1, source_target_pairs={{0,2},{1,3},{2,0},{3,1},{4,6},{5,7},{6,4},{7,5},{8,10},{9,11},{10,... | collective-permute-start | bytes 3145736 | tf_op jit(solution)/shard_map/ppermute | solution.py:372
  244.0 32.4 %collective-permute-start.33 = (bf16[512,1024]{1,0:T(8,128)(2,1)}, bf16[512,1024]{1,0:T(8,128)(2,1)}, u32[]{:S(2)}, u32[]{:S(2)}) collective-permute-start(bf16[512,1024]{1,0:T(8,128)(2,1)} %get-tuple-element.147), channel_id=1, source_target_pairs={{0,1},{1,0},{2,3},{3,2},{4,5},{5,4},{6,7},{7,6},{8,9},{9,8},{10,11... | collective-permute-start | bytes 3145736 | tf_op jit(solution)/shard_map/ppermute | solution.py:372
  249.6 26.8 %collective-permute-start.35 = (bf16[512,1024]{1,0:T(8,128)(2,1)}, bf16[512,1024]{1,0:T(8,128)(2,1)}, u32[]{:S(2)}, u32[]{:S(2)}) collective-permute-start(bf16[512,1024]{1,0:T(8,128)(2,1)} %add_convert_fusion.4), channel_id=1, source_target_pairs={{0,2},{1,3},{2,0},{3,1},{4,6},{5,7},{6,4},{7,5},{8,10},{9,11},{10,... | collective-permute-start | bytes 3145736 | tf_op jit(solution)/shard_map/ppermute | solution.py:372
  274.2 53.5 %collective-permute-start.38 = (bf16[4,192,1536]{2,1,0:T(8,128)(2,1)}, bf16[4,192,1536]{2,1,0:T(8,128)(2,1)}, u32[]{:S(2)}, u32[]{:S(2)}) collective-permute-start(bf16[4,192,1536]{2,1,0:T(8,128)(2,1)} %fusion.4), channel_id=1, source_target_pairs={{0,4},{4,0},{8,12},{12,8},{16,20},{20,16},{24,28},{28,24},{1,5},{5... | collective-permute-start | bytes 7077896 | tf_op jit(solution)/shard_map/ppermute | solution.py:372
  284.6 46.8 %collective-permute-start.36 = (bf16[512,1024]{1,0:T(8,128)(2,1)}, bf16[512,1024]{1,0:T(8,128)(2,1)}, u32[]{:S(2)}, u32[]{:S(2)}) collective-permute-start(bf16[512,1024]{1,0:T(8,128)(2,1)} %get-tuple-element.212.branch_first_ref), channel_id=1, source_target_pairs={{0,2},{1,3},{2,0},{3,1},{4,6},{5,7},{6,4},{7,5},{8,10},{9,11},{10,... | collective-permute-start | bytes 3145736 | tf_op jit(solution)/shard_map/ppermute | solution.py:372
  332.6 80.3 %collective-permute-start.29 = (bf16[512,1024]{1,0:T(8,128)(2,1)}, bf16[512,1024]{1,0:T(8,128)(2,1)}, u32[]{:S(2)}, u32[]{:S(2)}) collective-permute-start(bf16[512,1024]{1,0:T(8,128)(2,1)} %get-tuple-element.139), channel_id=1, source_target_pairs={{0,1},{1,0},{2,3},{3,2},{4,5},{5,4},{6,7},{7,6},{8,9},{9,8},{10,11... | collective-permute-start | bytes 3145736 | tf_op jit(solution)/shard_map/ppermute | solution.py:372
  332.6 25.3 %collective-permute-start.32 = (bf16[512,1024]{1,0:T(8,128)(2,1)}, bf16[512,1024]{1,0:T(8,128)(2,1)S(1)}, u32[]{:S(2)}, u32[]{:S(2)}) collective-permute-start(bf16[512,1024]{1,0:T(8,128)(2,1)} %get-tuple-element.145), channel_id=1, source_target_pairs={{0,1},{1,0},{2,3},{3,2},{4,5},{5,4},{6,7},{7,6},{8,9},{9,8},{10,11... | collective-permute-start | bytes 3145736 | tf_op jit(solution)/shard_map/ppermute | solution.py:372
  335.1 25.8 %collective-permute-start.40 = (bf16[128,1536]{1,0:T(8,128)(2,1)}, bf16[128,1536]{1,0:T(8,128)(2,1)S(1)}, u32[]{:S(2)}, u32[]{:S(2)}) collective-permute-start(bf16[128,1536]{1,0:T(8,128)(2,1)} %get-tuple-element.218), channel_id=1, source_target_pairs={{0,8},{4,12},{8,16},{12,20},{16,24},{20,28},{24,0},{28,4},{1,9},{5... | collective-permute-start | bytes 1179656 | tf_op jit(solution)/shard_map/ppermute | solution.py:391
  335.1 33.4 %collective-permute-start.41 = (bf16[128,1536]{1,0:T(8,128)(2,1)}, bf16[128,1536]{1,0:T(8,128)(2,1)S(1)}, u32[]{:S(2)}, u32[]{:S(2)}) collective-permute-start(bf16[128,1536]{1,0:T(8,128)(2,1)} %get-tuple-element.217), channel_id=1, source_target_pairs={{0,16},{4,20},{8,24},{12,28},{16,0},{20,4},{24,8},{28,12},{1,17},{... | collective-permute-start | bytes 1179656 | tf_op jit(solution)/shard_map/ppermute | solution.py:391
  335.2 33.4 %collective-permute-start.42 = (bf16[128,1536]{1,0:T(8,128)(2,1)}, bf16[128,1536]{1,0:T(8,128)(2,1)}, u32[]{:S(2)}, u32[]{:S(2)}) collective-permute-start(bf16[128,1536]{1,0:T(8,128)(2,1)} %get-tuple-element.216), channel_id=1, source_target_pairs={{0,24},{4,28},{8,0},{12,4},{16,8},{20,12},{24,16},{28,20},{1,25},{... | collective-permute-start | bytes 1179656 | tf_op jit(solution)/shard_map/ppermute | solution.py:391
  358.0 30.8 %collective-permute-start.44 = (bf16[4,64,1024]{2,1,0:T(8,128)(2,1)S(1)}, bf16[4,64,1024]{2,1,0:T(8,128)(2,1)S(1)}, u32[]{:S(2)}, u32[]{:S(2)}) collective-permute-start(bf16[4,64,1024]{2,1,0:T(8,128)(2,1)S(1)} %dynamic-slice_bitcast_fusion), channel_id=1, source_target_pairs={{0,4},{4,0},{8,12},{12,8},{16,20},{20,16},{24,28},{28,24},{1,5},{5... | collective-permute-start | bytes 1572872 | tf_op jit(solution)/shard_map/ppermute | solution.py:372
  369.4 22.9 %collective-permute-start.45 = (bf16[64,1536]{1,0:T(8,128)(2,1)S(1)}, bf16[64,1536]{1,0:T(8,128)(2,1)S(1)}, u32[]{:S(2)}, u32[]{:S(2)}) collective-permute-start(bf16[64,1536]{1,0:T(8,128)(2,1)S(1)} %get-tuple-element.229), channel_id=1, source_target_pairs={{0,8},{4,12},{8,16},{12,20},{16,24},{20,28},{24,0},{28,4},{1,9},{5... | collective-permute-start | bytes 589832 | tf_op jit(solution)/shard_map/ppermute | solution.py:391
  369.4 22.9 %collective-permute-start.46 = (bf16[64,1536]{1,0:T(8,128)(2,1)S(1)}, bf16[64,1536]{1,0:T(8,128)(2,1)S(1)}, u32[]{:S(2)}, u32[]{:S(2)}) collective-permute-start(bf16[64,1536]{1,0:T(8,128)(2,1)S(1)} %get-tuple-element.228), channel_id=1, source_target_pairs={{0,16},{4,20},{8,24},{12,28},{16,0},{20,4},{24,8},{28,12},{1,17},{... | collective-permute-start | bytes 589832 | tf_op jit(solution)/shard_map/ppermute | solution.py:391
  373.5 18.8 %collective-permute-start.47 = (bf16[64,1536]{1,0:T(8,128)(2,1)S(1)}, bf16[64,1536]{1,0:T(8,128)(2,1)S(1)}, u32[]{:S(2)}, u32[]{:S(2)}) collective-permute-start(bf16[64,1536]{1,0:T(8,128)(2,1)S(1)} %get-tuple-element.227), channel_id=1, source_target_pairs={{0,24},{4,28},{8,0},{12,4},{16,8},{20,12},{24,16},{28,20},{1,25},{... | collective-permute-start | bytes 589832 | tf_op jit(solution)/shard_map/ppermute | solution.py:391
  388.8 24.4 %collective-permute-start.43 = (bf16[512,1024]{1,0:T(8,128)(2,1)}, bf16[512,1024]{1,0:T(8,128)(2,1)}, u32[]{:S(2)}, u32[]{:S(2)}) collective-permute-start(bf16[512,1024]{1,0:T(8,128)(2,1)} %add_convert_fusion.5), channel_id=1, source_target_pairs={{0,2},{1,3},{2,0},{3,1},{4,6},{5,7},{6,4},{7,5},{8,10},{9,11},{10,... | collective-permute-start | bytes 3145736 | tf_op jit(solution)/shard_map/ppermute | solution.py:372
  408.1 8.4 %collective-permute-start.49 = (bf16[512,1024]{1,0:T(8,128)(2,1)S(1)}, bf16[512,1024]{1,0:T(8,128)(2,1)S(1)}, u32[]{:S(2)}, u32[]{:S(2)}) collective-permute-start(bf16[512,1024]{1,0:T(8,128)(2,1)S(1)} %convolution_convert_fusion.1), channel_id=1, source_target_pairs={{0,1},{1,0},{2,3},{3,2},{4,5},{5,4},{6,7},{7,6},{8,9},{9,8},{10,11... | collective-permute-start | bytes 3145736 | tf_op jit(solution)/shard_map/ppermute | solution.py:372
  410.4 38.9 %collective-permute-start.51 = (bf16[4,144,1024]{2,1,0:T(8,128)(2,1)}, bf16[4,144,1024]{2,1,0:T(8,128)(2,1)}, u32[]{:S(2)}, u32[]{:S(2)}) collective-permute-start(bf16[4,144,1024]{2,1,0:T(8,128)(2,1)} %fusion.18), channel_id=1, source_target_pairs={{0,4},{4,0},{8,12},{12,8},{16,20},{20,16},{24,28},{28,24},{1,5},{5... | collective-permute-start | bytes 3538952 | tf_op jit(solution)/shard_map/ppermute | solution.py:372
  418.8 71.9 %collective-permute-start.50 = (bf16[512,1024]{1,0:T(8,128)(2,1)}, bf16[512,1024]{1,0:T(8,128)(2,1)}, u32[]{:S(2)}, u32[]{:S(2)}) collective-permute-start(bf16[512,1024]{1,0:T(8,128)(2,1)} %add_convert_fusion.2), channel_id=1, source_target_pairs={{0,2},{1,3},{2,0},{3,1},{4,6},{5,7},{6,4},{7,5},{8,10},{9,11},{10,... | collective-permute-start | bytes 3145736 | tf_op jit(solution)/shard_map/ppermute | solution.py:372
  425.4 17.8 %collective-permute-start.63 = (bf16[32,1536]{1,0:T(8,128)(2,1)S(1)}, bf16[32,1536]{1,0:T(8,128)(2,1)S(1)}, u32[]{:S(2)}, u32[]{:S(2)}) collective-permute-start(bf16[32,1536]{1,0:T(8,128)(2,1)S(1)} %get-tuple-element.241), channel_id=1, source_target_pairs={{0,2},{1,3},{2,0},{3,1},{4,6},{5,7},{6,4},{7,5},{8,10},{9,11},{10,... | collective-permute-start | bytes 294920 | tf_op jit(solution)/shard_map/ppermute | solution.py:372
  425.4 22.7 %collective-permute-start.64 = (bf16[32,1536]{1,0:T(8,128)(2,1)S(1)}, bf16[32,1536]{1,0:T(8,128)(2,1)S(1)}, u32[]{:S(2)}, u32[]{:S(2)}) collective-permute-start(bf16[32,1536]{1,0:T(8,128)(2,1)S(1)} %get-tuple-element.240), channel_id=1, source_target_pairs={{0,3},{1,2},{2,1},{3,0},{4,7},{5,6},{6,5},{7,4},{8,11},{9,10},{10,... | collective-permute-start | bytes 294920 | tf_op jit(solution)/shard_map/ppermute | solution.py:372
  427.2 28.4 %collective-permute-start.52 = (bf16[64,1024]{1,0:T(8,128)(2,1)S(1)}, bf16[64,1024]{1,0:T(8,128)(2,1)S(1)}, u32[]{:S(2)}, u32[]{:S(2)}) collective-permute-start(bf16[64,1024]{1,0:T(8,128)(2,1)S(1)} %get-tuple-element.233), channel_id=1, source_target_pairs={{0,8},{4,12},{8,16},{12,20},{16,24},{20,28},{24,0},{28,4},{1,9},{5... | collective-permute-start | bytes 393224 | tf_op jit(solution)/shard_map/ppermute | solution.py:391
  443.2 13.1 %collective-permute-start.53 = (bf16[64,1024]{1,0:T(8,128)(2,1)S(1)}, bf16[64,1024]{1,0:T(8,128)(2,1)S(1)}, u32[]{:S(2)}, u32[]{:S(2)}) collective-permute-start(bf16[64,1024]{1,0:T(8,128)(2,1)S(1)} %get-tuple-element.232), channel_id=1, source_target_pairs={{0,16},{4,20},{8,24},{12,28},{16,0},{20,4},{24,8},{28,12},{1,17},{... | collective-permute-start | bytes 393224 | tf_op jit(solution)/shard_map/ppermute | solution.py:391
  448.1 8.3 %collective-permute-start.54 = (bf16[64,1024]{1,0:T(8,128)(2,1)S(1)}, bf16[64,1024]{1,0:T(8,128)(2,1)S(1)}, u32[]{:S(2)}, u32[]{:S(2)}) collective-permute-start(bf16[64,1024]{1,0:T(8,128)(2,1)S(1)} %get-tuple-element.231), channel_id=1, source_target_pairs={{0,24},{4,28},{8,0},{12,4},{16,8},{20,12},{24,16},{28,20},{1,25},{... | collective-permute-start | bytes 393224 | tf_op jit(solution)/shard_map/ppermute | solution.py:391
  449.4 18.5 %collective-permute-start.65 = (bf16[96,1024]{1,0:T(8,128)(2,1)S(1)}, bf16[96,1024]{1,0:T(8,128)(2,1)S(1)}, u32[]{:S(2)}, u32[]{:S(2)}) collective-permute-start(bf16[96,1024]{1,0:T(8,128)(2,1)S(1)} %copy-done.33), channel_id=1, source_target_pairs={{0,0},{4,1},{8,2},{12,3},{16,4},{20,5},{24,6},{28,7},{1,8},{5,9},{... | collective-permute-start | bytes 589832 | tf_op jit(solution)/shard_map/ppermute | solution.py:1251
  455.6 41.4 %collective-permute-start.48 = (bf16[512,1024]{1,0:T(8,128)(2,1)S(1)}, bf16[512,1024]{1,0:T(8,128)(2,1)S(1)}, u32[]{:S(2)}, u32[]{:S(2)}) collective-permute-start(bf16[512,1024]{1,0:T(8,128)(2,1)S(1)} %copy-done.52), channel_id=1, source_target_pairs={{0,1},{1,0},{2,3},{3,2},{4,5},{5,4},{6,7},{7,6},{8,9},{9,8},{10,11... | collective-permute-start | bytes 3145736 | tf_op jit(solution)/shard_map/ppermute | solution.py:372
  456.4 18.1 %collective-permute-start.55 = (bf16[144,1024]{1,0:T(8,128)(2,1)S(1)}, bf16[144,1024]{1,0:T(8,128)(2,1)S(1)}, u32[]{:S(2)}, u32[]{:S(2)}) collective-permute-start(bf16[144,1024]{1,0:T(8,128)(2,1)S(1)} %get-tuple-element.222), channel_id=1, source_target_pairs={{0,8},{4,12},{8,16},{12,20},{16,24},{20,28},{24,0},{28,4},{1,9},{5... | collective-permute-start | bytes 884744 | tf_op jit(solution)/shard_map/ppermute | solution.py:391
  459.2 31.5 %collective-permute-start.56 = (bf16[144,1024]{1,0:T(8,128)(2,1)S(1)}, bf16[144,1024]{1,0:T(8,128)(2,1)S(1)}, u32[]{:S(2)}, u32[]{:S(2)}) collective-permute-start(bf16[144,1024]{1,0:T(8,128)(2,1)S(1)} %get-tuple-element.221), channel_id=1, source_target_pairs={{0,16},{4,20},{8,24},{12,28},{16,0},{20,4},{24,8},{28,12},{1,17},{... | collective-permute-start | bytes 884744 | tf_op jit(solution)/shard_map/ppermute | solution.py:391
  467.9 22.8 %collective-permute-start.57 = (bf16[144,1024]{1,0:T(8,128)(2,1)S(1)}, bf16[144,1024]{1,0:T(8,128)(2,1)S(1)}, u32[]{:S(2)}, u32[]{:S(2)}) collective-permute-start(bf16[144,1024]{1,0:T(8,128)(2,1)S(1)} %get-tuple-element.220), channel_id=1, source_target_pairs={{0,24},{4,28},{8,0},{12,4},{16,8},{20,12},{24,16},{28,20},{1,25},{... | collective-permute-start | bytes 884744 | tf_op jit(solution)/shard_map/ppermute | solution.py:391
  491.0 11.0 %collective-permute-start.58 = (bf16[48,1024]{1,0:T(8,128)(2,1)S(1)}, bf16[48,1024]{1,0:T(8,128)(2,1)S(1)}, u32[]{:S(2)}, u32[]{:S(2)}) collective-permute-start(bf16[48,1024]{1,0:T(8,128)(2,1)S(1)} %get-tuple-element.250), channel_id=1, source_target_pairs={{0,1},{1,0},{2,3},{3,2},{4,5},{5,4},{6,7},{7,6},{8,9},{9,8},{10,11... | collective-permute-start | bytes 294920 | tf_op jit(solution)/shard_map/ppermute | solution.py:372
  491.9 10.1 %collective-permute-start.59 = (bf16[48,1024]{1,0:T(8,128)(2,1)S(1)}, bf16[48,1024]{1,0:T(8,128)(2,1)S(1)}, u32[]{:S(2)}, u32[]{:S(2)}) collective-permute-start(bf16[48,1024]{1,0:T(8,128)(2,1)S(1)} %get-tuple-element.251), channel_id=1, source_target_pairs={{0,2},{1,3},{2,0},{3,1},{4,6},{5,7},{6,4},{7,5},{8,10},{9,11},{10,... | collective-permute-start | bytes 294920 | tf_op jit(solution)/shard_map/ppermute | solution.py:372
  491.9 10.1 %collective-permute-start.60 = (bf16[48,1024]{1,0:T(8,128)(2,1)S(1)}, bf16[48,1024]{1,0:T(8,128)(2,1)S(1)}, u32[]{:S(2)}, u32[]{:S(2)}) collective-permute-start(bf16[48,1024]{1,0:T(8,128)(2,1)S(1)} %get-tuple-element.252), channel_id=1, source_target_pairs={{0,3},{1,2},{2,1},{3,0},{4,7},{5,6},{6,5},{7,4},{8,11},{9,10},{10,... | collective-permute-start | bytes 294920 | tf_op jit(solution)/shard_map/ppermute | solution.py:372
  493.7 11.2 %collective-permute-start.61 = (bf16[64,1024]{1,0:T(8,128)(2,1)S(1)}, bf16[64,1024]{1,0:T(8,128)(2,1)S(1)}, u32[]{:S(2)}, u32[]{:S(2)}) collective-permute-start(bf16[64,1024]{1,0:T(8,128)(2,1)S(1)} %add_convert_fusion.10), channel_id=1, source_target_pairs={{0,0},{4,1},{8,2},{12,3},{16,4},{20,5},{24,6},{28,7},{1,8},{5,9},{... | collective-permute-start | bytes 393224 | tf_op jit(solution)/shard_map/ppermute | solution.py:1250
  (84 other events, 709.8 us)
Sparse Core Ops, SparseCore 0:
  95.3 77.2 all-gather.1
